TPU v7x, 32 devices: a whole 2x2x4 slice. The times are simulated.
32 devices in a mesh: subj: 4 (over y, x), slab: 8 (over z, core).
Axes of the slice: x: 2, y: 2, z: 4, core: 2. Of those that a mesh axis runs over, the one named last changes fastest.
Arguments:
- template: float32 [4096, 128], P('slab'), may hold values from -6 to 6
- images: float32 [4, 4096, 128], P('subj', 'slab'), may hold values from -6 to 6
- velocity: float32 [4, 3, 4096, 128], P('subj', None, 'slab'), may hold values from -6 to 6
- stiffness: float32 [4096, 128], P('slab'), may hold values from 0.1 to 1
- send_rows: int32 [4, 8, 8, 64], P('subj', 'slab'), may hold values from 0 to 511, as said below
- ref_slot: int32 [4, 4096, 8], P('subj', 'slab'), may hold values from 0 to 511, as said below
- columns: int32 [4, 4096, 8, 128], P('subj', 'slab'), may hold values from 0 to 127, as said below
- weights: bfloat16 [4, 4096, 8, 128], P('subj', 'slab'), may hold values from 0 to 0.25
Outputs:
- template_out: float32 [4096, 128], P('slab')
- velocity_out: float32 [4, 3, 4096, 128], P('subj', None, 'slab')
Inputs may be any that keep to these rules, and one draw needn't show every extreme that they name: `send_rows`: local rows of the owner slab. `ref_slot`: for each subject and each owner k and destination slab j, the referenced c lie below a count of that pair between 32 and 64; for each subject one destination slab has the count 64 from every owner. columns[s, g, b, x] differs from x by at most 2.
All inputs are finite; a program needn't handle non-finite values.
Results may differ from a plain program's by a relative error of at most 0.0003.
Values sent between devices are 32-bit elements; how exact they have to be, the bound alone decides.
No kernel may reach another device: no remote copies, remote signals or barrier semaphores. Data moves between devices by JAX's collectives and lax.ppermute only.
A program may use at most 64 MiB of HBM per device.

v0:
```python
import jax
import jax.numpy as jnp
from jax import lax
from jax.sharding import PartitionSpec as P

YR = 256
SMOOTH = 2


force_step = 1.0
diffusion_dt = 0.16
template_rate = 2.0


def extended(cells, sides, width):
    for axis, dim in sides:
        count = lax.axis_size(axis)
        ends = count - 1
        head = lax.slice_in_dim(cells, 0, width, axis=dim)
        tail = lax.slice_in_dim(cells, cells.shape[dim] - width, cells.shape[dim], axis=dim)
        cells = jnp.concatenate(
            [
                lax.ppermute(tail, axis, [(i, (i + 1) % count) for i in range(ends)]),
                cells,
                lax.ppermute(head, axis, [((i + 1) % count, i) for i in range(ends)]),
            ],
            axis=dim,
        )
    return cells


def smooth_step(field_padded, coef_padded):
    center = field_padded[:, 1:-1]
    coef_center = coef_padded[1:-1]
    field_yx = jnp.pad(center, ((0, 0), (0, 0), (1, 1), (1, 1)))
    coef_yx = jnp.pad(coef_center, ((0, 0), (1, 1), (1, 1)))
    pairs = [
        (field_padded[:, 2:], coef_padded[2:]),
        (field_padded[:, :-2], coef_padded[:-2]),
        (field_yx[:, :, 2:, 1:-1], coef_yx[:, 2:, 1:-1]),
        (field_yx[:, :, :-2, 1:-1], coef_yx[:, :-2, 1:-1]),
        (field_yx[:, :, 1:-1, 2:], coef_yx[:, 1:-1, 2:]),
        (field_yx[:, :, 1:-1, :-2], coef_yx[:, 1:-1, :-2]),
    ]
    summed = jnp.zeros(center.shape, jnp.float32)
    for neighbour, coef_near in pairs:
        face_coef = 0.5 * (coef_center + coef_near)
        summed = summed + face_coef[None] * (neighbour - center)
    return center + diffusion_dt * summed


def read_ahead(values, offset):
    if offset > 0:
        return jnp.concatenate(
            [values[..., offset:], jnp.zeros(values.shape[:-1] + (offset,), values.dtype)], axis=-1
        )
    if offset < 0:
        return jnp.concatenate(
            [jnp.zeros(values.shape[:-1] + (-offset,), values.dtype), values[..., :offset]], axis=-1
        )
    return values


def per_device(template, images, velocity, stiffness, send_rows, ref_slot, columns, weights):
    slabs = lax.axis_size("slab")
    subjects = lax.axis_size("subj")
    capacity = send_rows.shape[3]
    rows = template.shape[0]
    width = template.shape[1]
    planes = rows // YR
    send_one = send_rows[0, 0]
    sending = template[send_one]
    received = lax.all_to_all(sending, "slab", split_axis=0, concat_axis=0, tiled=True)
    flat_rows = received.reshape(slabs * capacity, width)
    slot_one = ref_slot[0]
    offset_one = columns[0] - jnp.arange(width, dtype=jnp.int32)
    picked = flat_rows[slot_one]
    weight_f = weights[0].astype(jnp.float32)
    values = jnp.zeros(picked.shape, jnp.float32)
    for offset in range(-2, 3):
        values = values + jnp.where(offset_one == offset, read_ahead(picked, offset), 0.0)
    warped = jnp.sum(weight_f * values, axis=1)
    mismatch = warped - images[0]
    contrib = weight_f * mismatch[:, None, :]
    placed = jnp.zeros(contrib.shape, jnp.float32)
    for offset in range(-2, 3):
        placed = placed + read_ahead(jnp.where(offset_one == offset, contrib, 0.0), -offset)
    slot_grad = (
        jnp.zeros((slabs * capacity, width), jnp.float32)
        .at[slot_one.reshape(-1)]
        .add(placed.reshape(-1, width))
    )
    slot_grad = slot_grad.reshape(slabs, capacity, width)
    returned = lax.all_to_all(slot_grad, "slab", split_axis=0, concat_axis=0, tiled=True)
    row_grad = (
        jnp.zeros((rows, width), jnp.float32)
        .at[send_one.reshape(-1)]
        .add(returned.reshape(-1, width))
    )
    summed = lax.psum(row_grad, "subj")
    template_out = template - template_rate * summed / subjects
    warped_grid = warped.reshape(planes, YR, width)
    warped_padded = extended(warped_grid, (("slab", 0),), 1)
    warped_yx = jnp.pad(warped_grid, ((0, 0), (1, 1), (1, 1)))
    along_x = 0.5 * (warped_yx[:, 1:-1, 2:] - warped_yx[:, 1:-1, :-2])
    along_y = 0.5 * (warped_yx[:, 2:, 1:-1] - warped_yx[:, :-2, 1:-1])
    along_z = 0.5 * (warped_padded[2:] - warped_padded[:-2])
    slopes = jnp.stack([along_x, along_y, along_z])
    field = (
        velocity[0].reshape(3, planes, YR, width)
        - force_step * mismatch.reshape(planes, YR, width)[None] * slopes
    )
    coef_grid = stiffness.reshape(planes, YR, width)
    coef_padded = extended(coef_grid, (("slab", 0),), 1)
    for repeat in range(SMOOTH):
        field_padded = extended(field, (("slab", 1),), 1)
        field = smooth_step(field_padded, coef_padded)
    velocity_out = field.reshape(3, rows, width)[None]
    return (template_out, velocity_out)


def solution(mesh):
    return jax.shard_map(
        per_device,
        mesh=mesh,
        in_specs=(
            P("slab", None),
            P("subj", "slab", None),
            P("subj", None, "slab", None),
            P("slab", None),
            P("subj", "slab", None, None),
            P("subj", "slab", None),
            P("subj", "slab", None, None),
            P("subj", "slab", None, None),
        ),
        out_specs=(P("slab", None), P("subj", None, "slab", None)),
        check_vma=False,
    )
```

profile of v0, /device:TPU:0, one launch (start us, length us, event | category | flops | bytes accessed | tf_op | source)
XLA Modules:
  0.0 150.6 jit_solution(5364139183156494013)
XLA Ops:
  8.0 2.6 %gather_fusion = f32[512,128]{1,0:T(8,128)} fusion(f32[512,128]{1,0:T(8,128)} %param.8, s32[1024]{0:T(1024)S(1)} %pad_clamp_fusion), kind=kCustom, calls=%fused_computation | custom fusion | bytes 526336 | tf_op jit(solution)/shard_map/gather | solution.py:72
  10.6 6.3 %all-to-all-start = ((f32[8,64,128]{2,1,0:T(8,128)}), f32[8,64,128]{2,1,0:T(8,128)S(1)}, u32[]{:S(2)}, u32[]{:S(2)}) async-start(f32[8,64,128]{2,1,0:T(8,128)} %bitcast.6), calls=%async_computation | async-start | bytes 524288 | tf_op jit(solution)/shard_map/all_to_all | solution.py:73
  17.7 1.3 collective-permute-start.2
  19.0 3.7 %collective-permute-start.4 = (f32[1,256,128]{2,1,0:T(8,128)}, f32[1,256,128]{2,1,0:T(8,128)}, u32[]{:S(2)}, u32[]{:S(2)}) collective-permute-start(f32[1,256,128]{2,1,0:T(8,128)} %get-tuple-element.27), channel_id=1, source_target_pairs={{0,1},{1,2},{2,3},{3,4},{4,5},{5,6},{6,7},{8,9},{9,10},{10,11},{11... | collective-permute-start | bytes 393224 | tf_op jit(solution)/shard_map/ppermute | solution.py:23
  24.0 2.8 %all-to-all-done = f32[8,64,128]{2,1,0:T(8,128)S(1)} async-done(((f32[8,64,128]{2,1,0:T(8,128)}), f32[8,64,128]{2,1,0:T(8,128)S(1)}, u32[]{:S(2)}, u32[]{:S(2)}) %all-to-all-start) | async-done | bytes 262176 | tf_op jit(solution)/shard_map/all_to_all | solution.py:73
  26.8 10.8 %gather_fusion.1 = f32[4096,128]{1,0:T(8,128)S(1)} fusion(f32[512,128]{1,0:T(8,128)S(1)} %bitcast.66, s32[4096]{0:T(1024)S(1)} %broadcast_clamp_fusion), kind=kCustom, calls=%fused_computation.1 | custom fusion | bytes 4210688 | tf_op jit(solution)/shard_map/gather | solution.py:77
  40.2 3.9 %fusion = (f32[512,128]{1,0:T(8,128)S(1)}, pred[512,8,128]{2,1,0:T(8,128)(4,1)S(1)}, pred[512,8,128]{2,1,0:T(8,128)(4,1)S(1)}, pred[512,8,128]{2,1,0:T(8,128)(4,...) fusion(f32[512,8,126]{2,1,0:T(8,128)S(1)} %get-tuple-element.13, ...), kind=kLoop, calls=%fused_computation.14 | loop fusion | flops 9371648 | bytes 16416768 | tf_op jit(solution)/shard_map/reduce_sum | solution.py:82
  44.8 1.3 collective-permute-start
  46.1 3.7 %collective-permute-start.1 = (f32[1,256,128]{2,1,0:T(8,128)}, f32[1,256,128]{2,1,0:T(8,128)}, u32[]{:S(2)}, u32[]{:S(2)}) collective-permute-start(f32[1,256,128]{2,1,0:T(8,128)} %get-tuple-element.33), channel_id=1, source_target_pairs={{0,1},{1,2},{2,3},{3,4},{4,5},{5,6},{6,7},{8,9},{9,10},{10,11},{11... | collective-permute-start | bytes 393224 | tf_op jit(solution)/shard_map/ppermute | solution.py:23
  50.5 2.6 %slice_select_fusion.2 = (f32[512,8,127]{2,1,0:T(8,128)S(1)}, f32[512,8,127]{2,1,0:T(8,128)}) fusion(f32[512,8,128]{2,1,0:T(8,128)S(1)} %convert_multiply_fusion, pred[512,8,128]{2,1,0:T(8,128)(4,1)S(1)} %get-tuple-element.4, pred[512,8,128]{2,1,0:T(8,128)(4,1)S(1)} %get-tuple-element.6), kind=kLoop, calls=%fused_computation.17 | loop fusion | flops 1040384 | bytes 9363456 | tf_op jit(solution)/shard_map/jit(_where)/select_n | solution.py:87
  53.2 3.2 %slice_select_fusion.3 = (f32[512,8,126]{2,1,0:T(8,128)}, f32[512,8,126]{2,1,0:T(8,128)}) fusion(f32[512,8,128]{2,1,0:T(8,128)S(1)} %convert_multiply_fusion, pred[512,8,128]{2,1,0:T(8,128)(4,1)S(1)} %get-tuple-element.3, pred[512,8,128]{2,1,0:T(8,128)(4,1)S(1)} %get-tuple-element.7), kind=kLoop, calls=%fused_computation.18 | loop fusion | flops 1032192 | bytes 9289728 | tf_op jit(solution)/shard_map/jit(_where)/select_n | solution.py:87
  56.3 23.1 %scatter_custom_fusion = f32[512,128]{1,0:T(8,128)} fusion(s32[4096]{0:T(1024)S(1)} %bitcast.75, f32[512,8,126]{2,1,0:T(8,128)} %get-tuple-element.9, f32[]{:T(128)} %constant.9.clone.1, f32[512,8,127]{2,1,0:T(8,128)} %get-tuple-element.11, pred[512,8,128]{2,1,0:T(8,128)(4,1)} %get-tuple-element.5, f32[512,8,127]{2,1,0:T(8,128)S(1)} %get-tuple-element.10, ...), kind=kCustom, calls=%fused_computation.19 | custom fusion | flops 4194304 | bytes 10487296 | tf_op jit(solution)/shard_map/scatter-add | solution.py:91
  79.4 4.2 %all-to-all-start.1 = ((f32[8,64,128]{2,1,0:T(8,128)}), f32[8,64,128]{2,1,0:T(8,128)}, u32[]{:S(2)}, u32[]{:S(2)}) async-start(f32[8,64,128]{2,1,0:T(8,128)} %bitcast.71), calls=%async_computation.1 | async-start | bytes 524288 | tf_op jit(solution)/shard_map/all_to_all | solution.py:94
  83.7 1.2 fusion.90
  85.1 1.3 collective-permute-start.3
  86.4 3.8 %collective-permute-start.5 = (f32[3,1,256,128]{3,2,1,0:T(8,128)S(1)}, f32[3,1,256,128]{3,2,1,0:T(8,128)}, u32[]{:S(2)}, u32[]{:S(2)}) collective-permute-start(f32[3,1,256,128]{3,2,1,0:T(8,128)S(1)} %get-tuple-element.19), channel_id=1, source_target_pairs={{0,1},{1,2},{2,3},{3,4},{4,5},{5,6},{6,7},{8,9},{9,10},{10,11},{11... | collective-permute-start | bytes 1179656 | tf_op jit(solution)/shard_map/ppermute | solution.py:23
  91.4 2.1 %all-to-all-done.1 = f32[8,64,128]{2,1,0:T(8,128)} async-done(((f32[8,64,128]{2,1,0:T(8,128)}), f32[8,64,128]{2,1,0:T(8,128)}, u32[]{:S(2)}, u32[]{:S(2)}) %all-to-all-start.1) | async-done | bytes 262176 | tf_op jit(solution)/shard_map/all_to_all | solution.py:94
  93.5 3.3 %scatter_custom_fusion.1 = f32[512,128]{1,0:T(8,128)} fusion(s32[512]{0:T(512)S(1)} %bitcast.76, f32[512,128]{1,0:T(8,128)} %bitcast.13, f32[]{:T(128)} %constant.9.clone.1), kind=kCustom, calls=%fused_computation.120 | custom fusion | flops 65536 | bytes 262656 | tf_op jit(solution)/shard_map/scatter-add | solution.py:98
  96.9 1.8 %fusion.25 = f32[3,2,256,128]{3,2,1,0:T(8,128)S(1)} fusion(f32[3,2,256,128]{3,2,1,0:T(8,128)S(1)} %fusion.56, f32[3,1,256,128]{3,2,1,0:T(8,128)} %collective-permute-done.5, f32[3,1,256,128]{3,2,1,0:T(8,128)} %collective-permute-done.3, f32[2,256,128]{2,1,0:T(8,128)S(1)} %get-tuple-element.22, f32[2,256,128]{2,1,0:T(8,128)S(1)} %get-tuple-element.25, ...), kind=kLoop, calls=%fused_computation.52 | loop fusion | flops 4128768 | bytes 3932160 | tf_op jit(solution)/shard_map/add | solution.py:49
  98.7 1.3 collective-permute-start.6
  100.0 3.8 %collective-permute-start.7 = (f32[3,1,256,128]{3,2,1,0:T(8,128)S(1)}, f32[3,1,256,128]{3,2,1,0:T(8,128)}, u32[]{:S(2)}, u32[]{:S(2)}) collective-permute-start(f32[3,1,256,128]{3,2,1,0:T(8,128)S(1)} %get-tuple-element.17), channel_id=1, source_target_pairs={{0,1},{1,2},{2,3},{3,4},{4,5},{5,6},{6,7},{8,9},{9,10},{10,11},{11... | collective-permute-start | bytes 1179656 | tf_op jit(solution)/shard_map/ppermute | solution.py:23
  103.8 35.6 %all-reduce.14.cloned.1.call-done = f32[512,128]{1,0:T(8,128)} async-done(((f32[512,128]{1,0:T(8,128)}), f32[512,128]{1,0:T(8,128)}) %all-reduce.14.cloned.1.call-update) | async-done | bytes 262160 | tf_op jit(solution)/shard_map/psum | solution.py:100
  139.4 1.7 %multiply_subtract_fusion = f32[512,128]{1,0:T(8,128)} fusion(f32[512,128]{1,0:T(8,128)S(1)} %copy-done, f32[512,128]{1,0:T(8,128)} %all-reduce.14.cloned.1.call-done), kind=kLoop, calls=%fused_computation.115 | loop fusion | flops 131072 | bytes 786432 | tf_op jit(solution)/shard_map/sub | solution.py:101
  141.1 2.6 %fusion.39 = f32[3,2,256,128]{3,2,1,0:T(8,128)} fusion(f32[3,2,256,128]{3,2,1,0:T(8,128)S(1)} %fusion.25, f32[3,1,256,128]{3,2,1,0:T(8,128)} %collective-permute-done.7, f32[3,1,256,128]{3,2,1,0:T(8,128)} %collective-permute-done.6, f32[2,256,128]{2,1,0:T(8,128)S(1)} %get-tuple-element.22, f32[2,256,128]{2,1,0:T(8,128)S(1)} %get-tuple-element.25, ...), kind=kLoop, calls=%fused_computation.66 | loop fusion | flops 4128768 | bytes 3932160 | tf_op jit(solution)/shard_map/add | solution.py:49
  (54 shorter events, 8.4 us)
Async XLA Ops:
  7.2 15.8 %copy-start.9 = (s32[1,1,8,64]{3,2,1,0:T(8,128)S(1)}, s32[1,1,8,64]{3,2,1,0:T(8,128)}, u32[]{:S(2)}) copy-start(s32[1,1,8,64]{3,2,1,0:T(8,128)} %param.12) | copy-start | bytes 6148
  7.2 9.8 %copy-start.5 = (f32[512,128]{1,0:T(8,128)S(1)}, f32[512,128]{1,0:T(8,128)}, u32[]{:S(2)}) copy-start(f32[512,128]{1,0:T(8,128)} %param.11) | copy-start | bytes 786436
  7.2 15.5 %copy-start.8 = (s32[1,512,8]{1,2,0:T(8,128)S(1)}, s32[1,512,8]{1,2,0:T(8,128)}, u32[]{:S(2)}) copy-start(s32[1,512,8]{1,2,0:T(8,128)} %param.13) | copy-start | bytes 49156
  10.6 16.2 %all-to-all-start = ((f32[8,64,128]{2,1,0:T(8,128)}), f32[8,64,128]{2,1,0:T(8,128)S(1)}, u32[]{:S(2)}, u32[]{:S(2)}) async-start(f32[8,64,128]{2,1,0:T(8,128)} %bitcast.6), calls=%async_computation | async-start | bytes 524288 | tf_op jit(solution)/shard_map/all_to_all | solution.py:73
  17.7 72.6 %collective-permute-start.2 = (f32[1,256,128]{2,1,0:T(8,128)}, f32[1,256,128]{2,1,0:T(8,128)}, u32[]{:S(2)}, u32[]{:S(2)}) collective-permute-start(f32[1,256,128]{2,1,0:T(8,128)} %get-tuple-element.26), channel_id=1, source_target_pairs={{1,0},{2,1},{3,2},{4,3},{5,4},{6,5},{7,6},{9,8},{10,9},{11,10},{12... | collective-permute-start | bytes 393224 | tf_op jit(solution)/shard_map/ppermute | solution.py:25
  19.0 71.3 %collective-permute-start.4 = (f32[1,256,128]{2,1,0:T(8,128)}, f32[1,256,128]{2,1,0:T(8,128)}, u32[]{:S(2)}, u32[]{:S(2)}) collective-permute-start(f32[1,256,128]{2,1,0:T(8,128)} %get-tuple-element.27), channel_id=1, source_target_pairs={{0,1},{1,2},{2,3},{3,4},{4,5},{5,6},{6,7},{8,9},{9,10},{10,11},{11... | collective-permute-start | bytes 393224 | tf_op jit(solution)/shard_map/ppermute | solution.py:23
  38.2 1.2 copy-start.1
  38.2 1.9 %copy-start.3 = (s32[1,512,8,128]{3,2,1,0:T(8,128)S(1)}, s32[1,512,8,128]{3,2,1,0:T(8,128)}, u32[]{:S(2)}) copy-start(s32[1,512,8,128]{3,2,1,0:T(8,128)} %param.14) | copy-start | bytes 6291460
  40.2 9.6 %copy-start.4 = (f32[1,512,128]{2,1,0:T(8,128)S(1)}, f32[1,512,128]{2,1,0:T(8,128)}, u32[]{:S(2)}) copy-start(f32[1,512,128]{2,1,0:T(8,128)} %param.9) | copy-start | bytes 786436
  44.8 38.8 %collective-permute-start = (f32[1,256,128]{2,1,0:T(8,128)}, f32[1,256,128]{2,1,0:T(8,128)S(1)}, u32[]{:S(2)}, u32[]{:S(2)}) collective-permute-start(f32[1,256,128]{2,1,0:T(8,128)} %get-tuple-element.32), channel_id=1, source_target_pairs={{1,0},{2,1},{3,2},{4,3},{5,4},{6,5},{7,6},{9,8},{10,9},{11,10},{12... | collective-permute-start | bytes 393224 | tf_op jit(solution)/shard_map/ppermute | solution.py:25
  46.1 37.6 %collective-permute-start.1 = (f32[1,256,128]{2,1,0:T(8,128)}, f32[1,256,128]{2,1,0:T(8,128)}, u32[]{:S(2)}, u32[]{:S(2)}) collective-permute-start(f32[1,256,128]{2,1,0:T(8,128)} %get-tuple-element.33), channel_id=1, source_target_pairs={{0,1},{1,2},{2,3},{3,4},{4,5},{5,6},{6,7},{8,9},{9,10},{10,11},{11... | collective-permute-start | bytes 393224 | tf_op jit(solution)/shard_map/ppermute | solution.py:23
  49.8 0.7 copy-start.2
  79.4 5.5 %copy-start.7 = (f32[1,3,512,128]{3,2,1,0:T(8,128)S(1)}, f32[1,3,512,128]{3,2,1,0:T(8,128)}, u32[]{:S(2)}) copy-start(f32[1,3,512,128]{3,2,1,0:T(8,128)} %param.10) | copy-start | bytes 2359300
  79.4 14.1 %all-to-all-start.1 = ((f32[8,64,128]{2,1,0:T(8,128)}), f32[8,64,128]{2,1,0:T(8,128)}, u32[]{:S(2)}, u32[]{:S(2)}) async-start(f32[8,64,128]{2,1,0:T(8,128)} %bitcast.71), calls=%async_computation.1 | async-start | bytes 524288 | tf_op jit(solution)/shard_map/all_to_all | solution.py:94
  83.6 55.8 %all-reduce.14.cloned.1.call-start = ((), (), s32[]{:S(2)}) async-start(), calls=%async_computation.2 | async-start | bytes 524288 | tf_op jit(solution)/shard_map/psum | solution.py:100
  84.9 5.3 %copy-start.10 = (s32[512,1]{0,1:T(1,128)S(1)}, s32[512,1]{0,1:T(1,128)}, u32[]{:S(2)}) copy-start(s32[512,1]{0,1:T(1,128)} %reshape_squeeze.9) | copy-start | bytes 6148
  84.9 5.3 %copy-start.6 = (f32[512,128]{1,0:T(8,128)S(1)}, f32[512,128]{1,0:T(8,128)}, u32[]{:S(2)}) copy-start(f32[512,128]{1,0:T(8,128)} %param.11) | copy-start | bytes 786436
  85.1 11.7 %collective-permute-start.3 = (f32[3,1,256,128]{3,2,1,0:T(8,128)S(1)}, f32[3,1,256,128]{3,2,1,0:T(8,128)}, u32[]{:S(2)}, u32[]{:S(2)}) collective-permute-start(f32[3,1,256,128]{3,2,1,0:T(8,128)S(1)} %get-tuple-element.18), channel_id=1, source_target_pairs={{1,0},{2,1},{3,2},{4,3},{5,4},{6,5},{7,6},{9,8},{10,9},{11,10},{12... | collective-permute-start | bytes 1179656 | tf_op jit(solution)/shard_map/ppermute | solution.py:25
  86.4 10.4 %collective-permute-start.5 = (f32[3,1,256,128]{3,2,1,0:T(8,128)S(1)}, f32[3,1,256,128]{3,2,1,0:T(8,128)}, u32[]{:S(2)}, u32[]{:S(2)}) collective-permute-start(f32[3,1,256,128]{3,2,1,0:T(8,128)S(1)} %get-tuple-element.19), channel_id=1, source_target_pairs={{0,1},{1,2},{2,3},{3,4},{4,5},{5,6},{6,7},{8,9},{9,10},{10,11},{11... | collective-permute-start | bytes 1179656 | tf_op jit(solution)/shard_map/ppermute | solution.py:23
  96.8 42.5 %copy-start = (f32[512,128]{1,0:T(8,128)S(1)}, f32[512,128]{1,0:T(8,128)}, u32[]{:S(2)}) copy-start(f32[512,128]{1,0:T(8,128)} %param.8) | copy-start | bytes 786436
  98.7 42.3 %collective-permute-start.6 = (f32[3,1,256,128]{3,2,1,0:T(8,128)S(1)}, f32[3,1,256,128]{3,2,1,0:T(8,128)}, u32[]{:S(2)}, u32[]{:S(2)}) collective-permute-start(f32[3,1,256,128]{3,2,1,0:T(8,128)S(1)} %get-tuple-element.16), channel_id=1, source_target_pairs={{1,0},{2,1},{3,2},{4,3},{5,4},{6,5},{7,6},{9,8},{10,9},{11,10},{12... | collective-permute-start | bytes 1179656 | tf_op jit(solution)/shard_map/ppermute | solution.py:25
  100.0 41.0 %collective-permute-start.7 = (f32[3,1,256,128]{3,2,1,0:T(8,128)S(1)}, f32[3,1,256,128]{3,2,1,0:T(8,128)}, u32[]{:S(2)}, u32[]{:S(2)}) collective-permute-start(f32[3,1,256,128]{3,2,1,0:T(8,128)S(1)} %get-tuple-element.17), channel_id=1, source_target_pairs={{0,1},{1,2},{2,3},{3,4},{4,5},{5,6},{6,7},{8,9},{9,10},{10,11},{11... | collective-permute-start | bytes 1179656 | tf_op jit(solution)/shard_map/ppermute | solution.py:23
Sparse Core Ops, SparseCore 0:
  96.9 42.3 all-reduce.13
where the time goes:
time: 151 us
  other arithmetic  45.8 us (30%)
  waiting for transfers between devices  40.5 us (27%)
  starting transfers between devices  30.6 us (20%)
  local copies, waits for them, and re-layouts  19.3 us (13%)
  between operations  14.3 us (9%)
    psum x1, waiting for transfers between devices, per_device(): summed = lax.psum(row_grad, 'subj')  35.6 us
    scatter-add x1, other arithmetic, per_device(): slot_grad = jnp.zeros((slabs * capacity, width), jnp.float32).at[slot_one...  23.1 us
    ppermute x4, starting transfers between devices, extended(): lax.ppermute(tail, axis, [(i, (i + 1) % count) for i in range(ends)])  14.9 us
    gather x1, local copies, waits for them, and re-layouts, per_device(): picked = flat_rows[slot_one]  10.8 us
    all_to_all x1, starting transfers between devices, per_device(): lax.all_to_all(sending, 'slab', split_axis=0, concat_axis=0, tiled=True)  6.33 us
    select_n x2, other arithmetic, per_device(): jnp.where(offset_one == offset, contrib, 0.0)  5.79 us
    ppermute x4, starting transfers between devices, extended(): lax.ppermute(head, axis, [((i + 1) % count, i) for i in range(ends)])  5.14 us
    add x2, other arithmetic, smooth_step(): return center + diffusion_dt * summed  4.45 us
  transfers between devices with their start and end apart: 11, of which 3 were waited for; matrix products, arithmetic and copies ran while one was open for 38% of the time, Pallas kernels for 0%

commit v1 on v0

--- a/solution.py
+++ b/solution.py
@@ -1,15 +1,178 @@
+import functools
+
 import jax
 import jax.numpy as jnp
 from jax import lax
+from jax.experimental import pallas as pl
+from jax.experimental.pallas import tpu as pltpu
 from jax.sharding import PartitionSpec as P
 
 YR = 256
 SMOOTH = 2
+LANES = 128
 
 
 force_step = 1.0
 diffusion_dt = 0.16
 template_rate = 2.0
+
+VMEM_LIMIT = 48 * 1024 * 1024
+
+
+def call(kernel, out_shape, *args, scratch=()):
+    return pl.pallas_call(
+        kernel,
+        out_shape=out_shape,
+        scratch_shapes=scratch,
+        compiler_params=pltpu.CompilerParams(vmem_limit_bytes=VMEM_LIMIT),
+    )(*args)
+
+
+def halves(values):
+    high = values.astype(jnp.bfloat16)
+    low = (values - high.astype(jnp.float32)).astype(jnp.bfloat16)
+    return jnp.concatenate([high, low], axis=1)
+
+
+def joined(pair):
+    width = pair.shape[1] // 2
+    return pair[:, :width] + pair[:, width:]
+
+
+def dot(left, right):
+    return jnp.dot(left, right, preferred_element_type=jnp.float32)
+
+
+def one_hot(matches):
+    return jnp.where(matches, 1.0, 0.0).astype(jnp.bfloat16)
+
+
+def send_kernel(send_ref, template_ref, out_ref):
+    slabs, capacity = send_ref.shape
+    rows = template_ref.shape[0]
+    pair = halves(template_ref[...])
+    padded = jnp.concatenate(
+        [send_ref[...], jnp.zeros((slabs, LANES - capacity), jnp.int32)], axis=1
+    )
+    turned = padded.T
+    number = lax.broadcasted_iota(jnp.int32, (capacity, rows), 1)
+    for k in range(slabs):
+        wanted = jnp.broadcast_to(turned[:capacity, k : k + 1], (capacity, rows))
+        out_ref[k * capacity : (k + 1) * capacity, :] = joined(dot(one_hot(wanted == number), pair))
+
+
+def pick_kernel(step, wide_ref, flat_ref, pick_ref, drop_ref):
+    terms, slots = pick_ref.shape
+    lane = lax.broadcasted_iota(jnp.int32, (step, LANES), 1)
+    row = lax.broadcasted_iota(jnp.int32, (slots, step), 0)
+
+    def body(i, carry):
+        at = pl.multiple_of(i * step, step)
+        wide = wide_ref[pl.ds(at, step), :]
+        for t in range(slots // LANES):
+            pick_ref[pl.ds(at, step), t * LANES : (t + 1) * LANES] = one_hot(wide == lane + t * LANES)
+        flat = jnp.broadcast_to(flat_ref[:, pl.ds(at, step)], (slots, step))
+        drop_ref[:, pl.ds(at, step)] = one_hot(flat == row)
+        return carry
+
+    lax.fori_loop(0, terms // step, body, 0)
+
+
+def warp_kernel(
+    step,
+    subjects,
+    received_ref,
+    pick_ref,
+    drop_ref,
+    columns_ref,
+    weights_ref,
+    images_ref,
+    warped_ref,
+    sent_ref,
+    total_ref,
+):
+    terms, slots = pick_ref.shape
+    rows, width = images_ref.shape
+    each = terms // rows
+    step_rows = step // each
+    pair = halves(received_ref[...])
+    total_ref[...] = jnp.zeros_like(total_ref)
+    cell = lax.broadcasted_iota(jnp.int32, (step, width), 1)
+
+    def body(i, carry):
+        at = pl.multiple_of(i * step, step)
+        at_row = pl.multiple_of(i * step_rows, step_rows)
+        picked = joined(dot(pick_ref[pl.ds(at, step), :], pair))
+        columns = columns_ref[pl.ds(at, step), :]
+        weights = weights_ref[pl.ds(at, step), :].astype(jnp.float32)
+        values = weights * jnp.take_along_axis(picked, columns, axis=1, mode="promise_in_bounds")
+        warped = jnp.sum(values.reshape(step_rows, each, width), axis=1)
+        warped_ref[pl.ds(at_row, step_rows), :] = warped
+        mismatch = warped - images_ref[pl.ds(at_row, step_rows), :]
+        spread = jnp.broadcast_to(mismatch[:, None, :], (step_rows, each, width)).reshape(step, width)
+        contrib = weights * spread
+        offset = columns - cell
+        placed = jnp.where(offset == 0, contrib, 0.0)
+        for o in (-2, -1, 1, 2):
+            placed = placed + pltpu.roll(jnp.where(offset == o, contrib, 0.0), o % width, axis=1)
+        total_ref[...] += dot(drop_ref[:, pl.ds(at, step)], halves(placed))
+        return carry
+
+    lax.fori_loop(0, terms // step, body, 0)
+    block = width // subjects
+    group = slots // subjects
+    place = lax.broadcasted_iota(jnp.int32, (group, width), 1) // block
+    groups = [joined(total_ref[q * group : (q + 1) * group, :]) for q in range(subjects)]
+    for p in range(subjects):
+        out = jnp.zeros((group, width), jnp.float32)
+        for q in range(subjects):
+            turn = ((q - p) * block) % width
+            moved = pltpu.roll(groups[q], turn, axis=1) if turn else groups[q]
+            out = jnp.where(place == q, moved, out)
+        sent_ref[p * group : (p + 1) * group, :] = out
+
+
+def collect_kernel(subjects, index_ref, returned_ref, out_ref):
+    slots, width = returned_ref.shape
+    rows = out_ref.shape[0] * subjects
+    block = width // subjects
+    pair = halves(returned_ref[...])
+    number = lax.broadcasted_iota(jnp.int32, (rows, slots), 0)
+    place = lax.broadcasted_iota(jnp.int32, (rows, width), 1) // block
+    kept = jnp.zeros((rows, width), jnp.float32)
+    for q in range(subjects):
+        wanted = jnp.broadcast_to(index_ref[q : q + 1, :], (rows, slots))
+        kept = jnp.where(place == q, joined(dot(one_hot(wanted == number), pair)), kept)
+    turn = block
+    while turn < width:
+        kept = kept + pltpu.roll(kept, turn, axis=1)
+        turn *= 2
+    part = rows // subjects
+    out = jnp.zeros((part, width), jnp.float32)
+    for p in range(subjects):
+        out = jnp.where(place[:part] == p, kept[p * part : (p + 1) * part], out)
+    out_ref[...] = out
+
+
+def update_kernel(subjects, template_ref, parts_ref, out_ref):
+    rows, width = template_ref.shape
+    block = width // subjects
+    part = rows // subjects
+    place = lax.broadcasted_iota(jnp.int32, (part, width), 1) // block
+    for p in range(subjects):
+        total = jnp.zeros((part, width), jnp.float32)
+        for s in range(subjects):
+            turn = ((s - p) * block) % width
+            held = parts_ref[s]
+            moved = pltpu.roll(held, turn, axis=1) if turn else held
+            total = jnp.where(place == s, moved, total)
+        at = slice(p * part, (p + 1) * part)
+        out_ref[at, :] = template_ref[at, :] - template_rate * total / subjects
+
+
+def over_subjects(values):
+    count = lax.axis_size("subj")
+    return lax.all_gather(values, "subj")
 
 
 def extended(cells, sides, width):
@@ -49,56 +212,70 @@
     return center + diffusion_dt * summed
 
 
-def read_ahead(values, offset):
-    if offset > 0:
-        return jnp.concatenate(
-            [values[..., offset:], jnp.zeros(values.shape[:-1] + (offset,), values.dtype)], axis=-1
-        )
-    if offset < 0:
-        return jnp.concatenate(
-            [jnp.zeros(values.shape[:-1] + (-offset,), values.dtype), values[..., :offset]], axis=-1
-        )
-    return values
-
-
 def per_device(template, images, velocity, stiffness, send_rows, ref_slot, columns, weights):
+    f32 = jnp.float32
     slabs = lax.axis_size("slab")
     subjects = lax.axis_size("subj")
     capacity = send_rows.shape[3]
-    rows = template.shape[0]
-    width = template.shape[1]
+    rows, width = template.shape
     planes = rows // YR
-    send_one = send_rows[0, 0]
-    sending = template[send_one]
+    each = ref_slot.shape[2]
+    terms = rows * each
+    slots = slabs * capacity
+    group = capacity // subjects
+    step = 256
+
+    sending = call(
+        send_kernel, jax.ShapeDtypeStruct((slots, width), f32), send_rows[0, 0], template
+    )
     received = lax.all_to_all(sending, "slab", split_axis=0, concat_axis=0, tiled=True)
-    flat_rows = received.reshape(slabs * capacity, width)
-    slot_one = ref_slot[0]
-    offset_one = columns[0] - jnp.arange(width, dtype=jnp.int32)
-    picked = flat_rows[slot_one]
-    weight_f = weights[0].astype(jnp.float32)
-    values = jnp.zeros(picked.shape, jnp.float32)
-    for offset in range(-2, 3):
-        values = values + jnp.where(offset_one == offset, read_ahead(picked, offset), 0.0)
-    warped = jnp.sum(weight_f * values, axis=1)
+
+    slot_flat = ref_slot.reshape(terms)
+    slot_wide = jnp.broadcast_to(slot_flat[:, None], (terms, LANES))
+    owner, inner = slot_flat // capacity, slot_flat % capacity
+    slot_packed = (inner // group) * (slabs * group) + owner * group + inner % group
+    pick, drop = call(
+        functools.partial(pick_kernel, step),
+        (
+            jax.ShapeDtypeStruct((terms, slots), jnp.bfloat16),
+            jax.ShapeDtypeStruct((slots, terms), jnp.bfloat16),
+        ),
+        slot_wide,
+        slot_packed[None],
+    )
+    all_rows = over_subjects(send_rows[0, 0]).reshape(subjects, slabs, subjects, group)
+    row_index = jnp.transpose(all_rows, (2, 0, 1, 3)).reshape(subjects, slots)
+
+    warped, sent = call(
+        functools.partial(warp_kernel, step, subjects),
+        (
+            jax.ShapeDtypeStruct((rows, width), f32),
+            jax.ShapeDtypeStruct((slots, width), f32),
+        ),
+        received,
+        pick,
+        drop,
+        columns.reshape(terms, width),
+        weights.reshape(terms, width),
+        images[0],
+        scratch=(pltpu.VMEM((slots, 2 * width), f32),),
+    )
+    returned = lax.all_to_all(sent, ("subj", "slab"), split_axis=0, concat_axis=0, tiled=True)
+    part = call(
+        functools.partial(collect_kernel, subjects),
+        jax.ShapeDtypeStruct((rows // subjects, width), f32),
+        row_index,
+        returned,
+    )
+    parts = over_subjects(part)
+    template_out = call(
+        functools.partial(update_kernel, subjects),
+        jax.ShapeDtypeStruct((rows, width), f32),
+        template,
+        parts,
+    )
+
     mismatch = warped - images[0]
-    contrib = weight_f * mismatch[:, None, :]
-    placed = jnp.zeros(contrib.shape, jnp.float32)
-    for offset in range(-2, 3):
-        placed = placed + read_ahead(jnp.where(offset_one == offset, contrib, 0.0), -offset)
-    slot_grad = (
-        jnp.zeros((slabs * capacity, width), jnp.float32)
-        .at[slot_one.reshape(-1)]
-        .add(placed.reshape(-1, width))
-    )
-    slot_grad = slot_grad.reshape(slabs, capacity, width)
-    returned = lax.all_to_all(slot_grad, "slab", split_axis=0, concat_axis=0, tiled=True)
-    row_grad = (
-        jnp.zeros((rows, width), jnp.float32)
-        .at[send_one.reshape(-1)]
-        .add(returned.reshape(-1, width))
-    )
-    summed = lax.psum(row_grad, "subj")
-    template_out = template - template_rate * summed / subjects
     warped_grid = warped.reshape(planes, YR, width)
     warped_padded = extended(warped_grid, (("slab", 0),), 1)
     warped_yx = jnp.pad(warped_grid, ((0, 0), (1, 1), (1, 1)))

time: 151 us -> 93.4 us (0.62)
  other arithmetic: 45.8 us -> 6.1 us
  waiting for transfers between devices: 40.5 us -> 0.94 us
  Pallas kernels: 0 us -> 24.7 us
  blocking collectives: 0 us -> 17.3 us
  between operations: 14.3 us -> 0.93 us
  local copies, waits for them, and re-layouts: 19.3 us -> 6.94 us
  starting transfers between devices: 30.6 us -> 35.8 us
    psum x1 -> x0, waiting for transfers between devices: 35.6 us -> none  [per_device(): summed = lax.psum(row_grad, 'subj')]
    scatter-add x2 -> x0, other arithmetic: 26.4 us -> none  [the longest x1 23.1 us: per_device(): slot_grad = jnp.zeros((slabs * capacity, width), jnp.float32).at[slot_one...]
    pallas_call x0 -> x5, Pallas kernels: none -> 24.7 us  [call(): pl.pallas_call(kernel, out_shape=out_shape, scratch_shapes=scratch, compi...]
    all_gather x0 -> x2, blocking collectives: none -> 17.3 us  [over_subjects(): return lax.all_gather(values, 'subj')]
    gather x2 -> x0, local copies, waits for them, and re-layouts: 13.4 us -> none  [the longest x1 10.8 us: per_device(): picked = flat_rows[slot_one]]
    select_n x6 -> x0, other arithmetic: 6.55 us -> none  [the longest x2 5.79 us: per_device(): jnp.where(offset_one == offset, contrib, 0.0)]
    reduce_sum x1 -> x0, other arithmetic: 3.94 us -> none  [per_device(): warped = jnp.sum(weight_f * values, axis=1)]
    all_to_all x1, starting transfers between devices: 4.18 us -> 7.08 us  [per_device(): lax.all_to_all(sent, ('subj', 'slab'), split_axis=0, concat_axis=0, tiled...]
  transfers between devices with their start and end apart: 11 -> 10, of which waited for: 3 -> 1; matrix products, arithmetic and copies ran while one was open for 38% -> 9% of each run, Pallas kernels for 0% -> 25%
where the time goes in v1:
time: 93.4 us; the launch traced here: 92.7 us
  starting transfers between devices  35.8 us (38%)
  Pallas kernels  24.7 us (26%)
  blocking collectives  17.3 us (19%)
  local copies, waits for them, and re-layouts  6.94 us (7%)
  other arithmetic  6.1 us (7%)
  waiting for transfers between devices  0.94 us (1%)
    pallas_call x5, Pallas kernels, call(): pl.pallas_call(kernel, out_shape=out_shape, scratch_shapes=scratch, compi...  24.7 us
    all_gather x2, blocking collectives, over_subjects(): return lax.all_gather(values, 'subj')  17.3 us
    ppermute x4, starting transfers between devices, extended(): lax.ppermute(tail, axis, [(i, (i + 1) % count) for i in range(ends)])  17.1 us
    all_to_all x1, starting transfers between devices, per_device(): lax.all_to_all(sent, ('subj', 'slab'), split_axis=0, concat_axis=0, tiled...  7.08 us
    all_to_all x1, starting transfers between devices, per_device(): lax.all_to_all(sending, 'slab', split_axis=0, concat_axis=0, tiled=True)  6.32 us
    ppermute x4, starting transfers between devices, extended(): lax.ppermute(head, axis, [((i + 1) % count, i) for i in range(ends)])  5.26 us
    add x2, other arithmetic, smooth_step(): return center + diffusion_dt * summed  4.41 us
    slice x4, local copies, waits for them, and re-layouts, extended(): head = lax.slice_in_dim(cells, 0, width, axis=dim)  3.32 us
  transfers between devices with their start and end apart: 10, of which 1 were waited for; matrix products, arithmetic and copies ran while one was open for 9% of the time, Pallas kernels for 25%

profile of v1, /device:TPU:0, one launch (start us, length us, event | category | flops | bytes accessed | tf_op | source)
XLA Modules:
  0.0 92.7 jit_solution(17425771741996927293)
XLA Ops:
  0.6 0.9 %copy-done.3 = f32[512,128]{1,0:T(8,128)S(1)} copy-done((f32[512,128]{1,0:T(8,128)S(1)}, f32[512,128]{1,0:T(8,128)}, u32[]{:S(2)}) %copy-start.3) | copy-done | bytes 262168
  2.3 1.3 %shard_map.95 = f32[512,128]{1,0:T(8,128)} custom-call(s32[8,64]{1,0:T(8,128)S(1)} %bitcast.43, f32[512,128]{1,0:T(8,128)S(1)} %copy-done.3), custom_call_target="tpu_custom_call" | custom-call | tf_op jit(solution)/shard_map/pallas_call | solution.py:23
  3.6 6.3 %all-to-all-start = ((f32[8,64,128]{2,1,0:T(8,128)}), f32[8,64,128]{2,1,0:T(8,128)}, u32[]{:S(2)}, u32[]{:S(2)}) async-start(f32[8,64,128]{2,1,0:T(8,128)} %bitcast.2), calls=%async_computation | async-start | bytes 524288 | tf_op jit(solution)/shard_map/all_to_all | solution.py:231
  9.9 1.7 %slice_bitcast_fusion.1 = (f32[1,256,128]{2,1,0:T(8,128)}, f32[1,256,128]{2,1,0:T(8,128)}) fusion(f32[512,128]{1,0:T(8,128)} %param.11), kind=kLoop, calls=%fused_computation.86 | loop fusion | bytes 524288 | tf_op jit(solution)/shard_map/slice | solution.py:182
  11.6 1.3 %collective-permute-start.2 = (f32[1,256,128]{2,1,0:T(8,128)}, f32[1,256,128]{2,1,0:T(8,128)S(1)}, u32[]{:S(2)}, u32[]{:S(2)}) collective-permute-start(f32[1,256,128]{2,1,0:T(8,128)} %get-tuple-element.20), channel_id=1, source_target_pairs={{1,0},{2,1},{3,2},{4,3},{5,4},{6,5},{7,6},{9,8},{10,9},{11,10},{12... | collective-permute-start | bytes 393224 | tf_op jit(solution)/shard_map/ppermute | solution.py:188
  12.9 3.7 %collective-permute-start.4 = (f32[1,256,128]{2,1,0:T(8,128)}, f32[1,256,128]{2,1,0:T(8,128)}, u32[]{:S(2)}, u32[]{:S(2)}) collective-permute-start(f32[1,256,128]{2,1,0:T(8,128)} %get-tuple-element.21), channel_id=1, source_target_pairs={{0,1},{1,2},{2,3},{3,4},{4,5},{5,6},{6,7},{8,9},{9,10},{10,11},{11... | collective-permute-start | bytes 393224 | tf_op jit(solution)/shard_map/ppermute | solution.py:186
  16.6 0.8 copy.16
  18.6 5.0 %shard_map.96 = (bf16[4096,512]{1,0:T(8,128)(2,1)}, bf16[512,4096]{1,0:T(8,128)(2,1)}) custom-call(s32[4096,128]{1,0:T(8,128)S(1)} %broadcast_in_dim.5.wide_ref, s32[1,4096]{1,0:T(1,128)S(1)} %fusion.60.flat_ref), custom_call_target="tpu_custom_call" | custom-call | tf_op jit(solution)/shard_map/pallas_call | solution.py:23
  23.6 16.5 %shard_map.97 = (f32[512,128]{1,0:T(8,128)S(1)}, f32[512,128]{1,0:T(8,128)S(1)}) custom-call(f32[512,128]{1,0:T(8,128)} %bitcast.3.received_ref, bf16[4096,512]{1,0:T(8,128)(2,1)} %get-tuple-element.6.pick_ref, bf16[512,4096]{1,0:T(8,128)(2,1)} %get-tuple-element.7.drop_ref, s32[4096,128]{1,0:T(8,128)S(1)} %bitcast.37, bf16[4096,128]{1,0:T(8,128)(2,1)S(1)} %bitcast.38, ...), custom_call_target="tpu_custom_call" | custom-call | tf_op jit(solution)/shard_map/pallas_call | solution.py:23
  40.2 1.4 %collective-permute-start = (f32[1,256,128]{2,1,0:T(8,128)S(1)}, f32[1,256,128]{2,1,0:T(8,128)S(1)}, u32[]{:S(2)}, u32[]{:S(2)}) collective-permute-start(f32[1,256,128]{2,1,0:T(8,128)S(1)} %get-tuple-element.25), channel_id=1, source_target_pairs={{1,0},{2,1},{3,2},{4,3},{5,4},{6,5},{7,6},{9,8},{10,9},{11,10},{12... | collective-permute-start | bytes 393224 | tf_op jit(solution)/shard_map/ppermute | solution.py:188
  41.7 3.6 %collective-permute-start.1 = (f32[1,256,128]{2,1,0:T(8,128)S(1)}, f32[1,256,128]{2,1,0:T(8,128)S(1)}, u32[]{:S(2)}, u32[]{:S(2)}) collective-permute-start(f32[1,256,128]{2,1,0:T(8,128)S(1)} %get-tuple-element.26), channel_id=1, source_target_pairs={{0,1},{1,2},{2,3},{3,4},{4,5},{5,6},{6,7},{8,9},{9,10},{10,11},{11... | collective-permute-start | bytes 393224 | tf_op jit(solution)/shard_map/ppermute | solution.py:186
  45.4 0.9 collective-permute-done.1
  47.4 1.3 %collective-permute-start.3 = (f32[3,1,256,128]{3,2,1,0:T(8,128)}, f32[3,1,256,128]{3,2,1,0:T(8,128)}, u32[]{:S(2)}, u32[]{:S(2)}) collective-permute-start(f32[3,1,256,128]{3,2,1,0:T(8,128)} %get-tuple-element.12), channel_id=1, source_target_pairs={{1,0},{2,1},{3,2},{4,3},{5,4},{6,5},{7,6},{9,8},{10,9},{11,10},{12... | collective-permute-start | bytes 1179656 | tf_op jit(solution)/shard_map/ppermute | solution.py:188
  48.7 6.0 %collective-permute-start.5 = (f32[3,1,256,128]{3,2,1,0:T(8,128)S(1)}, f32[3,1,256,128]{3,2,1,0:T(8,128)}, u32[]{:S(2)}, u32[]{:S(2)}) collective-permute-start(f32[3,1,256,128]{3,2,1,0:T(8,128)S(1)} %get-tuple-element.13), channel_id=1, source_target_pairs={{0,1},{1,2},{2,3},{3,4},{4,5},{5,6},{6,7},{8,9},{9,10},{10,11},{11... | collective-permute-start | bytes 1179656 | tf_op jit(solution)/shard_map/ppermute | solution.py:186
  54.7 1.1 %fusion.56 = (f32[2,256,128]{2,1,0:T(8,128)S(1)}, f32[2,256,128]{2,1,0:T(8,128)S(1)}, f32[2,256,128]{2,1,0:T(8,128)S(1)}, f32[2,256,128]{2,1,0:T(8,128)S(1)}, f3...) fusion(f32[2,256,128]{2,1,0:T(8,128)S(1)} %bitcast.45, f32[1,256,128]{2,1,0:T(8,128)S(1)} %collective-permute-done.2, ...), kind=kLoop, calls=%fused_computation.79 | loop fusion | flops 917504 | bytes 2097152 | tf_op jit(solution)/shard_map/mul | solution.py:210
  55.8 7.1 %all-to-all-start.1 = ((f32[32,16,128]{2,1,0:T(8,128)}), f32[32,16,128]{2,1,0:T(8,128)S(1)}, u32[]{:S(2)}, u32[]{:S(2)}) async-start(f32[32,16,128]{2,1,0:T(8,128)} %bitcast.42), calls=%async_computation.1 | async-start | bytes 524288 | tf_op jit(solution)/shard_map/all_to_all | solution.py:263
  62.9 1.8 %fusion.7 = f32[3,2,256,128]{3,2,1,0:T(8,128)S(1)} fusion(f32[3,2,256,128]{3,2,1,0:T(8,128)S(1)} %fusion.38, f32[3,1,256,128]{3,2,1,0:T(8,128)} %collective-permute-done.5, f32[3,1,256,128]{3,2,1,0:T(8,128)} %collective-permute-done.3, f32[2,256,128]{2,1,0:T(8,128)S(1)} %get-tuple-element.16, f32[2,256,128]{2,1,0:T(8,128)S(1)} %get-tuple-element.19, ...), kind=kLoop, calls=%fused_computation.23 | loop fusion | flops 4128768 | bytes 3932160 | tf_op jit(solution)/shard_map/add | solution.py:212
  65.5 1.3 %collective-permute-start.6 = (f32[3,1,256,128]{3,2,1,0:T(8,128)}, f32[3,1,256,128]{3,2,1,0:T(8,128)}, u32[]{:S(2)}, u32[]{:S(2)}) collective-permute-start(f32[3,1,256,128]{3,2,1,0:T(8,128)} %get-tuple-element.10), channel_id=1, source_target_pairs={{1,0},{2,1},{3,2},{4,3},{5,4},{6,5},{7,6},{9,8},{10,9},{11,10},{12... | collective-permute-start | bytes 1179656 | tf_op jit(solution)/shard_map/ppermute | solution.py:188
  66.8 3.8 %collective-permute-start.7 = (f32[3,1,256,128]{3,2,1,0:T(8,128)S(1)}, f32[3,1,256,128]{3,2,1,0:T(8,128)}, u32[]{:S(2)}, u32[]{:S(2)}) collective-permute-start(f32[3,1,256,128]{3,2,1,0:T(8,128)S(1)} %get-tuple-element.11), channel_id=1, source_target_pairs={{0,1},{1,2},{2,3},{3,4},{4,5},{5,6},{6,7},{8,9},{9,10},{10,11},{11... | collective-permute-start | bytes 1179656 | tf_op jit(solution)/shard_map/ppermute | solution.py:186
  70.6 8.4 %all-gather = s32[4,1,8,64]{3,2,1,0:T(8,128)S(1)} all-gather(s32[1,1,8,64]{3,2,1,0:T(8,128)S(1)} %copy-done.7), channel_id=2, replica_groups=mesh['subj'=4,'slab'=8] {'subj'}, dimensions={0}, use_global_device_ids=true | all-gather | bytes 10240 | tf_op jit(solution)/shard_map/all_gather | solution.py:175
  79.2 0.9 shard_map.98
  80.1 8.9 %all-gather.1 = f32[512,128]{1,0:T(8,128)S(1)} all-gather(f32[128,128]{1,0:T(8,128)S(1)} %shard_map.98), channel_id=3, replica_groups=mesh['subj'=4,'slab'=8] {'subj'}, dimensions={0}, use_global_device_ids=true | all-gather | bytes 327680 | tf_op jit(solution)/shard_map/all_gather | solution.py:175
  89.1 1.0 %shard_map.99 = f32[512,128]{1,0:T(8,128)} custom-call(f32[512,128]{1,0:T(8,128)S(1)} %copy-done.4, f32[4,128,128]{2,1,0:T(8,128)S(1)} %bitcast.40), custom_call_target="tpu_custom_call" | custom-call | tf_op jit(solution)/shard_map/pallas_call | solution.py:23
  90.1 2.6 %fusion.21 = f32[3,2,256,128]{3,2,1,0:T(8,128)} fusion(f32[3,2,256,128]{3,2,1,0:T(8,128)S(1)} %fusion.7, f32[3,1,256,128]{3,2,1,0:T(8,128)} %collective-permute-done.7, f32[3,1,256,128]{3,2,1,0:T(8,128)} %collective-permute-done.6, f32[2,256,128]{2,1,0:T(8,128)S(1)} %get-tuple-element.16, f32[2,256,128]{2,1,0:T(8,128)S(1)} %get-tuple-element.19, ...), kind=kLoop, calls=%fused_computation.37 | loop fusion | flops 4128768 | bytes 3932160 | tf_op jit(solution)/shard_map/add | solution.py:212
  (41 shorter events, 4.1 us)
Async XLA Ops:
  0.6 1.0 %copy-start.3 = (f32[512,128]{1,0:T(8,128)S(1)}, f32[512,128]{1,0:T(8,128)}, u32[]{:S(2)}) copy-start(f32[512,128]{1,0:T(8,128)} %template_ref.3) | copy-start | bytes 786436
  1.6 0.7 copy-start.6
  3.6 20.1 %all-to-all-start = ((f32[8,64,128]{2,1,0:T(8,128)}), f32[8,64,128]{2,1,0:T(8,128)}, u32[]{:S(2)}, u32[]{:S(2)}) async-start(f32[8,64,128]{2,1,0:T(8,128)} %bitcast.2), calls=%async_computation | async-start | bytes 524288 | tf_op jit(solution)/shard_map/all_to_all | solution.py:231
  11.6 43.1 %collective-permute-start.2 = (f32[1,256,128]{2,1,0:T(8,128)}, f32[1,256,128]{2,1,0:T(8,128)S(1)}, u32[]{:S(2)}, u32[]{:S(2)}) collective-permute-start(f32[1,256,128]{2,1,0:T(8,128)} %get-tuple-element.20), channel_id=1, source_target_pairs={{1,0},{2,1},{3,2},{4,3},{5,4},{6,5},{7,6},{9,8},{10,9},{11,10},{12... | collective-permute-start | bytes 393224 | tf_op jit(solution)/shard_map/ppermute | solution.py:188
  12.9 41.8 %collective-permute-start.4 = (f32[1,256,128]{2,1,0:T(8,128)}, f32[1,256,128]{2,1,0:T(8,128)}, u32[]{:S(2)}, u32[]{:S(2)}) collective-permute-start(f32[1,256,128]{2,1,0:T(8,128)} %get-tuple-element.21), channel_id=1, source_target_pairs={{0,1},{1,2},{2,3},{3,4},{4,5},{5,6},{6,7},{8,9},{9,10},{10,11},{11... | collective-permute-start | bytes 393224 | tf_op jit(solution)/shard_map/ppermute | solution.py:186
  18.0 5.6 %copy-start = (s32[1,512,8,128]{3,2,1,0:T(8,128)S(1)}, s32[1,512,8,128]{3,2,1,0:T(8,128)}, u32[]{:S(2)}) copy-start(s32[1,512,8,128]{3,2,1,0:T(8,128)} %param.14) | copy-start | bytes 6291460
  18.0 5.6 %copy-start.1 = (bf16[1,512,8,128]{3,2,1,0:T(8,128)(2,1)S(1)}, bf16[1,512,8,128]{3,2,1,0:T(8,128)(2,1)}, u32[]{:S(2)}) copy-start(bf16[1,512,8,128]{3,2,1,0:T(8,128)(2,1)} %param.15) | copy-start | bytes 3145732
  18.0 5.6 %copy-start.2 = (f32[1,512,128]{2,1,0:T(8,128)S(1)}, f32[1,512,128]{2,1,0:T(8,128)}, u32[]{:S(2)}) copy-start(f32[1,512,128]{2,1,0:T(8,128)} %param.9) | copy-start | bytes 786436
  40.2 15.6 %copy-start.5 = (f32[512,128]{1,0:T(8,128)}, f32[512,128]{1,0:T(8,128)S(1)}, u32[]{:S(2)}) copy-start(f32[512,128]{1,0:T(8,128)S(1)} %get-tuple-element.8) | copy-start | bytes 786436
  40.2 6.3 %copy-start.9 = (f32[1,3,512,128]{3,2,1,0:T(8,128)S(1)}, f32[1,3,512,128]{3,2,1,0:T(8,128)}, u32[]{:S(2)}) copy-start(f32[1,3,512,128]{3,2,1,0:T(8,128)} %param.10) | copy-start | bytes 2359300
  40.2 5.1 %collective-permute-start = (f32[1,256,128]{2,1,0:T(8,128)S(1)}, f32[1,256,128]{2,1,0:T(8,128)S(1)}, u32[]{:S(2)}, u32[]{:S(2)}) collective-permute-start(f32[1,256,128]{2,1,0:T(8,128)S(1)} %get-tuple-element.25), channel_id=1, source_target_pairs={{1,0},{2,1},{3,2},{4,3},{5,4},{6,5},{7,6},{9,8},{10,9},{11,10},{12... | collective-permute-start | bytes 393224 | tf_op jit(solution)/shard_map/ppermute | solution.py:188
  41.7 4.6 %collective-permute-start.1 = (f32[1,256,128]{2,1,0:T(8,128)S(1)}, f32[1,256,128]{2,1,0:T(8,128)S(1)}, u32[]{:S(2)}, u32[]{:S(2)}) collective-permute-start(f32[1,256,128]{2,1,0:T(8,128)S(1)} %get-tuple-element.26), channel_id=1, source_target_pairs={{0,1},{1,2},{2,3},{3,4},{4,5},{5,6},{6,7},{8,9},{9,10},{10,11},{11... | collective-permute-start | bytes 393224 | tf_op jit(solution)/shard_map/ppermute | solution.py:186
  46.5 8.2 %copy-start.8 = (f32[512,128]{1,0:T(8,128)S(1)}, f32[512,128]{1,0:T(8,128)}, u32[]{:S(2)}) copy-start(f32[512,128]{1,0:T(8,128)} %param.11) | copy-start | bytes 786436
  47.4 15.5 %collective-permute-start.3 = (f32[3,1,256,128]{3,2,1,0:T(8,128)}, f32[3,1,256,128]{3,2,1,0:T(8,128)}, u32[]{:S(2)}, u32[]{:S(2)}) collective-permute-start(f32[3,1,256,128]{3,2,1,0:T(8,128)} %get-tuple-element.12), channel_id=1, source_target_pairs={{1,0},{2,1},{3,2},{4,3},{5,4},{6,5},{7,6},{9,8},{10,9},{11,10},{12... | collective-permute-start | bytes 1179656 | tf_op jit(solution)/shard_map/ppermute | solution.py:188
  48.7 14.2 %collective-permute-start.5 = (f32[3,1,256,128]{3,2,1,0:T(8,128)S(1)}, f32[3,1,256,128]{3,2,1,0:T(8,128)}, u32[]{:S(2)}, u32[]{:S(2)}) collective-permute-start(f32[3,1,256,128]{3,2,1,0:T(8,128)S(1)} %get-tuple-element.13), channel_id=1, source_target_pairs={{0,1},{1,2},{2,3},{3,4},{4,5},{5,6},{6,7},{8,9},{9,10},{10,11},{11... | collective-permute-start | bytes 1179656 | tf_op jit(solution)/shard_map/ppermute | solution.py:186
  55.8 23.4 %all-to-all-start.1 = ((f32[32,16,128]{2,1,0:T(8,128)}), f32[32,16,128]{2,1,0:T(8,128)S(1)}, u32[]{:S(2)}, u32[]{:S(2)}) async-start(f32[32,16,128]{2,1,0:T(8,128)} %bitcast.42), calls=%async_computation.1 | async-start | bytes 524288 | tf_op jit(solution)/shard_map/all_to_all | solution.py:263
  62.9 7.7 %copy-start.7 = (s32[1,1,8,64]{3,2,1,0:T(8,128)S(1)}, s32[1,1,8,64]{3,2,1,0:T(8,128)}, u32[]{:S(2)}) copy-start(s32[1,1,8,64]{3,2,1,0:T(8,128)} %param.12) | copy-start | bytes 6148
  64.7 24.3 %copy-start.4 = (f32[512,128]{1,0:T(8,128)S(1)}, f32[512,128]{1,0:T(8,128)}, u32[]{:S(2)}) copy-start(f32[512,128]{1,0:T(8,128)} %template_ref.3) | copy-start | bytes 786436
  65.5 24.5 %collective-permute-start.6 = (f32[3,1,256,128]{3,2,1,0:T(8,128)}, f32[3,1,256,128]{3,2,1,0:T(8,128)}, u32[]{:S(2)}, u32[]{:S(2)}) collective-permute-start(f32[3,1,256,128]{3,2,1,0:T(8,128)} %get-tuple-element.10), channel_id=1, source_target_pairs={{1,0},{2,1},{3,2},{4,3},{5,4},{6,5},{7,6},{9,8},{10,9},{11,10},{12... | collective-permute-start | bytes 1179656 | tf_op jit(solution)/shard_map/ppermute | solution.py:188
  66.8 23.2 %collective-permute-start.7 = (f32[3,1,256,128]{3,2,1,0:T(8,128)S(1)}, f32[3,1,256,128]{3,2,1,0:T(8,128)}, u32[]{:S(2)}, u32[]{:S(2)}) collective-permute-start(f32[3,1,256,128]{3,2,1,0:T(8,128)S(1)} %get-tuple-element.11), channel_id=1, source_target_pairs={{0,1},{1,2},{2,3},{3,4},{4,5},{5,6},{6,7},{8,9},{9,10},{10,11},{11... | collective-permute-start | bytes 1179656 | tf_op jit(solution)/shard_map/ppermute | solution.py:186

commit v2 on v1

v2 whole, which is shorter than its diff:
```python
import functools

import jax
import jax.numpy as jnp
from jax import lax
from jax.experimental import pallas as pl
from jax.experimental.pallas import tpu as pltpu
from jax.sharding import PartitionSpec as P

YR = 256
LANES = 128
OFFSETS = (0, -2, -1, 1, 2)


force_step = 1.0
diffusion_dt = 0.16
template_rate = 2.0

VMEM_LIMIT = 32 * 1024 * 1024


def call(kernel, out_shape, *args, scratch=(), smem=()):
    spaces = [pltpu.SMEM if i in smem else pltpu.VMEM for i in range(len(args))]
    return pl.pallas_call(
        kernel,
        out_shape=out_shape,
        in_specs=[pl.BlockSpec(memory_space=space) for space in spaces],
        scratch_shapes=scratch,
        compiler_params=pltpu.CompilerParams(vmem_limit_bytes=VMEM_LIMIT),
    )(*args)


def halves(values):
    high = values.astype(jnp.bfloat16)
    low = (values - high.astype(jnp.float32)).astype(jnp.bfloat16)
    return jnp.concatenate([high, low], axis=1)


def joined(pair):
    width = pair.shape[1] // 2
    return pair[:, :width] + pair[:, width:]


def turned(values, shift):
    shift %= values.shape[1]
    return pltpu.roll(values, shift, axis=1) if shift else values


def dot(left, right):
    return jnp.dot(left, right, preferred_element_type=jnp.float32)


def one_hot(matches):
    return jnp.where(matches, 1.0, 0.0).astype(jnp.bfloat16)


def send_kernel(send_ref, template_ref, out_ref):
    slabs, capacity = send_ref.shape
    rows = template_ref.shape[0]
    pair = halves(template_ref[...])
    padded = jnp.concatenate(
        [send_ref[...], jnp.zeros((slabs, LANES - capacity), jnp.int32)], axis=1
    )
    turned = padded.T
    number = lax.broadcasted_iota(jnp.int32, (capacity, rows), 1)
    for k in range(slabs):
        wanted = jnp.broadcast_to(turned[:capacity, k : k + 1], (capacity, rows))
        out_ref[k * capacity : (k + 1) * capacity, :] = joined(dot(one_hot(wanted == number), pair))


def prepare_kernel(
    step, wide_ref, flat_ref, columns_ref, weights_ref, pick_ref, drop_ref, moved_ref, plain_ref
):
    terms, slots = pick_ref.shape
    each, rows, width = moved_ref.shape[1:]
    lane = lax.broadcasted_iota(jnp.int32, (step, LANES), 1)
    row = lax.broadcasted_iota(jnp.int32, (slots, step), 0)

    def hot(i, carry):
        at = pl.multiple_of(i * step, step)
        wide = wide_ref[pl.ds(at, step), :]
        for t in range(slots // LANES):
            pick_ref[pl.ds(at, step), t * LANES : (t + 1) * LANES] = one_hot(wide == lane + t * LANES)
        flat = jnp.broadcast_to(flat_ref[:, pl.ds(at, step)], (slots, step))
        drop_ref[:, pl.ds(at, step)] = one_hot(flat == row)
        return carry

    lax.fori_loop(0, terms // step, hot, 0)
    plain_ref[...] = weights_ref[...].astype(jnp.float32)
    some = step // each
    cell = lax.broadcasted_iota(jnp.int32, (some, width), 1)

    def move(i, carry):
        at = pl.multiple_of(i * step, step)
        at_row = pl.multiple_of(i * some, some)
        for b in range(each):
            offset = columns_ref[pl.ds(at + b, some, stride=each), :] - cell
            weights = plain_ref[pl.ds(at + b, some, stride=each), :]
            for j, o in enumerate(OFFSETS):
                kept = jnp.where(offset == o, weights, 0.0)
                moved_ref[j, b, pl.ds(at_row, some), :] = turned(kept, o).astype(jnp.bfloat16)
        return carry

    lax.fori_loop(0, terms // step, move, 0)


def warp_kernel(
    some,
    subjects,
    received_ref,
    pick_ref,
    drop_ref,
    moved_ref,
    images_ref,
    warped_ref,
    sent_ref,
    picked_ref,
    placed_ref,
):
    slots, width = received_ref.shape
    each, rows = moved_ref.shape[1:3]
    terms = each * rows
    pair = halves(received_ref[...])
    for b in range(each):
        picked_ref[b] = joined(dot(pick_ref[b * rows : (b + 1) * rows, :], pair))

    def body(i, carry):
        at = pl.multiple_of(i * some, some)
        sums = [jnp.zeros((some, width), jnp.float32) for _ in OFFSETS]
        for b in range(each):
            picked = picked_ref[b, pl.ds(at, some), :]
            for j in range(len(OFFSETS)):
                sums[j] = sums[j] + moved_ref[j, b, pl.ds(at, some), :].astype(jnp.float32) * picked
        warped = sums[0]
        for j, o in enumerate(OFFSETS[1:], 1):
            warped = warped + turned(sums[j], -o)
        warped_ref[pl.ds(at, some), :] = warped
        mismatch = warped - images_ref[pl.ds(at, some), :]
        ahead = [turned(mismatch, o) for o in OFFSETS]
        for b in range(each):
            placed = moved_ref[0, b, pl.ds(at, some), :].astype(jnp.float32) * ahead[0]
            for j in range(1, len(OFFSETS)):
                placed = placed + moved_ref[j, b, pl.ds(at, some), :].astype(jnp.float32) * ahead[j]
            placed_ref[b, pl.ds(at, some), :] = halves(placed)
        return carry

    lax.fori_loop(0, rows // some, body, 0)
    total = joined(dot(drop_ref[...], placed_ref[...].reshape(terms, 2 * width)))
    block = width // subjects
    group = slots // subjects
    place = lax.broadcasted_iota(jnp.int32, (group, width), 1) // block
    groups = [total[q * group : (q + 1) * group, :] for q in range(subjects)]
    for p in range(subjects):
        out = jnp.zeros((group, width), jnp.float32)
        for q in range(subjects):
            out = jnp.where(place == q, turned(groups[q], (q - p) * block), out)
        sent_ref[p * group : (p + 1) * group, :] = out


def collect_kernel(subjects, index_ref, me_ref, returned_ref, out_ref):
    slots, width = returned_ref.shape
    rows = out_ref.shape[0] * subjects
    block = width // subjects
    group = slots // subjects
    me = me_ref[0]
    pair = halves(
        jnp.concatenate(
            [
                returned_ref[pl.ds(pl.multiple_of((me ^ d) * group, group), group), :]
                for d in range(subjects)
            ]
        )
    )
    number = lax.broadcasted_iota(jnp.int32, (rows, slots), 0)
    place = lax.broadcasted_iota(jnp.int32, (rows, width), 1) // block
    kept = jnp.zeros((rows, width), jnp.float32)
    for q in range(subjects):
        wanted = jnp.broadcast_to(index_ref[q : q + 1, :], (rows, slots))
        kept = jnp.where(place == q, joined(dot(one_hot(wanted == number), pair)), kept)
    turn = block
    while turn < width:
        kept = kept + turned(kept, turn)
        turn *= 2
    part = rows // subjects
    out = jnp.zeros((part, width), jnp.float32)
    for p in range(subjects):
        out = jnp.where(place[:part] == p, kept[p * part : (p + 1) * part], out)
    out_ref[...] = out


def update_kernel(subjects, me_ref, template_ref, *refs):
    parts, out_ref = refs[:-1], refs[-1]
    rows, width = template_ref.shape
    block = width // subjects
    part = rows // subjects
    me = me_ref[0]
    place = lax.broadcasted_iota(jnp.int32, (part, width), 1) // block
    for p in range(subjects):
        total = jnp.zeros((part, width), jnp.float32)
        for d in range(subjects):
            source = me ^ d
            turn = lax.rem((source - p) * block + width, width)
            total = jnp.where(place == source, pltpu.roll(parts[d][...], turn, axis=1), total)
        at = slice(p * part, (p + 1) * part)
        out_ref[at, :] = template_ref[at, :] - template_rate * total / subjects


def over_subjects(values):
    count = lax.axis_size("subj")
    return [values] + [
        lax.ppermute(values, "subj", [(i, i ^ d) for i in range(count)]) for d in range(1, count)
    ]


def with_neighbours(low_side, high_side):
    count = lax.axis_size("slab")
    odd = lax.axis_index("slab") % 2 == 1
    near = [(i, i ^ 1) for i in range(count)]
    far = [(i, i + 1 if i % 2 else i - 1) for i in range(1, count - 1)]
    from_far = lax.ppermute(jnp.where(odd, high_side, low_side), "slab", far)
    from_near = lax.ppermute(jnp.where(odd, low_side, high_side), "slab", near)
    return jnp.where(odd, from_near, from_far), jnp.where(odd, from_far, from_near)


def shifted(values, step, axis):
    size = values.shape[axis]
    index = lax.broadcasted_iota(jnp.int32, values.shape, axis)
    edge = size - 1 if step > 0 else 0
    return jnp.where(index == edge, 0.0, pltpu.roll(values, (-step) % size, axis=axis))


def diffuse(below, center, above, coef_below, coef, coef_above):
    summed = 0.5 * (coef + coef_above) * (above - center)
    summed = summed + 0.5 * (coef + coef_below) * (below - center)
    for axis in (0, 1):
        for step in (1, -1):
            face = 0.5 * (coef + shifted(coef, step, axis))
            summed = summed + face * (shifted(center, step, axis) - center)
    return center + diffusion_dt * summed


def force_kernel(
    velocity_ref,
    images_ref,
    stiffness_ref,
    warped_ref,
    low_ref,
    high_ref,
    warped_low_ref,
    warped_high_ref,
    out_ref,
):
    planes = out_ref.shape[1]
    components = out_ref.shape[0]
    coefs = [low_ref[components]] + [stiffness_ref[p] for p in range(planes)] + [high_ref[components]]
    images = [low_ref[components + 1]] + [images_ref[p] for p in range(planes)] + [high_ref[components + 1]]
    near = [warped_low_ref[p] for p in range(2)]
    far = [warped_high_ref[p] for p in range(2)]
    warped = near + [warped_ref[p] for p in range(planes)] + far
    fields = [[] for _ in range(components)]
    for p in range(planes + 2):
        here = warped[p + 1]
        mismatch = here - images[p]
        slopes = [
            0.5 * (shifted(here, 1, 1) - shifted(here, -1, 1)),
            0.5 * (shifted(here, 1, 0) - shifted(here, -1, 0)),
            0.5 * (warped[p + 2] - warped[p]),
        ]
        for a in range(components):
            if p == 0:
                velocity = low_ref[a]
            elif p == planes + 1:
                velocity = high_ref[a]
            else:
                velocity = velocity_ref[a, p - 1]
            fields[a].append(velocity - force_step * mismatch * slopes[a])
    for a in range(components):
        for p in range(planes):
            out_ref[a, p] = diffuse(*fields[a][p : p + 3], *coefs[p : p + 3])


def last_kernel(field_ref, stiffness_ref, low_ref, high_ref, coef_low_ref, coef_high_ref, out_ref):
    components, planes = out_ref.shape[:2]
    coefs = [coef_low_ref[0]] + [stiffness_ref[p] for p in range(planes)] + [coef_high_ref[0]]
    for a in range(components):
        fields = [low_ref[a]] + [field_ref[a, p] for p in range(planes)] + [high_ref[a]]
        for p in range(planes):
            out_ref[a, p] = diffuse(*fields[p : p + 3], *coefs[p : p + 3])


def per_device(template, images, velocity, stiffness, send_rows, ref_slot, columns, weights):
    f32, bf16 = jnp.float32, jnp.bfloat16
    shape = jax.ShapeDtypeStruct
    slabs = lax.axis_size("slab")
    subjects = lax.axis_size("subj")
    me = lax.axis_index("subj").astype(jnp.int32).reshape(1)
    capacity = send_rows.shape[3]
    rows, width = template.shape
    planes = rows // YR
    each = ref_slot.shape[2]
    terms = rows * each
    slots = slabs * capacity
    group = capacity // subjects
    step = 256

    sending = call(send_kernel, shape((slots, width), f32), send_rows[0, 0], template)
    received = lax.all_to_all(sending, "slab", split_axis=0, concat_axis=0, tiled=True)

    slot_flat = ref_slot[0].T.reshape(terms)
    slot_wide = jnp.broadcast_to(slot_flat[:, None], (terms, LANES))
    owner, inner = slot_flat // capacity, slot_flat % capacity
    slot_packed = (inner // group) * (slabs * group) + owner * group + inner % group
    pick, drop, moved = call(
        functools.partial(prepare_kernel, step),
        (
            shape((terms, slots), bf16),
            shape((slots, terms), bf16),
            shape((len(OFFSETS), each, rows, width), bf16),
        ),
        slot_wide,
        slot_packed[None],
        columns.reshape(terms, width),
        weights.reshape(terms, width),
        scratch=(pltpu.VMEM((terms, width), f32),),
    )
    all_rows = jnp.stack(over_subjects(send_rows[0, 0])).reshape(subjects, slabs, subjects, group)
    row_index = jnp.transpose(all_rows, (2, 0, 1, 3)).reshape(subjects, slots)

    velocity_grid = velocity[0].reshape(3, planes, YR, width)
    images_grid = images[0].reshape(planes, YR, width)
    coef_grid = stiffness.reshape(planes, YR, width)
    edges = lambda p: jnp.concatenate([velocity_grid[:, p], coef_grid[p][None], images_grid[p][None]])
    low_side, high_side = edges(0), edges(planes - 1)
    low, high = with_neighbours(low_side, high_side)

    warped, sent = call(
        functools.partial(warp_kernel, 64, subjects),
        (shape((rows, width), f32), shape((slots, width), f32)),
        received,
        pick,
        drop,
        moved,
        images[0],
        scratch=(
            pltpu.VMEM((each, rows, width), f32),
            pltpu.VMEM((each, rows, 2 * width), bf16),
        ),
    )
    returned = lax.all_to_all(sent, ("subj", "slab"), split_axis=0, concat_axis=0, tiled=True)
    warped_grid = warped.reshape(planes, YR, width)
    warped_low, warped_high = with_neighbours(warped_grid[:2], warped_grid[-2:])

    part = call(
        functools.partial(collect_kernel, subjects),
        shape((rows // subjects, width), f32),
        row_index,
        me,
        returned,
        smem=(1,),
    )
    parts = over_subjects(part)

    warped_grid, _ = lax.optimization_barrier((warped_grid, part))
    field = call(
        force_kernel,
        shape((3, planes, YR, width), f32),
        velocity_grid,
        images_grid,
        coef_grid,
        warped_grid,
        low,
        high,
        warped_low,
        warped_high,
    )
    field_low, field_high = with_neighbours(field[:, 0], field[:, -1])
    template_out = call(
        functools.partial(update_kernel, subjects),
        shape((rows, width), f32),
        me,
        template,
        *parts,
        smem=(0,),
    )
    field = call(
        last_kernel,
        shape((3, planes, YR, width), f32),
        field,
        coef_grid,
        field_low,
        field_high,
        low[3:4],
        high[3:4],
    )
    velocity_out = field.reshape(3, rows, width)[None]
    return (template_out, velocity_out)


def solution(mesh):
    return jax.shard_map(
        per_device,
        mesh=mesh,
        in_specs=(
            P("slab", None),
            P("subj", "slab", None),
            P("subj", None, "slab", None),
            P("slab", None),
            P("subj", "slab", None, None),
            P("subj", "slab", None),
            P("subj", "slab", None, None),
            P("subj", "slab", None, None),
        ),
        out_specs=(P("slab", None), P("subj", None, "slab", None)),
        check_vma=False,
    )
```

time: 93.4 us -> 83.8 us (0.90)
  blocking collectives: 17.3 us -> 0 us
  local copies, waits for them, and re-layouts: 6.94 us -> 21.9 us
  waiting for transfers between devices: 0.94 us -> 10.6 us
  starting transfers between devices: 35.8 us -> 26.5 us
  Pallas kernels: 24.7 us -> 19.1 us
  other arithmetic: 6.1 us -> 4.02 us
    all_gather x2 -> x0, blocking collectives: 17.3 us -> none  [over_subjects(): return lax.all_gather(values, 'subj')]
    unnamed x21 -> x40, local copies, waits for them, and re-layouts: 2.52 us -> 17.8 us
    ppermute x8 -> x12, starting transfers between devices: 22.4 us -> 14.8 us  [the longest x6 8.1 us: over_subjects(): lax.ppermute(values, 'subj', [(i, i ^ d) for i in range(count)])]
    all_to_all x1, waiting for transfers between devices: 0.01 us -> 7.16 us  [per_device(): lax.all_to_all(sent, ('subj', 'slab'), split_axis=0, concat_axis=0, tiled...]
    pallas_call x5 -> x7, Pallas kernels: 24.7 us -> 19.1 us  [call(): pl.pallas_call(kernel, out_shape=out_shape, in_specs=[pl.BlockSpec(memory...]
    add x2 -> x0, other arithmetic: 4.41 us -> none  [smooth_step(): return center + diffusion_dt * summed]
    select_n x0 -> x5, other arithmetic: none -> 3.77 us  [the longest x3 2.52 us: with_neighbours(): jnp.where(odd, from_far, from_near)]
    ppermute x8 -> x12, waiting for transfers between devices: 0.93 us -> 3.49 us  [the longest x6 3.47 us: over_subjects(): lax.ppermute(values, 'subj', [(i, i ^ d) for i in range(count)])]
  transfers between devices with their start and end apart: 10 -> 14, of which waited for: 1 -> 4; matrix products, arithmetic and copies ran while one was open for 9% -> 10% of each run, Pallas kernels for 25% -> 18%
where the time goes in v2:
time: 83.8 us; the launch traced here: 83.1 us
  starting transfers between devices  26.5 us (32%)
  local copies, waits for them, and re-layouts  21.9 us (26%)
  Pallas kernels  19.1 us (23%)
  waiting for transfers between devices  10.6 us (13%)
  other arithmetic  4.02 us (5%)
  between operations  0.91 us (1%)
    pallas_call x7, Pallas kernels, call(): pl.pallas_call(kernel, out_shape=out_shape, in_specs=[pl.BlockSpec(memory...  19.1 us
    unnamed x40, local copies, waits for them, and re-layouts  17.8 us
    ppermute x6, starting transfers between devices, over_subjects(): lax.ppermute(values, 'subj', [(i, i ^ d) for i in range(count)])  8.1 us
    all_to_all x1, waiting for transfers between devices, per_device(): lax.all_to_all(sent, ('subj', 'slab'), split_axis=0, concat_axis=0, tiled...  7.16 us
    all_to_all x1, starting transfers between devices, per_device(): lax.all_to_all(sent, ('subj', 'slab'), split_axis=0, concat_axis=0, tiled...  6.37 us
    all_to_all x1, starting transfers between devices, per_device(): lax.all_to_all(sending, 'slab', split_axis=0, concat_axis=0, tiled=True)  5.34 us
    ppermute x3, starting transfers between devices, with_neighbours(): from_far = lax.ppermute(jnp.where(odd, high_side, low_side), 'slab', far)  3.55 us
    ppermute x6, waiting for transfers between devices, over_subjects(): lax.ppermute(values, 'subj', [(i, i ^ d) for i in range(count)])  3.47 us
  transfers between devices with their start and end apart: 14, of which 4 were waited for; matrix products, arithmetic and copies ran while one was open for 10% of the time, Pallas kernels for 18%

profile of v2, /device:TPU:0, one launch (start us, length us, event | category | flops | bytes accessed | tf_op | source)
XLA Modules:
  0.0 83.1 jit_solution(10355370250213386705)
XLA Ops:
  0.6 3.0 %collective-permute-start = (s32[8,64]{1,0:T(8,128)}, s32[8,64]{1,0:T(8,128)S(1)}, u32[]{:S(2)}, u32[]{:S(2)}) collective-permute-start(s32[8,64]{1,0:T(8,128)} %bitcast.69), channel_id=1, source_target_pairs={{0,8},{8,0},{16,24},{24,16},{1,9},{9,1},{17,25},{25,17},{2,10},{10... | collective-permute-start | bytes 6152 | tf_op jit(solution)/shard_map/ppermute | solution.py:211
  3.6 1.5 %collective-permute-start.1 = (s32[8,64]{1,0:T(8,128)}, s32[8,64]{1,0:T(8,128)S(1)}, u32[]{:S(2)}, u32[]{:S(2)}) collective-permute-start(s32[8,64]{1,0:T(8,128)} %bitcast.70), channel_id=1, source_target_pairs={{0,16},{8,24},{16,0},{24,8},{1,17},{9,25},{17,1},{25,9},{2,18},{10... | collective-permute-start | bytes 6152 | tf_op jit(solution)/shard_map/ppermute | solution.py:211
  6.8 1.3 %shard_map.95 = f32[512,128]{1,0:T(8,128)} custom-call(s32[8,64]{1,0:T(8,128)S(1)} %bitcast.72, f32[512,128]{1,0:T(8,128)S(1)} %copy-done.11), custom_call_target="tpu_custom_call" | custom-call | tf_op jit(solution)/shard_map/pallas_call | solution.py:24
  8.1 5.3 %all-to-all-start = ((f32[8,64,128]{2,1,0:T(8,128)}), f32[8,64,128]{2,1,0:T(8,128)S(1)}, u32[]{:S(2)}, u32[]{:S(2)}) async-start(f32[8,64,128]{2,1,0:T(8,128)} %bitcast.3), calls=%async_computation | async-start | bytes 524288 | tf_op jit(solution)/shard_map/all_to_all | solution.py:307
  16.6 1.2 %fusion = (f32[5,256,128]{2,1,0:T(8,128)}, f32[5,256,128]{2,1,0:T(8,128)}) fusion(f32[1,256,128]{2,1,0:T(8,128)S(1)} %get-tuple-element.29, f32[1,256,128]{2,1,0:T(8,128)S(1)} %get-tuple-element.27, f32[3,256,128]{2,1,0:T(8,128)S(1)} %get-tuple-element.23, f32[1,256,128]{2,1,0:T(8,128)S(1)} %get-tuple-element.28, f32[1,256,128]{2,1,0:T(8,128)S(1)} %get-tuple-element.26, ...), kind=kLoop, calls=%fused_computation.2 | loop fusion | flops 983040 | bytes 2621441 | tf_op jit(solution)/shard_map/jit(_where)/select_n | solution.py:220
  18.3 1.5 %collective-permute-start.7 = (f32[5,256,128]{2,1,0:T(8,128)}, f32[5,256,128]{2,1,0:T(8,128)}, u32[]{:S(2)}, u32[]{:S(2)}) collective-permute-start(f32[5,256,128]{2,1,0:T(8,128)} %get-tuple-element.16), channel_id=1, source_target_pairs={{1,2},{2,1},{3,4},{4,3},{5,6},{6,5},{9,10},{10,9},{11,12},{12,11},... | collective-permute-start | bytes 1966088 | tf_op jit(solution)/shard_map/ppermute | solution.py:220
  20.8 1.2 %copy-done.10 = bf16[1,512,8,128]{3,2,1,0:T(8,128)(2,1)S(1)} copy-done((bf16[1,512,8,128]{3,2,1,0:T(8,128)(2,1)S(1)}, bf16[1,512,8,128]{3,2,1,0:T(8,128)(2,1)}, u32[]{:S(2)}) %copy-start.10) | copy-done | bytes 1048600
  22.0 4.3 %shard_map.96 = (bf16[4096,512]{1,0:T(8,128)(2,1)S(1)}, bf16[512,4096]{1,0:T(8,128)(2,1)S(1)}, bf16[5,8,512,128]{3,2,1,0:T(8,128)(2,1)S(1)}) custom-call(s32[4096,128]{1,0:T(8,128)S(1)} %broadcast_in_dim.9.wide_ref, s32[1,4096]{1,0:T(1,128)S(1)} %fusion.2.flat_ref, s32[4096,128]{1,0:T(8,128)S(1)} %bitcast.62, bf16[4096,128]{1,0:T(8,128)(2,1)S(1)} %bitcast.64), custom_call_target="tpu_custom_call" | custom-call | tf_op jit(solution)/shard_map/pallas_call | solution.py:24
  26.3 2.3 %copy-done = bf16[5,8,512,128]{3,2,1,0:T(8,128)(2,1)} copy-done((bf16[5,8,512,128]{3,2,1,0:T(8,128)(2,1)}, bf16[5,8,512,128]{3,2,1,0:T(8,128)(2,1)S(1)}, u32[]{:S(2)}) %copy-start) | copy-done | bytes 5242904
  28.6 2.0 %copy-done.2 = bf16[4096,512]{1,0:T(8,128)(2,1)} copy-done((bf16[4096,512]{1,0:T(8,128)(2,1)}, bf16[4096,512]{1,0:T(8,128)(2,1)S(1)}, u32[]{:S(2)}) %copy-start.2) | copy-done | bytes 4194328
  30.6 2.1 %copy-done.4 = bf16[512,4096]{1,0:T(8,128)(2,1)} copy-done((bf16[512,4096]{1,0:T(8,128)(2,1)}, bf16[512,4096]{1,0:T(8,128)(2,1)S(1)}, u32[]{:S(2)}) %copy-start.4) | copy-done | bytes 4194328
  33.1 2.5 %copy-done.1 = bf16[5,8,512,128]{3,2,1,0:T(8,128)(2,1)S(1)} copy-done((bf16[5,8,512,128]{3,2,1,0:T(8,128)(2,1)S(1)}, bf16[5,8,512,128]{3,2,1,0:T(8,128)(2,1)}, u32[]{:S(2)}) %copy-start.1) | copy-done | bytes 5242904
  35.6 2.2 %copy-done.3 = bf16[4096,512]{1,0:T(8,128)(2,1)S(1)} copy-done((bf16[4096,512]{1,0:T(8,128)(2,1)S(1)}, bf16[4096,512]{1,0:T(8,128)(2,1)}, u32[]{:S(2)}) %copy-start.3) | copy-done | bytes 4194328
  37.7 2.2 %copy-done.5 = bf16[512,4096]{1,0:T(8,128)(2,1)S(1)} copy-done((bf16[512,4096]{1,0:T(8,128)(2,1)S(1)}, bf16[512,4096]{1,0:T(8,128)(2,1)}, u32[]{:S(2)}) %copy-start.5) | copy-done | bytes 4194328
  39.9 8.3 %shard_map.97 = (f32[512,128]{1,0:T(8,128)S(1)}, f32[512,128]{1,0:T(8,128)}) custom-call(f32[512,128]{1,0:T(8,128)S(1)} %bitcast.63, bf16[4096,512]{1,0:T(8,128)(2,1)S(1)} %copy-done.3, bf16[512,4096]{1,0:T(8,128)(2,1)S(1)} %copy-done.5, bf16[5,8,512,128]{3,2,1,0:T(8,128)(2,1)S(1)} %copy-done.1, f32[512,128]{1,0:T(8,128)S(1)} %bitcast.58), custom_call_target="tpu_custom_call" | custom-call | tf_op jit(solution)/shard_map/pallas_call | solution.py:24
  48.3 2.2 %collective-permute-start.8 = (f32[2,256,128]{2,1,0:T(8,128)S(1)}, f32[2,256,128]{2,1,0:T(8,128)S(1)}, u32[]{:S(2)}, u32[]{:S(2)}) collective-permute-start(f32[2,256,128]{2,1,0:T(8,128)S(1)} %bitcast.66), channel_id=1, source_target_pairs={{0,1},{1,0},{2,3},{3,2},{4,5},{5,4},{6,7},{7,6},{8,9},{9,8},{10,11... | collective-permute-start | bytes 786440 | tf_op jit(solution)/shard_map/ppermute | solution.py:221
  50.5 1.4 %collective-permute-start.9 = (f32[2,256,128]{2,1,0:T(8,128)S(1)}, f32[2,256,128]{2,1,0:T(8,128)}, u32[]{:S(2)}, u32[]{:S(2)}) collective-permute-start(f32[2,256,128]{2,1,0:T(8,128)S(1)} %bitcast.67), channel_id=1, source_target_pairs={{1,2},{2,1},{3,4},{4,3},{5,6},{6,5},{9,10},{10,9},{11,12},{12,11},... | collective-permute-start | bytes 786440 | tf_op jit(solution)/shard_map/ppermute | solution.py:220
  51.8 6.4 %all-to-all-start.1 = ((f32[32,16,128]{2,1,0:T(8,128)}), f32[32,16,128]{2,1,0:T(8,128)S(1)}, u32[]{:S(2)}, u32[]{:S(2)}) async-start(f32[32,16,128]{2,1,0:T(8,128)} %bitcast.11), calls=%async_computation.1 | async-start | bytes 524288 | tf_op jit(solution)/shard_map/all_to_all | solution.py:349
  58.2 1.4 %broadcast_select_fusion = (f32[5,256,128]{2,1,0:T(8,128)S(1)}, f32[5,256,128]{2,1,0:T(8,128)S(1)}) fusion(f32[5,256,128]{2,1,0:T(8,128)} %collective-permute-done.7, f32[5,256,128]{2,1,0:T(8,128)} %collective-permute-done.6, pred[]{:T(512)S(6)} %eq.12), kind=kLoop, calls=%fused_computation.10 | loop fusion | flops 327680 | bytes 2621441 | tf_op jit(solution)/shard_map/jit(_where)/select_n | solution.py:222
  61.4 7.2 %all-to-all-done.1 = f32[32,16,128]{2,1,0:T(8,128)S(1)} async-done(((f32[32,16,128]{2,1,0:T(8,128)}), f32[32,16,128]{2,1,0:T(8,128)S(1)}, u32[]{:S(2)}, u32[]{:S(2)}) %all-to-all-start.1) | async-done | bytes 262176 | tf_op jit(solution)/shard_map/all_to_all | solution.py:349
  70.4 1.4 %shard_map.100.field_ref = f32[3,2,256,128]{3,2,1,0:T(8,128)S(1)} custom-call(f32[3,2,256,128]{3,2,1,0:T(8,128)S(1)} %bitcast.57, f32[2,256,128]{2,1,0:T(8,128)S(1)} %bitcast.59, f32[2,256,128]{2,1,0:T(8,128)S(1)} %bitcast.60, f32[2,256,128]{2,1,0:T(8,128)S(1)} %bitcast.68, f32[5,256,128]{2,1,0:T(8,128)S(1)} %get-tuple-element.15.low_ref, ...), custom_call_target="tpu_custom_call" | custom-call | tf_op jit(solution)/shard_map/pallas_call | solution.py:24
  74.5 2.1 %collective-permute-start.5 = (f32[128,128]{1,0:T(8,128)S(1)}, f32[128,128]{1,0:T(8,128)S(1)}, u32[]{:S(2)}, u32[]{:S(2)}) collective-permute-start(f32[128,128]{1,0:T(8,128)S(1)} %shard_map.98.refs_0_), channel_id=1, source_target_pairs={{0,24},{8,16},{16,8},{24,0},{1,25},{9,17},{17,9},{25,1},{2,26},{10... | collective-permute-start | bytes 196616 | tf_op jit(solution)/shard_map/ppermute | solution.py:211
  78.6 1.5 %collective-permute-done.5.refs_3_ = f32[128,128]{1,0:T(8,128)S(1)} collective-permute-done((f32[128,128]{1,0:T(8,128)S(1)}, f32[128,128]{1,0:T(8,128)S(1)}, u32[]{:S(2)}, u32[]{:S(2)}) %collective-permute-start.5) | collective-permute-done | bytes 65568 | tf_op jit(solution)/shard_map/ppermute | solution.py:211
  81.2 1.9 %shard_map.101 = f32[3,2,256,128]{3,2,1,0:T(8,128)} custom-call(f32[3,2,256,128]{3,2,1,0:T(8,128)S(1)} %shard_map.100.field_ref, f32[2,256,128]{2,1,0:T(8,128)S(1)} %bitcast.61, f32[3,256,128]{2,1,0:T(8,128)S(1)} %get-tuple-element.19.low_ref, f32[3,256,128]{2,1,0:T(8,128)S(1)} %get-tuple-element.18.high_ref, f32[1,256,128]{2,1,0:T(8,128)S(1)} %slice.54.coef_low_ref, ...), custom_call_target="tpu_custom_call" | custom-call | tf_op jit(solution)/shard_map/pallas_call | solution.py:24
  (73 shorter events, 15.9 us)
Async XLA Ops:
  0.6 20.2 %copy-start.9 = (s32[1,512,8,128]{3,2,1,0:T(8,128)S(1)}, s32[1,512,8,128]{3,2,1,0:T(8,128)}, u32[]{:S(2)}) copy-start(s32[1,512,8,128]{3,2,1,0:T(8,128)} %param.14) | copy-start | bytes 6291460
  0.6 32.0 %collective-permute-start = (s32[8,64]{1,0:T(8,128)}, s32[8,64]{1,0:T(8,128)S(1)}, u32[]{:S(2)}, u32[]{:S(2)}) collective-permute-start(s32[8,64]{1,0:T(8,128)} %bitcast.69), channel_id=1, source_target_pairs={{0,8},{8,0},{16,24},{24,16},{1,9},{9,1},{17,25},{25,17},{2,10},{10... | collective-permute-start | bytes 6152 | tf_op jit(solution)/shard_map/ppermute | solution.py:211
  3.6 29.1 %collective-permute-start.1 = (s32[8,64]{1,0:T(8,128)}, s32[8,64]{1,0:T(8,128)S(1)}, u32[]{:S(2)}, u32[]{:S(2)}) collective-permute-start(s32[8,64]{1,0:T(8,128)} %bitcast.70), channel_id=1, source_target_pairs={{0,16},{8,24},{16,0},{24,8},{1,17},{9,25},{17,1},{25,9},{2,18},{10... | collective-permute-start | bytes 6152 | tf_op jit(solution)/shard_map/ppermute | solution.py:211
  5.2 27.7 %collective-permute-start.2 = (s32[8,64]{1,0:T(8,128)}, s32[8,64]{1,0:T(8,128)S(1)}, u32[]{:S(2)}, u32[]{:S(2)}) collective-permute-start(s32[8,64]{1,0:T(8,128)} %bitcast.71), channel_id=1, source_target_pairs={{0,24},{8,16},{16,8},{24,0},{1,25},{9,17},{17,9},{25,1},{2,26},{10... | collective-permute-start | bytes 6152 | tf_op jit(solution)/shard_map/ppermute | solution.py:211
  6.8 13.0 %copy-start.18 = (s32[1,512,8]{1,2,0:T(8,128)S(1)}, s32[1,512,8]{1,2,0:T(8,128)}, u32[]{:S(2)}) copy-start(s32[1,512,8]{1,2,0:T(8,128)} %param.13) | copy-start | bytes 49156
  6.8 13.3 %copy-start.16 = (s32[1,1,8,64]{3,2,1,0:T(8,128)S(1)}, s32[1,1,8,64]{3,2,1,0:T(8,128)}, u32[]{:S(2)}) copy-start(s32[1,1,8,64]{3,2,1,0:T(8,128)} %param.12) | copy-start | bytes 6148
  8.1 24.9 %all-to-all-start = ((f32[8,64,128]{2,1,0:T(8,128)}), f32[8,64,128]{2,1,0:T(8,128)S(1)}, u32[]{:S(2)}, u32[]{:S(2)}) async-start(f32[8,64,128]{2,1,0:T(8,128)} %bitcast.3), calls=%async_computation | async-start | bytes 524288 | tf_op jit(solution)/shard_map/all_to_all | solution.py:307
  17.8 15.3 %copy-start.7 = (f32[1,512,128]{2,1,0:T(8,128)S(1)}, f32[1,512,128]{2,1,0:T(8,128)}, u32[]{:S(2)}) copy-start(f32[1,512,128]{2,1,0:T(8,128)} %param.9) | copy-start | bytes 786436
  17.8 40.4 %collective-permute-start.6 = (f32[5,256,128]{2,1,0:T(8,128)}, f32[5,256,128]{2,1,0:T(8,128)}, u32[]{:S(2)}, u32[]{:S(2)}) collective-permute-start(f32[5,256,128]{2,1,0:T(8,128)} %get-tuple-element.17), channel_id=1, source_target_pairs={{0,1},{1,0},{2,3},{3,2},{4,5},{5,4},{6,7},{7,6},{8,9},{9,8},{10,11... | collective-permute-start | bytes 1966088 | tf_op jit(solution)/shard_map/ppermute | solution.py:221
  18.3 39.9 %collective-permute-start.7 = (f32[5,256,128]{2,1,0:T(8,128)}, f32[5,256,128]{2,1,0:T(8,128)}, u32[]{:S(2)}, u32[]{:S(2)}) collective-permute-start(f32[5,256,128]{2,1,0:T(8,128)} %get-tuple-element.16), channel_id=1, source_target_pairs={{1,2},{2,1},{3,4},{4,3},{5,6},{6,5},{9,10},{10,9},{11,12},{12,11},... | collective-permute-start | bytes 1966088 | tf_op jit(solution)/shard_map/ppermute | solution.py:220
  26.3 2.3 %copy-start = (bf16[5,8,512,128]{3,2,1,0:T(8,128)(2,1)}, bf16[5,8,512,128]{3,2,1,0:T(8,128)(2,1)S(1)}, u32[]{:S(2)}) copy-start(bf16[5,8,512,128]{3,2,1,0:T(8,128)(2,1)S(1)} %get-tuple-element.10.moved_ref) | copy-start | bytes 15728644
  33.1 2.5 %copy-start.1 = (bf16[5,8,512,128]{3,2,1,0:T(8,128)(2,1)S(1)}, bf16[5,8,512,128]{3,2,1,0:T(8,128)(2,1)}, u32[]{:S(2)}) copy-start(bf16[5,8,512,128]{3,2,1,0:T(8,128)(2,1)} %copy-done) | copy-start | bytes 15728644
  48.3 11.4 %copy-start.13 = (f32[512,128]{1,0:T(8,128)}, f32[512,128]{1,0:T(8,128)S(1)}, u32[]{:S(2)}) copy-start(f32[512,128]{1,0:T(8,128)S(1)} %get-tuple-element.12) | copy-start | bytes 786436
  48.3 21.2 %copy-start.6 = (f32[1,3,512,128]{3,2,1,0:T(8,128)S(1)}, f32[1,3,512,128]{3,2,1,0:T(8,128)}, u32[]{:S(2)}) copy-start(f32[1,3,512,128]{3,2,1,0:T(8,128)} %param.10) | copy-start | bytes 2359300
  48.3 21.2 %copy-start.8 = (f32[512,128]{1,0:T(8,128)S(1)}, f32[512,128]{1,0:T(8,128)}, u32[]{:S(2)}) copy-start(f32[512,128]{1,0:T(8,128)} %param.11) | copy-start | bytes 786436
  48.3 11.4 %collective-permute-start.8 = (f32[2,256,128]{2,1,0:T(8,128)S(1)}, f32[2,256,128]{2,1,0:T(8,128)S(1)}, u32[]{:S(2)}, u32[]{:S(2)}) collective-permute-start(f32[2,256,128]{2,1,0:T(8,128)S(1)} %bitcast.66), channel_id=1, source_target_pairs={{0,1},{1,0},{2,3},{3,2},{4,5},{5,4},{6,7},{7,6},{8,9},{9,8},{10,11... | collective-permute-start | bytes 786440 | tf_op jit(solution)/shard_map/ppermute | solution.py:221
  50.5 9.9 %collective-permute-start.9 = (f32[2,256,128]{2,1,0:T(8,128)S(1)}, f32[2,256,128]{2,1,0:T(8,128)}, u32[]{:S(2)}, u32[]{:S(2)}) collective-permute-start(f32[2,256,128]{2,1,0:T(8,128)S(1)} %bitcast.67), channel_id=1, source_target_pairs={{1,2},{2,1},{3,4},{4,3},{5,6},{6,5},{9,10},{10,9},{11,12},{12,11},... | collective-permute-start | bytes 786440 | tf_op jit(solution)/shard_map/ppermute | solution.py:220
  51.8 16.8 %all-to-all-start.1 = ((f32[32,16,128]{2,1,0:T(8,128)}), f32[32,16,128]{2,1,0:T(8,128)S(1)}, u32[]{:S(2)}, u32[]{:S(2)}) async-start(f32[32,16,128]{2,1,0:T(8,128)} %bitcast.11), calls=%async_computation.1 | async-start | bytes 524288 | tf_op jit(solution)/shard_map/all_to_all | solution.py:349
  68.6 11.5 %copy-start.12 = (f32[512,128]{1,0:T(8,128)S(1)}, f32[512,128]{1,0:T(8,128)}, u32[]{:S(2)}) copy-start(f32[512,128]{1,0:T(8,128)} %template_ref.3) | copy-start | bytes 786436
  71.9 9.2 %collective-permute-start.10 = (f32[3,256,128]{2,1,0:T(8,128)S(1)}, f32[3,256,128]{2,1,0:T(8,128)S(1)}, u32[]{:S(2)}, u32[]{:S(2)}) collective-permute-start(f32[3,256,128]{2,1,0:T(8,128)S(1)} %get-tuple-element.21), channel_id=1, source_target_pairs={{0,1},{1,0},{2,3},{3,2},{4,5},{5,4},{6,7},{7,6},{8,9},{9,8},{10,11... | collective-permute-start | bytes 1179656 | tf_op jit(solution)/shard_map/ppermute | solution.py:221
  72.4 8.8 %collective-permute-start.11 = (f32[3,256,128]{2,1,0:T(8,128)S(1)}, f32[3,256,128]{2,1,0:T(8,128)S(1)}, u32[]{:S(2)}, u32[]{:S(2)}) collective-permute-start(f32[3,256,128]{2,1,0:T(8,128)S(1)} %get-tuple-element.20), channel_id=1, source_target_pairs={{1,2},{2,1},{3,4},{4,3},{5,6},{6,5},{9,10},{10,9},{11,12},{12,11},... | collective-permute-start | bytes 1179656 | tf_op jit(solution)/shard_map/ppermute | solution.py:220
  73.1 4.6 %collective-permute-start.3 = (f32[128,128]{1,0:T(8,128)S(1)}, f32[128,128]{1,0:T(8,128)S(1)}, u32[]{:S(2)}, u32[]{:S(2)}) collective-permute-start(f32[128,128]{1,0:T(8,128)S(1)} %shard_map.98.refs_0_), channel_id=1, source_target_pairs={{0,8},{8,0},{16,24},{24,16},{1,9},{9,1},{17,25},{25,17},{2,10},{10... | collective-permute-start | bytes 196616 | tf_op jit(solution)/shard_map/ppermute | solution.py:211
  73.9 4.7 %collective-permute-start.4 = (f32[128,128]{1,0:T(8,128)S(1)}, f32[128,128]{1,0:T(8,128)S(1)}, u32[]{:S(2)}, u32[]{:S(2)}) collective-permute-start(f32[128,128]{1,0:T(8,128)S(1)} %shard_map.98.refs_0_), channel_id=1, source_target_pairs={{0,16},{8,24},{16,0},{24,8},{1,17},{9,25},{17,1},{25,9},{2,18},{10... | collective-permute-start | bytes 196616 | tf_op jit(solution)/shard_map/ppermute | solution.py:211
  74.5 5.6 %collective-permute-start.5 = (f32[128,128]{1,0:T(8,128)S(1)}, f32[128,128]{1,0:T(8,128)S(1)}, u32[]{:S(2)}, u32[]{:S(2)}) collective-permute-start(f32[128,128]{1,0:T(8,128)S(1)} %shard_map.98.refs_0_), channel_id=1, source_target_pairs={{0,24},{8,16},{16,8},{24,0},{1,25},{9,17},{17,9},{25,1},{2,26},{10... | collective-permute-start | bytes 196616 | tf_op jit(solution)/shard_map/ppermute | solution.py:211
  (9 other events, 13.0 us)

commit v3 on v2

v3 whole, which is shorter than its diff:
```python
import functools

import jax
import jax.numpy as jnp
from jax import lax
from jax.experimental import pallas as pl
from jax.experimental.pallas import tpu as pltpu
from jax.sharding import PartitionSpec as P

YR = 256
LANES = 128
OFFSETS = (0, -2, -1, 1, 2)


force_step = 1.0
diffusion_dt = 0.16
template_rate = 2.0

VMEM_LIMIT = 40 * 1024 * 1024
COST = 1024


def call(kernel, out_shape, *args, scratch=(), smem=(), far=(), out_far=(), cost=None):
    many = isinstance(out_shape, tuple)
    shapes = [
        pltpu.HBM(s.shape, s.dtype) if i in out_far else s
        for i, s in enumerate(out_shape if many else (out_shape,))
    ]
    spaces = [pltpu.HBM if i in out_far else pltpu.VMEM for i in range(len(shapes))]
    specs = [pl.BlockSpec(memory_space=space) for space in spaces]
    return pl.pallas_call(
        kernel,
        out_shape=tuple(shapes) if many else shapes[0],
        in_specs=[
            pl.BlockSpec(
                memory_space=pltpu.SMEM if i in smem else pltpu.HBM if i in far else pltpu.VMEM
            )
            for i in range(len(args))
        ],
        out_specs=tuple(specs) if many else specs[0],
        scratch_shapes=scratch,
        cost_estimate=cost and pl.CostEstimate(flops=0, transcendentals=0, bytes_accessed=cost),
        compiler_params=pltpu.CompilerParams(vmem_limit_bytes=VMEM_LIMIT),
    )(
        *[
            pltpu.with_memory_space_constraint(arg, pltpu.HBM) if i in far else arg
            for i, arg in enumerate(args)
        ]
    )


def halves(values):
    high = values.astype(jnp.bfloat16)
    low = (values - high.astype(jnp.float32)).astype(jnp.bfloat16)
    return jnp.concatenate([high, low], axis=1)


def joined(pair):
    width = pair.shape[1] // 2
    return pair[:, :width] + pair[:, width:]


def turned(values, shift):
    shift %= values.shape[1]
    return pltpu.roll(values, shift, axis=1) if shift else values


def dot(left, right):
    return jnp.dot(left, right, preferred_element_type=jnp.float32)


def one_hot(matches):
    return jnp.where(matches, 1.0, 0.0).astype(jnp.bfloat16)


def send_kernel(send_ref, template_ref, out_ref, send, template, sem):
    slabs, capacity = send.shape
    rows = template.shape[0]
    copies = [
        pltpu.make_async_copy(send_ref, send, sem.at[0]),
        pltpu.make_async_copy(template_ref, template, sem.at[1]),
    ]
    for copy in copies:
        copy.start()
    copies[0].wait()
    padded = jnp.concatenate([send[...], jnp.zeros((slabs, LANES - capacity), jnp.int32)], axis=1)
    columns = padded.T
    number = lax.broadcasted_iota(jnp.int32, (capacity, rows), 1)
    chosen = [
        one_hot(jnp.broadcast_to(columns[:capacity, k : k + 1], (capacity, rows)) == number)
        for k in range(slabs)
    ]
    copies[1].wait()
    pair = halves(template[...])
    for k in range(slabs):
        out_ref[k * capacity : (k + 1) * capacity, :] = joined(dot(chosen[k], pair))


def prepare_kernel(
    place_ref,
    columns_ref,
    weights_ref,
    velocity_ref,
    stiffness_ref,
    images_ref,
    moved_ref,
    near_ref,
    far_ref,
    columns,
    weights,
    plain,
    moved,
    edge,
    in_sem,
    out_sem,
    edge_sem,
):
    chunks, each, count, some, width = moved.shape
    odd = place_ref[0]
    near_plane, far_plane = pl.ds((edge.shape[1] - 1) * (1 - odd), 1), pl.ds((edge.shape[1] - 1) * odd, 1)
    step = some * each
    parts = velocity_ref.shape[0]
    reads = [
        (
            pltpu.make_async_copy(
                columns_ref.at[pl.ds(i * step, step)], columns.at[pl.ds(i * step, step)], in_sem.at[i]
            ),
            pltpu.make_async_copy(
                weights_ref.at[pl.ds(i * step, step)],
                weights.at[pl.ds(i * step, step)],
                in_sem.at[chunks + i],
            ),
        )
        for i in range(chunks)
    ]
    edges = [
        pltpu.make_async_copy(velocity_ref, edge.at[pl.ds(0, parts)], edge_sem.at[0]),
        pltpu.make_async_copy(stiffness_ref, edge.at[parts], edge_sem.at[1]),
        pltpu.make_async_copy(images_ref, edge.at[parts + 1], edge_sem.at[2]),
    ]
    writes = [
        pltpu.make_async_copy(moved.at[i], moved_ref.at[i], out_sem.at[i]) for i in range(chunks)
    ] + [
        pltpu.make_async_copy(edge.at[:, near_plane], near_ref, out_sem.at[chunks]),
        pltpu.make_async_copy(edge.at[:, far_plane], far_ref, out_sem.at[chunks + 1]),
    ]
    for copy in reads[0]:
        copy.start()
    for copy in edges:
        copy.start()
    for pair in reads[1:]:
        for copy in pair:
            copy.start()
    cell = lax.broadcasted_iota(jnp.int32, (some, width), 1)
    for i in range(chunks):
        at = i * step
        for copy in reads[i]:
            copy.wait()
        plain[...] = weights[at : at + step, :].astype(jnp.float32)
        for b in range(each):
            offset = columns[pl.ds(at + b, some, stride=each), :] - cell
            here = plain[pl.ds(b, some, stride=each), :]
            for j, o in enumerate(OFFSETS):
                kept = jnp.where(offset == o, here, 0.0)
                moved[i, b, j] = turned(kept, o).astype(jnp.bfloat16)
        writes[i].start()
        if i == 0:
            for copy in edges:
                copy.wait()
            for copy in writes[chunks:]:
                copy.start()
    for copy in writes:
        copy.wait()


def warp_kernel(
    slabs,
    subjects,
    slot_ref,
    received_ref,
    moved_ref,
    images_ref,
    warped_ref,
    sent_ref,
    received,
    images,
    moved,
    picked,
    placed,
    first_sem,
    moved_sem,
):
    slots, width = received.shape
    chunks, each, count, some = moved.shape[:4]
    rows = chunks * some
    block = width // subjects
    group = slots // subjects
    capacity = slots // slabs
    held = capacity // subjects
    first = [
        pltpu.make_async_copy(received_ref, received, first_sem.at[0]),
        pltpu.make_async_copy(images_ref, images, first_sem.at[1]),
    ]
    moves = [
        pltpu.make_async_copy(moved_ref.at[i], moved.at[i], moved_sem.at[i]) for i in range(chunks)
    ]
    for copy in first + moves:
        copy.start()
    slot = slot_ref[...]
    slot_wide = jnp.concatenate([slot, jnp.zeros((LANES - each, rows), jnp.int32)], axis=0).T
    inner = slot % capacity
    packed = (inner // held) * group + (slot // capacity) * held + inner % held
    lane = lax.broadcasted_iota(jnp.int32, (rows, LANES), 1)
    number = lax.broadcasted_iota(jnp.int32, (slots, rows), 0)
    first[0].wait()
    pair = halves(received[...])
    for b in range(each):
        wide = jnp.broadcast_to(slot_wide[:, b : b + 1], (rows, LANES))
        pick = jnp.concatenate(
            [one_hot(wide == lane + t * LANES) for t in range(slots // LANES)], axis=1
        )
        picked[b] = joined(dot(pick, pair))
    first[1].wait()
    for i in range(chunks):
        moves[i].wait()
        at = slice(i * some, (i + 1) * some)
        sums = [jnp.zeros((some, width), jnp.float32) for _ in OFFSETS]
        for b in range(each):
            values = picked[b, at, :]
            for j in range(count):
                sums[j] = sums[j] + moved[i, b, j].astype(jnp.float32) * values
        warped = sums[0]
        for j, o in enumerate(OFFSETS[1:], 1):
            warped = warped + turned(sums[j], -o)
        warped_ref[at, :] = warped
        mismatch = warped - images[at, :]
        ahead = [turned(mismatch, o) for o in OFFSETS]
        for b in range(each):
            total = moved[i, b, 0].astype(jnp.float32) * ahead[0]
            for j in range(1, count):
                total = total + moved[i, b, j].astype(jnp.float32) * ahead[j]
            placed[b, at, :] = halves(total)
    total = jnp.zeros((slots, 2 * width), jnp.float32)
    for b in range(each):
        drop = one_hot(jnp.broadcast_to(packed[b : b + 1], (slots, rows)) == number)
        total = total + dot(drop, placed[b])
    total = joined(total)
    place = lax.broadcasted_iota(jnp.int32, (group, width), 1) // block
    groups = [total[q * group : (q + 1) * group, :] for q in range(subjects)]
    for p in range(subjects):
        out = jnp.zeros((group, width), jnp.float32)
        for q in range(subjects):
            out = jnp.where(place == q, turned(groups[q], (q - p) * block), out)
        sent_ref[p * group : (p + 1) * group, :] = out


def collect_kernel(subjects, me_ref, returned_ref, *refs):
    row_refs, out_ref = refs[:-1], refs[-1]
    slots, width = returned_ref.shape
    slabs, capacity = row_refs[0].shape
    rows = out_ref.shape[0] * subjects
    block = width // subjects
    group = slots // subjects
    held = capacity // subjects
    me = me_ref[0]
    pair = halves(
        jnp.concatenate(
            [
                returned_ref[pl.ds(pl.multiple_of((me ^ d) * group, group), group), :]
                for d in range(subjects)
            ]
        )
    )
    lane = lax.broadcasted_iota(jnp.int32, (slabs, LANES), 1)
    slab = lax.broadcasted_iota(jnp.int32, (slabs, LANES), 0)
    fill = jnp.zeros((slabs, LANES - capacity), jnp.int32)
    wanted = []
    for q in range(subjects):
        chunks = [jnp.zeros((1, LANES), jnp.int32) for _ in range(slots // LANES)]
        for d in range(subjects):
            spread = jnp.concatenate([row_refs[d][...], fill], axis=1)
            spread = turned(spread, d * group - q * held)
            spread = pltpu.roll(spread, 0, axis=1, stride=held, stride_axis=0)
            first = (d * group) % LANES + slab * held
            kept = jnp.where((lane >= first) & (lane < first + held), spread, 0)
            chunks[d * group // LANES] += jnp.sum(kept, axis=0, keepdims=True)
        wanted.append(jnp.concatenate(chunks, axis=1))
    number = lax.broadcasted_iota(jnp.int32, (rows, slots), 0)
    place = lax.broadcasted_iota(jnp.int32, (rows, width), 1) // block
    kept = jnp.zeros((rows, width), jnp.float32)
    for q in range(subjects):
        match = jnp.broadcast_to(wanted[q], (rows, slots)) == number
        kept = jnp.where(place == q, joined(dot(one_hot(match), pair)), kept)
    turn = block
    while turn < width:
        kept = kept + turned(kept, turn)
        turn *= 2
    part = rows // subjects
    out = jnp.zeros((part, width), jnp.float32)
    for p in range(subjects):
        out = jnp.where(place[:part] == p, kept[p * part : (p + 1) * part], out)
    out_ref[...] = out


def update_kernel(subjects, me_ref, template_ref, *refs):
    parts, out_ref = refs[:-1], refs[-1]
    rows, width = template_ref.shape
    block = width // subjects
    part = rows // subjects
    me = me_ref[0]
    place = lax.broadcasted_iota(jnp.int32, (part, width), 1) // block
    for p in range(subjects):
        total = jnp.zeros((part, width), jnp.float32)
        for d in range(subjects):
            source = me ^ d
            turn = lax.rem((source - p) * block + width, width)
            total = jnp.where(place == source, pltpu.roll(parts[d][...], turn, axis=1), total)
        at = slice(p * part, (p + 1) * part)
        out_ref[at, :] = template_ref[at, :] - template_rate * total / subjects


def over_subjects(values):
    count = lax.axis_size("subj")
    return [values] + [
        lax.ppermute(values, "subj", [(i, i ^ d) for i in range(count)]) for d in range(1, count)
    ]


def swap_near(values):
    return lax.ppermute(values, "slab", [(i, i ^ 1) for i in range(lax.axis_size("slab"))])


def swap_far(values):
    count = lax.axis_size("slab")
    return lax.ppermute(
        values, "slab", [(i, i + 1 if i % 2 else i - 1) for i in range(1, count - 1)]
    )


def shifted(values, step, axis):
    size = values.shape[axis]
    index = lax.broadcasted_iota(jnp.int32, values.shape, axis)
    edge = size - 1 if step > 0 else 0
    return jnp.where(index == edge, 0.0, pltpu.roll(values, (-step) % size, axis=axis))


def flow(center, half, faces):
    total = None
    for axis in (0, 1):
        flux = faces[axis] * (shifted(center, 1, axis) - center)
        index = lax.broadcasted_iota(jnp.int32, center.shape, axis)
        behind = jnp.where(index == 0, half * center, pltpu.roll(flux, 1, axis=axis))
        total = flux - behind if total is None else total + (flux - behind)
    return total


def by_side(odd, pairs):
    copies = [
        (
            [pltpu.make_async_copy(near, low, sems[0]), pltpu.make_async_copy(far, high, sems[1])],
            [pltpu.make_async_copy(near, high, sems[0]), pltpu.make_async_copy(far, low, sems[1])],
        )
        for near, far, low, high, sems in pairs
    ]

    @pl.when(odd)
    def _():
        for when_odd, _ in copies:
            for copy in when_odd:
                copy.start()

    @pl.when(jnp.logical_not(odd))
    def _():
        for _, when_even in copies:
            for copy in when_even:
                copy.start()

    return [copy for when_odd, _ in copies for copy in when_odd]


def diffuse(now, coefs, first, last):
    half = [0.5 * coef for coef in coefs]
    gaps = {p: half[p] + half[p + 1] for p in range(first - 1, last + 1)}
    faces = {
        p: [half[p] + shifted(half[p], 1, axis) for axis in (0, 1)] for p in range(first, last + 1)
    }
    later = []
    for field in now:
        rise = {p: gaps[p] * (field[p + 1] - field[p]) for p in gaps}
        later.append(
            [
                field[p]
                + diffusion_dt * (rise[p] - rise[p - 1] + flow(field[p], half[p], faces[p]))
                for p in range(first, last + 1)
            ]
        )
    return later


def force_kernel(
    place_ref,
    velocity_ref,
    images_ref,
    stiffness_ref,
    warped_ref,
    edge_near_ref,
    edge_far_ref,
    warped_near_ref,
    warped_far_ref,
    out_ref,
    near_ref,
    far_ref,
    fields,
    images,
    coefs,
    warped,
    sem,
):
    parts, planes = out_ref.shape[:2]
    odd = place_ref[0] == 1
    low, mid, high = pl.ds(0, 1), pl.ds(1, planes), pl.ds(planes + 1, 1)
    every = pl.ds(0, parts)
    waits = by_side(
        odd,
        [
            (
                warped_near_ref,
                warped_far_ref,
                warped.at[pl.ds(0, 2)],
                warped.at[pl.ds(planes + 2, 2)],
                (sem.at[0], sem.at[1]),
            ),
            (
                edge_near_ref.at[parts],
                edge_far_ref.at[parts],
                coefs.at[low],
                coefs.at[high],
                (sem.at[2], sem.at[3]),
            ),
            (
                edge_near_ref.at[parts + 1],
                edge_far_ref.at[parts + 1],
                images.at[low],
                images.at[high],
                (sem.at[4], sem.at[5]),
            ),
            (
                edge_near_ref.at[every],
                edge_far_ref.at[every],
                fields.at[:, low],
                fields.at[:, high],
                (sem.at[6], sem.at[7]),
            ),
        ],
    )
    own = [
        pltpu.make_async_copy(warped_ref, warped.at[pl.ds(2, planes)], sem.at[8]),
        pltpu.make_async_copy(stiffness_ref, coefs.at[mid], sem.at[9]),
        pltpu.make_async_copy(images_ref, images.at[mid], sem.at[10]),
        pltpu.make_async_copy(velocity_ref, fields.at[:, mid], sem.at[11]),
    ]
    for copy in own:
        copy.start()
    for copy in waits + own:
        copy.wait()
    now = [[] for _ in range(parts)]
    for p in range(planes + 2):
        here = warped[p + 1]
        mismatch = here - images[p]
        slopes = [
            0.5 * (shifted(here, 1, 1) - shifted(here, -1, 1)),
            0.5 * (shifted(here, 1, 0) - shifted(here, -1, 0)),
            0.5 * (warped[p + 2] - warped[p]),
        ]
        for a in range(parts):
            now[a].append(fields[a, p] - force_step * mismatch * slopes[a])
    later = diffuse(now, [coefs[p] for p in range(planes + 2)], 1, planes)
    for a in range(parts):
        for p in range(planes):
            out_ref[a, p] = later[a][p]
        near_ref[a, 0] = jnp.where(odd, later[a][0], later[a][-1])
        far_ref[a, 0] = jnp.where(odd, later[a][-1], later[a][0])


def last_kernel(
    place_ref,
    field_ref,
    stiffness_ref,
    edge_near_ref,
    edge_far_ref,
    near_ref,
    far_ref,
    out_ref,
    fields,
    coefs,
    sem,
):
    parts, planes = out_ref.shape[:2]
    low, mid, high = pl.ds(0, 1), pl.ds(1, planes), pl.ds(planes + 1, 1)
    waits = by_side(
        place_ref[0] == 1,
        [
            (near_ref, far_ref, fields.at[:, low], fields.at[:, high], (sem.at[0], sem.at[1])),
            (
                edge_near_ref.at[parts],
                edge_far_ref.at[parts],
                coefs.at[low],
                coefs.at[high],
                (sem.at[2], sem.at[3]),
            ),
        ],
    )
    own = [
        pltpu.make_async_copy(field_ref, fields.at[:, mid], sem.at[4]),
        pltpu.make_async_copy(stiffness_ref, coefs.at[mid], sem.at[5]),
    ]
    for copy in own:
        copy.start()
    for copy in waits + own:
        copy.wait()
    now = [[fields[a, p] for p in range(planes + 2)] for a in range(parts)]
    later = diffuse(now, [coefs[p] for p in range(planes + 2)], 1, planes)
    for a in range(parts):
        for p in range(planes):
            out_ref[a, p] = later[a][p]


def per_device(template, images, velocity, stiffness, send_rows, ref_slot, columns, weights):
    f32, bf16 = jnp.float32, jnp.bfloat16
    shape = jax.ShapeDtypeStruct
    slabs = lax.axis_size("slab")
    subjects = lax.axis_size("subj")
    me = lax.axis_index("subj").astype(jnp.int32).reshape(1)
    slab = lax.axis_index("slab")
    odd = slab % 2 == 1
    place = odd.astype(jnp.int32).reshape(1)
    capacity = send_rows.shape[3]
    rows, width = template.shape
    planes = rows // YR
    parts = velocity.shape[1]
    each = ref_slot.shape[2]
    terms = rows * each
    slots = slabs * capacity
    grid = (planes, YR, width)
    velocity_grid = velocity[0].reshape((parts,) + grid)
    images_grid = images[0].reshape(grid)
    coef_grid = stiffness.reshape(grid)
    dma = pltpu.SemaphoreType.DMA

    sending = call(
        send_kernel,
        shape((slots, width), f32),
        send_rows[0, 0],
        template,
        far=(0, 1),
        scratch=(pltpu.VMEM((slabs, capacity), jnp.int32), pltpu.VMEM((rows, width), f32), dma((2,))),
    )
    received = lax.all_to_all(sending, "slab", split_axis=0, concat_axis=0, tiled=True)

    chunks = 4
    moved_shape = (chunks, each, len(OFFSETS), rows // chunks, width)
    edge_shape = (parts + 2, 1, YR, width)
    moved, edge_near, edge_far = call(
        prepare_kernel,
        (shape(moved_shape, bf16), shape(edge_shape, f32), shape(edge_shape, f32)),
        place,
        columns.reshape(terms, width),
        weights.reshape(terms, width),
        velocity_grid,
        coef_grid,
        images_grid,
        smem=(0,),
        far=(1, 2, 3, 4, 5),
        out_far=(0, 1, 2),
        scratch=(
            pltpu.VMEM((terms, width), jnp.int32),
            pltpu.VMEM((terms, width), bf16),
            pltpu.VMEM((terms // chunks, width), f32),
            pltpu.VMEM(moved_shape, bf16),
            pltpu.VMEM((parts + 2,) + grid, f32),
            dma((2 * chunks,)),
            dma((chunks + 2,)),
            dma((3,)),
        ),
    )
    edge_far, edge_near = swap_far(edge_far), swap_near(edge_near)

    warped, sent = call(
        functools.partial(warp_kernel, slabs, subjects),
        (shape((rows, width), f32), shape((slots, width), f32)),
        ref_slot[0].T,
        received,
        moved,
        images[0],
        far=(1, 2, 3),
        cost=COST,
        scratch=(
            pltpu.VMEM((slots, width), f32),
            pltpu.VMEM((rows, width), f32),
            pltpu.VMEM(moved_shape, bf16),
            pltpu.VMEM((each, rows, width), f32),
            pltpu.VMEM((each, rows, 2 * width), bf16),
            dma((2,)),
            dma((chunks,)),
        ),
    )
    sent, edge_far, edge_near = lax.optimization_barrier((sent, edge_far, edge_near))
    returned = lax.all_to_all(sent, ("subj", "slab"), split_axis=0, concat_axis=0, tiled=True)

    own_rows, warped = lax.optimization_barrier((send_rows[0, 0], warped))
    warped_grid = warped.reshape(grid)
    warped_far, warped_near = swap_far(warped_grid), swap_near(warped_grid)
    all_rows = over_subjects(own_rows)

    field, field_near, field_far = call(
        force_kernel,
        (
            shape((parts,) + grid, f32),
            shape((parts, 1, YR, width), f32),
            shape((parts, 1, YR, width), f32),
        ),
        place,
        velocity_grid,
        images_grid,
        coef_grid,
        warped_grid,
        edge_near,
        edge_far,
        warped_near,
        warped_far,
        smem=(0,),
        far=tuple(range(1, 9)),
        cost=COST,
        scratch=(
            pltpu.VMEM((parts, planes + 2, YR, width), f32),
            pltpu.VMEM((planes + 2, YR, width), f32),
            pltpu.VMEM((planes + 2, YR, width), f32),
            pltpu.VMEM((planes + 4, YR, width), f32),
            dma((12,)),
        ),
    )
    field_far, field_near = swap_far(field_far), swap_near(field_near)

    part = call(
        functools.partial(collect_kernel, subjects),
        shape((rows // subjects, width), f32),
        me,
        returned,
        *all_rows,
        smem=(0,),
    )
    pieces = over_subjects(part)
    template_out = call(
        functools.partial(update_kernel, subjects),
        shape((rows, width), f32),
        me,
        template,
        *pieces,
        smem=(0,),
    )
    field = call(
        last_kernel,
        shape((parts,) + grid, f32),
        place,
        field,
        coef_grid,
        edge_near,
        edge_far,
        field_near,
        field_far,
        smem=(0,),
        far=tuple(range(1, 7)),
        scratch=(
            pltpu.VMEM((parts, planes + 2, YR, width), f32),
            pltpu.VMEM((planes + 2, YR, width), f32),
            dma((6,)),
        ),
    )
    velocity_out = field.reshape(parts, rows, width)[None]
    return (template_out, velocity_out)


def solution(mesh):
    return jax.shard_map(
        per_device,
        mesh=mesh,
        in_specs=(
            P("slab", None),
            P("subj", "slab", None),
            P("subj", None, "slab", None),
            P("slab", None),
            P("subj", "slab", None, None),
            P("subj", "slab", None),
            P("subj", "slab", None, None),
            P("subj", "slab", None, None),
        ),
        out_specs=(P("slab", None), P("subj", None, "slab", None)),
        check_vma=False,
    )
```

time: 83.8 us -> 65.3 us (0.78)
  local copies, waits for them, and re-layouts: 21.9 us -> 3.13 us
  blocking collectives: 0 us -> 13.8 us
  waiting for transfers between devices: 10.6 us -> 3.1 us
  starting transfers between devices: 26.5 us -> 20.7 us
  Pallas kernels: 19.1 us -> 23.3 us
  other arithmetic: 4.02 us -> 0 us
    unnamed x40 -> x22, local copies, waits for them, and re-layouts: 17.8 us -> 3.13 us
    all_to_all x0 -> x1, blocking collectives: none -> 13.8 us  [per_device(): lax.all_to_all(sending, 'slab', split_axis=0, concat_axis=0, tiled=True)]
    all_to_all x1, waiting for transfers between devices: 7.16 us -> 0.01 us  [per_device(): lax.all_to_all(sent, ('subj', 'slab'), split_axis=0, concat_axis=0, tiled...]
    all_to_all x1 -> x0, starting transfers between devices: 5.34 us -> none  [per_device(): lax.all_to_all(sending, 'slab', split_axis=0, concat_axis=0, tiled=True)]
    pallas_call x7, Pallas kernels: 19.1 us -> 23.3 us  [call(): pl.pallas_call(kernel, out_shape=tuple(shapes) if many else shapes[0], in...]
    select_n x5 -> x0, other arithmetic: 3.77 us -> none  [the longest x3 2.52 us: with_neighbours(): jnp.where(odd, from_far, from_near)]
    ppermute x6, starting transfers between devices: 6.71 us -> 9.56 us  [the longest x3 7.19 us: swap_near(): lax.ppermute(values, 'slab', [(i, i ^ 1) for i in range(lax.axis_size('sl...]
    all_to_all x1, starting transfers between devices: 6.37 us -> 4.04 us  [per_device(): lax.all_to_all(sent, ('subj', 'slab'), split_axis=0, concat_axis=0, tiled...]
  transfers between devices with their start and end apart: 14 -> 13, of which waited for: 4 -> 3; matrix products, arithmetic and copies ran while one was open for 10% -> 0% of each run, Pallas kernels for 18% -> 27%
where the time goes in v3:
time: 65.3 us; the launch traced here: 65 us
  Pallas kernels  23.3 us (36%)
  starting transfers between devices  20.7 us (32%)
  blocking collectives  13.8 us (21%)
  local copies, waits for them, and re-layouts  3.13 us (5%)
  waiting for transfers between devices  3.1 us (5%)
  between operations  0.88 us (1%)
    pallas_call x7, Pallas kernels, call(): pl.pallas_call(kernel, out_shape=tuple(shapes) if many else shapes[0], in...  23.3 us
    all_to_all x1, blocking collectives, per_device(): lax.all_to_all(sending, 'slab', split_axis=0, concat_axis=0, tiled=True)  13.8 us
    ppermute x3, starting transfers between devices, swap_near(): lax.ppermute(values, 'slab', [(i, i ^ 1) for i in range(lax.axis_size('sl...  7.19 us
    ppermute x6, starting transfers between devices, over_subjects(): lax.ppermute(values, 'subj', [(i, i ^ d) for i in range(count)])  7.11 us
    all_to_all x1, starting transfers between devices, per_device(): lax.all_to_all(sent, ('subj', 'slab'), split_axis=0, concat_axis=0, tiled...  4.04 us
    unnamed x22, local copies, waits for them, and re-layouts  3.13 us
    ppermute x6, waiting for transfers between devices, over_subjects(): lax.ppermute(values, 'subj', [(i, i ^ d) for i in range(count)])  3.08 us
    ppermute x3, starting transfers between devices, swap_far(): lax.ppermute(values, 'slab', [(i, i + 1 if i % 2 else i - 1) for i in ran...  2.37 us
  transfers between devices with their start and end apart: 13, of which 3 were waited for; matrix products, arithmetic and copies ran while one was open for 0% of the time, Pallas kernels for 27%

profile of v3, /device:TPU:0, one launch (start us, length us, event | category | flops | bytes accessed | tf_op | source)
XLA Modules:
  0.0 65.0 jit_solution(3423723335822954276)
XLA Ops:
  0.7 4.8 %shard_map.96 = (bf16[4,8,5,128,128]{4,3,2,1,0:T(8,128)(2,1)}, f32[5,1,256,128]{3,2,1,0:T(8,128)}, f32[5,1,256,128]{3,2,1,0:T(8,128)}) custom-call(s32[1]{0:T(128)} %bitcast.6.place_ref, s32[4096,128]{1,0:T(8,128)} %bitcast.37, bf16[4096,128]{1,0:T(8,128)(2,1)} %bitcast.38, f32[3,2,256,128]{3,2,1,0:T(8,128)} %bitcast.29, f32[2,256,128]{2,1,0:T(8,128)} %bitcast.34, ...), custom_call_target="tpu_custom_call" | custom-call | tf_op jit(solution)/shard_map/pallas_call | solution.py:31
  5.5 0.7 %collective-permute-start = (f32[5,1,256,128]{3,2,1,0:T(8,128)}, f32[5,1,256,128]{3,2,1,0:T(8,128)S(1)}, u32[]{:S(2)}, u32[]{:S(2)}) collective-permute-start(f32[5,1,256,128]{3,2,1,0:T(8,128)} %get-tuple-element.17), channel_id=1, source_target_pairs={{1,2},{2,1},{3,4},{4,3},{5,6},{6,5},{9,10},{10,9},{11,12},{12,11},... | collective-permute-start | bytes 1966088 | tf_op jit(solution)/shard_map/ppermute | solution.py:335
  6.2 4.4 %collective-permute-start.1 = (f32[5,1,256,128]{3,2,1,0:T(8,128)}, f32[5,1,256,128]{3,2,1,0:T(8,128)S(1)}, u32[]{:S(2)}, u32[]{:S(2)}) collective-permute-start(f32[5,1,256,128]{3,2,1,0:T(8,128)} %get-tuple-element.18), channel_id=1, source_target_pairs={{0,1},{1,0},{2,3},{3,2},{4,5},{5,4},{6,7},{7,6},{8,9},{9,8},{10,11... | collective-permute-start | bytes 1966088 | tf_op jit(solution)/shard_map/ppermute | solution.py:330
  10.6 1.5 %shard_map.95 = f32[512,128]{1,0:T(8,128)S(1)} custom-call(s32[8,64]{1,0:T(8,128)} %bitcast.24, f32[512,128]{1,0:T(8,128)} %template_ref.3), custom_call_target="tpu_custom_call" | custom-call | tf_op jit(solution)/shard_map/pallas_call | solution.py:31
  12.1 13.8 %all_to_all.22 = f32[8,64,128]{2,1,0:T(8,128)} all-to-all(f32[8,64,128]{2,1,0:T(8,128)S(1)} %bitcast.19), channel_id=1, replica_groups=mesh['subj'=4,'slab'=8] {'slab'}, dimensions={0} | all-to-all | bytes 524288 | tf_op jit(solution)/shard_map/all_to_all | solution.py:558
  25.9 8.5 %shard_map.97 = (f32[512,128]{1,0:T(8,128)S(1)}, f32[512,128]{1,0:T(8,128)}) custom-call(s32[8,512]{1,0:T(8,128)S(1)} %bitcast.23, f32[512,128]{1,0:T(8,128)} %bitcast.39, bf16[4,8,5,128,128]{4,3,2,1,0:T(8,128)(2,1)} %get-tuple-element.15.moved_ref, f32[512,128]{1,0:T(8,128)} %bitcast.32), custom_call_target="tpu_custom_call" | custom-call | bytes 1024 | tf_op jit(solution)/shard_map/pallas_call | solution.py:31
  34.4 0.8 %collective-permute-start.9 = (f32[2,256,128]{2,1,0:T(8,128)S(1)}, f32[2,256,128]{2,1,0:T(8,128)S(1)}, u32[]{:S(2)}, u32[]{:S(2)}) collective-permute-start(f32[2,256,128]{2,1,0:T(8,128)S(1)} %bitcast.20), channel_id=1, source_target_pairs={{1,2},{2,1},{3,4},{4,3},{5,6},{6,5},{9,10},{10,9},{11,12},{12,11},... | collective-permute-start | bytes 786440 | tf_op jit(solution)/shard_map/ppermute | solution.py:335
  35.3 1.7 %collective-permute-start.8 = (f32[2,256,128]{2,1,0:T(8,128)S(1)}, f32[2,256,128]{2,1,0:T(8,128)S(1)}, u32[]{:S(2)}, u32[]{:S(2)}) collective-permute-start(f32[2,256,128]{2,1,0:T(8,128)S(1)} %bitcast.21), channel_id=1, source_target_pairs={{0,1},{1,0},{2,3},{3,2},{4,5},{5,4},{6,7},{7,6},{8,9},{9,8},{10,11... | collective-permute-start | bytes 786440 | tf_op jit(solution)/shard_map/ppermute | solution.py:330
  37.0 4.0 %all-to-all-start.1 = ((f32[32,16,128]{2,1,0:T(8,128)}), f32[32,16,128]{2,1,0:T(8,128)S(1)}, u32[]{:S(2)}, u32[]{:S(2)}) async-start(f32[32,16,128]{2,1,0:T(8,128)} %bitcast.13), calls=%async_computation.1 | async-start | bytes 524288 | tf_op jit(solution)/shard_map/all_to_all | solution.py:608
  41.1 0.7 %copy-done.9 = f32[2,256,128]{2,1,0:T(8,128)} copy-done((f32[2,256,128]{2,1,0:T(8,128)}, f32[2,256,128]{2,1,0:T(8,128)S(1)}, u32[]{:S(2)}) %copy-start.9) | copy-done | bytes 262168
  41.7 0.7 %copy-done.10 = f32[2,256,128]{2,1,0:T(8,128)} copy-done((f32[2,256,128]{2,1,0:T(8,128)}, f32[2,256,128]{2,1,0:T(8,128)S(1)}, u32[]{:S(2)}) %copy-start.10) | copy-done | bytes 262168
  42.4 3.2 %shard_map.100 = (f32[3,2,256,128]{3,2,1,0:T(8,128)S(1)}, f32[3,1,256,128]{3,2,1,0:T(8,128)S(1)}, f32[3,1,256,128]{3,2,1,0:T(8,128)S(1)}) custom-call(s32[1]{0:T(128)} %bitcast.6.place_ref, f32[3,2,256,128]{3,2,1,0:T(8,128)} %bitcast.30, f32[2,256,128]{2,1,0:T(8,128)} %bitcast.33, f32[2,256,128]{2,1,0:T(8,128)} %bitcast.35, f32[2,256,128]{2,1,0:T(8,128)} %bitcast.22, ...), custom_call_target="tpu_custom_call" | custom-call | bytes 1024 | tf_op jit(solution)/shard_map/pallas_call | solution.py:31
  45.7 0.9 %copy-done.1 = f32[3,2,256,128]{3,2,1,0:T(8,128)} copy-done((f32[3,2,256,128]{3,2,1,0:T(8,128)}, f32[3,2,256,128]{3,2,1,0:T(8,128)S(1)}, u32[]{:S(2)}) %copy-start.1) | copy-done | bytes 786456
  46.6 1.1 %collective-permute-start.10 = (f32[3,1,256,128]{3,2,1,0:T(8,128)S(1)}, f32[3,1,256,128]{3,2,1,0:T(8,128)S(1)}, u32[]{:S(2)}, u32[]{:S(2)}) collective-permute-start(f32[3,1,256,128]{3,2,1,0:T(8,128)S(1)} %get-tuple-element.26), channel_id=1, source_target_pairs={{0,1},{1,0},{2,3},{3,2},{4,5},{5,4},{6,7},{7,6},{8,9},{9,8},{10,11... | collective-permute-start | bytes 1179656 | tf_op jit(solution)/shard_map/ppermute | solution.py:330
  47.7 0.9 %collective-permute-start.11 = (f32[3,1,256,128]{3,2,1,0:T(8,128)S(1)}, f32[3,1,256,128]{3,2,1,0:T(8,128)S(1)}, u32[]{:S(2)}, u32[]{:S(2)}) collective-permute-start(f32[3,1,256,128]{3,2,1,0:T(8,128)S(1)} %get-tuple-element.27), channel_id=1, source_target_pairs={{1,2},{2,1},{3,4},{4,3},{5,6},{6,5},{9,10},{10,9},{11,12},{12,11},... | collective-permute-start | bytes 1179656 | tf_op jit(solution)/shard_map/ppermute | solution.py:335
  48.5 2.5 %collective-permute-start.4 = (s32[8,64]{1,0:T(8,128)S(1)}, s32[8,64]{1,0:T(8,128)S(1)}, u32[]{:S(2)}, u32[]{:S(2)}) collective-permute-start(s32[8,64]{1,0:T(8,128)S(1)} %bitcast.25), channel_id=1, source_target_pairs={{0,24},{8,16},{16,8},{24,0},{1,25},{9,17},{17,9},{25,1},{2,26},{10... | collective-permute-start | bytes 6152 | tf_op jit(solution)/shard_map/ppermute | solution.py:325
  52.1 1.0 %collective-permute-done.4.refs_3_ = s32[8,64]{1,0:T(8,128)S(1)} collective-permute-done((s32[8,64]{1,0:T(8,128)S(1)}, s32[8,64]{1,0:T(8,128)S(1)}, u32[]{:S(2)}, u32[]{:S(2)}) %collective-permute-start.4) | collective-permute-done | bytes 2080 | tf_op jit(solution)/shard_map/ppermute | solution.py:325
  53.1 1.5 %collective-permute-done.3.refs_2_ = s32[8,64]{1,0:T(8,128)S(1)} collective-permute-done((s32[8,64]{1,0:T(8,128)S(1)}, s32[8,64]{1,0:T(8,128)S(1)}, u32[]{:S(2)}, u32[]{:S(2)}) %collective-permute-start.3) | collective-permute-done | bytes 2080 | tf_op jit(solution)/shard_map/ppermute | solution.py:325
  55.2 0.9 %shard_map.98.refs_0_ = f32[128,128]{1,0:T(8,128)S(1)} custom-call(s32[1]{0:T(128)} %bitcast.me_ref, f32[512,128]{1,0:T(8,128)S(1)} %bitcast.18, s32[8,64]{1,0:T(8,128)S(1)} %bitcast.28, s32[8,64]{1,0:T(8,128)S(1)} %collective-permute-done.2.refs_1_, s32[8,64]{1,0:T(8,128)S(1)} %collective-permute-done.3.refs_2_, s32[8,64]{1,0:T(8,128)S(1)} %collective-permute-done.4.refs_3_), custom_call_target="tpu_custom_call" | custom-call | tf_op jit(solution)/shard_map/pallas_call | solution.py:31
  56.1 1.6 %collective-permute-start.7 = (f32[128,128]{1,0:T(8,128)S(1)}, f32[128,128]{1,0:T(8,128)S(1)}, u32[]{:S(2)}, u32[]{:S(2)}) collective-permute-start(f32[128,128]{1,0:T(8,128)S(1)} %shard_map.98.refs_0_), channel_id=1, source_target_pairs={{0,24},{8,16},{16,8},{24,0},{1,25},{9,17},{17,9},{25,1},{2,26},{10... | collective-permute-start | bytes 196616 | tf_op jit(solution)/shard_map/ppermute | solution.py:325
  58.2 1.5 %collective-permute-start.5 = (f32[128,128]{1,0:T(8,128)S(1)}, f32[128,128]{1,0:T(8,128)S(1)}, u32[]{:S(2)}, u32[]{:S(2)}) collective-permute-start(f32[128,128]{1,0:T(8,128)S(1)} %shard_map.98.refs_0_), channel_id=1, source_target_pairs={{0,8},{8,0},{16,24},{24,16},{1,9},{9,1},{17,25},{25,17},{2,10},{10... | collective-permute-start | bytes 196616 | tf_op jit(solution)/shard_map/ppermute | solution.py:325
  59.7 0.7 %copy-done.7 = f32[3,1,256,128]{3,2,1,0:T(8,128)} copy-done((f32[3,1,256,128]{3,2,1,0:T(8,128)}, f32[3,1,256,128]{3,2,1,0:T(8,128)S(1)}, u32[]{:S(2)}) %copy-start.7) | copy-done | bytes 393240
  60.6 3.3 %shard_map.101 = f32[3,2,256,128]{3,2,1,0:T(8,128)} custom-call(s32[1]{0:T(128)} %bitcast.6.place_ref, f32[3,2,256,128]{3,2,1,0:T(8,128)} %copy-done.1, f32[2,256,128]{2,1,0:T(8,128)} %bitcast.36, f32[5,1,256,128]{3,2,1,0:T(8,128)} %copy-done.6, f32[5,1,256,128]{3,2,1,0:T(8,128)} %copy-done.5, f32[3,1,256,128]{3,2,1,0:T(8,128)} %copy-done.7, ...), custom_call_target="tpu_custom_call" | custom-call | tf_op jit(solution)/shard_map/pallas_call | solution.py:31
  63.9 1.1 %shard_map.99 = f32[512,128]{1,0:T(8,128)} custom-call(s32[1]{0:T(128)} %bitcast.me_ref, f32[512,128]{1,0:T(8,128)S(1)} %copy-done, f32[128,128]{1,0:T(8,128)S(1)} %shard_map.98.refs_0_, f32[128,128]{1,0:T(8,128)S(1)} %collective-permute-done.5.refs_1_, f32[128,128]{1,0:T(8,128)S(1)} %collective-permute-done.6.refs_2_, ...), custom_call_target="tpu_custom_call" | custom-call | tf_op jit(solution)/shard_map/pallas_call | solution.py:31
  (32 shorter events, 2.3 us)
Async XLA Ops:
  0.6 25.3 %copy-start.3 = (s32[1,512,8]{1,2,0:T(8,128)S(1)}, s32[1,512,8]{1,2,0:T(8,128)}, u32[]{:S(2)}) copy-start(s32[1,512,8]{1,2,0:T(8,128)} %param.13) | copy-start | bytes 49156
  5.5 31.5 %collective-permute-start = (f32[5,1,256,128]{3,2,1,0:T(8,128)}, f32[5,1,256,128]{3,2,1,0:T(8,128)S(1)}, u32[]{:S(2)}, u32[]{:S(2)}) collective-permute-start(f32[5,1,256,128]{3,2,1,0:T(8,128)} %get-tuple-element.17), channel_id=1, source_target_pairs={{1,2},{2,1},{3,4},{4,3},{5,6},{6,5},{9,10},{10,9},{11,12},{12,11},... | collective-permute-start | bytes 1966088 | tf_op jit(solution)/shard_map/ppermute | solution.py:335
  6.2 30.8 %collective-permute-start.1 = (f32[5,1,256,128]{3,2,1,0:T(8,128)}, f32[5,1,256,128]{3,2,1,0:T(8,128)S(1)}, u32[]{:S(2)}, u32[]{:S(2)}) collective-permute-start(f32[5,1,256,128]{3,2,1,0:T(8,128)} %get-tuple-element.18), channel_id=1, source_target_pairs={{0,1},{1,0},{2,3},{3,2},{4,5},{5,4},{6,7},{7,6},{8,9},{9,8},{10,11... | collective-permute-start | bytes 1966088 | tf_op jit(solution)/shard_map/ppermute | solution.py:330
  12.1 36.5 %copy-start.4 = (s32[1,1,8,64]{3,2,1,0:T(8,128)S(1)}, s32[1,1,8,64]{3,2,1,0:T(8,128)}, u32[]{:S(2)}) copy-start(s32[1,1,8,64]{3,2,1,0:T(8,128)} %param.12) | copy-start | bytes 6148
  34.4 6.6 %copy-start.2 = (f32[512,128]{1,0:T(8,128)}, f32[512,128]{1,0:T(8,128)S(1)}, u32[]{:S(2)}) copy-start(f32[512,128]{1,0:T(8,128)S(1)} %get-tuple-element.22) | copy-start | bytes 786436
  34.4 29.5 %copy-start = (f32[512,128]{1,0:T(8,128)S(1)}, f32[512,128]{1,0:T(8,128)}, u32[]{:S(2)}) copy-start(f32[512,128]{1,0:T(8,128)} %template_ref.3) | copy-start | bytes 786436
  34.4 6.6 %collective-permute-start.9 = (f32[2,256,128]{2,1,0:T(8,128)S(1)}, f32[2,256,128]{2,1,0:T(8,128)S(1)}, u32[]{:S(2)}, u32[]{:S(2)}) collective-permute-start(f32[2,256,128]{2,1,0:T(8,128)S(1)} %bitcast.20), channel_id=1, source_target_pairs={{1,2},{2,1},{3,4},{4,3},{5,6},{6,5},{9,10},{10,9},{11,12},{12,11},... | collective-permute-start | bytes 786440 | tf_op jit(solution)/shard_map/ppermute | solution.py:335
  35.3 5.8 %collective-permute-start.8 = (f32[2,256,128]{2,1,0:T(8,128)S(1)}, f32[2,256,128]{2,1,0:T(8,128)S(1)}, u32[]{:S(2)}, u32[]{:S(2)}) collective-permute-start(f32[2,256,128]{2,1,0:T(8,128)S(1)} %bitcast.21), channel_id=1, source_target_pairs={{0,1},{1,0},{2,3},{3,2},{4,5},{5,4},{6,7},{7,6},{8,9},{9,8},{10,11... | collective-permute-start | bytes 786440 | tf_op jit(solution)/shard_map/ppermute | solution.py:330
  37.0 4.1 %copy-start.5 = (f32[5,1,256,128]{3,2,1,0:T(8,128)}, f32[5,1,256,128]{3,2,1,0:T(8,128)S(1)}, u32[]{:S(2)}) copy-start(f32[5,1,256,128]{3,2,1,0:T(8,128)S(1)} %collective-permute-done.edge_far_ref) | copy-start | bytes 1966084
  37.0 4.1 %copy-start.6 = (f32[5,1,256,128]{3,2,1,0:T(8,128)}, f32[5,1,256,128]{3,2,1,0:T(8,128)S(1)}, u32[]{:S(2)}) copy-start(f32[5,1,256,128]{3,2,1,0:T(8,128)S(1)} %collective-permute-done.1.edge_near_ref) | copy-start | bytes 1966084
  37.0 18.2 %all-to-all-start.1 = ((f32[32,16,128]{2,1,0:T(8,128)}), f32[32,16,128]{2,1,0:T(8,128)S(1)}, u32[]{:S(2)}, u32[]{:S(2)}) async-start(f32[32,16,128]{2,1,0:T(8,128)} %bitcast.13), calls=%async_computation.1 | async-start | bytes 524288 | tf_op jit(solution)/shard_map/all_to_all | solution.py:608
  41.0 0.7 %copy-start.9 = (f32[2,256,128]{2,1,0:T(8,128)}, f32[2,256,128]{2,1,0:T(8,128)S(1)}, u32[]{:S(2)}) copy-start(f32[2,256,128]{2,1,0:T(8,128)S(1)} %collective-permute-done.9.warped_far_ref) | copy-start | bytes 786436
  41.7 0.7 %copy-start.10 = (f32[2,256,128]{2,1,0:T(8,128)}, f32[2,256,128]{2,1,0:T(8,128)S(1)}, u32[]{:S(2)}) copy-start(f32[2,256,128]{2,1,0:T(8,128)S(1)} %collective-permute-done.8.warped_near_ref) | copy-start | bytes 786436
  45.7 0.9 %copy-start.1 = (f32[3,2,256,128]{3,2,1,0:T(8,128)}, f32[3,2,256,128]{3,2,1,0:T(8,128)S(1)}, u32[]{:S(2)}) copy-start(f32[3,2,256,128]{3,2,1,0:T(8,128)S(1)} %get-tuple-element.25.field_ref) | copy-start | bytes 2359300
  46.6 13.1 %collective-permute-start.10 = (f32[3,1,256,128]{3,2,1,0:T(8,128)S(1)}, f32[3,1,256,128]{3,2,1,0:T(8,128)S(1)}, u32[]{:S(2)}, u32[]{:S(2)}) collective-permute-start(f32[3,1,256,128]{3,2,1,0:T(8,128)S(1)} %get-tuple-element.26), channel_id=1, source_target_pairs={{0,1},{1,0},{2,3},{3,2},{4,5},{5,4},{6,7},{7,6},{8,9},{9,8},{10,11... | collective-permute-start | bytes 1179656 | tf_op jit(solution)/shard_map/ppermute | solution.py:330
  47.7 12.0 %collective-permute-start.11 = (f32[3,1,256,128]{3,2,1,0:T(8,128)S(1)}, f32[3,1,256,128]{3,2,1,0:T(8,128)S(1)}, u32[]{:S(2)}, u32[]{:S(2)}) collective-permute-start(f32[3,1,256,128]{3,2,1,0:T(8,128)S(1)} %get-tuple-element.27), channel_id=1, source_target_pairs={{1,2},{2,1},{3,4},{4,3},{5,6},{6,5},{9,10},{10,9},{11,12},{12,11},... | collective-permute-start | bytes 1179656 | tf_op jit(solution)/shard_map/ppermute | solution.py:335
  48.5 4.6 %collective-permute-start.4 = (s32[8,64]{1,0:T(8,128)S(1)}, s32[8,64]{1,0:T(8,128)S(1)}, u32[]{:S(2)}, u32[]{:S(2)}) collective-permute-start(s32[8,64]{1,0:T(8,128)S(1)} %bitcast.25), channel_id=1, source_target_pairs={{0,24},{8,16},{16,8},{24,0},{1,25},{9,17},{17,9},{25,1},{2,26},{10... | collective-permute-start | bytes 6152 | tf_op jit(solution)/shard_map/ppermute | solution.py:325
  51.1 3.6 %collective-permute-start.3 = (s32[8,64]{1,0:T(8,128)S(1)}, s32[8,64]{1,0:T(8,128)S(1)}, u32[]{:S(2)}, u32[]{:S(2)}) collective-permute-start(s32[8,64]{1,0:T(8,128)S(1)} %bitcast.26), channel_id=1, source_target_pairs={{0,16},{8,24},{16,0},{24,8},{1,17},{9,25},{17,1},{25,9},{2,18},{10... | collective-permute-start | bytes 6152 | tf_op jit(solution)/shard_map/ppermute | solution.py:325
  51.6 3.6 %collective-permute-start.2 = (s32[8,64]{1,0:T(8,128)S(1)}, s32[8,64]{1,0:T(8,128)S(1)}, u32[]{:S(2)}, u32[]{:S(2)}) collective-permute-start(s32[8,64]{1,0:T(8,128)S(1)} %bitcast.27), channel_id=1, source_target_pairs={{0,8},{8,0},{16,24},{24,16},{1,9},{9,1},{17,25},{25,17},{2,10},{10... | collective-permute-start | bytes 6152 | tf_op jit(solution)/shard_map/ppermute | solution.py:325
  56.1 7.7 %collective-permute-start.7 = (f32[128,128]{1,0:T(8,128)S(1)}, f32[128,128]{1,0:T(8,128)S(1)}, u32[]{:S(2)}, u32[]{:S(2)}) collective-permute-start(f32[128,128]{1,0:T(8,128)S(1)} %shard_map.98.refs_0_), channel_id=1, source_target_pairs={{0,24},{8,16},{16,8},{24,0},{1,25},{9,17},{17,9},{25,1},{2,26},{10... | collective-permute-start | bytes 196616 | tf_op jit(solution)/shard_map/ppermute | solution.py:325
  57.7 6.2 %collective-permute-start.6 = (f32[128,128]{1,0:T(8,128)S(1)}, f32[128,128]{1,0:T(8,128)S(1)}, u32[]{:S(2)}, u32[]{:S(2)}) collective-permute-start(f32[128,128]{1,0:T(8,128)S(1)} %shard_map.98.refs_0_), channel_id=1, source_target_pairs={{0,16},{8,24},{16,0},{24,8},{1,17},{9,25},{17,1},{25,9},{2,18},{10... | collective-permute-start | bytes 196616 | tf_op jit(solution)/shard_map/ppermute | solution.py:325
  58.2 5.7 %collective-permute-start.5 = (f32[128,128]{1,0:T(8,128)S(1)}, f32[128,128]{1,0:T(8,128)S(1)}, u32[]{:S(2)}, u32[]{:S(2)}) collective-permute-start(f32[128,128]{1,0:T(8,128)S(1)} %shard_map.98.refs_0_), channel_id=1, source_target_pairs={{0,8},{8,0},{16,24},{24,16},{1,9},{9,1},{17,25},{25,17},{2,10},{10... | collective-permute-start | bytes 196616 | tf_op jit(solution)/shard_map/ppermute | solution.py:325
  59.7 0.7 %copy-start.7 = (f32[3,1,256,128]{3,2,1,0:T(8,128)}, f32[3,1,256,128]{3,2,1,0:T(8,128)S(1)}, u32[]{:S(2)}) copy-start(f32[3,1,256,128]{3,2,1,0:T(8,128)S(1)} %collective-permute-done.10.near_ref) | copy-start | bytes 1179652
  59.7 0.9 %copy-start.8 = (f32[3,1,256,128]{3,2,1,0:T(8,128)}, f32[3,1,256,128]{3,2,1,0:T(8,128)S(1)}, u32[]{:S(2)}) copy-start(f32[3,1,256,128]{3,2,1,0:T(8,128)S(1)} %collective-permute-done.11.far_ref) | copy-start | bytes 1179652

commit v4 on v3

--- a/solution.py
+++ b/solution.py
@@ -17,10 +17,9 @@
 template_rate = 2.0
 
 VMEM_LIMIT = 40 * 1024 * 1024
-COST = 1024
-
-
-def call(kernel, out_shape, *args, scratch=(), smem=(), far=(), out_far=(), cost=None):
+
+
+def call(kernel, out_shape, *args, scratch=(), smem=(), far=(), free=(), out_far=()):
     many = isinstance(out_shape, tuple)
     shapes = [
         pltpu.HBM(s.shape, s.dtype) if i in out_far else s
@@ -33,13 +32,20 @@
         out_shape=tuple(shapes) if many else shapes[0],
         in_specs=[
             pl.BlockSpec(
-                memory_space=pltpu.SMEM if i in smem else pltpu.HBM if i in far else pltpu.VMEM
+                memory_space=(
+                    pltpu.SMEM
+                    if i in smem
+                    else pltpu.HBM
+                    if i in far
+                    else pl.ANY
+                    if i in free
+                    else pltpu.VMEM
+                )
             )
             for i in range(len(args))
         ],
         out_specs=tuple(specs) if many else specs[0],
         scratch_shapes=scratch,
-        cost_estimate=cost and pl.CostEstimate(flops=0, transcendentals=0, bytes_accessed=cost),
         compiler_params=pltpu.CompilerParams(vmem_limit_bytes=VMEM_LIMIT),
     )(
         *[
@@ -182,7 +188,6 @@
     images_ref,
     warped_ref,
     sent_ref,
-    received,
     images,
     moved,
     picked,
@@ -190,21 +195,18 @@
     first_sem,
     moved_sem,
 ):
-    slots, width = received.shape
+    slots, width = received_ref.shape
     chunks, each, count, some = moved.shape[:4]
     rows = chunks * some
     block = width // subjects
     group = slots // subjects
     capacity = slots // slabs
     held = capacity // subjects
-    first = [
-        pltpu.make_async_copy(received_ref, received, first_sem.at[0]),
-        pltpu.make_async_copy(images_ref, images, first_sem.at[1]),
-    ]
+    first = pltpu.make_async_copy(images_ref, images, first_sem)
     moves = [
         pltpu.make_async_copy(moved_ref.at[i], moved.at[i], moved_sem.at[i]) for i in range(chunks)
     ]
-    for copy in first + moves:
+    for copy in moves[:1] + [first] + moves[1:]:
         copy.start()
     slot = slot_ref[...]
     slot_wide = jnp.concatenate([slot, jnp.zeros((LANES - each, rows), jnp.int32)], axis=0).T
@@ -212,15 +214,14 @@
     packed = (inner // held) * group + (slot // capacity) * held + inner % held
     lane = lax.broadcasted_iota(jnp.int32, (rows, LANES), 1)
     number = lax.broadcasted_iota(jnp.int32, (slots, rows), 0)
-    first[0].wait()
-    pair = halves(received[...])
+    pair = halves(received_ref[...])
     for b in range(each):
         wide = jnp.broadcast_to(slot_wide[:, b : b + 1], (rows, LANES))
         pick = jnp.concatenate(
             [one_hot(wide == lane + t * LANES) for t in range(slots // LANES)], axis=1
         )
         picked[b] = joined(dot(pick, pair))
-    first[1].wait()
+    first.wait()
     for i in range(chunks):
         moves[i].wait()
         at = slice(i * some, (i + 1) * some)
@@ -583,6 +584,7 @@
             dma((3,)),
         ),
     )
+    received, edge_far, edge_near = lax.optimization_barrier((received, edge_far, edge_near))
     edge_far, edge_near = swap_far(edge_far), swap_near(edge_near)
 
     warped, sent = call(
@@ -592,15 +594,13 @@
         received,
         moved,
         images[0],
-        far=(1, 2, 3),
-        cost=COST,
+        far=(2, 3),
         scratch=(
-            pltpu.VMEM((slots, width), f32),
             pltpu.VMEM((rows, width), f32),
             pltpu.VMEM(moved_shape, bf16),
             pltpu.VMEM((each, rows, width), f32),
             pltpu.VMEM((each, rows, 2 * width), bf16),
-            dma((2,)),
+            dma,
             dma((chunks,)),
         ),
     )
@@ -629,8 +629,8 @@
         warped_near,
         warped_far,
         smem=(0,),
-        far=tuple(range(1, 9)),
-        cost=COST,
+        far=(1, 2, 3),
+        free=(4, 5, 6, 7, 8),
         scratch=(
             pltpu.VMEM((parts, planes + 2, YR, width), f32),
             pltpu.VMEM((planes + 2, YR, width), f32),
@@ -669,7 +669,8 @@
         field_near,
         field_far,
         smem=(0,),
-        far=tuple(range(1, 7)),
+        far=(2,),
+        free=(1, 3, 4, 5, 6),
         scratch=(
             pltpu.VMEM((parts, planes + 2, YR, width), f32),
             pltpu.VMEM((planes + 2, YR, width), f32),

time: 65.3 us -> 58.5 us (0.90)
  blocking collectives: 13.8 us -> 0 us
  waiting for transfers between devices: 3.1 us -> 8.52 us
  starting transfers between devices: 20.7 us -> 24.4 us
  local copies, waits for them, and re-layouts: 3.13 us -> 0.02 us
  Pallas kernels: 23.3 us -> 24.4 us
    all_to_all x1 -> x0, blocking collectives: 13.8 us -> none  [per_device(): lax.all_to_all(sending, 'slab', split_axis=0, concat_axis=0, tiled=True)]
    all_to_all x0 -> x1, starting transfers between devices: none -> 6.34 us  [per_device(): lax.all_to_all(sending, 'slab', split_axis=0, concat_axis=0, tiled=True)]
    all_to_all x0 -> x1, waiting for transfers between devices: none -> 4.94 us  [per_device(): lax.all_to_all(sending, 'slab', split_axis=0, concat_axis=0, tiled=True)]
    unnamed x22 -> x6, local copies, waits for them, and re-layouts: 3.13 us -> 0.02 us
    ppermute x3, starting transfers between devices: 7.19 us -> 4.44 us  [swap_near(): lax.ppermute(values, 'slab', [(i, i ^ 1) for i in range(lax.axis_size('sl...]
    pallas_call x7, Pallas kernels: 23.3 us -> 24.4 us  [call(): pl.pallas_call(kernel, out_shape=tuple(shapes) if many else shapes[0], in...]
  transfers between devices with their start and end apart: 13 -> 14, of which waited for: 3 -> 6; matrix products, arithmetic and copies ran while one was open for 0% -> 0% of each run, Pallas kernels for 27% -> 36%
where the time goes in v4:
time: 58.5 us; the launch traced here: 58.1 us
  Pallas kernels  24.4 us (42%)
  starting transfers between devices  24.4 us (42%)
  waiting for transfers between devices  8.52 us (15%)
  between operations  0.78 us (1%)
    pallas_call x7, Pallas kernels, call(): pl.pallas_call(kernel, out_shape=tuple(shapes) if many else shapes[0], in...  24.4 us
    ppermute x6, starting transfers between devices, over_subjects(): lax.ppermute(values, 'subj', [(i, i ^ d) for i in range(count)])  7.13 us
    all_to_all x1, starting transfers between devices, per_device(): lax.all_to_all(sending, 'slab', split_axis=0, concat_axis=0, tiled=True)  6.34 us
    all_to_all x1, waiting for transfers between devices, per_device(): lax.all_to_all(sending, 'slab', split_axis=0, concat_axis=0, tiled=True)  4.94 us
    ppermute x3, starting transfers between devices, swap_near(): lax.ppermute(values, 'slab', [(i, i ^ 1) for i in range(lax.axis_size('sl...  4.44 us
    all_to_all x1, starting transfers between devices, per_device(): lax.all_to_all(sent, ('subj', 'slab'), split_axis=0, concat_axis=0, tiled...  4.15 us
    ppermute x6, waiting for transfers between devices, over_subjects(): lax.ppermute(values, 'subj', [(i, i ^ d) for i in range(count)])  3.56 us
    ppermute x3, starting transfers between devices, swap_far(): lax.ppermute(values, 'slab', [(i, i + 1 if i % 2 else i - 1) for i in ran...  2.35 us
  transfers between devices with their start and end apart: 14, of which 6 were waited for; matrix products, arithmetic and copies ran while one was open for 0% of the time, Pallas kernels for 36%

profile of v4, /device:TPU:0, one launch (start us, length us, event | category | flops | bytes accessed | tf_op | source)
XLA Modules:
  0.0 58.1 jit_solution(1343873683606497386)
XLA Ops:
  0.6 2.2 %shard_map.95 = f32[512,128]{1,0:T(8,128)} custom-call(s32[8,64]{1,0:T(8,128)} %bitcast.24, f32[512,128]{1,0:T(8,128)} %template_ref.3), custom_call_target="tpu_custom_call" | custom-call | tf_op jit(solution)/shard_map/pallas_call | solution.py:30
  2.8 6.3 %all-to-all-start = ((f32[8,64,128]{2,1,0:T(8,128)}), f32[8,64,128]{2,1,0:T(8,128)S(1)}, u32[]{:S(2)}, u32[]{:S(2)}) async-start(f32[8,64,128]{2,1,0:T(8,128)} %bitcast.4), calls=%async_computation | async-start | bytes 524288 | tf_op jit(solution)/shard_map/all_to_all | solution.py:559
  9.2 4.8 %shard_map.96 = (bf16[4,8,5,128,128]{4,3,2,1,0:T(8,128)(2,1)}, f32[5,1,256,128]{3,2,1,0:T(8,128)}, f32[5,1,256,128]{3,2,1,0:T(8,128)}) custom-call(s32[1]{0:T(128)} %bitcast.6.place_ref, s32[4096,128]{1,0:T(8,128)} %bitcast.37, bf16[4096,128]{1,0:T(8,128)(2,1)} %bitcast.38, f32[3,2,256,128]{3,2,1,0:T(8,128)} %bitcast.29, f32[2,256,128]{2,1,0:T(8,128)} %bitcast.34, ...), custom_call_target="tpu_custom_call" | custom-call | tf_op jit(solution)/shard_map/pallas_call | solution.py:30
  14.0 4.9 %all-to-all-done = f32[8,64,128]{2,1,0:T(8,128)S(1)} async-done(((f32[8,64,128]{2,1,0:T(8,128)}), f32[8,64,128]{2,1,0:T(8,128)S(1)}, u32[]{:S(2)}, u32[]{:S(2)}) %all-to-all-start) | async-done | bytes 262176 | tf_op jit(solution)/shard_map/all_to_all | solution.py:559
  18.9 0.7 %collective-permute-start = (f32[5,1,256,128]{3,2,1,0:T(8,128)}, f32[5,1,256,128]{3,2,1,0:T(8,128)S(1)}, u32[]{:S(2)}, u32[]{:S(2)}) collective-permute-start(f32[5,1,256,128]{3,2,1,0:T(8,128)} %get-tuple-element.23), channel_id=1, source_target_pairs={{1,2},{2,1},{3,4},{4,3},{5,6},{6,5},{9,10},{10,9},{11,12},{12,11},... | collective-permute-start | bytes 1966088 | tf_op jit(solution)/shard_map/ppermute | solution.py:336
  19.6 1.5 %collective-permute-start.1 = (f32[5,1,256,128]{3,2,1,0:T(8,128)}, f32[5,1,256,128]{3,2,1,0:T(8,128)S(1)}, u32[]{:S(2)}, u32[]{:S(2)}) collective-permute-start(f32[5,1,256,128]{3,2,1,0:T(8,128)} %get-tuple-element.24), channel_id=1, source_target_pairs={{0,1},{1,0},{2,3},{3,2},{4,5},{5,4},{6,7},{7,6},{8,9},{9,8},{10,11... | collective-permute-start | bytes 1966088 | tf_op jit(solution)/shard_map/ppermute | solution.py:331
  21.2 7.8 %shard_map.97 = (f32[512,128]{1,0:T(8,128)S(1)}, f32[512,128]{1,0:T(8,128)}) custom-call(s32[8,512]{1,0:T(8,128)S(1)} %bitcast.23, f32[512,128]{1,0:T(8,128)S(1)} %bitcast.18, bf16[4,8,5,128,128]{4,3,2,1,0:T(8,128)(2,1)} %get-tuple-element.21.moved_ref, f32[512,128]{1,0:T(8,128)} %bitcast.32), custom_call_target="tpu_custom_call" | custom-call | tf_op jit(solution)/shard_map/pallas_call | solution.py:30
  28.9 0.8 %collective-permute-start.9 = (f32[2,256,128]{2,1,0:T(8,128)S(1)}, f32[2,256,128]{2,1,0:T(8,128)S(1)}, u32[]{:S(2)}, u32[]{:S(2)}) collective-permute-start(f32[2,256,128]{2,1,0:T(8,128)S(1)} %bitcast.20), channel_id=1, source_target_pairs={{1,2},{2,1},{3,4},{4,3},{5,6},{6,5},{9,10},{10,9},{11,12},{12,11},... | collective-permute-start | bytes 786440 | tf_op jit(solution)/shard_map/ppermute | solution.py:336
  29.8 2.3 %collective-permute-start.8 = (f32[2,256,128]{2,1,0:T(8,128)S(1)}, f32[2,256,128]{2,1,0:T(8,128)S(1)}, u32[]{:S(2)}, u32[]{:S(2)}) collective-permute-start(f32[2,256,128]{2,1,0:T(8,128)S(1)} %bitcast.21), channel_id=1, source_target_pairs={{0,1},{1,0},{2,3},{3,2},{4,5},{5,4},{6,7},{7,6},{8,9},{9,8},{10,11... | collective-permute-start | bytes 786440 | tf_op jit(solution)/shard_map/ppermute | solution.py:331
  32.0 4.2 %all-to-all-start.1 = ((f32[32,16,128]{2,1,0:T(8,128)}), f32[32,16,128]{2,1,0:T(8,128)S(1)}, u32[]{:S(2)}, u32[]{:S(2)}) async-start(f32[32,16,128]{2,1,0:T(8,128)} %bitcast.13), calls=%async_computation.1 | async-start | bytes 524288 | tf_op jit(solution)/shard_map/all_to_all | solution.py:608
  36.2 4.3 %shard_map.100 = (f32[3,2,256,128]{3,2,1,0:T(8,128)S(1)}, f32[3,1,256,128]{3,2,1,0:T(8,128)}, f32[3,1,256,128]{3,2,1,0:T(8,128)}) custom-call(s32[1]{0:T(128)} %bitcast.6.place_ref, f32[3,2,256,128]{3,2,1,0:T(8,128)} %bitcast.30, f32[2,256,128]{2,1,0:T(8,128)} %bitcast.33, f32[2,256,128]{2,1,0:T(8,128)} %bitcast.35, f32[2,256,128]{2,1,0:T(8,128)S(1)} %bitcast.22, ...), custom_call_target="tpu_custom_call" | custom-call | tf_op jit(solution)/shard_map/pallas_call | solution.py:30
  40.5 0.6 %collective-permute-start.10 = (f32[3,1,256,128]{3,2,1,0:T(8,128)}, f32[3,1,256,128]{3,2,1,0:T(8,128)S(1)}, u32[]{:S(2)}, u32[]{:S(2)}) collective-permute-start(f32[3,1,256,128]{3,2,1,0:T(8,128)} %get-tuple-element.32), channel_id=1, source_target_pairs={{0,1},{1,0},{2,3},{3,2},{4,5},{5,4},{6,7},{7,6},{8,9},{9,8},{10,11... | collective-permute-start | bytes 1179656 | tf_op jit(solution)/shard_map/ppermute | solution.py:331
  41.2 0.9 %collective-permute-start.11 = (f32[3,1,256,128]{3,2,1,0:T(8,128)}, f32[3,1,256,128]{3,2,1,0:T(8,128)S(1)}, u32[]{:S(2)}, u32[]{:S(2)}) collective-permute-start(f32[3,1,256,128]{3,2,1,0:T(8,128)} %get-tuple-element.33), channel_id=1, source_target_pairs={{1,2},{2,1},{3,4},{4,3},{5,6},{6,5},{9,10},{10,9},{11,12},{12,11},... | collective-permute-start | bytes 1179656 | tf_op jit(solution)/shard_map/ppermute | solution.py:336
  42.1 2.5 %collective-permute-start.4 = (s32[8,64]{1,0:T(8,128)S(1)}, s32[8,64]{1,0:T(8,128)S(1)}, u32[]{:S(2)}, u32[]{:S(2)}) collective-permute-start(s32[8,64]{1,0:T(8,128)S(1)} %bitcast.25), channel_id=1, source_target_pairs={{0,24},{8,16},{16,8},{24,0},{1,25},{9,17},{17,9},{25,1},{2,26},{10... | collective-permute-start | bytes 6152 | tf_op jit(solution)/shard_map/ppermute | solution.py:326
  44.6 0.5 collective-permute-start.3
  45.1 0.5 collective-permute-start.2
  45.6 1.0 %collective-permute-done.4.refs_3_ = s32[8,64]{1,0:T(8,128)S(1)} collective-permute-done((s32[8,64]{1,0:T(8,128)S(1)}, s32[8,64]{1,0:T(8,128)S(1)}, u32[]{:S(2)}, u32[]{:S(2)}) %collective-permute-start.4) | collective-permute-done | bytes 2080 | tf_op jit(solution)/shard_map/ppermute | solution.py:326
  46.6 1.5 %collective-permute-done.3.refs_2_ = s32[8,64]{1,0:T(8,128)S(1)} collective-permute-done((s32[8,64]{1,0:T(8,128)S(1)}, s32[8,64]{1,0:T(8,128)S(1)}, u32[]{:S(2)}, u32[]{:S(2)}) %collective-permute-start.3) | collective-permute-done | bytes 2080 | tf_op jit(solution)/shard_map/ppermute | solution.py:326
  48.2 0.5 collective-permute-done.2.refs_1_
  48.7 0.9 %shard_map.98.refs_0_ = f32[128,128]{1,0:T(8,128)S(1)} custom-call(s32[1]{0:T(128)} %bitcast.me_ref, f32[512,128]{1,0:T(8,128)S(1)} %bitcast.19, s32[8,64]{1,0:T(8,128)S(1)} %bitcast.28, s32[8,64]{1,0:T(8,128)S(1)} %collective-permute-done.2.refs_1_, s32[8,64]{1,0:T(8,128)S(1)} %collective-permute-done.3.refs_2_, s32[8,64]{1,0:T(8,128)S(1)} %collective-permute-done.4.refs_3_), custom_call_target="tpu_custom_call" | custom-call | tf_op jit(solution)/shard_map/pallas_call | solution.py:30
  49.6 1.6 %collective-permute-start.7 = (f32[128,128]{1,0:T(8,128)S(1)}, f32[128,128]{1,0:T(8,128)S(1)}, u32[]{:S(2)}, u32[]{:S(2)}) collective-permute-start(f32[128,128]{1,0:T(8,128)S(1)} %shard_map.98.refs_0_), channel_id=1, source_target_pairs={{0,24},{8,16},{16,8},{24,0},{1,25},{9,17},{17,9},{25,1},{2,26},{10... | collective-permute-start | bytes 196616 | tf_op jit(solution)/shard_map/ppermute | solution.py:326
  51.7 1.5 %collective-permute-start.5 = (f32[128,128]{1,0:T(8,128)S(1)}, f32[128,128]{1,0:T(8,128)S(1)}, u32[]{:S(2)}, u32[]{:S(2)}) collective-permute-start(f32[128,128]{1,0:T(8,128)S(1)} %shard_map.98.refs_0_), channel_id=1, source_target_pairs={{0,8},{8,0},{16,24},{24,16},{1,9},{9,1},{17,25},{25,17},{2,10},{10... | collective-permute-start | bytes 196616 | tf_op jit(solution)/shard_map/ppermute | solution.py:326
  53.2 3.3 %shard_map.101 = f32[3,2,256,128]{3,2,1,0:T(8,128)} custom-call(s32[1]{0:T(128)} %bitcast.6.place_ref, f32[3,2,256,128]{3,2,1,0:T(8,128)S(1)} %get-tuple-element.31.field_ref, f32[2,256,128]{2,1,0:T(8,128)} %bitcast.36, f32[5,1,256,128]{3,2,1,0:T(8,128)S(1)} %collective-permute-done.1.edge_near_ref, ...), custom_call_target="tpu_custom_call" | custom-call | tf_op jit(solution)/shard_map/pallas_call | solution.py:30
  57.1 1.0 %shard_map.99 = f32[512,128]{1,0:T(8,128)} custom-call(s32[1]{0:T(128)} %bitcast.me_ref, f32[512,128]{1,0:T(8,128)S(1)} %copy-done, f32[128,128]{1,0:T(8,128)S(1)} %shard_map.98.refs_0_, f32[128,128]{1,0:T(8,128)S(1)} %collective-permute-done.5.refs_1_, f32[128,128]{1,0:T(8,128)S(1)} %collective-permute-done.6.refs_2_, ...), custom_call_target="tpu_custom_call" | custom-call | tf_op jit(solution)/shard_map/pallas_call | solution.py:30
  (17 shorter events, 1.0 us)
Async XLA Ops:
  0.6 20.5 %copy-start.1 = (s32[1,512,8]{1,2,0:T(8,128)S(1)}, s32[1,512,8]{1,2,0:T(8,128)}, u32[]{:S(2)}) copy-start(s32[1,512,8]{1,2,0:T(8,128)} %param.13) | copy-start | bytes 49156
  2.8 16.1 %all-to-all-start = ((f32[8,64,128]{2,1,0:T(8,128)}), f32[8,64,128]{2,1,0:T(8,128)S(1)}, u32[]{:S(2)}, u32[]{:S(2)}) async-start(f32[8,64,128]{2,1,0:T(8,128)} %bitcast.4), calls=%async_computation | async-start | bytes 524288 | tf_op jit(solution)/shard_map/all_to_all | solution.py:559
  13.9 28.1 %copy-start.2 = (s32[1,1,8,64]{3,2,1,0:T(8,128)S(1)}, s32[1,1,8,64]{3,2,1,0:T(8,128)}, u32[]{:S(2)}) copy-start(s32[1,1,8,64]{3,2,1,0:T(8,128)} %param.12) | copy-start | bytes 6148
  18.9 13.1 %collective-permute-start = (f32[5,1,256,128]{3,2,1,0:T(8,128)}, f32[5,1,256,128]{3,2,1,0:T(8,128)S(1)}, u32[]{:S(2)}, u32[]{:S(2)}) collective-permute-start(f32[5,1,256,128]{3,2,1,0:T(8,128)} %get-tuple-element.23), channel_id=1, source_target_pairs={{1,2},{2,1},{3,4},{4,3},{5,6},{6,5},{9,10},{10,9},{11,12},{12,11},... | collective-permute-start | bytes 1966088 | tf_op jit(solution)/shard_map/ppermute | solution.py:336
  19.6 12.4 %collective-permute-start.1 = (f32[5,1,256,128]{3,2,1,0:T(8,128)}, f32[5,1,256,128]{3,2,1,0:T(8,128)S(1)}, u32[]{:S(2)}, u32[]{:S(2)}) collective-permute-start(f32[5,1,256,128]{3,2,1,0:T(8,128)} %get-tuple-element.24), channel_id=1, source_target_pairs={{0,1},{1,0},{2,3},{3,2},{4,5},{5,4},{6,7},{7,6},{8,9},{9,8},{10,11... | collective-permute-start | bytes 1966088 | tf_op jit(solution)/shard_map/ppermute | solution.py:331
  28.9 28.1 %copy-start = (f32[512,128]{1,0:T(8,128)S(1)}, f32[512,128]{1,0:T(8,128)}, u32[]{:S(2)}) copy-start(f32[512,128]{1,0:T(8,128)} %template_ref.3) | copy-start | bytes 786436
  28.9 7.2 %collective-permute-start.9 = (f32[2,256,128]{2,1,0:T(8,128)S(1)}, f32[2,256,128]{2,1,0:T(8,128)S(1)}, u32[]{:S(2)}, u32[]{:S(2)}) collective-permute-start(f32[2,256,128]{2,1,0:T(8,128)S(1)} %bitcast.20), channel_id=1, source_target_pairs={{1,2},{2,1},{3,4},{4,3},{5,6},{6,5},{9,10},{10,9},{11,12},{12,11},... | collective-permute-start | bytes 786440 | tf_op jit(solution)/shard_map/ppermute | solution.py:336
  29.8 6.4 %collective-permute-start.8 = (f32[2,256,128]{2,1,0:T(8,128)S(1)}, f32[2,256,128]{2,1,0:T(8,128)S(1)}, u32[]{:S(2)}, u32[]{:S(2)}) collective-permute-start(f32[2,256,128]{2,1,0:T(8,128)S(1)} %bitcast.21), channel_id=1, source_target_pairs={{0,1},{1,0},{2,3},{3,2},{4,5},{5,4},{6,7},{7,6},{8,9},{9,8},{10,11... | collective-permute-start | bytes 786440 | tf_op jit(solution)/shard_map/ppermute | solution.py:331
  32.0 16.7 %all-to-all-start.1 = ((f32[32,16,128]{2,1,0:T(8,128)}), f32[32,16,128]{2,1,0:T(8,128)S(1)}, u32[]{:S(2)}, u32[]{:S(2)}) async-start(f32[32,16,128]{2,1,0:T(8,128)} %bitcast.13), calls=%async_computation.1 | async-start | bytes 524288 | tf_op jit(solution)/shard_map/all_to_all | solution.py:608
  40.5 12.7 %collective-permute-start.10 = (f32[3,1,256,128]{3,2,1,0:T(8,128)}, f32[3,1,256,128]{3,2,1,0:T(8,128)S(1)}, u32[]{:S(2)}, u32[]{:S(2)}) collective-permute-start(f32[3,1,256,128]{3,2,1,0:T(8,128)} %get-tuple-element.32), channel_id=1, source_target_pairs={{0,1},{1,0},{2,3},{3,2},{4,5},{5,4},{6,7},{7,6},{8,9},{9,8},{10,11... | collective-permute-start | bytes 1179656 | tf_op jit(solution)/shard_map/ppermute | solution.py:331
  41.2 12.0 %collective-permute-start.11 = (f32[3,1,256,128]{3,2,1,0:T(8,128)}, f32[3,1,256,128]{3,2,1,0:T(8,128)S(1)}, u32[]{:S(2)}, u32[]{:S(2)}) collective-permute-start(f32[3,1,256,128]{3,2,1,0:T(8,128)} %get-tuple-element.33), channel_id=1, source_target_pairs={{1,2},{2,1},{3,4},{4,3},{5,6},{6,5},{9,10},{10,9},{11,12},{12,11},... | collective-permute-start | bytes 1179656 | tf_op jit(solution)/shard_map/ppermute | solution.py:336
  42.1 4.6 %collective-permute-start.4 = (s32[8,64]{1,0:T(8,128)S(1)}, s32[8,64]{1,0:T(8,128)S(1)}, u32[]{:S(2)}, u32[]{:S(2)}) collective-permute-start(s32[8,64]{1,0:T(8,128)S(1)} %bitcast.25), channel_id=1, source_target_pairs={{0,24},{8,16},{16,8},{24,0},{1,25},{9,17},{17,9},{25,1},{2,26},{10... | collective-permute-start | bytes 6152 | tf_op jit(solution)/shard_map/ppermute | solution.py:326
  44.6 3.6 %collective-permute-start.3 = (s32[8,64]{1,0:T(8,128)S(1)}, s32[8,64]{1,0:T(8,128)S(1)}, u32[]{:S(2)}, u32[]{:S(2)}) collective-permute-start(s32[8,64]{1,0:T(8,128)S(1)} %bitcast.26), channel_id=1, source_target_pairs={{0,16},{8,24},{16,0},{24,8},{1,17},{9,25},{17,1},{25,9},{2,18},{10... | collective-permute-start | bytes 6152 | tf_op jit(solution)/shard_map/ppermute | solution.py:326
  45.1 3.6 %collective-permute-start.2 = (s32[8,64]{1,0:T(8,128)S(1)}, s32[8,64]{1,0:T(8,128)S(1)}, u32[]{:S(2)}, u32[]{:S(2)}) collective-permute-start(s32[8,64]{1,0:T(8,128)S(1)} %bitcast.27), channel_id=1, source_target_pairs={{0,8},{8,0},{16,24},{24,16},{1,9},{9,1},{17,25},{25,17},{2,10},{10... | collective-permute-start | bytes 6152 | tf_op jit(solution)/shard_map/ppermute | solution.py:326
  49.6 6.9 %collective-permute-start.7 = (f32[128,128]{1,0:T(8,128)S(1)}, f32[128,128]{1,0:T(8,128)S(1)}, u32[]{:S(2)}, u32[]{:S(2)}) collective-permute-start(f32[128,128]{1,0:T(8,128)S(1)} %shard_map.98.refs_0_), channel_id=1, source_target_pairs={{0,24},{8,16},{16,8},{24,0},{1,25},{9,17},{17,9},{25,1},{2,26},{10... | collective-permute-start | bytes 196616 | tf_op jit(solution)/shard_map/ppermute | solution.py:326
  51.2 5.8 %collective-permute-start.6 = (f32[128,128]{1,0:T(8,128)S(1)}, f32[128,128]{1,0:T(8,128)S(1)}, u32[]{:S(2)}, u32[]{:S(2)}) collective-permute-start(f32[128,128]{1,0:T(8,128)S(1)} %shard_map.98.refs_0_), channel_id=1, source_target_pairs={{0,16},{8,24},{16,0},{24,8},{1,17},{9,25},{17,1},{25,9},{2,18},{10... | collective-permute-start | bytes 196616 | tf_op jit(solution)/shard_map/ppermute | solution.py:326
  51.7 5.3 %collective-permute-start.5 = (f32[128,128]{1,0:T(8,128)S(1)}, f32[128,128]{1,0:T(8,128)S(1)}, u32[]{:S(2)}, u32[]{:S(2)}) collective-permute-start(f32[128,128]{1,0:T(8,128)S(1)} %shard_map.98.refs_0_), channel_id=1, source_target_pairs={{0,8},{8,0},{16,24},{24,16},{1,9},{9,1},{17,25},{25,17},{2,10},{10... | collective-permute-start | bytes 196616 | tf_op jit(solution)/shard_map/ppermute | solution.py:326

commit v5 on v4

--- a/solution.py
+++ b/solution.py
@@ -9,6 +9,7 @@
 
 YR = 256
 LANES = 128
+PAD = 8
 OFFSETS = (0, -2, -1, 1, 2)
 
 
@@ -19,7 +20,7 @@
 VMEM_LIMIT = 40 * 1024 * 1024
 
 
-def call(kernel, out_shape, *args, scratch=(), smem=(), far=(), free=(), out_far=()):
+def call(kernel, out_shape, *args, scratch=(), smem=(), far=(), out_far=()):
     many = isinstance(out_shape, tuple)
     shapes = [
         pltpu.HBM(s.shape, s.dtype) if i in out_far else s
@@ -32,15 +33,7 @@
         out_shape=tuple(shapes) if many else shapes[0],
         in_specs=[
             pl.BlockSpec(
-                memory_space=(
-                    pltpu.SMEM
-                    if i in smem
-                    else pltpu.HBM
-                    if i in far
-                    else pl.ANY
-                    if i in free
-                    else pltpu.VMEM
-                )
+                memory_space=pltpu.SMEM if i in smem else pltpu.HBM if i in far else pltpu.VMEM
             )
             for i in range(len(args))
         ],
@@ -338,63 +331,66 @@
     )
 
 
-def shifted(values, step, axis):
-    size = values.shape[axis]
-    index = lax.broadcasted_iota(jnp.int32, values.shape, axis)
-    edge = size - 1 if step > 0 else 0
-    return jnp.where(index == edge, 0.0, pltpu.roll(values, (-step) % size, axis=axis))
-
-
-def flow(center, half, faces):
-    total = None
-    for axis in (0, 1):
-        flux = faces[axis] * (shifted(center, 1, axis) - center)
-        index = lax.broadcasted_iota(jnp.int32, center.shape, axis)
-        behind = jnp.where(index == 0, half * center, pltpu.roll(flux, 1, axis=axis))
-        total = flux - behind if total is None else total + (flux - behind)
-    return total
-
-
-def by_side(odd, pairs):
-    copies = [
-        (
-            [pltpu.make_async_copy(near, low, sems[0]), pltpu.make_async_copy(far, high, sems[1])],
-            [pltpu.make_async_copy(near, high, sems[0]), pltpu.make_async_copy(far, low, sems[1])],
-        )
-        for near, far, low, high, sems in pairs
-    ]
-
-    @pl.when(odd)
-    def _():
-        for when_odd, _ in copies:
-            for copy in when_odd:
-                copy.start()
-
-    @pl.when(jnp.logical_not(odd))
-    def _():
-        for _, when_even in copies:
-            for copy in when_even:
-                copy.start()
-
-    return [copy for when_odd, _ in copies for copy in when_odd]
-
-
-def diffuse(now, coefs, first, last):
-    half = [0.5 * coef for coef in coefs]
-    gaps = {p: half[p] + half[p + 1] for p in range(first - 1, last + 1)}
-    faces = {
-        p: [half[p] + shifted(half[p], 1, axis) for axis in (0, 1)] for p in range(first, last + 1)
-    }
+def clear_pads(ref):
+    rows = ref.shape[-2] - 2 * PAD
+    zeros = jnp.zeros(ref.shape[:-2] + (PAD, ref.shape[-1]), ref.dtype)
+    ref[..., :PAD, :] = zeros
+    ref[..., PAD + rows :, :] = zeros
+
+
+def plane_of(ref, *at, step=0):
+    rows = ref.shape[-2] - 2 * PAD
+    return ref[(*at, slice(PAD + step, PAD + step + rows), slice(None))]
+
+
+def sides(odd, near, far):
+    return jnp.where(odd, near, far), jnp.where(odd, far, near)
+
+
+def step_weights(coefs, p, below, above):
+    center = plane_of(coefs, p)
+    lane = lax.broadcasted_iota(jnp.int32, center.shape, 1)
+    scale = 0.5 * diffusion_dt
+    last = center.shape[1] - 1
+    right = center + jnp.where(lane == last, 0.0, turned(center, -1))
+    left = center + jnp.where(lane == 0, 0.0, turned(center, 1))
+    others = [
+        center + near
+        for near in (plane_of(coefs, p, step=1), plane_of(coefs, p, step=-1), above, below)
+    ]
+    total = right + left
+    for face in others:
+        total = total + face
+    return [
+        1.0 - scale * total,
+        jnp.where(lane == last, 0.0, scale * right),
+        jnp.where(lane == 0, 0.0, scale * left),
+    ] + [scale * face for face in others]
+
+
+def all_weights(coefs, low, high):
+    planes = coefs.shape[0]
+    column = [low] + [plane_of(coefs, p) for p in range(planes)] + [high]
+    return [step_weights(coefs, p, column[p], column[p + 2]) for p in range(planes)]
+
+
+def stepped(fields, a, low, high, weights):
+    planes = fields.shape[1]
+    column = [low] + [plane_of(fields, a, p) for p in range(planes)] + [high]
     later = []
-    for field in now:
-        rise = {p: gaps[p] * (field[p + 1] - field[p]) for p in gaps}
-        later.append(
-            [
-                field[p]
-                + diffusion_dt * (rise[p] - rise[p - 1] + flow(field[p], half[p], faces[p]))
-                for p in range(first, last + 1)
-            ]
-        )
+    for p in range(planes):
+        values = [
+            turned(column[p + 1], -1),
+            turned(column[p + 1], 1),
+            plane_of(fields, a, p, step=1),
+            plane_of(fields, a, p, step=-1),
+            column[p + 2],
+            column[p],
+        ]
+        total = weights[p][0] * column[p + 1]
+        for weight, value in zip(weights[p][1:], values):
+            total = total + weight * value
+        later.append(total)
     return later
 
 
@@ -408,122 +404,96 @@
     edge_far_ref,
     warped_near_ref,
     warped_far_ref,
-    out_ref,
+    field_ref,
+    coefs_ref,
     near_ref,
     far_ref,
+    velocity,
+    images,
+    warped,
     fields,
-    images,
-    coefs,
-    warped,
+    outer,
     sem,
 ):
-    parts, planes = out_ref.shape[:2]
+    parts, planes, rows = velocity.shape[:3]
     odd = place_ref[0] == 1
-    low, mid, high = pl.ds(0, 1), pl.ds(1, planes), pl.ds(planes + 1, 1)
-    every = pl.ds(0, parts)
-    waits = by_side(
-        odd,
-        [
-            (
-                warped_near_ref,
-                warped_far_ref,
-                warped.at[pl.ds(0, 2)],
-                warped.at[pl.ds(planes + 2, 2)],
-                (sem.at[0], sem.at[1]),
-            ),
-            (
-                edge_near_ref.at[parts],
-                edge_far_ref.at[parts],
-                coefs.at[low],
-                coefs.at[high],
-                (sem.at[2], sem.at[3]),
-            ),
-            (
-                edge_near_ref.at[parts + 1],
-                edge_far_ref.at[parts + 1],
-                images.at[low],
-                images.at[high],
-                (sem.at[4], sem.at[5]),
-            ),
-            (
-                edge_near_ref.at[every],
-                edge_far_ref.at[every],
-                fields.at[:, low],
-                fields.at[:, high],
-                (sem.at[6], sem.at[7]),
-            ),
-        ],
-    )
-    own = [
-        pltpu.make_async_copy(warped_ref, warped.at[pl.ds(2, planes)], sem.at[8]),
-        pltpu.make_async_copy(stiffness_ref, coefs.at[mid], sem.at[9]),
-        pltpu.make_async_copy(images_ref, images.at[mid], sem.at[10]),
-        pltpu.make_async_copy(velocity_ref, fields.at[:, mid], sem.at[11]),
-    ]
-    for copy in own:
+    body = slice(PAD, PAD + rows)
+    copies = [
+        pltpu.make_async_copy(stiffness_ref, coefs_ref.at[:, pl.ds(PAD, rows)], sem.at[0]),
+        pltpu.make_async_copy(images_ref, images, sem.at[1]),
+    ] + [pltpu.make_async_copy(velocity_ref.at[a], velocity.at[a], sem.at[2 + a]) for a in range(parts)]
+    for copy in copies:
         copy.start()
-    for copy in waits + own:
+    for ref in (field_ref, fields, coefs_ref, warped):
+        clear_pads(ref)
+    lowest = jnp.where(odd, warped_near_ref[0], warped_far_ref[0])
+    highest = jnp.where(odd, warped_far_ref[1], warped_near_ref[1])
+    warped[0, body, :] = jnp.where(odd, warped_near_ref[1], warped_far_ref[1])
+    warped[planes + 1, body, :] = jnp.where(odd, warped_far_ref[0], warped_near_ref[0])
+    for p in range(planes):
+        warped[p + 1, body, :] = warped_ref[p]
+    column = [lowest] + [plane_of(warped, p) for p in range(planes + 2)] + [highest]
+    image_low, image_high = sides(odd, edge_near_ref[parts + 1, 0], edge_far_ref[parts + 1, 0])
+    lane = lax.broadcasted_iota(jnp.int32, (rows, LANES), 1)
+    right = jnp.where(lane == LANES - 1, 0.0, 0.5 * force_step)
+    left = jnp.where(lane == 0, 0.0, 0.5 * force_step)
+
+    def forces(p, image):
+        here = column[p + 1]
+        mismatch = here - image
+        half = (0.5 * force_step) * mismatch
+        return [
+            mismatch * (right * turned(here, -1) - left * turned(here, 1)),
+            half * (plane_of(warped, p, step=1) - plane_of(warped, p, step=-1)),
+            half * (column[p + 2] - column[p]),
+        ]
+
+    for side, p, image in ((0, 0, image_low), (1, planes + 1, image_high)):
+        force = forces(p, image)
+        for a in range(parts):
+            outer[side, a] = sides(odd, edge_near_ref[a, 0], edge_far_ref[a, 0])[side] - force[a]
+    copies[0].wait()
+    weights = all_weights(
+        coefs_ref, *sides(odd, edge_near_ref[parts, 0], edge_far_ref[parts, 0])
+    )
+    for copy in copies[1:]:
         copy.wait()
-    now = [[] for _ in range(parts)]
-    for p in range(planes + 2):
-        here = warped[p + 1]
-        mismatch = here - images[p]
-        slopes = [
-            0.5 * (shifted(here, 1, 1) - shifted(here, -1, 1)),
-            0.5 * (shifted(here, 1, 0) - shifted(here, -1, 0)),
-            0.5 * (warped[p + 2] - warped[p]),
-        ]
+    for p in range(planes):
+        force = forces(p + 1, images[p])
         for a in range(parts):
-            now[a].append(fields[a, p] - force_step * mismatch * slopes[a])
-    later = diffuse(now, [coefs[p] for p in range(planes + 2)], 1, planes)
+            fields[a, p, body, :] = velocity[a, p] - force[a]
     for a in range(parts):
+        later = stepped(fields, a, outer[0, a], outer[1, a], weights)
         for p in range(planes):
-            out_ref[a, p] = later[a][p]
-        near_ref[a, 0] = jnp.where(odd, later[a][0], later[a][-1])
-        far_ref[a, 0] = jnp.where(odd, later[a][-1], later[a][0])
+            field_ref[a, p, body, :] = later[p]
+        near_ref[a, 0], far_ref[a, 0] = sides(odd, later[0], later[-1])
 
 
 def last_kernel(
     place_ref,
     field_ref,
-    stiffness_ref,
+    coefs_ref,
     edge_near_ref,
     edge_far_ref,
     near_ref,
     far_ref,
     out_ref,
-    fields,
-    coefs,
+    done,
     sem,
 ):
-    parts, planes = out_ref.shape[:2]
-    low, mid, high = pl.ds(0, 1), pl.ds(1, planes), pl.ds(planes + 1, 1)
-    waits = by_side(
-        place_ref[0] == 1,
-        [
-            (near_ref, far_ref, fields.at[:, low], fields.at[:, high], (sem.at[0], sem.at[1])),
-            (
-                edge_near_ref.at[parts],
-                edge_far_ref.at[parts],
-                coefs.at[low],
-                coefs.at[high],
-                (sem.at[2], sem.at[3]),
-            ),
-        ],
-    )
-    own = [
-        pltpu.make_async_copy(field_ref, fields.at[:, mid], sem.at[4]),
-        pltpu.make_async_copy(stiffness_ref, coefs.at[mid], sem.at[5]),
-    ]
-    for copy in own:
-        copy.start()
-    for copy in waits + own:
+    parts, planes = done.shape[:2]
+    odd = place_ref[0] == 1
+    weights = all_weights(
+        coefs_ref, *sides(odd, edge_near_ref[parts, 0], edge_far_ref[parts, 0])
+    )
+    writes = [pltpu.make_async_copy(done.at[a], out_ref.at[a], sem.at[a]) for a in range(parts)]
+    for a in range(parts):
+        later = stepped(field_ref, a, *sides(odd, near_ref[a, 0], far_ref[a, 0]), weights)
+        for p in range(planes):
+            done[a, p] = later[p]
+        writes[a].start()
+    for copy in writes:
         copy.wait()
-    now = [[fields[a, p] for p in range(planes + 2)] for a in range(parts)]
-    later = diffuse(now, [coefs[p] for p in range(planes + 2)], 1, planes)
-    for a in range(parts):
-        for p in range(planes):
-            out_ref[a, p] = later[a][p]
 
 
 def per_device(template, images, velocity, stiffness, send_rows, ref_slot, columns, weights):
@@ -556,6 +526,8 @@
         far=(0, 1),
         scratch=(pltpu.VMEM((slabs, capacity), jnp.int32), pltpu.VMEM((rows, width), f32), dma((2,))),
     )
+    sending, own_rows = lax.optimization_barrier((sending, send_rows[0, 0]))
+    all_rows = over_subjects(own_rows)
     received = lax.all_to_all(sending, "slab", split_axis=0, concat_axis=0, tiled=True)
 
     chunks = 4
@@ -584,7 +556,9 @@
             dma((3,)),
         ),
     )
-    received, edge_far, edge_near = lax.optimization_barrier((received, edge_far, edge_near))
+    received, edge_far, edge_near, *all_rows = lax.optimization_barrier(
+        (received, edge_far, edge_near, *all_rows)
+    )
     edge_far, edge_near = swap_far(edge_far), swap_near(edge_near)
 
     warped, sent = call(
@@ -607,15 +581,15 @@
     sent, edge_far, edge_near = lax.optimization_barrier((sent, edge_far, edge_near))
     returned = lax.all_to_all(sent, ("subj", "slab"), split_axis=0, concat_axis=0, tiled=True)
 
-    own_rows, warped = lax.optimization_barrier((send_rows[0, 0], warped))
     warped_grid = warped.reshape(grid)
     warped_far, warped_near = swap_far(warped_grid), swap_near(warped_grid)
-    all_rows = over_subjects(own_rows)
-
-    field, field_near, field_far = call(
+
+    high = YR + 2 * PAD
+    field, coefs, field_near, field_far = call(
         force_kernel,
         (
-            shape((parts,) + grid, f32),
+            shape((parts, planes, high, width), f32),
+            shape((planes, high, width), f32),
             shape((parts, 1, YR, width), f32),
             shape((parts, 1, YR, width), f32),
         ),
@@ -630,13 +604,13 @@
         warped_far,
         smem=(0,),
         far=(1, 2, 3),
-        free=(4, 5, 6, 7, 8),
         scratch=(
-            pltpu.VMEM((parts, planes + 2, YR, width), f32),
-            pltpu.VMEM((planes + 2, YR, width), f32),
-            pltpu.VMEM((planes + 2, YR, width), f32),
-            pltpu.VMEM((planes + 4, YR, width), f32),
-            dma((12,)),
+            pltpu.VMEM((parts,) + grid, f32),
+            pltpu.VMEM(grid, f32),
+            pltpu.VMEM((planes + 2, high, width), f32),
+            pltpu.VMEM((parts, planes, high, width), f32),
+            pltpu.VMEM((2, parts, YR, width), f32),
+            dma((2 + parts,)),
         ),
     )
     field_far, field_near = swap_far(field_far), swap_near(field_near)
@@ -663,19 +637,14 @@
         shape((parts,) + grid, f32),
         place,
         field,
-        coef_grid,
+        coefs,
         edge_near,
         edge_far,
         field_near,
         field_far,
         smem=(0,),
-        far=(2,),
-        free=(1, 3, 4, 5, 6),
-        scratch=(
-            pltpu.VMEM((parts, planes + 2, YR, width), f32),
-            pltpu.VMEM((planes + 2, YR, width), f32),
-            dma((6,)),
-        ),
+        out_far=(0,),
+        scratch=(pltpu.VMEM((parts,) + grid, f32), dma((parts,))),
     )
     velocity_out = field.reshape(parts, rows, width)[None]
     return (template_out, velocity_out)

time: 58.5 us -> 56.6 us (0.968)
  Pallas kernels: 24.4 us -> 21.8 us
  local copies, waits for them, and re-layouts: 0.02 us -> 1.68 us
  waiting for transfers between devices: 8.52 us -> 6.94 us
  starting transfers between devices: 24.4 us -> 25 us
    all_to_all x1, waiting for transfers between devices: 0.01 us -> 5.34 us  [per_device(): lax.all_to_all(sent, ('subj', 'slab'), split_axis=0, concat_axis=0, tiled...]
    all_to_all x1, waiting for transfers between devices: 4.94 us -> 1.41 us  [per_device(): lax.all_to_all(sending, 'slab', split_axis=0, concat_axis=0, tiled=True)]
    ppermute x6, waiting for transfers between devices: 3.56 us -> 0.17 us  [over_subjects(): lax.ppermute(values, 'subj', [(i, i ^ d) for i in range(count)])]
    pallas_call x7, Pallas kernels: 24.4 us -> 21.8 us  [call(): pl.pallas_call(kernel, out_shape=tuple(shapes) if many else shapes[0], in...]
    unnamed x6 -> x10, local copies, waits for them, and re-layouts: 0.02 us -> 1.68 us
    ppermute x3, starting transfers between devices: 4.44 us -> 5.14 us  [swap_near(): lax.ppermute(values, 'slab', [(i, i ^ 1) for i in range(lax.axis_size('sl...]
  transfers between devices with their start and end apart: 14 -> 14, of which waited for: 6 -> 3; matrix products, arithmetic and copies ran while one was open for 0% -> 0% of each run, Pallas kernels for 36% -> 33%
where the time goes in v5:
time: 56.6 us; the launch traced here: 56.1 us
  starting transfers between devices  25 us (44%)
  Pallas kernels  21.8 us (39%)
  waiting for transfers between devices  6.94 us (12%)
  local copies, waits for them, and re-layouts  1.68 us (3%)
  between operations  0.81 us (1%)
    pallas_call x7, Pallas kernels, call(): pl.pallas_call(kernel, out_shape=tuple(shapes) if many else shapes[0], in...  21.8 us
    ppermute x6, starting transfers between devices, over_subjects(): lax.ppermute(values, 'subj', [(i, i ^ d) for i in range(count)])  7.07 us
    all_to_all x1, starting transfers between devices, per_device(): lax.all_to_all(sending, 'slab', split_axis=0, concat_axis=0, tiled=True)  6.34 us
    all_to_all x1, waiting for transfers between devices, per_device(): lax.all_to_all(sent, ('subj', 'slab'), split_axis=0, concat_axis=0, tiled...  5.34 us
    ppermute x3, starting transfers between devices, swap_near(): lax.ppermute(values, 'slab', [(i, i ^ 1) for i in range(lax.axis_size('sl...  5.14 us
    all_to_all x1, starting transfers between devices, per_device(): lax.all_to_all(sent, ('subj', 'slab'), split_axis=0, concat_axis=0, tiled...  4.24 us
    ppermute x3, starting transfers between devices, swap_far(): lax.ppermute(values, 'slab', [(i, i + 1 if i % 2 else i - 1) for i in ran...  2.17 us
    unnamed x10, local copies, waits for them, and re-layouts  1.68 us
  transfers between devices with their start and end apart: 14, of which 3 were waited for; matrix products, arithmetic and copies ran while one was open for 0% of the time, Pallas kernels for 33%

profile of v5, /device:TPU:0, one launch (start us, length us, event | category | flops | bytes accessed | tf_op | source)
XLA Modules:
  0.0 56.1 jit_solution(5181499863974376992)
XLA Ops:
  0.6 2.2 %shard_map.95 = f32[512,128]{1,0:T(8,128)} custom-call(s32[8,64]{1,0:T(8,128)} %bitcast.24, f32[512,128]{1,0:T(8,128)} %template_ref.3), custom_call_target="tpu_custom_call" | custom-call | tf_op jit(solution)/shard_map/pallas_call | solution.py:31
  2.8 6.3 %all-to-all-start = ((f32[8,64,128]{2,1,0:T(8,128)}), f32[8,64,128]{2,1,0:T(8,128)S(1)}, u32[]{:S(2)}, u32[]{:S(2)}) async-start(f32[8,64,128]{2,1,0:T(8,128)} %bitcast.4), calls=%async_computation | async-start | bytes 524288 | tf_op jit(solution)/shard_map/all_to_all | solution.py:531
  9.2 2.4 %collective-permute-start.2 = (s32[8,64]{1,0:T(8,128)}, s32[8,64]{1,0:T(8,128)S(1)}, u32[]{:S(2)}, u32[]{:S(2)}) collective-permute-start(s32[8,64]{1,0:T(8,128)} %bitcast.25), channel_id=1, source_target_pairs={{0,24},{8,16},{16,8},{24,0},{1,25},{9,17},{17,9},{25,1},{2,26},{10... | collective-permute-start | bytes 6152 | tf_op jit(solution)/shard_map/ppermute | solution.py:319
  11.6 0.5 collective-permute-start.1
  12.1 0.5 collective-permute-start
  12.6 4.8 %shard_map.96 = (bf16[4,8,5,128,128]{4,3,2,1,0:T(8,128)(2,1)}, f32[5,1,256,128]{3,2,1,0:T(8,128)}, f32[5,1,256,128]{3,2,1,0:T(8,128)}) custom-call(s32[1]{0:T(128)} %bitcast.6.place_ref, s32[4096,128]{1,0:T(8,128)} %bitcast.34, bf16[4096,128]{1,0:T(8,128)(2,1)} %bitcast.35, f32[3,2,256,128]{3,2,1,0:T(8,128)} %bitcast.29, f32[2,256,128]{2,1,0:T(8,128)} %bitcast.36, ...), custom_call_target="tpu_custom_call" | custom-call | tf_op jit(solution)/shard_map/pallas_call | solution.py:31
  17.5 1.4 %all-to-all-done = f32[8,64,128]{2,1,0:T(8,128)S(1)} async-done(((f32[8,64,128]{2,1,0:T(8,128)}), f32[8,64,128]{2,1,0:T(8,128)S(1)}, u32[]{:S(2)}, u32[]{:S(2)}) %all-to-all-start) | async-done | bytes 262176 | tf_op jit(solution)/shard_map/all_to_all | solution.py:531
  18.9 0.7 %collective-permute-start.3 = (f32[5,1,256,128]{3,2,1,0:T(8,128)}, f32[5,1,256,128]{3,2,1,0:T(8,128)S(1)}, u32[]{:S(2)}, u32[]{:S(2)}) collective-permute-start(f32[5,1,256,128]{3,2,1,0:T(8,128)} %get-tuple-element.30), channel_id=1, source_target_pairs={{1,2},{2,1},{3,4},{4,3},{5,6},{6,5},{9,10},{10,9},{11,12},{12,11},... | collective-permute-start | bytes 1966088 | tf_op jit(solution)/shard_map/ppermute | solution.py:329
  19.6 2.0 %collective-permute-start.4 = (f32[5,1,256,128]{3,2,1,0:T(8,128)}, f32[5,1,256,128]{3,2,1,0:T(8,128)S(1)}, u32[]{:S(2)}, u32[]{:S(2)}) collective-permute-start(f32[5,1,256,128]{3,2,1,0:T(8,128)} %get-tuple-element.31), channel_id=1, source_target_pairs={{0,1},{1,0},{2,3},{3,2},{4,5},{5,4},{6,7},{7,6},{8,9},{9,8},{10,11... | collective-permute-start | bytes 1966088 | tf_op jit(solution)/shard_map/ppermute | solution.py:324
  21.6 7.8 %shard_map.97 = (f32[512,128]{1,0:T(8,128)S(1)}, f32[512,128]{1,0:T(8,128)}) custom-call(s32[8,512]{1,0:T(8,128)S(1)} %bitcast.23, f32[512,128]{1,0:T(8,128)S(1)} %bitcast.18, bf16[4,8,5,128,128]{4,3,2,1,0:T(8,128)(2,1)} %get-tuple-element.28.moved_ref, f32[512,128]{1,0:T(8,128)} %bitcast.32), custom_call_target="tpu_custom_call" | custom-call | tf_op jit(solution)/shard_map/pallas_call | solution.py:31
  29.4 0.8 %collective-permute-start.9 = (f32[2,256,128]{2,1,0:T(8,128)S(1)}, f32[2,256,128]{2,1,0:T(8,128)S(1)}, u32[]{:S(2)}, u32[]{:S(2)}) collective-permute-start(f32[2,256,128]{2,1,0:T(8,128)S(1)} %bitcast.20), channel_id=1, source_target_pairs={{1,2},{2,1},{3,4},{4,3},{5,6},{6,5},{9,10},{10,9},{11,12},{12,11},... | collective-permute-start | bytes 786440 | tf_op jit(solution)/shard_map/ppermute | solution.py:329
  30.2 2.9 %collective-permute-start.8 = (f32[2,256,128]{2,1,0:T(8,128)S(1)}, f32[2,256,128]{2,1,0:T(8,128)S(1)}, u32[]{:S(2)}, u32[]{:S(2)}) collective-permute-start(f32[2,256,128]{2,1,0:T(8,128)S(1)} %bitcast.21), channel_id=1, source_target_pairs={{0,1},{1,0},{2,3},{3,2},{4,5},{5,4},{6,7},{7,6},{8,9},{9,8},{10,11... | collective-permute-start | bytes 786440 | tf_op jit(solution)/shard_map/ppermute | solution.py:324
  33.1 4.2 %all-to-all-start.1 = ((f32[32,16,128]{2,1,0:T(8,128)}), f32[32,16,128]{2,1,0:T(8,128)S(1)}, u32[]{:S(2)}, u32[]{:S(2)}) async-start(f32[32,16,128]{2,1,0:T(8,128)} %bitcast.13), calls=%async_computation.1 | async-start | bytes 524288 | tf_op jit(solution)/shard_map/all_to_all | solution.py:582
  37.4 3.4 %shard_map.100 = (f32[3,2,272,128]{3,2,1,0:T(8,128)S(1)}, f32[2,272,128]{2,1,0:T(8,128)S(1)}, f32[3,1,256,128]{3,2,1,0:T(8,128)}, f32[3,1,256,128]{3,2,1,0:T(8,128)}) custom-call(s32[1]{0:T(128)} %bitcast.6.place_ref, f32[3,2,256,128]{3,2,1,0:T(8,128)} %bitcast.30, f32[2,256,128]{2,1,0:T(8,128)} %bitcast.33, f32[2,256,128]{2,1,0:T(8,128)} %bitcast.37, ...), custom_call_target="tpu_custom_call" | custom-call | tf_op jit(solution)/shard_map/pallas_call | solution.py:31
  40.8 0.7 %copy-done.1 = f32[2,272,128]{2,1,0:T(8,128)} copy-done((f32[2,272,128]{2,1,0:T(8,128)}, f32[2,272,128]{2,1,0:T(8,128)S(1)}, u32[]{:S(2)}) %copy-start.1) | copy-done | bytes 278552
  41.7 0.7 %collective-permute-start.11 = (f32[3,1,256,128]{3,2,1,0:T(8,128)}, f32[3,1,256,128]{3,2,1,0:T(8,128)S(1)}, u32[]{:S(2)}, u32[]{:S(2)}) collective-permute-start(f32[3,1,256,128]{3,2,1,0:T(8,128)} %get-tuple-element.43), channel_id=1, source_target_pairs={{1,2},{2,1},{3,4},{4,3},{5,6},{6,5},{9,10},{10,9},{11,12},{12,11},... | collective-permute-start | bytes 1179656 | tf_op jit(solution)/shard_map/ppermute | solution.py:329
  42.4 5.3 %all-to-all-done.1 = f32[32,16,128]{2,1,0:T(8,128)S(1)} async-done(((f32[32,16,128]{2,1,0:T(8,128)}), f32[32,16,128]{2,1,0:T(8,128)S(1)}, u32[]{:S(2)}, u32[]{:S(2)}) %all-to-all-start.1) | async-done | bytes 262176 | tf_op jit(solution)/shard_map/all_to_all | solution.py:582
  47.7 0.9 %shard_map.98.refs_0_ = f32[128,128]{1,0:T(8,128)S(1)} custom-call(s32[1]{0:T(128)} %bitcast.me_ref, f32[512,128]{1,0:T(8,128)S(1)} %bitcast.19, s32[8,64]{1,0:T(8,128)S(1)} %bitcast.28, s32[8,64]{1,0:T(8,128)S(1)} %collective-permute-done.refs_1_, s32[8,64]{1,0:T(8,128)S(1)} %collective-permute-done.1.refs_2_, s32[8,64]{1,0:T(8,128)S(1)} %collective-permute-done.2.refs_3_), custom_call_target="tpu_custom_call" | custom-call | tf_op jit(solution)/shard_map/pallas_call | solution.py:31
  48.7 0.8 %collective-permute-start.7 = (f32[128,128]{1,0:T(8,128)S(1)}, f32[128,128]{1,0:T(8,128)S(1)}, u32[]{:S(2)}, u32[]{:S(2)}) collective-permute-start(f32[128,128]{1,0:T(8,128)S(1)} %shard_map.98.refs_0_), channel_id=1, source_target_pairs={{0,24},{8,16},{16,8},{24,0},{1,25},{9,17},{17,9},{25,1},{2,26},{10... | collective-permute-start | bytes 196616 | tf_op jit(solution)/shard_map/ppermute | solution.py:319
  49.5 1.2 %collective-permute-start.6 = (f32[128,128]{1,0:T(8,128)S(1)}, f32[128,128]{1,0:T(8,128)S(1)}, u32[]{:S(2)}, u32[]{:S(2)}) collective-permute-start(f32[128,128]{1,0:T(8,128)S(1)} %shard_map.98.refs_0_), channel_id=1, source_target_pairs={{0,16},{8,24},{16,0},{24,8},{1,17},{9,25},{17,1},{25,9},{2,18},{10... | collective-permute-start | bytes 196616 | tf_op jit(solution)/shard_map/ppermute | solution.py:319
  50.7 1.5 %collective-permute-start.5 = (f32[128,128]{1,0:T(8,128)S(1)}, f32[128,128]{1,0:T(8,128)S(1)}, u32[]{:S(2)}, u32[]{:S(2)}) collective-permute-start(f32[128,128]{1,0:T(8,128)S(1)} %shard_map.98.refs_0_), channel_id=1, source_target_pairs={{0,8},{8,0},{16,24},{24,16},{1,9},{9,1},{17,25},{25,17},{2,10},{10... | collective-permute-start | bytes 196616 | tf_op jit(solution)/shard_map/ppermute | solution.py:319
  52.3 1.0 %copy-done.2 = f32[2,272,128]{2,1,0:T(8,128)S(1)} copy-done((f32[2,272,128]{2,1,0:T(8,128)S(1)}, f32[2,272,128]{2,1,0:T(8,128)}, u32[]{:S(2)}) %copy-start.2) | copy-done | bytes 278552
  53.2 1.7 %shard_map.101 = f32[3,2,256,128]{3,2,1,0:T(8,128)} custom-call(s32[1]{0:T(128)} %bitcast.6.place_ref, f32[3,2,272,128]{3,2,1,0:T(8,128)S(1)} %get-tuple-element.40.field_ref, f32[2,272,128]{2,1,0:T(8,128)S(1)} %copy-done.2, f32[5,1,256,128]{3,2,1,0:T(8,128)S(1)} %collective-permute-done.4.edge_near_ref, ...), custom_call_target="tpu_custom_call" | custom-call | tf_op jit(solution)/shard_map/pallas_call | solution.py:31
  55.1 1.0 %shard_map.99 = f32[512,128]{1,0:T(8,128)} custom-call(s32[1]{0:T(128)} %bitcast.me_ref, f32[512,128]{1,0:T(8,128)S(1)} %copy-done, f32[128,128]{1,0:T(8,128)S(1)} %shard_map.98.refs_0_, f32[128,128]{1,0:T(8,128)S(1)} %collective-permute-done.5.refs_1_, f32[128,128]{1,0:T(8,128)S(1)} %collective-permute-done.6.refs_2_, ...), custom_call_target="tpu_custom_call" | custom-call | tf_op jit(solution)/shard_map/pallas_call | solution.py:31
  (21 shorter events, 0.5 us)
Async XLA Ops:
  0.6 21.0 %copy-start.3 = (s32[1,512,8]{1,2,0:T(8,128)S(1)}, s32[1,512,8]{1,2,0:T(8,128)}, u32[]{:S(2)}) copy-start(s32[1,512,8]{1,2,0:T(8,128)} %param.13) | copy-start | bytes 49156
  2.8 16.1 %all-to-all-start = ((f32[8,64,128]{2,1,0:T(8,128)}), f32[8,64,128]{2,1,0:T(8,128)S(1)}, u32[]{:S(2)}, u32[]{:S(2)}) async-start(f32[8,64,128]{2,1,0:T(8,128)} %bitcast.4), calls=%async_computation | async-start | bytes 524288 | tf_op jit(solution)/shard_map/all_to_all | solution.py:531
  9.2 8.3 %collective-permute-start.2 = (s32[8,64]{1,0:T(8,128)}, s32[8,64]{1,0:T(8,128)S(1)}, u32[]{:S(2)}, u32[]{:S(2)}) collective-permute-start(s32[8,64]{1,0:T(8,128)} %bitcast.25), channel_id=1, source_target_pairs={{0,24},{8,16},{16,8},{24,0},{1,25},{9,17},{17,9},{25,1},{2,26},{10... | collective-permute-start | bytes 6152 | tf_op jit(solution)/shard_map/ppermute | solution.py:319
  11.6 5.9 %collective-permute-start.1 = (s32[8,64]{1,0:T(8,128)}, s32[8,64]{1,0:T(8,128)S(1)}, u32[]{:S(2)}, u32[]{:S(2)}) collective-permute-start(s32[8,64]{1,0:T(8,128)} %bitcast.26), channel_id=1, source_target_pairs={{0,16},{8,24},{16,0},{24,8},{1,17},{9,25},{17,1},{25,9},{2,18},{10... | collective-permute-start | bytes 6152 | tf_op jit(solution)/shard_map/ppermute | solution.py:319
  12.1 5.4 %collective-permute-start = (s32[8,64]{1,0:T(8,128)}, s32[8,64]{1,0:T(8,128)S(1)}, u32[]{:S(2)}, u32[]{:S(2)}) collective-permute-start(s32[8,64]{1,0:T(8,128)} %bitcast.27), channel_id=1, source_target_pairs={{0,8},{8,0},{16,24},{24,16},{1,9},{9,1},{17,25},{25,17},{2,10},{10... | collective-permute-start | bytes 6152 | tf_op jit(solution)/shard_map/ppermute | solution.py:319
  17.4 30.3 %copy-start.4 = (s32[1,1,8,64]{3,2,1,0:T(8,128)S(1)}, s32[1,1,8,64]{3,2,1,0:T(8,128)}, u32[]{:S(2)}) copy-start(s32[1,1,8,64]{3,2,1,0:T(8,128)} %param.12) | copy-start | bytes 6148
  18.9 14.2 %collective-permute-start.3 = (f32[5,1,256,128]{3,2,1,0:T(8,128)}, f32[5,1,256,128]{3,2,1,0:T(8,128)S(1)}, u32[]{:S(2)}, u32[]{:S(2)}) collective-permute-start(f32[5,1,256,128]{3,2,1,0:T(8,128)} %get-tuple-element.30), channel_id=1, source_target_pairs={{1,2},{2,1},{3,4},{4,3},{5,6},{6,5},{9,10},{10,9},{11,12},{12,11},... | collective-permute-start | bytes 1966088 | tf_op jit(solution)/shard_map/ppermute | solution.py:329
  19.6 13.5 %collective-permute-start.4 = (f32[5,1,256,128]{3,2,1,0:T(8,128)}, f32[5,1,256,128]{3,2,1,0:T(8,128)S(1)}, u32[]{:S(2)}, u32[]{:S(2)}) collective-permute-start(f32[5,1,256,128]{3,2,1,0:T(8,128)} %get-tuple-element.31), channel_id=1, source_target_pairs={{0,1},{1,0},{2,3},{3,2},{4,5},{5,4},{6,7},{7,6},{8,9},{9,8},{10,11... | collective-permute-start | bytes 1966088 | tf_op jit(solution)/shard_map/ppermute | solution.py:324
  29.4 25.7 %copy-start = (f32[512,128]{1,0:T(8,128)S(1)}, f32[512,128]{1,0:T(8,128)}, u32[]{:S(2)}) copy-start(f32[512,128]{1,0:T(8,128)} %template_ref.3) | copy-start | bytes 786436
  29.4 7.9 %collective-permute-start.9 = (f32[2,256,128]{2,1,0:T(8,128)S(1)}, f32[2,256,128]{2,1,0:T(8,128)S(1)}, u32[]{:S(2)}, u32[]{:S(2)}) collective-permute-start(f32[2,256,128]{2,1,0:T(8,128)S(1)} %bitcast.20), channel_id=1, source_target_pairs={{1,2},{2,1},{3,4},{4,3},{5,6},{6,5},{9,10},{10,9},{11,12},{12,11},... | collective-permute-start | bytes 786440 | tf_op jit(solution)/shard_map/ppermute | solution.py:329
  30.2 7.1 %collective-permute-start.8 = (f32[2,256,128]{2,1,0:T(8,128)S(1)}, f32[2,256,128]{2,1,0:T(8,128)S(1)}, u32[]{:S(2)}, u32[]{:S(2)}) collective-permute-start(f32[2,256,128]{2,1,0:T(8,128)S(1)} %bitcast.21), channel_id=1, source_target_pairs={{0,1},{1,0},{2,3},{3,2},{4,5},{5,4},{6,7},{7,6},{8,9},{9,8},{10,11... | collective-permute-start | bytes 786440 | tf_op jit(solution)/shard_map/ppermute | solution.py:324
  33.1 14.6 %all-to-all-start.1 = ((f32[32,16,128]{2,1,0:T(8,128)}), f32[32,16,128]{2,1,0:T(8,128)S(1)}, u32[]{:S(2)}, u32[]{:S(2)}) async-start(f32[32,16,128]{2,1,0:T(8,128)} %bitcast.13), calls=%async_computation.1 | async-start | bytes 524288 | tf_op jit(solution)/shard_map/all_to_all | solution.py:582
  40.7 0.7 %copy-start.1 = (f32[2,272,128]{2,1,0:T(8,128)}, f32[2,272,128]{2,1,0:T(8,128)S(1)}, u32[]{:S(2)}) copy-start(f32[2,272,128]{2,1,0:T(8,128)S(1)} %get-tuple-element.41.coefs_ref) | copy-start | bytes 835588
  41.5 10.8 %collective-permute-start.10 = (f32[3,1,256,128]{3,2,1,0:T(8,128)}, f32[3,1,256,128]{3,2,1,0:T(8,128)S(1)}, u32[]{:S(2)}, u32[]{:S(2)}) collective-permute-start(f32[3,1,256,128]{3,2,1,0:T(8,128)} %get-tuple-element.42), channel_id=1, source_target_pairs={{0,1},{1,0},{2,3},{3,2},{4,5},{5,4},{6,7},{7,6},{8,9},{9,8},{10,11... | collective-permute-start | bytes 1179656 | tf_op jit(solution)/shard_map/ppermute | solution.py:324
  41.7 10.6 %collective-permute-start.11 = (f32[3,1,256,128]{3,2,1,0:T(8,128)}, f32[3,1,256,128]{3,2,1,0:T(8,128)S(1)}, u32[]{:S(2)}, u32[]{:S(2)}) collective-permute-start(f32[3,1,256,128]{3,2,1,0:T(8,128)} %get-tuple-element.43), channel_id=1, source_target_pairs={{1,2},{2,1},{3,4},{4,3},{5,6},{6,5},{9,10},{10,9},{11,12},{12,11},... | collective-permute-start | bytes 1179656 | tf_op jit(solution)/shard_map/ppermute | solution.py:329
  48.7 6.2 %collective-permute-start.7 = (f32[128,128]{1,0:T(8,128)S(1)}, f32[128,128]{1,0:T(8,128)S(1)}, u32[]{:S(2)}, u32[]{:S(2)}) collective-permute-start(f32[128,128]{1,0:T(8,128)S(1)} %shard_map.98.refs_0_), channel_id=1, source_target_pairs={{0,24},{8,16},{16,8},{24,0},{1,25},{9,17},{17,9},{25,1},{2,26},{10... | collective-permute-start | bytes 196616 | tf_op jit(solution)/shard_map/ppermute | solution.py:319
  49.5 5.6 %collective-permute-start.6 = (f32[128,128]{1,0:T(8,128)S(1)}, f32[128,128]{1,0:T(8,128)S(1)}, u32[]{:S(2)}, u32[]{:S(2)}) collective-permute-start(f32[128,128]{1,0:T(8,128)S(1)} %shard_map.98.refs_0_), channel_id=1, source_target_pairs={{0,16},{8,24},{16,0},{24,8},{1,17},{9,25},{17,1},{25,9},{2,18},{10... | collective-permute-start | bytes 196616 | tf_op jit(solution)/shard_map/ppermute | solution.py:319
  50.7 4.4 %collective-permute-start.5 = (f32[128,128]{1,0:T(8,128)S(1)}, f32[128,128]{1,0:T(8,128)S(1)}, u32[]{:S(2)}, u32[]{:S(2)}) collective-permute-start(f32[128,128]{1,0:T(8,128)S(1)} %shard_map.98.refs_0_), channel_id=1, source_target_pairs={{0,8},{8,0},{16,24},{24,16},{1,9},{9,1},{17,25},{25,17},{2,10},{10... | collective-permute-start | bytes 196616 | tf_op jit(solution)/shard_map/ppermute | solution.py:319
  52.3 1.0 %copy-start.2 = (f32[2,272,128]{2,1,0:T(8,128)S(1)}, f32[2,272,128]{2,1,0:T(8,128)}, u32[]{:S(2)}) copy-start(f32[2,272,128]{2,1,0:T(8,128)} %copy-done.1) | copy-start | bytes 835588

commit v6 on v5

--- a/solution.py
+++ b/solution.py
@@ -214,9 +214,9 @@
             [one_hot(wide == lane + t * LANES) for t in range(slots // LANES)], axis=1
         )
         picked[b] = joined(dot(pick, pair))
-    first.wait()
+    for copy in [first] + moves:
+        copy.wait()
     for i in range(chunks):
-        moves[i].wait()
         at = slice(i * some, (i + 1) * some)
         sums = [jnp.zeros((some, width), jnp.float32) for _ in OFFSETS]
         for b in range(each):
@@ -347,7 +347,7 @@
     return jnp.where(odd, near, far), jnp.where(odd, far, near)
 
 
-def step_weights(coefs, p, below, above):
+def step_weights(coefs, p):
     center = plane_of(coefs, p)
     lane = lax.broadcasted_iota(jnp.int32, center.shape, 1)
     scale = 0.5 * diffusion_dt
@@ -356,7 +356,12 @@
     left = center + jnp.where(lane == 0, 0.0, turned(center, 1))
     others = [
         center + near
-        for near in (plane_of(coefs, p, step=1), plane_of(coefs, p, step=-1), above, below)
+        for near in (
+            plane_of(coefs, p, step=1),
+            plane_of(coefs, p, step=-1),
+            plane_of(coefs, p + 1),
+            plane_of(coefs, p - 1),
+        )
     ]
     total = right + left
     for face in others:
@@ -368,10 +373,8 @@
     ] + [scale * face for face in others]
 
 
-def all_weights(coefs, low, high):
-    planes = coefs.shape[0]
-    column = [low] + [plane_of(coefs, p) for p in range(planes)] + [high]
-    return [step_weights(coefs, p, column[p], column[p + 2]) for p in range(planes)]
+def all_weights(coefs):
+    return [step_weights(coefs, p) for p in range(1, coefs.shape[0] - 1)]
 
 
 def stepped(fields, a, low, high, weights):
@@ -392,6 +395,30 @@
             total = total + weight * value
         later.append(total)
     return later
+
+
+def by_side(odd, pairs):
+    copies = [
+        (
+            [pltpu.make_async_copy(near, low, sems[0]), pltpu.make_async_copy(far, high, sems[1])],
+            [pltpu.make_async_copy(near, high, sems[0]), pltpu.make_async_copy(far, low, sems[1])],
+        )
+        for near, far, low, high, sems in pairs
+    ]
+
+    @pl.when(odd)
+    def _():
+        for when_odd, _ in copies:
+            for copy in when_odd:
+                copy.start()
+
+    @pl.when(jnp.logical_not(odd))
+    def _():
+        for _, when_even in copies:
+            for copy in when_even:
+                copy.start()
+
+    return [copy for when_odd, _ in copies for copy in when_odd]
 
 
 def force_kernel(
@@ -418,12 +445,41 @@
     parts, planes, rows = velocity.shape[:3]
     odd = place_ref[0] == 1
     body = slice(PAD, PAD + rows)
+    within, every = pl.ds(PAD, rows), pl.ds(0, parts)
+    low, mid, high = pl.ds(0, 1), pl.ds(1, planes), pl.ds(planes + 1, 1)
     copies = [
-        pltpu.make_async_copy(stiffness_ref, coefs_ref.at[:, pl.ds(PAD, rows)], sem.at[0]),
-        pltpu.make_async_copy(images_ref, images, sem.at[1]),
-    ] + [pltpu.make_async_copy(velocity_ref.at[a], velocity.at[a], sem.at[2 + a]) for a in range(parts)]
+        pltpu.make_async_copy(stiffness_ref, coefs_ref.at[mid, within], sem.at[0]),
+        pltpu.make_async_copy(images_ref, images.at[mid], sem.at[1]),
+        pltpu.make_async_copy(velocity_ref, velocity, sem.at[2]),
+    ]
     for copy in copies:
         copy.start()
+    copies += by_side(
+        odd,
+        [
+            (
+                edge_near_ref.at[parts],
+                edge_far_ref.at[parts],
+                coefs_ref.at[low, within],
+                coefs_ref.at[high, within],
+                (sem.at[3], sem.at[4]),
+            ),
+            (
+                edge_near_ref.at[parts + 1],
+                edge_far_ref.at[parts + 1],
+                images.at[low],
+                images.at[high],
+                (sem.at[5], sem.at[6]),
+            ),
+            (
+                edge_near_ref.at[every],
+                edge_far_ref.at[every],
+                outer.at[:, low],
+                outer.at[:, pl.ds(1, 1)],
+                (sem.at[7], sem.at[8]),
+            ),
+        ],
+    )
     for ref in (field_ref, fields, coefs_ref, warped):
         clear_pads(ref)
     lowest = jnp.where(odd, warped_near_ref[0], warped_far_ref[0])
@@ -433,7 +489,6 @@
     for p in range(planes):
         warped[p + 1, body, :] = warped_ref[p]
     column = [lowest] + [plane_of(warped, p) for p in range(planes + 2)] + [highest]
-    image_low, image_high = sides(odd, edge_near_ref[parts + 1, 0], edge_far_ref[parts + 1, 0])
     lane = lax.broadcasted_iota(jnp.int32, (rows, LANES), 1)
     right = jnp.where(lane == LANES - 1, 0.0, 0.5 * force_step)
     left = jnp.where(lane == 0, 0.0, 0.5 * force_step)
@@ -448,22 +503,22 @@
             half * (column[p + 2] - column[p]),
         ]
 
-    for side, p, image in ((0, 0, image_low), (1, planes + 1, image_high)):
-        force = forces(p, image)
+    for copy in (copies[0], copies[3], copies[4]):
+        copy.wait()
+    weights = all_weights(coefs_ref)
+    for copy in copies[1:3] + copies[5:]:
+        copy.wait()
+    for p in range(planes + 2):
+        force = forces(p, images[p])
         for a in range(parts):
-            outer[side, a] = sides(odd, edge_near_ref[a, 0], edge_far_ref[a, 0])[side] - force[a]
-    copies[0].wait()
-    weights = all_weights(
-        coefs_ref, *sides(odd, edge_near_ref[parts, 0], edge_far_ref[parts, 0])
-    )
-    for copy in copies[1:]:
-        copy.wait()
-    for p in range(planes):
-        force = forces(p + 1, images[p])
-        for a in range(parts):
-            fields[a, p, body, :] = velocity[a, p] - force[a]
+            if p == 0:
+                outer[a, 0] = outer[a, 0] - force[a]
+            elif p == planes + 1:
+                outer[a, 1] = outer[a, 1] - force[a]
+            else:
+                fields[a, p - 1, body, :] = velocity[a, p - 1] - force[a]
     for a in range(parts):
-        later = stepped(fields, a, outer[0, a], outer[1, a], weights)
+        later = stepped(fields, a, outer[a, 0], outer[a, 1], weights)
         for p in range(planes):
             field_ref[a, p, body, :] = later[p]
         near_ref[a, 0], far_ref[a, 0] = sides(odd, later[0], later[-1])
@@ -473,8 +528,6 @@
     place_ref,
     field_ref,
     coefs_ref,
-    edge_near_ref,
-    edge_far_ref,
     near_ref,
     far_ref,
     out_ref,
@@ -483,9 +536,7 @@
 ):
     parts, planes = done.shape[:2]
     odd = place_ref[0] == 1
-    weights = all_weights(
-        coefs_ref, *sides(odd, edge_near_ref[parts, 0], edge_far_ref[parts, 0])
-    )
+    weights = all_weights(coefs_ref)
     writes = [pltpu.make_async_copy(done.at[a], out_ref.at[a], sem.at[a]) for a in range(parts)]
     for a in range(parts):
         later = stepped(field_ref, a, *sides(odd, near_ref[a, 0], far_ref[a, 0]), weights)
@@ -589,7 +640,7 @@
         force_kernel,
         (
             shape((parts, planes, high, width), f32),
-            shape((planes, high, width), f32),
+            shape((planes + 2, high, width), f32),
             shape((parts, 1, YR, width), f32),
             shape((parts, 1, YR, width), f32),
         ),
@@ -603,14 +654,14 @@
         warped_near,
         warped_far,
         smem=(0,),
-        far=(1, 2, 3),
+        far=(1, 2, 3, 5, 6),
         scratch=(
             pltpu.VMEM((parts,) + grid, f32),
-            pltpu.VMEM(grid, f32),
+            pltpu.VMEM((planes + 2, YR, width), f32),
             pltpu.VMEM((planes + 2, high, width), f32),
             pltpu.VMEM((parts, planes, high, width), f32),
-            pltpu.VMEM((2, parts, YR, width), f32),
-            dma((2 + parts,)),
+            pltpu.VMEM((parts, 2, YR, width), f32),
+            dma((9,)),
         ),
     )
     field_far, field_near = swap_far(field_far), swap_near(field_near)
@@ -638,8 +689,6 @@
         place,
         field,
         coefs,
-        edge_near,
-        edge_far,
         field_near,
         field_far,
         smem=(0,),

time: 56.6 us -> 55.8 us (0.986)
  waiting for transfers between devices: 6.94 us -> 9.05 us
  local copies, waits for them, and re-layouts: 1.68 us -> 0.02 us
  Pallas kernels: 21.8 us -> 20.6 us
    unnamed x10, local copies, waits for them, and re-layouts: 1.68 us -> 0.02 us
    pallas_call x7, Pallas kernels: 21.8 us -> 20.6 us  [call(): pl.pallas_call(kernel, out_shape=tuple(shapes) if many else shapes[0], in...]
    all_to_all x1, waiting for transfers between devices: 5.34 us -> 6.46 us  [per_device(): lax.all_to_all(sent, ('subj', 'slab'), split_axis=0, concat_axis=0, tiled...]
    ppermute x6, waiting for transfers between devices: 0.17 us -> 1.16 us  [over_subjects(): lax.ppermute(values, 'subj', [(i, i ^ d) for i in range(count)])]
  transfers between devices with their start and end apart: 14 -> 14, of which waited for: 3 -> 4; matrix products, arithmetic and copies ran while one was open for 0% -> 0% of each run, Pallas kernels for 33% -> 31%
where the time goes in v6:
time: 55.8 us; the launch traced here: 55.4 us
  starting transfers between devices  24.9 us (45%)
  Pallas kernels  20.6 us (37%)
  waiting for transfers between devices  9.05 us (16%)
  between operations  0.81 us (1%)
    pallas_call x7, Pallas kernels, call(): pl.pallas_call(kernel, out_shape=tuple(shapes) if many else shapes[0], in...  20.6 us
    ppermute x6, starting transfers between devices, over_subjects(): lax.ppermute(values, 'subj', [(i, i ^ d) for i in range(count)])  7.07 us
    all_to_all x1, waiting for transfers between devices, per_device(): lax.all_to_all(sent, ('subj', 'slab'), split_axis=0, concat_axis=0, tiled...  6.46 us
    all_to_all x1, starting transfers between devices, per_device(): lax.all_to_all(sending, 'slab', split_axis=0, concat_axis=0, tiled=True)  6.34 us
    ppermute x3, starting transfers between devices, swap_near(): lax.ppermute(values, 'slab', [(i, i ^ 1) for i in range(lax.axis_size('sl...  5.21 us
    all_to_all x1, starting transfers between devices, per_device(): lax.all_to_all(sent, ('subj', 'slab'), split_axis=0, concat_axis=0, tiled...  4.25 us
    ppermute x3, starting transfers between devices, swap_far(): lax.ppermute(values, 'slab', [(i, i + 1 if i % 2 else i - 1) for i in ran...  2.04 us
    all_to_all x1, waiting for transfers between devices, per_device(): lax.all_to_all(sending, 'slab', split_axis=0, concat_axis=0, tiled=True)  1.41 us
  transfers between devices with their start and end apart: 14, of which 4 were waited for; matrix products, arithmetic and copies ran while one was open for 0% of the time, Pallas kernels for 31%

profile of v6, /device:TPU:0, one launch (start us, length us, event | category | flops | bytes accessed | tf_op | source)
XLA Modules:
  0.0 55.4 jit_solution(18386247312118743635)
XLA Ops:
  0.6 2.2 %shard_map.95 = f32[512,128]{1,0:T(8,128)} custom-call(s32[8,64]{1,0:T(8,128)} %bitcast.24, f32[512,128]{1,0:T(8,128)} %template_ref.3), custom_call_target="tpu_custom_call" | custom-call | tf_op jit(solution)/shard_map/pallas_call | solution.py:31
  2.8 6.3 %all-to-all-start = ((f32[8,64,128]{2,1,0:T(8,128)}), f32[8,64,128]{2,1,0:T(8,128)S(1)}, u32[]{:S(2)}, u32[]{:S(2)}) async-start(f32[8,64,128]{2,1,0:T(8,128)} %bitcast.4), calls=%async_computation | async-start | bytes 524288 | tf_op jit(solution)/shard_map/all_to_all | solution.py:582
  9.2 2.4 %collective-permute-start.2 = (s32[8,64]{1,0:T(8,128)}, s32[8,64]{1,0:T(8,128)S(1)}, u32[]{:S(2)}, u32[]{:S(2)}) collective-permute-start(s32[8,64]{1,0:T(8,128)} %bitcast.25), channel_id=1, source_target_pairs={{0,24},{8,16},{16,8},{24,0},{1,25},{9,17},{17,9},{25,1},{2,26},{10... | collective-permute-start | bytes 6152 | tf_op jit(solution)/shard_map/ppermute | solution.py:319
  11.6 0.5 collective-permute-start.1
  12.1 0.5 collective-permute-start
  12.6 4.8 %shard_map.96 = (bf16[4,8,5,128,128]{4,3,2,1,0:T(8,128)(2,1)}, f32[5,1,256,128]{3,2,1,0:T(8,128)}, f32[5,1,256,128]{3,2,1,0:T(8,128)}) custom-call(s32[1]{0:T(128)} %bitcast.6.place_ref, s32[4096,128]{1,0:T(8,128)} %bitcast.34, bf16[4096,128]{1,0:T(8,128)(2,1)} %bitcast.35, f32[3,2,256,128]{3,2,1,0:T(8,128)} %bitcast.29, f32[2,256,128]{2,1,0:T(8,128)} %bitcast.36, ...), custom_call_target="tpu_custom_call" | custom-call | tf_op jit(solution)/shard_map/pallas_call | solution.py:31
  17.5 1.4 %all-to-all-done = f32[8,64,128]{2,1,0:T(8,128)S(1)} async-done(((f32[8,64,128]{2,1,0:T(8,128)}), f32[8,64,128]{2,1,0:T(8,128)S(1)}, u32[]{:S(2)}, u32[]{:S(2)}) %all-to-all-start) | async-done | bytes 262176 | tf_op jit(solution)/shard_map/all_to_all | solution.py:582
  18.9 0.7 %collective-permute-start.3 = (f32[5,1,256,128]{3,2,1,0:T(8,128)}, f32[5,1,256,128]{3,2,1,0:T(8,128)S(1)}, u32[]{:S(2)}, u32[]{:S(2)}) collective-permute-start(f32[5,1,256,128]{3,2,1,0:T(8,128)} %get-tuple-element.30), channel_id=1, source_target_pairs={{1,2},{2,1},{3,4},{4,3},{5,6},{6,5},{9,10},{10,9},{11,12},{12,11},... | collective-permute-start | bytes 1966088 | tf_op jit(solution)/shard_map/ppermute | solution.py:329
  19.6 2.0 %collective-permute-start.4 = (f32[5,1,256,128]{3,2,1,0:T(8,128)}, f32[5,1,256,128]{3,2,1,0:T(8,128)S(1)}, u32[]{:S(2)}, u32[]{:S(2)}) collective-permute-start(f32[5,1,256,128]{3,2,1,0:T(8,128)} %get-tuple-element.31), channel_id=1, source_target_pairs={{0,1},{1,0},{2,3},{3,2},{4,5},{5,4},{6,7},{7,6},{8,9},{9,8},{10,11... | collective-permute-start | bytes 1966088 | tf_op jit(solution)/shard_map/ppermute | solution.py:324
  21.6 7.2 %shard_map.97 = (f32[512,128]{1,0:T(8,128)S(1)}, f32[512,128]{1,0:T(8,128)}) custom-call(s32[8,512]{1,0:T(8,128)S(1)} %bitcast.23, f32[512,128]{1,0:T(8,128)S(1)} %bitcast.18, bf16[4,8,5,128,128]{4,3,2,1,0:T(8,128)(2,1)} %get-tuple-element.28.moved_ref, f32[512,128]{1,0:T(8,128)} %bitcast.32), custom_call_target="tpu_custom_call" | custom-call | tf_op jit(solution)/shard_map/pallas_call | solution.py:31
  28.8 0.7 %collective-permute-start.9 = (f32[2,256,128]{2,1,0:T(8,128)S(1)}, f32[2,256,128]{2,1,0:T(8,128)S(1)}, u32[]{:S(2)}, u32[]{:S(2)}) collective-permute-start(f32[2,256,128]{2,1,0:T(8,128)S(1)} %bitcast.20), channel_id=1, source_target_pairs={{1,2},{2,1},{3,4},{4,3},{5,6},{6,5},{9,10},{10,9},{11,12},{12,11},... | collective-permute-start | bytes 786440 | tf_op jit(solution)/shard_map/ppermute | solution.py:329
  29.5 2.9 %collective-permute-start.8 = (f32[2,256,128]{2,1,0:T(8,128)S(1)}, f32[2,256,128]{2,1,0:T(8,128)S(1)}, u32[]{:S(2)}, u32[]{:S(2)}) collective-permute-start(f32[2,256,128]{2,1,0:T(8,128)S(1)} %bitcast.21), channel_id=1, source_target_pairs={{0,1},{1,0},{2,3},{3,2},{4,5},{5,4},{6,7},{7,6},{8,9},{9,8},{10,11... | collective-permute-start | bytes 786440 | tf_op jit(solution)/shard_map/ppermute | solution.py:324
  32.4 4.3 %all-to-all-start.1 = ((f32[32,16,128]{2,1,0:T(8,128)}), f32[32,16,128]{2,1,0:T(8,128)S(1)}, u32[]{:S(2)}, u32[]{:S(2)}) async-start(f32[32,16,128]{2,1,0:T(8,128)} %bitcast.13), calls=%async_computation.1 | async-start | bytes 524288 | tf_op jit(solution)/shard_map/all_to_all | solution.py:633
  36.7 2.9 %shard_map.100 = (f32[3,2,272,128]{3,2,1,0:T(8,128)S(1)}, f32[4,272,128]{2,1,0:T(8,128)S(1)}, f32[3,1,256,128]{3,2,1,0:T(8,128)S(1)}, f32[3,1,256,128]{3,2,1,0:T(8,128)S(1)}) custom-call(s32[1]{0:T(128)} %bitcast.6.place_ref, f32[3,2,256,128]{3,2,1,0:T(8,128)} %bitcast.30, f32[2,256,128]{2,1,0:T(8,128)} %bitcast.33, f32[2,256,128]{2,1,0:T(8,128)} %bitcast.37, ...), custom_call_target="tpu_custom_call" | custom-call | tf_op jit(solution)/shard_map/pallas_call | solution.py:31
  39.9 0.7 %collective-permute-start.11 = (f32[3,1,256,128]{3,2,1,0:T(8,128)S(1)}, f32[3,1,256,128]{3,2,1,0:T(8,128)S(1)}, u32[]{:S(2)}, u32[]{:S(2)}) collective-permute-start(f32[3,1,256,128]{3,2,1,0:T(8,128)S(1)} %get-tuple-element.43), channel_id=1, source_target_pairs={{1,2},{2,1},{3,4},{4,3},{5,6},{6,5},{9,10},{10,9},{11,12},{12,11},... | collective-permute-start | bytes 1179656 | tf_op jit(solution)/shard_map/ppermute | solution.py:329
  40.5 6.5 %all-to-all-done.1 = f32[32,16,128]{2,1,0:T(8,128)S(1)} async-done(((f32[32,16,128]{2,1,0:T(8,128)}), f32[32,16,128]{2,1,0:T(8,128)S(1)}, u32[]{:S(2)}, u32[]{:S(2)}) %all-to-all-start.1) | async-done | bytes 262176 | tf_op jit(solution)/shard_map/all_to_all | solution.py:633
  47.0 0.9 %shard_map.98.refs_0_ = f32[128,128]{1,0:T(8,128)S(1)} custom-call(s32[1]{0:T(128)} %bitcast.me_ref, f32[512,128]{1,0:T(8,128)S(1)} %bitcast.19, s32[8,64]{1,0:T(8,128)S(1)} %bitcast.28, s32[8,64]{1,0:T(8,128)S(1)} %collective-permute-done.refs_1_, s32[8,64]{1,0:T(8,128)S(1)} %collective-permute-done.1.refs_2_, s32[8,64]{1,0:T(8,128)S(1)} %collective-permute-done.2.refs_3_), custom_call_target="tpu_custom_call" | custom-call | tf_op jit(solution)/shard_map/pallas_call | solution.py:31
  48.0 0.8 %collective-permute-start.7 = (f32[128,128]{1,0:T(8,128)S(1)}, f32[128,128]{1,0:T(8,128)S(1)}, u32[]{:S(2)}, u32[]{:S(2)}) collective-permute-start(f32[128,128]{1,0:T(8,128)S(1)} %shard_map.98.refs_0_), channel_id=1, source_target_pairs={{0,24},{8,16},{16,8},{24,0},{1,25},{9,17},{17,9},{25,1},{2,26},{10... | collective-permute-start | bytes 196616 | tf_op jit(solution)/shard_map/ppermute | solution.py:319
  48.8 1.2 %collective-permute-start.6 = (f32[128,128]{1,0:T(8,128)S(1)}, f32[128,128]{1,0:T(8,128)S(1)}, u32[]{:S(2)}, u32[]{:S(2)}) collective-permute-start(f32[128,128]{1,0:T(8,128)S(1)} %shard_map.98.refs_0_), channel_id=1, source_target_pairs={{0,16},{8,24},{16,0},{24,8},{1,17},{9,25},{17,1},{25,9},{2,18},{10... | collective-permute-start | bytes 196616 | tf_op jit(solution)/shard_map/ppermute | solution.py:319
  50.0 1.6 %collective-permute-start.5 = (f32[128,128]{1,0:T(8,128)S(1)}, f32[128,128]{1,0:T(8,128)S(1)}, u32[]{:S(2)}, u32[]{:S(2)}) collective-permute-start(f32[128,128]{1,0:T(8,128)S(1)} %shard_map.98.refs_0_), channel_id=1, source_target_pairs={{0,8},{8,0},{16,24},{24,16},{1,9},{9,1},{17,25},{25,17},{2,10},{10... | collective-permute-start | bytes 196616 | tf_op jit(solution)/shard_map/ppermute | solution.py:319
  51.6 1.6 %shard_map.101 = f32[3,2,256,128]{3,2,1,0:T(8,128)} custom-call(s32[1]{0:T(128)} %bitcast.6.place_ref, f32[3,2,272,128]{3,2,1,0:T(8,128)S(1)} %get-tuple-element.40.field_ref, f32[4,272,128]{2,1,0:T(8,128)S(1)} %get-tuple-element.41.coefs_ref, f32[3,1,256,128]{3,2,1,0:T(8,128)S(1)} %collective-permute-done.10.near_ref, ...), custom_call_target="tpu_custom_call" | custom-call | tf_op jit(solution)/shard_map/pallas_call | solution.py:31
  53.2 0.7 %collective-permute-done.7.refs_3_ = f32[128,128]{1,0:T(8,128)S(1)} collective-permute-done((f32[128,128]{1,0:T(8,128)S(1)}, f32[128,128]{1,0:T(8,128)S(1)}, u32[]{:S(2)}, u32[]{:S(2)}) %collective-permute-start.7) | collective-permute-done | bytes 65568 | tf_op jit(solution)/shard_map/ppermute | solution.py:319
  53.9 0.5 collective-permute-done.6.refs_2_
  54.4 1.0 %shard_map.99 = f32[512,128]{1,0:T(8,128)} custom-call(s32[1]{0:T(128)} %bitcast.me_ref, f32[512,128]{1,0:T(8,128)S(1)} %copy-done, f32[128,128]{1,0:T(8,128)S(1)} %shard_map.98.refs_0_, f32[128,128]{1,0:T(8,128)S(1)} %collective-permute-done.5.refs_1_, f32[128,128]{1,0:T(8,128)S(1)} %collective-permute-done.6.refs_2_, ...), custom_call_target="tpu_custom_call" | custom-call | tf_op jit(solution)/shard_map/pallas_call | solution.py:31
  (21 shorter events, 0.4 us)
Async XLA Ops:
  0.6 21.0 %copy-start.1 = (s32[1,512,8]{1,2,0:T(8,128)S(1)}, s32[1,512,8]{1,2,0:T(8,128)}, u32[]{:S(2)}) copy-start(s32[1,512,8]{1,2,0:T(8,128)} %param.13) | copy-start | bytes 49156
  2.8 16.1 %all-to-all-start = ((f32[8,64,128]{2,1,0:T(8,128)}), f32[8,64,128]{2,1,0:T(8,128)S(1)}, u32[]{:S(2)}, u32[]{:S(2)}) async-start(f32[8,64,128]{2,1,0:T(8,128)} %bitcast.4), calls=%async_computation | async-start | bytes 524288 | tf_op jit(solution)/shard_map/all_to_all | solution.py:582
  9.2 8.3 %collective-permute-start.2 = (s32[8,64]{1,0:T(8,128)}, s32[8,64]{1,0:T(8,128)S(1)}, u32[]{:S(2)}, u32[]{:S(2)}) collective-permute-start(s32[8,64]{1,0:T(8,128)} %bitcast.25), channel_id=1, source_target_pairs={{0,24},{8,16},{16,8},{24,0},{1,25},{9,17},{17,9},{25,1},{2,26},{10... | collective-permute-start | bytes 6152 | tf_op jit(solution)/shard_map/ppermute | solution.py:319
  11.6 5.9 %collective-permute-start.1 = (s32[8,64]{1,0:T(8,128)}, s32[8,64]{1,0:T(8,128)S(1)}, u32[]{:S(2)}, u32[]{:S(2)}) collective-permute-start(s32[8,64]{1,0:T(8,128)} %bitcast.26), channel_id=1, source_target_pairs={{0,16},{8,24},{16,0},{24,8},{1,17},{9,25},{17,1},{25,9},{2,18},{10... | collective-permute-start | bytes 6152 | tf_op jit(solution)/shard_map/ppermute | solution.py:319
  12.1 5.4 %collective-permute-start = (s32[8,64]{1,0:T(8,128)}, s32[8,64]{1,0:T(8,128)S(1)}, u32[]{:S(2)}, u32[]{:S(2)}) collective-permute-start(s32[8,64]{1,0:T(8,128)} %bitcast.27), channel_id=1, source_target_pairs={{0,8},{8,0},{16,24},{24,16},{1,9},{9,1},{17,25},{25,17},{2,10},{10... | collective-permute-start | bytes 6152 | tf_op jit(solution)/shard_map/ppermute | solution.py:319
  17.4 29.6 %copy-start.2 = (s32[1,1,8,64]{3,2,1,0:T(8,128)S(1)}, s32[1,1,8,64]{3,2,1,0:T(8,128)}, u32[]{:S(2)}) copy-start(s32[1,1,8,64]{3,2,1,0:T(8,128)} %param.12) | copy-start | bytes 6148
  18.9 13.4 %collective-permute-start.3 = (f32[5,1,256,128]{3,2,1,0:T(8,128)}, f32[5,1,256,128]{3,2,1,0:T(8,128)S(1)}, u32[]{:S(2)}, u32[]{:S(2)}) collective-permute-start(f32[5,1,256,128]{3,2,1,0:T(8,128)} %get-tuple-element.30), channel_id=1, source_target_pairs={{1,2},{2,1},{3,4},{4,3},{5,6},{6,5},{9,10},{10,9},{11,12},{12,11},... | collective-permute-start | bytes 1966088 | tf_op jit(solution)/shard_map/ppermute | solution.py:329
  19.6 12.8 %collective-permute-start.4 = (f32[5,1,256,128]{3,2,1,0:T(8,128)}, f32[5,1,256,128]{3,2,1,0:T(8,128)S(1)}, u32[]{:S(2)}, u32[]{:S(2)}) collective-permute-start(f32[5,1,256,128]{3,2,1,0:T(8,128)} %get-tuple-element.31), channel_id=1, source_target_pairs={{0,1},{1,0},{2,3},{3,2},{4,5},{5,4},{6,7},{7,6},{8,9},{9,8},{10,11... | collective-permute-start | bytes 1966088 | tf_op jit(solution)/shard_map/ppermute | solution.py:324
  21.6 32.8 %copy-start = (f32[512,128]{1,0:T(8,128)S(1)}, f32[512,128]{1,0:T(8,128)}, u32[]{:S(2)}) copy-start(f32[512,128]{1,0:T(8,128)} %template_ref.3) | copy-start | bytes 786436
  28.8 7.8 %collective-permute-start.9 = (f32[2,256,128]{2,1,0:T(8,128)S(1)}, f32[2,256,128]{2,1,0:T(8,128)S(1)}, u32[]{:S(2)}, u32[]{:S(2)}) collective-permute-start(f32[2,256,128]{2,1,0:T(8,128)S(1)} %bitcast.20), channel_id=1, source_target_pairs={{1,2},{2,1},{3,4},{4,3},{5,6},{6,5},{9,10},{10,9},{11,12},{12,11},... | collective-permute-start | bytes 786440 | tf_op jit(solution)/shard_map/ppermute | solution.py:329
  29.5 7.2 %collective-permute-start.8 = (f32[2,256,128]{2,1,0:T(8,128)S(1)}, f32[2,256,128]{2,1,0:T(8,128)S(1)}, u32[]{:S(2)}, u32[]{:S(2)}) collective-permute-start(f32[2,256,128]{2,1,0:T(8,128)S(1)} %bitcast.21), channel_id=1, source_target_pairs={{0,1},{1,0},{2,3},{3,2},{4,5},{5,4},{6,7},{7,6},{8,9},{9,8},{10,11... | collective-permute-start | bytes 786440 | tf_op jit(solution)/shard_map/ppermute | solution.py:324
  32.4 4.3 %copy-start.3 = (f32[5,1,256,128]{3,2,1,0:T(8,128)}, f32[5,1,256,128]{3,2,1,0:T(8,128)S(1)}, u32[]{:S(2)}) copy-start(f32[5,1,256,128]{3,2,1,0:T(8,128)S(1)} %collective-permute-done.3.edge_far_ref) | copy-start | bytes 1966084
  32.4 4.3 %copy-start.4 = (f32[5,1,256,128]{3,2,1,0:T(8,128)}, f32[5,1,256,128]{3,2,1,0:T(8,128)S(1)}, u32[]{:S(2)}) copy-start(f32[5,1,256,128]{3,2,1,0:T(8,128)S(1)} %collective-permute-done.4.edge_near_ref) | copy-start | bytes 1966084
  32.4 14.6 %all-to-all-start.1 = ((f32[32,16,128]{2,1,0:T(8,128)}), f32[32,16,128]{2,1,0:T(8,128)S(1)}, u32[]{:S(2)}, u32[]{:S(2)}) async-start(f32[32,16,128]{2,1,0:T(8,128)} %bitcast.13), calls=%async_computation.1 | async-start | bytes 524288 | tf_op jit(solution)/shard_map/all_to_all | solution.py:633
  39.5 12.0 %collective-permute-start.10 = (f32[3,1,256,128]{3,2,1,0:T(8,128)S(1)}, f32[3,1,256,128]{3,2,1,0:T(8,128)S(1)}, u32[]{:S(2)}, u32[]{:S(2)}) collective-permute-start(f32[3,1,256,128]{3,2,1,0:T(8,128)S(1)} %get-tuple-element.42), channel_id=1, source_target_pairs={{0,1},{1,0},{2,3},{3,2},{4,5},{5,4},{6,7},{7,6},{8,9},{9,8},{10,11... | collective-permute-start | bytes 1179656 | tf_op jit(solution)/shard_map/ppermute | solution.py:324
  39.9 11.7 %collective-permute-start.11 = (f32[3,1,256,128]{3,2,1,0:T(8,128)S(1)}, f32[3,1,256,128]{3,2,1,0:T(8,128)S(1)}, u32[]{:S(2)}, u32[]{:S(2)}) collective-permute-start(f32[3,1,256,128]{3,2,1,0:T(8,128)S(1)} %get-tuple-element.43), channel_id=1, source_target_pairs={{1,2},{2,1},{3,4},{4,3},{5,6},{6,5},{9,10},{10,9},{11,12},{12,11},... | collective-permute-start | bytes 1179656 | tf_op jit(solution)/shard_map/ppermute | solution.py:329
  48.0 5.9 %collective-permute-start.7 = (f32[128,128]{1,0:T(8,128)S(1)}, f32[128,128]{1,0:T(8,128)S(1)}, u32[]{:S(2)}, u32[]{:S(2)}) collective-permute-start(f32[128,128]{1,0:T(8,128)S(1)} %shard_map.98.refs_0_), channel_id=1, source_target_pairs={{0,24},{8,16},{16,8},{24,0},{1,25},{9,17},{17,9},{25,1},{2,26},{10... | collective-permute-start | bytes 196616 | tf_op jit(solution)/shard_map/ppermute | solution.py:319
  48.8 5.6 %collective-permute-start.6 = (f32[128,128]{1,0:T(8,128)S(1)}, f32[128,128]{1,0:T(8,128)S(1)}, u32[]{:S(2)}, u32[]{:S(2)}) collective-permute-start(f32[128,128]{1,0:T(8,128)S(1)} %shard_map.98.refs_0_), channel_id=1, source_target_pairs={{0,16},{8,24},{16,0},{24,8},{1,17},{9,25},{17,1},{25,9},{2,18},{10... | collective-permute-start | bytes 196616 | tf_op jit(solution)/shard_map/ppermute | solution.py:319
  50.0 4.4 %collective-permute-start.5 = (f32[128,128]{1,0:T(8,128)S(1)}, f32[128,128]{1,0:T(8,128)S(1)}, u32[]{:S(2)}, u32[]{:S(2)}) collective-permute-start(f32[128,128]{1,0:T(8,128)S(1)} %shard_map.98.refs_0_), channel_id=1, source_target_pairs={{0,8},{8,0},{16,24},{24,16},{1,9},{9,1},{17,25},{25,17},{2,10},{10... | collective-permute-start | bytes 196616 | tf_op jit(solution)/shard_map/ppermute | solution.py:319

commit v7 on v6

--- a/solution.py
+++ b/solution.py
@@ -482,25 +482,24 @@
     )
     for ref in (field_ref, fields, coefs_ref, warped):
         clear_pads(ref)
-    lowest = jnp.where(odd, warped_near_ref[0], warped_far_ref[0])
-    highest = jnp.where(odd, warped_far_ref[1], warped_near_ref[1])
-    warped[0, body, :] = jnp.where(odd, warped_near_ref[1], warped_far_ref[1])
-    warped[planes + 1, body, :] = jnp.where(odd, warped_far_ref[0], warped_near_ref[0])
+    for p in range(2):
+        warped[p, body, :], warped[planes + 2 + p, body, :] = sides(
+            odd, warped_near_ref[p], warped_far_ref[p]
+        )
     for p in range(planes):
-        warped[p + 1, body, :] = warped_ref[p]
-    column = [lowest] + [plane_of(warped, p) for p in range(planes + 2)] + [highest]
+        warped[p + 2, body, :] = warped_ref[p]
     lane = lax.broadcasted_iota(jnp.int32, (rows, LANES), 1)
     right = jnp.where(lane == LANES - 1, 0.0, 0.5 * force_step)
     left = jnp.where(lane == 0, 0.0, 0.5 * force_step)
 
     def forces(p, image):
-        here = column[p + 1]
+        here = plane_of(warped, p + 1)
         mismatch = here - image
         half = (0.5 * force_step) * mismatch
         return [
             mismatch * (right * turned(here, -1) - left * turned(here, 1)),
-            half * (plane_of(warped, p, step=1) - plane_of(warped, p, step=-1)),
-            half * (column[p + 2] - column[p]),
+            half * (plane_of(warped, p + 1, step=1) - plane_of(warped, p + 1, step=-1)),
+            half * (plane_of(warped, p + 2) - plane_of(warped, p)),
         ]
 
     for copy in (copies[0], copies[3], copies[4]):
@@ -577,8 +576,6 @@
         far=(0, 1),
         scratch=(pltpu.VMEM((slabs, capacity), jnp.int32), pltpu.VMEM((rows, width), f32), dma((2,))),
     )
-    sending, own_rows = lax.optimization_barrier((sending, send_rows[0, 0]))
-    all_rows = over_subjects(own_rows)
     received = lax.all_to_all(sending, "slab", split_axis=0, concat_axis=0, tiled=True)
 
     chunks = 4
@@ -607,9 +604,6 @@
             dma((3,)),
         ),
     )
-    received, edge_far, edge_near, *all_rows = lax.optimization_barrier(
-        (received, edge_far, edge_near, *all_rows)
-    )
     edge_far, edge_near = swap_far(edge_far), swap_near(edge_near)
 
     warped, sent = call(
@@ -629,9 +623,10 @@
             dma((chunks,)),
         ),
     )
-    sent, edge_far, edge_near = lax.optimization_barrier((sent, edge_far, edge_near))
     returned = lax.all_to_all(sent, ("subj", "slab"), split_axis=0, concat_axis=0, tiled=True)
 
+    own_rows, warped = lax.optimization_barrier((send_rows[0, 0], warped))
+    all_rows = over_subjects(own_rows)
     warped_grid = warped.reshape(grid)
     warped_far, warped_near = swap_far(warped_grid), swap_near(warped_grid)
 
@@ -658,12 +653,13 @@
         scratch=(
             pltpu.VMEM((parts,) + grid, f32),
             pltpu.VMEM((planes + 2, YR, width), f32),
-            pltpu.VMEM((planes + 2, high, width), f32),
+            pltpu.VMEM((planes + 4, high, width), f32),
             pltpu.VMEM((parts, planes, high, width), f32),
             pltpu.VMEM((parts, 2, YR, width), f32),
             dma((9,)),
         ),
     )
+    field_far, field_near, *all_rows = lax.optimization_barrier((field_far, field_near, *all_rows))
     field_far, field_near = swap_far(field_far), swap_near(field_near)
 
     part = call(
@@ -675,14 +671,6 @@
         smem=(0,),
     )
     pieces = over_subjects(part)
-    template_out = call(
-        functools.partial(update_kernel, subjects),
-        shape((rows, width), f32),
-        me,
-        template,
-        *pieces,
-        smem=(0,),
-    )
     field = call(
         last_kernel,
         shape((parts,) + grid, f32),
@@ -694,6 +682,15 @@
         smem=(0,),
         out_far=(0,),
         scratch=(pltpu.VMEM((parts,) + grid, f32), dma((parts,))),
+    )
+    field, *pieces = lax.optimization_barrier((field, *pieces))
+    template_out = call(
+        functools.partial(update_kernel, subjects),
+        shape((rows, width), f32),
+        me,
+        template,
+        *pieces,
+        smem=(0,),
     )
     velocity_out = field.reshape(parts, rows, width)[None]
     return (template_out, velocity_out)

time: 55.8 us -> 52.9 us (0.948)
  starting transfers between devices: 24.9 us -> 22.6 us
  waiting for transfers between devices: 9.05 us -> 7.66 us
  local copies, waits for them, and re-layouts: 0.02 us -> 0.62 us
    all_to_all x1, waiting for transfers between devices: 6.46 us -> 2.5 us  [per_device(): lax.all_to_all(sent, ('subj', 'slab'), split_axis=0, concat_axis=0, tiled...]
    ppermute x3, starting transfers between devices: 5.21 us -> 2.22 us  [swap_near(): lax.ppermute(values, 'slab', [(i, i ^ 1) for i in range(lax.axis_size('sl...]
    all_to_all x1, waiting for transfers between devices: 1.41 us -> 3.66 us  [per_device(): lax.all_to_all(sending, 'slab', split_axis=0, concat_axis=0, tiled=True)]
    all_to_all x1, starting transfers between devices: 4.25 us -> 4.87 us  [per_device(): lax.all_to_all(sent, ('subj', 'slab'), split_axis=0, concat_axis=0, tiled...]
    unnamed x10, local copies, waits for them, and re-layouts: 0.02 us -> 0.62 us
  transfers between devices with their start and end apart: 14 -> 14, of which waited for: 4 -> 4; matrix products, arithmetic and copies ran while one was open for 0% -> 0% of each run, Pallas kernels for 31% -> 33%
where the time goes in v7:
time: 52.9 us; the launch traced here: 52.3 us
  starting transfers between devices  22.6 us (43%)
  Pallas kernels  20.7 us (39%)
  waiting for transfers between devices  7.66 us (14%)
  between operations  0.78 us (1%)
  local copies, waits for them, and re-layouts  0.62 us (1%)
    pallas_call x7, Pallas kernels, call(): pl.pallas_call(kernel, out_shape=tuple(shapes) if many else shapes[0], in...  20.7 us
    ppermute x6, starting transfers between devices, over_subjects(): lax.ppermute(values, 'subj', [(i, i ^ d) for i in range(count)])  7.13 us
    all_to_all x1, starting transfers between devices, per_device(): lax.all_to_all(sending, 'slab', split_axis=0, concat_axis=0, tiled=True)  6.34 us
    all_to_all x1, starting transfers between devices, per_device(): lax.all_to_all(sent, ('subj', 'slab'), split_axis=0, concat_axis=0, tiled...  4.87 us
    all_to_all x1, waiting for transfers between devices, per_device(): lax.all_to_all(sending, 'slab', split_axis=0, concat_axis=0, tiled=True)  3.66 us
    all_to_all x1, waiting for transfers between devices, per_device(): lax.all_to_all(sent, ('subj', 'slab'), split_axis=0, concat_axis=0, tiled...  2.5 us
    ppermute x3, starting transfers between devices, swap_near(): lax.ppermute(values, 'slab', [(i, i ^ 1) for i in range(lax.axis_size('sl...  2.22 us
    ppermute x3, starting transfers between devices, swap_far(): lax.ppermute(values, 'slab', [(i, i + 1 if i % 2 else i - 1) for i in ran...  2.05 us
  transfers between devices with their start and end apart: 14, of which 4 were waited for; matrix products, arithmetic and copies ran while one was open for 0% of the time, Pallas kernels for 33%

profile of v7, /device:TPU:0, one launch (start us, length us, event | category | flops | bytes accessed | tf_op | source)
XLA Modules:
  0.0 52.3 jit_solution(5067166367940599496)
XLA Ops:
  0.6 2.2 %shard_map.95 = f32[512,128]{1,0:T(8,128)} custom-call(s32[8,64]{1,0:T(8,128)} %bitcast.24, f32[512,128]{1,0:T(8,128)} %template_ref.3), custom_call_target="tpu_custom_call" | custom-call | tf_op jit(solution)/shard_map/pallas_call | solution.py:31
  2.8 6.3 %all-to-all-start = ((f32[8,64,128]{2,1,0:T(8,128)}), f32[8,64,128]{2,1,0:T(8,128)S(1)}, u32[]{:S(2)}, u32[]{:S(2)}) async-start(f32[8,64,128]{2,1,0:T(8,128)} %bitcast.8), calls=%async_computation | async-start | bytes 524288 | tf_op jit(solution)/shard_map/all_to_all | solution.py:579
  9.2 4.8 %shard_map.96 = (bf16[4,8,5,128,128]{4,3,2,1,0:T(8,128)(2,1)}, f32[5,1,256,128]{3,2,1,0:T(8,128)}, f32[5,1,256,128]{3,2,1,0:T(8,128)}) custom-call(s32[1]{0:T(128)} %bitcast.1.place_ref, s32[4096,128]{1,0:T(8,128)} %bitcast.34, bf16[4096,128]{1,0:T(8,128)(2,1)} %bitcast.35, f32[3,2,256,128]{3,2,1,0:T(8,128)} %bitcast.29, f32[2,256,128]{2,1,0:T(8,128)} %bitcast.36, ...), custom_call_target="tpu_custom_call" | custom-call | tf_op jit(solution)/shard_map/pallas_call | solution.py:31
  14.0 0.6 %collective-permute-start = (f32[5,1,256,128]{3,2,1,0:T(8,128)}, f32[5,1,256,128]{3,2,1,0:T(8,128)S(1)}, u32[]{:S(2)}, u32[]{:S(2)}) collective-permute-start(f32[5,1,256,128]{3,2,1,0:T(8,128)} %get-tuple-element.27), channel_id=1, source_target_pairs={{0,1},{1,0},{2,3},{3,2},{4,5},{5,4},{6,7},{7,6},{8,9},{9,8},{10,11... | collective-permute-start | bytes 1966088 | tf_op jit(solution)/shard_map/ppermute | solution.py:324
  14.5 0.7 %collective-permute-start.1 = (f32[5,1,256,128]{3,2,1,0:T(8,128)}, f32[5,1,256,128]{3,2,1,0:T(8,128)S(1)}, u32[]{:S(2)}, u32[]{:S(2)}) collective-permute-start(f32[5,1,256,128]{3,2,1,0:T(8,128)} %get-tuple-element.28), channel_id=1, source_target_pairs={{1,2},{2,1},{3,4},{4,3},{5,6},{6,5},{9,10},{10,9},{11,12},{12,11},... | collective-permute-start | bytes 1966088 | tf_op jit(solution)/shard_map/ppermute | solution.py:329
  15.2 3.7 %all-to-all-done = f32[8,64,128]{2,1,0:T(8,128)S(1)} async-done(((f32[8,64,128]{2,1,0:T(8,128)}), f32[8,64,128]{2,1,0:T(8,128)S(1)}, u32[]{:S(2)}, u32[]{:S(2)}) %all-to-all-start) | async-done | bytes 262176 | tf_op jit(solution)/shard_map/all_to_all | solution.py:579
  18.9 7.2 %shard_map.97 = (f32[512,128]{1,0:T(8,128)S(1)}, f32[512,128]{1,0:T(8,128)}) custom-call(s32[8,512]{1,0:T(8,128)S(1)} %bitcast.23, f32[512,128]{1,0:T(8,128)S(1)} %bitcast.18, bf16[4,8,5,128,128]{4,3,2,1,0:T(8,128)(2,1)} %get-tuple-element.24.moved_ref, f32[512,128]{1,0:T(8,128)} %bitcast.32), custom_call_target="tpu_custom_call" | custom-call | tf_op jit(solution)/shard_map/pallas_call | solution.py:31
  26.1 0.7 %collective-permute-start.3 = (f32[2,256,128]{2,1,0:T(8,128)S(1)}, f32[2,256,128]{2,1,0:T(8,128)S(1)}, u32[]{:S(2)}, u32[]{:S(2)}) collective-permute-start(f32[2,256,128]{2,1,0:T(8,128)S(1)} %bitcast.20), channel_id=1, source_target_pairs={{1,2},{2,1},{3,4},{4,3},{5,6},{6,5},{9,10},{10,9},{11,12},{12,11},... | collective-permute-start | bytes 786440 | tf_op jit(solution)/shard_map/ppermute | solution.py:329
  26.8 1.6 %collective-permute-start.2 = (f32[2,256,128]{2,1,0:T(8,128)S(1)}, f32[2,256,128]{2,1,0:T(8,128)S(1)}, u32[]{:S(2)}, u32[]{:S(2)}) collective-permute-start(f32[2,256,128]{2,1,0:T(8,128)S(1)} %bitcast.21), channel_id=1, source_target_pairs={{0,1},{1,0},{2,3},{3,2},{4,5},{5,4},{6,7},{7,6},{8,9},{9,8},{10,11... | collective-permute-start | bytes 786440 | tf_op jit(solution)/shard_map/ppermute | solution.py:324
  28.3 4.9 %all-to-all-start.1 = ((f32[32,16,128]{2,1,0:T(8,128)}), f32[32,16,128]{2,1,0:T(8,128)S(1)}, u32[]{:S(2)}, u32[]{:S(2)}) async-start(f32[32,16,128]{2,1,0:T(8,128)} %bitcast.14), calls=%async_computation.1 | async-start | bytes 524288 | tf_op jit(solution)/shard_map/all_to_all | solution.py:626
  33.2 2.7 %collective-permute-start.6 = (s32[8,64]{1,0:T(8,128)S(1)}, s32[8,64]{1,0:T(8,128)S(1)}, u32[]{:S(2)}, u32[]{:S(2)}) collective-permute-start(s32[8,64]{1,0:T(8,128)S(1)} %bitcast.25), channel_id=1, source_target_pairs={{0,24},{8,16},{16,8},{24,0},{1,25},{9,17},{17,9},{25,1},{2,26},{10... | collective-permute-start | bytes 6152 | tf_op jit(solution)/shard_map/ppermute | solution.py:319
  36.0 0.6 %collective-permute-start.5 = (s32[8,64]{1,0:T(8,128)S(1)}, s32[8,64]{1,0:T(8,128)S(1)}, u32[]{:S(2)}, u32[]{:S(2)}) collective-permute-start(s32[8,64]{1,0:T(8,128)S(1)} %bitcast.26), channel_id=1, source_target_pairs={{0,16},{8,24},{16,0},{24,8},{1,17},{9,25},{17,1},{25,9},{2,18},{10... | collective-permute-start | bytes 6152 | tf_op jit(solution)/shard_map/ppermute | solution.py:319
  36.5 0.3 collective-permute-start.4
  36.8 0.6 %copy-done.4 = f32[5,1,256,128]{3,2,1,0:T(8,128)} copy-done((f32[5,1,256,128]{3,2,1,0:T(8,128)}, f32[5,1,256,128]{3,2,1,0:T(8,128)S(1)}, u32[]{:S(2)}) %copy-start.4) | copy-done | bytes 655384
  37.4 2.9 %shard_map.98 = (f32[3,2,272,128]{3,2,1,0:T(8,128)S(1)}, f32[4,272,128]{2,1,0:T(8,128)S(1)}, f32[3,1,256,128]{3,2,1,0:T(8,128)S(1)}, f32[3,1,256,128]{3,2,1,0:T(8,128)S(1)}) custom-call(s32[1]{0:T(128)} %bitcast.1.place_ref, f32[3,2,256,128]{3,2,1,0:T(8,128)} %bitcast.30, f32[2,256,128]{2,1,0:T(8,128)} %bitcast.33, f32[2,256,128]{2,1,0:T(8,128)} %bitcast.37, ...), custom_call_target="tpu_custom_call" | custom-call | tf_op jit(solution)/shard_map/pallas_call | solution.py:31
  40.4 0.7 %collective-permute-start.8 = (f32[3,1,256,128]{3,2,1,0:T(8,128)S(1)}, f32[3,1,256,128]{3,2,1,0:T(8,128)S(1)}, u32[]{:S(2)}, u32[]{:S(2)}) collective-permute-start(f32[3,1,256,128]{3,2,1,0:T(8,128)S(1)} %get-tuple-element.35), channel_id=1, source_target_pairs={{1,2},{2,1},{3,4},{4,3},{5,6},{6,5},{9,10},{10,9},{11,12},{12,11},... | collective-permute-start | bytes 1179656 | tf_op jit(solution)/shard_map/ppermute | solution.py:329
  41.1 2.5 %all-to-all-done.1 = f32[32,16,128]{2,1,0:T(8,128)S(1)} async-done(((f32[32,16,128]{2,1,0:T(8,128)}), f32[32,16,128]{2,1,0:T(8,128)S(1)}, u32[]{:S(2)}, u32[]{:S(2)}) %all-to-all-start.1) | async-done | bytes 262176 | tf_op jit(solution)/shard_map/all_to_all | solution.py:626
  43.6 0.9 %shard_map.100.refs_0_ = f32[128,128]{1,0:T(8,128)S(1)} custom-call(s32[1]{0:T(128)} %bitcast.me_ref, f32[512,128]{1,0:T(8,128)S(1)} %bitcast.19, s32[8,64]{1,0:T(8,128)S(1)} %bitcast.28, s32[8,64]{1,0:T(8,128)S(1)} %collective-permute-done.4.refs_1_, s32[8,64]{1,0:T(8,128)S(1)} %collective-permute-done.5.refs_2_, s32[8,64]{1,0:T(8,128)S(1)} %collective-permute-done.6.refs_3_), custom_call_target="tpu_custom_call" | custom-call | tf_op jit(solution)/shard_map/pallas_call | solution.py:31
  44.5 0.8 %collective-permute-start.11 = (f32[128,128]{1,0:T(8,128)S(1)}, f32[128,128]{1,0:T(8,128)S(1)}, u32[]{:S(2)}, u32[]{:S(2)}) collective-permute-start(f32[128,128]{1,0:T(8,128)S(1)} %shard_map.100.refs_0_), channel_id=1, source_target_pairs={{0,24},{8,16},{16,8},{24,0},{1,25},{9,17},{17,9},{25,1},{2,26},{10... | collective-permute-start | bytes 196616 | tf_op jit(solution)/shard_map/ppermute | solution.py:319
  45.4 1.2 %collective-permute-start.10 = (f32[128,128]{1,0:T(8,128)S(1)}, f32[128,128]{1,0:T(8,128)S(1)}, u32[]{:S(2)}, u32[]{:S(2)}) collective-permute-start(f32[128,128]{1,0:T(8,128)S(1)} %shard_map.100.refs_0_), channel_id=1, source_target_pairs={{0,16},{8,24},{16,0},{24,8},{1,17},{9,25},{17,1},{25,9},{2,18},{10... | collective-permute-start | bytes 196616 | tf_op jit(solution)/shard_map/ppermute | solution.py:319
  46.6 1.5 %collective-permute-start.9 = (f32[128,128]{1,0:T(8,128)S(1)}, f32[128,128]{1,0:T(8,128)S(1)}, u32[]{:S(2)}, u32[]{:S(2)}) collective-permute-start(f32[128,128]{1,0:T(8,128)S(1)} %shard_map.100.refs_0_), channel_id=1, source_target_pairs={{0,8},{8,0},{16,24},{24,16},{1,9},{9,1},{17,25},{25,17},{2,10},{10... | collective-permute-start | bytes 196616 | tf_op jit(solution)/shard_map/ppermute | solution.py:319
  48.1 1.6 %shard_map.99 = f32[3,2,256,128]{3,2,1,0:T(8,128)} custom-call(s32[1]{0:T(128)} %bitcast.1.place_ref, f32[3,2,272,128]{3,2,1,0:T(8,128)S(1)} %get-tuple-element.29.field_ref, f32[4,272,128]{2,1,0:T(8,128)S(1)} %get-tuple-element.30.coefs_ref, f32[3,1,256,128]{3,2,1,0:T(8,128)S(1)} %collective-permute-done.7.near_ref, ...), custom_call_target="tpu_custom_call" | custom-call | tf_op jit(solution)/shard_map/pallas_call | solution.py:31
  50.0 1.3 %collective-permute-done.10.refs_2_ = f32[128,128]{1,0:T(8,128)S(1)} collective-permute-done((f32[128,128]{1,0:T(8,128)S(1)}, f32[128,128]{1,0:T(8,128)S(1)}, u32[]{:S(2)}, u32[]{:S(2)}) %collective-permute-start.10) | collective-permute-done | bytes 65568 | tf_op jit(solution)/shard_map/ppermute | solution.py:319
  51.3 1.0 %shard_map.101 = f32[512,128]{1,0:T(8,128)} custom-call(s32[1]{0:T(128)} %bitcast.me_ref, f32[512,128]{1,0:T(8,128)S(1)} %copy-done, f32[128,128]{1,0:T(8,128)S(1)} %shard_map.100.refs_0_, f32[128,128]{1,0:T(8,128)S(1)} %collective-permute-done.9.refs_1_, f32[128,128]{1,0:T(8,128)S(1)} %collective-permute-done.10.refs_2_, ...), custom_call_target="tpu_custom_call" | custom-call | tf_op jit(solution)/shard_map/pallas_call | solution.py:31
  (21 shorter events, 0.3 us)
Async XLA Ops:
  0.6 18.3 %copy-start.1 = (s32[1,512,8]{1,2,0:T(8,128)S(1)}, s32[1,512,8]{1,2,0:T(8,128)}, u32[]{:S(2)}) copy-start(s32[1,512,8]{1,2,0:T(8,128)} %param.13) | copy-start | bytes 49156
  2.8 16.1 %all-to-all-start = ((f32[8,64,128]{2,1,0:T(8,128)}), f32[8,64,128]{2,1,0:T(8,128)S(1)}, u32[]{:S(2)}, u32[]{:S(2)}) async-start(f32[8,64,128]{2,1,0:T(8,128)} %bitcast.8), calls=%async_computation | async-start | bytes 524288 | tf_op jit(solution)/shard_map/all_to_all | solution.py:579
  9.2 24.1 %copy-start.2 = (s32[1,1,8,64]{3,2,1,0:T(8,128)S(1)}, s32[1,1,8,64]{3,2,1,0:T(8,128)}, u32[]{:S(2)}) copy-start(s32[1,1,8,64]{3,2,1,0:T(8,128)} %param.12) | copy-start | bytes 6148
  14.0 22.0 %collective-permute-start = (f32[5,1,256,128]{3,2,1,0:T(8,128)}, f32[5,1,256,128]{3,2,1,0:T(8,128)S(1)}, u32[]{:S(2)}, u32[]{:S(2)}) collective-permute-start(f32[5,1,256,128]{3,2,1,0:T(8,128)} %get-tuple-element.27), channel_id=1, source_target_pairs={{0,1},{1,0},{2,3},{3,2},{4,5},{5,4},{6,7},{7,6},{8,9},{9,8},{10,11... | collective-permute-start | bytes 1966088 | tf_op jit(solution)/shard_map/ppermute | solution.py:324
  14.5 22.0 %collective-permute-start.1 = (f32[5,1,256,128]{3,2,1,0:T(8,128)}, f32[5,1,256,128]{3,2,1,0:T(8,128)S(1)}, u32[]{:S(2)}, u32[]{:S(2)}) collective-permute-start(f32[5,1,256,128]{3,2,1,0:T(8,128)} %get-tuple-element.28), channel_id=1, source_target_pairs={{1,2},{2,1},{3,4},{4,3},{5,6},{6,5},{9,10},{10,9},{11,12},{12,11},... | collective-permute-start | bytes 1966088 | tf_op jit(solution)/shard_map/ppermute | solution.py:329
  18.9 32.4 %copy-start = (f32[512,128]{1,0:T(8,128)S(1)}, f32[512,128]{1,0:T(8,128)}, u32[]{:S(2)}) copy-start(f32[512,128]{1,0:T(8,128)} %template_ref.3) | copy-start | bytes 786436
  26.1 10.7 %collective-permute-start.3 = (f32[2,256,128]{2,1,0:T(8,128)S(1)}, f32[2,256,128]{2,1,0:T(8,128)S(1)}, u32[]{:S(2)}, u32[]{:S(2)}) collective-permute-start(f32[2,256,128]{2,1,0:T(8,128)S(1)} %bitcast.20), channel_id=1, source_target_pairs={{1,2},{2,1},{3,4},{4,3},{5,6},{6,5},{9,10},{10,9},{11,12},{12,11},... | collective-permute-start | bytes 786440 | tf_op jit(solution)/shard_map/ppermute | solution.py:329
  26.8 10.6 %collective-permute-start.2 = (f32[2,256,128]{2,1,0:T(8,128)S(1)}, f32[2,256,128]{2,1,0:T(8,128)S(1)}, u32[]{:S(2)}, u32[]{:S(2)}) collective-permute-start(f32[2,256,128]{2,1,0:T(8,128)S(1)} %bitcast.21), channel_id=1, source_target_pairs={{0,1},{1,0},{2,3},{3,2},{4,5},{5,4},{6,7},{7,6},{8,9},{9,8},{10,11... | collective-permute-start | bytes 786440 | tf_op jit(solution)/shard_map/ppermute | solution.py:324
  28.3 15.3 %all-to-all-start.1 = ((f32[32,16,128]{2,1,0:T(8,128)}), f32[32,16,128]{2,1,0:T(8,128)S(1)}, u32[]{:S(2)}, u32[]{:S(2)}) async-start(f32[32,16,128]{2,1,0:T(8,128)} %bitcast.14), calls=%async_computation.1 | async-start | bytes 524288 | tf_op jit(solution)/shard_map/all_to_all | solution.py:626
  33.2 7.1 %collective-permute-start.6 = (s32[8,64]{1,0:T(8,128)S(1)}, s32[8,64]{1,0:T(8,128)S(1)}, u32[]{:S(2)}, u32[]{:S(2)}) collective-permute-start(s32[8,64]{1,0:T(8,128)S(1)} %bitcast.25), channel_id=1, source_target_pairs={{0,24},{8,16},{16,8},{24,0},{1,25},{9,17},{17,9},{25,1},{2,26},{10... | collective-permute-start | bytes 6152 | tf_op jit(solution)/shard_map/ppermute | solution.py:319
  36.0 0.8 %copy-start.3 = (f32[5,1,256,128]{3,2,1,0:T(8,128)}, f32[5,1,256,128]{3,2,1,0:T(8,128)S(1)}, u32[]{:S(2)}) copy-start(f32[5,1,256,128]{3,2,1,0:T(8,128)S(1)} %collective-permute-done.edge_near_ref) | copy-start | bytes 1966084
  36.0 4.3 %collective-permute-start.5 = (s32[8,64]{1,0:T(8,128)S(1)}, s32[8,64]{1,0:T(8,128)S(1)}, u32[]{:S(2)}, u32[]{:S(2)}) collective-permute-start(s32[8,64]{1,0:T(8,128)S(1)} %bitcast.26), channel_id=1, source_target_pairs={{0,16},{8,24},{16,0},{24,8},{1,17},{9,25},{17,1},{25,9},{2,18},{10... | collective-permute-start | bytes 6152 | tf_op jit(solution)/shard_map/ppermute | solution.py:319
  36.5 0.9 %copy-start.4 = (f32[5,1,256,128]{3,2,1,0:T(8,128)}, f32[5,1,256,128]{3,2,1,0:T(8,128)S(1)}, u32[]{:S(2)}) copy-start(f32[5,1,256,128]{3,2,1,0:T(8,128)S(1)} %collective-permute-done.1.edge_far_ref) | copy-start | bytes 1966084
  36.5 3.8 %collective-permute-start.4 = (s32[8,64]{1,0:T(8,128)S(1)}, s32[8,64]{1,0:T(8,128)S(1)}, u32[]{:S(2)}, u32[]{:S(2)}) collective-permute-start(s32[8,64]{1,0:T(8,128)S(1)} %bitcast.27), channel_id=1, source_target_pairs={{0,8},{8,0},{16,24},{24,16},{1,9},{9,1},{17,25},{25,17},{2,10},{10... | collective-permute-start | bytes 6152 | tf_op jit(solution)/shard_map/ppermute | solution.py:319
  40.3 7.8 %collective-permute-start.7 = (f32[3,1,256,128]{3,2,1,0:T(8,128)S(1)}, f32[3,1,256,128]{3,2,1,0:T(8,128)S(1)}, u32[]{:S(2)}, u32[]{:S(2)}) collective-permute-start(f32[3,1,256,128]{3,2,1,0:T(8,128)S(1)} %get-tuple-element.34), channel_id=1, source_target_pairs={{0,1},{1,0},{2,3},{3,2},{4,5},{5,4},{6,7},{7,6},{8,9},{9,8},{10,11... | collective-permute-start | bytes 1179656 | tf_op jit(solution)/shard_map/ppermute | solution.py:324
  40.4 7.7 %collective-permute-start.8 = (f32[3,1,256,128]{3,2,1,0:T(8,128)S(1)}, f32[3,1,256,128]{3,2,1,0:T(8,128)S(1)}, u32[]{:S(2)}, u32[]{:S(2)}) collective-permute-start(f32[3,1,256,128]{3,2,1,0:T(8,128)S(1)} %get-tuple-element.35), channel_id=1, source_target_pairs={{1,2},{2,1},{3,4},{4,3},{5,6},{6,5},{9,10},{10,9},{11,12},{12,11},... | collective-permute-start | bytes 1179656 | tf_op jit(solution)/shard_map/ppermute | solution.py:329
  44.5 5.4 %collective-permute-start.11 = (f32[128,128]{1,0:T(8,128)S(1)}, f32[128,128]{1,0:T(8,128)S(1)}, u32[]{:S(2)}, u32[]{:S(2)}) collective-permute-start(f32[128,128]{1,0:T(8,128)S(1)} %shard_map.100.refs_0_), channel_id=1, source_target_pairs={{0,24},{8,16},{16,8},{24,0},{1,25},{9,17},{17,9},{25,1},{2,26},{10... | collective-permute-start | bytes 196616 | tf_op jit(solution)/shard_map/ppermute | solution.py:319
  45.4 5.9 %collective-permute-start.10 = (f32[128,128]{1,0:T(8,128)S(1)}, f32[128,128]{1,0:T(8,128)S(1)}, u32[]{:S(2)}, u32[]{:S(2)}) collective-permute-start(f32[128,128]{1,0:T(8,128)S(1)} %shard_map.100.refs_0_), channel_id=1, source_target_pairs={{0,16},{8,24},{16,0},{24,8},{1,17},{9,25},{17,1},{25,9},{2,18},{10... | collective-permute-start | bytes 196616 | tf_op jit(solution)/shard_map/ppermute | solution.py:319
  46.6 4.7 %collective-permute-start.9 = (f32[128,128]{1,0:T(8,128)S(1)}, f32[128,128]{1,0:T(8,128)S(1)}, u32[]{:S(2)}, u32[]{:S(2)}) collective-permute-start(f32[128,128]{1,0:T(8,128)S(1)} %shard_map.100.refs_0_), channel_id=1, source_target_pairs={{0,8},{8,0},{16,24},{24,16},{1,9},{9,1},{17,25},{25,17},{2,10},{10... | collective-permute-start | bytes 196616 | tf_op jit(solution)/shard_map/ppermute | solution.py:319

commit v8 on v7

--- a/solution.py
+++ b/solution.py
@@ -10,6 +10,7 @@
 YR = 256
 LANES = 128
 PAD = 8
+KEPT = 1
 OFFSETS = (0, -2, -1, 1, 2)
 
 
@@ -102,6 +103,7 @@
     velocity_ref,
     stiffness_ref,
     images_ref,
+    kept_ref,
     moved_ref,
     near_ref,
     far_ref,
@@ -114,7 +116,9 @@
     out_sem,
     edge_sem,
 ):
-    chunks, each, count, some, width = moved.shape
+    held = kept_ref.shape[0]
+    each, count, some, width = moved.shape[1:]
+    chunks = held + moved.shape[0]
     odd = place_ref[0]
     near_plane, far_plane = pl.ds((edge.shape[1] - 1) * (1 - odd), 1), pl.ds((edge.shape[1] - 1) * odd, 1)
     step = some * each
@@ -138,8 +142,10 @@
         pltpu.make_async_copy(images_ref, edge.at[parts + 1], edge_sem.at[2]),
     ]
     writes = [
-        pltpu.make_async_copy(moved.at[i], moved_ref.at[i], out_sem.at[i]) for i in range(chunks)
-    ] + [
+        pltpu.make_async_copy(moved.at[i], moved_ref.at[i], out_sem.at[i])
+        for i in range(chunks - held)
+    ]
+    edge_writes = [
         pltpu.make_async_copy(edge.at[:, near_plane], near_ref, out_sem.at[chunks]),
         pltpu.make_async_copy(edge.at[:, far_plane], far_ref, out_sem.at[chunks + 1]),
     ]
@@ -161,14 +167,16 @@
             here = plain[pl.ds(b, some, stride=each), :]
             for j, o in enumerate(OFFSETS):
                 kept = jnp.where(offset == o, here, 0.0)
-                moved[i, b, j] = turned(kept, o).astype(jnp.bfloat16)
-        writes[i].start()
+                target, at_chunk = (moved, i) if i < chunks - held else (kept_ref, i - chunks + held)
+                target[at_chunk, b, j] = turned(kept, o).astype(jnp.bfloat16)
+        if i < chunks - held:
+            writes[i].start()
         if i == 0:
             for copy in edges:
                 copy.wait()
-            for copy in writes[chunks:]:
+            for copy in edge_writes:
                 copy.start()
-    for copy in writes:
+    for copy in writes + edge_writes:
         copy.wait()
 
 
@@ -177,6 +185,7 @@
     subjects,
     slot_ref,
     received_ref,
+    kept_ref,
     moved_ref,
     images_ref,
     warped_ref,
@@ -189,7 +198,10 @@
     moved_sem,
 ):
     slots, width = received_ref.shape
-    chunks, each, count, some = moved.shape[:4]
+    each, count, some = moved.shape[1:4]
+    held = kept_ref.shape[0]
+    loaded = moved.shape[0]
+    chunks = loaded + held
     rows = chunks * some
     block = width // subjects
     group = slots // subjects
@@ -197,9 +209,9 @@
     held = capacity // subjects
     first = pltpu.make_async_copy(images_ref, images, first_sem)
     moves = [
-        pltpu.make_async_copy(moved_ref.at[i], moved.at[i], moved_sem.at[i]) for i in range(chunks)
-    ]
-    for copy in moves[:1] + [first] + moves[1:]:
+        pltpu.make_async_copy(moved_ref.at[i], moved.at[i], moved_sem.at[i]) for i in range(loaded)
+    ]
+    for copy in [first] + moves:
         copy.start()
     slot = slot_ref[...]
     slot_wide = jnp.concatenate([slot, jnp.zeros((LANES - each, rows), jnp.int32)], axis=0).T
@@ -214,15 +226,18 @@
             [one_hot(wide == lane + t * LANES) for t in range(slots // LANES)], axis=1
         )
         picked[b] = joined(dot(pick, pair))
-    for copy in [first] + moves:
-        copy.wait()
-    for i in range(chunks):
+    first.wait()
+    for i in list(range(loaded, chunks)) + list(range(loaded)):
+        if i == 0:
+            for copy in moves:
+                copy.wait()
+        here, h = (moved, i) if i < loaded else (kept_ref, i - loaded)
         at = slice(i * some, (i + 1) * some)
         sums = [jnp.zeros((some, width), jnp.float32) for _ in OFFSETS]
         for b in range(each):
             values = picked[b, at, :]
             for j in range(count):
-                sums[j] = sums[j] + moved[i, b, j].astype(jnp.float32) * values
+                sums[j] = sums[j] + here[h, b, j].astype(jnp.float32) * values
         warped = sums[0]
         for j, o in enumerate(OFFSETS[1:], 1):
             warped = warped + turned(sums[j], -o)
@@ -230,9 +245,9 @@
         mismatch = warped - images[at, :]
         ahead = [turned(mismatch, o) for o in OFFSETS]
         for b in range(each):
-            total = moved[i, b, 0].astype(jnp.float32) * ahead[0]
+            total = here[h, b, 0].astype(jnp.float32) * ahead[0]
             for j in range(1, count):
-                total = total + moved[i, b, j].astype(jnp.float32) * ahead[j]
+                total = total + here[h, b, j].astype(jnp.float32) * ahead[j]
             placed[b, at, :] = halves(total)
     total = jnp.zeros((slots, 2 * width), jnp.float32)
     for b in range(each):
@@ -579,11 +594,18 @@
     received = lax.all_to_all(sending, "slab", split_axis=0, concat_axis=0, tiled=True)
 
     chunks = 4
-    moved_shape = (chunks, each, len(OFFSETS), rows // chunks, width)
+    kept_chunks = KEPT
+    chunk_shape = (each, len(OFFSETS), rows // chunks, width)
+    kept_shape, moved_shape = (kept_chunks,) + chunk_shape, (chunks - kept_chunks,) + chunk_shape
     edge_shape = (parts + 2, 1, YR, width)
-    moved, edge_near, edge_far = call(
+    kept, moved, edge_near, edge_far = call(
         prepare_kernel,
-        (shape(moved_shape, bf16), shape(edge_shape, f32), shape(edge_shape, f32)),
+        (
+            shape(kept_shape, bf16),
+            shape(moved_shape, bf16),
+            shape(edge_shape, f32),
+            shape(edge_shape, f32),
+        ),
         place,
         columns.reshape(terms, width),
         weights.reshape(terms, width),
@@ -592,7 +614,7 @@
         images_grid,
         smem=(0,),
         far=(1, 2, 3, 4, 5),
-        out_far=(0, 1, 2),
+        out_far=(1, 2, 3),
         scratch=(
             pltpu.VMEM((terms, width), jnp.int32),
             pltpu.VMEM((terms, width), bf16),
@@ -611,16 +633,17 @@
         (shape((rows, width), f32), shape((slots, width), f32)),
         ref_slot[0].T,
         received,
+        kept,
         moved,
         images[0],
-        far=(2, 3),
+        far=(3, 4),
         scratch=(
             pltpu.VMEM((rows, width), f32),
             pltpu.VMEM(moved_shape, bf16),
             pltpu.VMEM((each, rows, width), f32),
             pltpu.VMEM((each, rows, 2 * width), bf16),
             dma,
-            dma((chunks,)),
+            dma((chunks - kept_chunks,)),
         ),
     )
     returned = lax.all_to_all(sent, ("subj", "slab"), split_axis=0, concat_axis=0, tiled=True)

time: 52.9 us -> 52.2 us (0.987)
  local copies, waits for them, and re-layouts: 0.62 us -> 0.01 us
    ppermute x3, starting transfers between devices: 2.05 us -> 2.86 us  [swap_far(): lax.ppermute(values, 'slab', [(i, i + 1 if i % 2 else i - 1) for i in ran...]
    unnamed x10 -> x6, local copies, waits for them, and re-layouts: 0.62 us -> 0.01 us
  transfers between devices with their start and end apart: 14 -> 14, of which waited for: 4 -> 6; matrix products, arithmetic and copies ran while one was open for 0% -> 0% of each run, Pallas kernels for 33% -> 33%
where the time goes in v8:
time: 52.2 us; the launch traced here: 51.8 us
  starting transfers between devices  22.9 us (44%)
  Pallas kernels  20.2 us (39%)
  waiting for transfers between devices  8.03 us (15%)
  between operations  0.75 us (1%)
    pallas_call x7, Pallas kernels, call(): pl.pallas_call(kernel, out_shape=tuple(shapes) if many else shapes[0], in...  20.2 us
    ppermute x6, starting transfers between devices, over_subjects(): lax.ppermute(values, 'subj', [(i, i ^ d) for i in range(count)])  7.13 us
    all_to_all x1, starting transfers between devices, per_device(): lax.all_to_all(sending, 'slab', split_axis=0, concat_axis=0, tiled=True)  6.34 us
    all_to_all x1, starting transfers between devices, per_device(): lax.all_to_all(sent, ('subj', 'slab'), split_axis=0, concat_axis=0, tiled...  4.39 us
    all_to_all x1, waiting for transfers between devices, per_device(): lax.all_to_all(sending, 'slab', split_axis=0, concat_axis=0, tiled=True)  3.33 us
    ppermute x3, starting transfers between devices, swap_far(): lax.ppermute(values, 'slab', [(i, i + 1 if i % 2 else i - 1) for i in ran...  2.86 us
    all_to_all x1, waiting for transfers between devices, per_device(): lax.all_to_all(sent, ('subj', 'slab'), split_axis=0, concat_axis=0, tiled...  2.75 us
    ppermute x3, starting transfers between devices, swap_near(): lax.ppermute(values, 'slab', [(i, i ^ 1) for i in range(lax.axis_size('sl...  2.15 us
  transfers between devices with their start and end apart: 14, of which 6 were waited for; matrix products, arithmetic and copies ran while one was open for 0% of the time, Pallas kernels for 33%

profile of v8, /device:TPU:0, one launch (start us, length us, event | category | flops | bytes accessed | tf_op | source)
XLA Modules:
  0.0 51.8 jit_solution(9402362400466051080)
XLA Ops:
  0.6 2.2 %shard_map.95 = f32[512,128]{1,0:T(8,128)} custom-call(s32[8,64]{1,0:T(8,128)} %bitcast.24, f32[512,128]{1,0:T(8,128)} %template_ref.3), custom_call_target="tpu_custom_call" | custom-call | tf_op jit(solution)/shard_map/pallas_call | solution.py:32
  2.8 6.3 %all-to-all-start = ((f32[8,64,128]{2,1,0:T(8,128)}), f32[8,64,128]{2,1,0:T(8,128)S(1)}, u32[]{:S(2)}, u32[]{:S(2)}) async-start(f32[8,64,128]{2,1,0:T(8,128)} %bitcast.8), calls=%async_computation | async-start | bytes 524288 | tf_op jit(solution)/shard_map/all_to_all | solution.py:594
  9.1 4.3 %shard_map.96 = (bf16[1,8,5,128,128]{4,3,2,1,0:T(8,128)(2,1)S(1)}, bf16[3,8,5,128,128]{4,3,2,1,0:T(8,128)(2,1)}, f32[5,1,256,128]{3,2,1,0:T(8,128)}, f32[5,1,256,128]{3,2,1,0:T(8,128)}) custom-call(s32[1]{0:T(128)} %bitcast.1.place_ref, s32[4096,128]{1,0:T(8,128)} %bitcast.34, bf16[4096,128]{1,0:T(8,128)(2,1)} %bitcast.35, f32[3,2,256,128]{3,2,1,0:T(8,128)} %bitcast.29, ...), custom_call_target="tpu_custom_call" | custom-call | tf_op jit(solution)/shard_map/pallas_call | solution.py:32
  13.5 0.6 %collective-permute-start = (f32[5,1,256,128]{3,2,1,0:T(8,128)}, f32[5,1,256,128]{3,2,1,0:T(8,128)}, u32[]{:S(2)}, u32[]{:S(2)}) collective-permute-start(f32[5,1,256,128]{3,2,1,0:T(8,128)} %get-tuple-element.29), channel_id=1, source_target_pairs={{0,1},{1,0},{2,3},{3,2},{4,5},{5,4},{6,7},{7,6},{8,9},{9,8},{10,11... | collective-permute-start | bytes 1966088 | tf_op jit(solution)/shard_map/ppermute | solution.py:339
  14.0 1.5 %collective-permute-start.1 = (f32[5,1,256,128]{3,2,1,0:T(8,128)}, f32[5,1,256,128]{3,2,1,0:T(8,128)}, u32[]{:S(2)}, u32[]{:S(2)}) collective-permute-start(f32[5,1,256,128]{3,2,1,0:T(8,128)} %get-tuple-element.30), channel_id=1, source_target_pairs={{1,2},{2,1},{3,4},{4,3},{5,6},{6,5},{9,10},{10,9},{11,12},{12,11},... | collective-permute-start | bytes 1966088 | tf_op jit(solution)/shard_map/ppermute | solution.py:344
  15.6 3.3 %all-to-all-done = f32[8,64,128]{2,1,0:T(8,128)S(1)} async-done(((f32[8,64,128]{2,1,0:T(8,128)}), f32[8,64,128]{2,1,0:T(8,128)S(1)}, u32[]{:S(2)}, u32[]{:S(2)}) %all-to-all-start) | async-done | bytes 262176 | tf_op jit(solution)/shard_map/all_to_all | solution.py:594
  18.9 7.2 %shard_map.97 = (f32[512,128]{1,0:T(8,128)S(1)}, f32[512,128]{1,0:T(8,128)}) custom-call(s32[8,512]{1,0:T(8,128)S(1)} %bitcast.23, f32[512,128]{1,0:T(8,128)S(1)} %bitcast.18, bf16[1,8,5,128,128]{4,3,2,1,0:T(8,128)(2,1)S(1)} %get-tuple-element.25.kept_ref, bf16[3,8,5,128,128]{4,3,2,1,0:T(8,128)(2,1)} %get-tuple-element.26.moved_ref, f32[512,128]{1,0:T(8,128)} %bitcast.32), custom_call_target="tpu_custom_call" | custom-call | tf_op jit(solution)/shard_map/pallas_call | solution.py:32
  26.1 0.7 %collective-permute-start.3 = (f32[2,256,128]{2,1,0:T(8,128)S(1)}, f32[2,256,128]{2,1,0:T(8,128)S(1)}, u32[]{:S(2)}, u32[]{:S(2)}) collective-permute-start(f32[2,256,128]{2,1,0:T(8,128)S(1)} %bitcast.20), channel_id=1, source_target_pairs={{1,2},{2,1},{3,4},{4,3},{5,6},{6,5},{9,10},{10,9},{11,12},{12,11},... | collective-permute-start | bytes 786440 | tf_op jit(solution)/shard_map/ppermute | solution.py:344
  26.8 1.6 %collective-permute-start.2 = (f32[2,256,128]{2,1,0:T(8,128)S(1)}, f32[2,256,128]{2,1,0:T(8,128)S(1)}, u32[]{:S(2)}, u32[]{:S(2)}) collective-permute-start(f32[2,256,128]{2,1,0:T(8,128)S(1)} %bitcast.21), channel_id=1, source_target_pairs={{0,1},{1,0},{2,3},{3,2},{4,5},{5,4},{6,7},{7,6},{8,9},{9,8},{10,11... | collective-permute-start | bytes 786440 | tf_op jit(solution)/shard_map/ppermute | solution.py:339
  28.3 4.4 %all-to-all-start.1 = ((f32[32,16,128]{2,1,0:T(8,128)}), f32[32,16,128]{2,1,0:T(8,128)S(1)}, u32[]{:S(2)}, u32[]{:S(2)}) async-start(f32[32,16,128]{2,1,0:T(8,128)} %bitcast.14), calls=%async_computation.1 | async-start | bytes 524288 | tf_op jit(solution)/shard_map/all_to_all | solution.py:649
  32.7 2.7 %collective-permute-start.6 = (s32[8,64]{1,0:T(8,128)S(1)}, s32[8,64]{1,0:T(8,128)S(1)}, u32[]{:S(2)}, u32[]{:S(2)}) collective-permute-start(s32[8,64]{1,0:T(8,128)S(1)} %bitcast.25), channel_id=1, source_target_pairs={{0,24},{8,16},{16,8},{24,0},{1,25},{9,17},{17,9},{25,1},{2,26},{10... | collective-permute-start | bytes 6152 | tf_op jit(solution)/shard_map/ppermute | solution.py:334
  35.5 0.6 %collective-permute-start.5 = (s32[8,64]{1,0:T(8,128)S(1)}, s32[8,64]{1,0:T(8,128)S(1)}, u32[]{:S(2)}, u32[]{:S(2)}) collective-permute-start(s32[8,64]{1,0:T(8,128)S(1)} %bitcast.26), channel_id=1, source_target_pairs={{0,16},{8,24},{16,0},{24,8},{1,17},{9,25},{17,1},{25,9},{2,18},{10... | collective-permute-start | bytes 6152 | tf_op jit(solution)/shard_map/ppermute | solution.py:334
  36.0 0.3 collective-permute-start.4
  36.3 2.9 %shard_map.98 = (f32[3,2,272,128]{3,2,1,0:T(8,128)S(1)}, f32[4,272,128]{2,1,0:T(8,128)S(1)}, f32[3,1,256,128]{3,2,1,0:T(8,128)S(1)}, f32[3,1,256,128]{3,2,1,0:T(8,128)S(1)}) custom-call(s32[1]{0:T(128)} %bitcast.1.place_ref, f32[3,2,256,128]{3,2,1,0:T(8,128)} %bitcast.30, f32[2,256,128]{2,1,0:T(8,128)} %bitcast.33, f32[2,256,128]{2,1,0:T(8,128)} %bitcast.37, ...), custom_call_target="tpu_custom_call" | custom-call | tf_op jit(solution)/shard_map/pallas_call | solution.py:32
  39.3 0.4 collective-permute-done.4.refs_1_
  39.7 0.7 %collective-permute-start.8 = (f32[3,1,256,128]{3,2,1,0:T(8,128)S(1)}, f32[3,1,256,128]{3,2,1,0:T(8,128)S(1)}, u32[]{:S(2)}, u32[]{:S(2)}) collective-permute-start(f32[3,1,256,128]{3,2,1,0:T(8,128)S(1)} %get-tuple-element.37), channel_id=1, source_target_pairs={{1,2},{2,1},{3,4},{4,3},{5,6},{6,5},{9,10},{10,9},{11,12},{12,11},... | collective-permute-start | bytes 1179656 | tf_op jit(solution)/shard_map/ppermute | solution.py:344
  40.4 2.7 %all-to-all-done.1 = f32[32,16,128]{2,1,0:T(8,128)S(1)} async-done(((f32[32,16,128]{2,1,0:T(8,128)}), f32[32,16,128]{2,1,0:T(8,128)S(1)}, u32[]{:S(2)}, u32[]{:S(2)}) %all-to-all-start.1) | async-done | bytes 262176 | tf_op jit(solution)/shard_map/all_to_all | solution.py:649
  43.1 0.9 %shard_map.100.refs_0_ = f32[128,128]{1,0:T(8,128)S(1)} custom-call(s32[1]{0:T(128)} %bitcast.me_ref, f32[512,128]{1,0:T(8,128)S(1)} %bitcast.19, s32[8,64]{1,0:T(8,128)S(1)} %bitcast.28, s32[8,64]{1,0:T(8,128)S(1)} %collective-permute-done.4.refs_1_, s32[8,64]{1,0:T(8,128)S(1)} %collective-permute-done.5.refs_2_, s32[8,64]{1,0:T(8,128)S(1)} %collective-permute-done.6.refs_3_), custom_call_target="tpu_custom_call" | custom-call | tf_op jit(solution)/shard_map/pallas_call | solution.py:32
  44.1 0.8 %collective-permute-start.11 = (f32[128,128]{1,0:T(8,128)S(1)}, f32[128,128]{1,0:T(8,128)S(1)}, u32[]{:S(2)}, u32[]{:S(2)}) collective-permute-start(f32[128,128]{1,0:T(8,128)S(1)} %shard_map.100.refs_0_), channel_id=1, source_target_pairs={{0,24},{8,16},{16,8},{24,0},{1,25},{9,17},{17,9},{25,1},{2,26},{10... | collective-permute-start | bytes 196616 | tf_op jit(solution)/shard_map/ppermute | solution.py:334
  44.9 1.2 %collective-permute-start.10 = (f32[128,128]{1,0:T(8,128)S(1)}, f32[128,128]{1,0:T(8,128)S(1)}, u32[]{:S(2)}, u32[]{:S(2)}) collective-permute-start(f32[128,128]{1,0:T(8,128)S(1)} %shard_map.100.refs_0_), channel_id=1, source_target_pairs={{0,16},{8,24},{16,0},{24,8},{1,17},{9,25},{17,1},{25,9},{2,18},{10... | collective-permute-start | bytes 196616 | tf_op jit(solution)/shard_map/ppermute | solution.py:334
  46.1 1.5 %collective-permute-start.9 = (f32[128,128]{1,0:T(8,128)S(1)}, f32[128,128]{1,0:T(8,128)S(1)}, u32[]{:S(2)}, u32[]{:S(2)}) collective-permute-start(f32[128,128]{1,0:T(8,128)S(1)} %shard_map.100.refs_0_), channel_id=1, source_target_pairs={{0,8},{8,0},{16,24},{24,16},{1,9},{9,1},{17,25},{25,17},{2,10},{10... | collective-permute-start | bytes 196616 | tf_op jit(solution)/shard_map/ppermute | solution.py:334
  47.7 1.6 %shard_map.99 = f32[3,2,256,128]{3,2,1,0:T(8,128)} custom-call(s32[1]{0:T(128)} %bitcast.1.place_ref, f32[3,2,272,128]{3,2,1,0:T(8,128)S(1)} %get-tuple-element.31.field_ref, f32[4,272,128]{2,1,0:T(8,128)S(1)} %get-tuple-element.32.coefs_ref, f32[3,1,256,128]{3,2,1,0:T(8,128)S(1)} %collective-permute-done.7.near_ref, ...), custom_call_target="tpu_custom_call" | custom-call | tf_op jit(solution)/shard_map/pallas_call | solution.py:32
  49.5 1.3 %collective-permute-done.10.refs_2_ = f32[128,128]{1,0:T(8,128)S(1)} collective-permute-done((f32[128,128]{1,0:T(8,128)S(1)}, f32[128,128]{1,0:T(8,128)S(1)}, u32[]{:S(2)}, u32[]{:S(2)}) %collective-permute-start.10) | collective-permute-done | bytes 65568 | tf_op jit(solution)/shard_map/ppermute | solution.py:334
  50.8 1.0 %shard_map.101 = f32[512,128]{1,0:T(8,128)} custom-call(s32[1]{0:T(128)} %bitcast.me_ref, f32[512,128]{1,0:T(8,128)S(1)} %copy-done, f32[128,128]{1,0:T(8,128)S(1)} %shard_map.100.refs_0_, f32[128,128]{1,0:T(8,128)S(1)} %collective-permute-done.9.refs_1_, f32[128,128]{1,0:T(8,128)S(1)} %collective-permute-done.10.refs_2_, ...), custom_call_target="tpu_custom_call" | custom-call | tf_op jit(solution)/shard_map/pallas_call | solution.py:32
  (17 shorter events, 0.3 us)
Async XLA Ops:
  2.8 16.1 %all-to-all-start = ((f32[8,64,128]{2,1,0:T(8,128)}), f32[8,64,128]{2,1,0:T(8,128)S(1)}, u32[]{:S(2)}, u32[]{:S(2)}) async-start(f32[8,64,128]{2,1,0:T(8,128)} %bitcast.8), calls=%async_computation | async-start | bytes 524288 | tf_op jit(solution)/shard_map/all_to_all | solution.py:594
  9.1 9.7 %copy-start.1 = (s32[1,512,8]{1,2,0:T(8,128)S(1)}, s32[1,512,8]{1,2,0:T(8,128)}, u32[]{:S(2)}) copy-start(s32[1,512,8]{1,2,0:T(8,128)} %param.13) | copy-start | bytes 49156
  13.5 22.0 %collective-permute-start = (f32[5,1,256,128]{3,2,1,0:T(8,128)}, f32[5,1,256,128]{3,2,1,0:T(8,128)}, u32[]{:S(2)}, u32[]{:S(2)}) collective-permute-start(f32[5,1,256,128]{3,2,1,0:T(8,128)} %get-tuple-element.29), channel_id=1, source_target_pairs={{0,1},{1,0},{2,3},{3,2},{4,5},{5,4},{6,7},{7,6},{8,9},{9,8},{10,11... | collective-permute-start | bytes 1966088 | tf_op jit(solution)/shard_map/ppermute | solution.py:339
  14.0 22.0 %collective-permute-start.1 = (f32[5,1,256,128]{3,2,1,0:T(8,128)}, f32[5,1,256,128]{3,2,1,0:T(8,128)}, u32[]{:S(2)}, u32[]{:S(2)}) collective-permute-start(f32[5,1,256,128]{3,2,1,0:T(8,128)} %get-tuple-element.30), channel_id=1, source_target_pairs={{1,2},{2,1},{3,4},{4,3},{5,6},{6,5},{9,10},{10,9},{11,12},{12,11},... | collective-permute-start | bytes 1966088 | tf_op jit(solution)/shard_map/ppermute | solution.py:344
  18.9 13.8 %copy-start.2 = (s32[1,1,8,64]{3,2,1,0:T(8,128)S(1)}, s32[1,1,8,64]{3,2,1,0:T(8,128)}, u32[]{:S(2)}) copy-start(s32[1,1,8,64]{3,2,1,0:T(8,128)} %param.12) | copy-start | bytes 6148
  26.1 10.2 %collective-permute-start.3 = (f32[2,256,128]{2,1,0:T(8,128)S(1)}, f32[2,256,128]{2,1,0:T(8,128)S(1)}, u32[]{:S(2)}, u32[]{:S(2)}) collective-permute-start(f32[2,256,128]{2,1,0:T(8,128)S(1)} %bitcast.20), channel_id=1, source_target_pairs={{1,2},{2,1},{3,4},{4,3},{5,6},{6,5},{9,10},{10,9},{11,12},{12,11},... | collective-permute-start | bytes 786440 | tf_op jit(solution)/shard_map/ppermute | solution.py:344
  26.8 9.5 %collective-permute-start.2 = (f32[2,256,128]{2,1,0:T(8,128)S(1)}, f32[2,256,128]{2,1,0:T(8,128)S(1)}, u32[]{:S(2)}, u32[]{:S(2)}) collective-permute-start(f32[2,256,128]{2,1,0:T(8,128)S(1)} %bitcast.21), channel_id=1, source_target_pairs={{0,1},{1,0},{2,3},{3,2},{4,5},{5,4},{6,7},{7,6},{8,9},{9,8},{10,11... | collective-permute-start | bytes 786440 | tf_op jit(solution)/shard_map/ppermute | solution.py:339
  28.3 14.8 %all-to-all-start.1 = ((f32[32,16,128]{2,1,0:T(8,128)}), f32[32,16,128]{2,1,0:T(8,128)S(1)}, u32[]{:S(2)}, u32[]{:S(2)}) async-start(f32[32,16,128]{2,1,0:T(8,128)} %bitcast.14), calls=%async_computation.1 | async-start | bytes 524288 | tf_op jit(solution)/shard_map/all_to_all | solution.py:649
  32.7 6.5 %collective-permute-start.6 = (s32[8,64]{1,0:T(8,128)S(1)}, s32[8,64]{1,0:T(8,128)S(1)}, u32[]{:S(2)}, u32[]{:S(2)}) collective-permute-start(s32[8,64]{1,0:T(8,128)S(1)} %bitcast.25), channel_id=1, source_target_pairs={{0,24},{8,16},{16,8},{24,0},{1,25},{9,17},{17,9},{25,1},{2,26},{10... | collective-permute-start | bytes 6152 | tf_op jit(solution)/shard_map/ppermute | solution.py:334
  35.5 3.8 %collective-permute-start.5 = (s32[8,64]{1,0:T(8,128)S(1)}, s32[8,64]{1,0:T(8,128)S(1)}, u32[]{:S(2)}, u32[]{:S(2)}) collective-permute-start(s32[8,64]{1,0:T(8,128)S(1)} %bitcast.26), channel_id=1, source_target_pairs={{0,16},{8,24},{16,0},{24,8},{1,17},{9,25},{17,1},{25,9},{2,18},{10... | collective-permute-start | bytes 6152 | tf_op jit(solution)/shard_map/ppermute | solution.py:334
  36.0 3.6 %collective-permute-start.4 = (s32[8,64]{1,0:T(8,128)S(1)}, s32[8,64]{1,0:T(8,128)S(1)}, u32[]{:S(2)}, u32[]{:S(2)}) collective-permute-start(s32[8,64]{1,0:T(8,128)S(1)} %bitcast.27), channel_id=1, source_target_pairs={{0,8},{8,0},{16,24},{24,16},{1,9},{9,1},{17,25},{25,17},{2,10},{10... | collective-permute-start | bytes 6152 | tf_op jit(solution)/shard_map/ppermute | solution.py:334
  39.2 11.6 %copy-start = (f32[512,128]{1,0:T(8,128)S(1)}, f32[512,128]{1,0:T(8,128)}, u32[]{:S(2)}) copy-start(f32[512,128]{1,0:T(8,128)} %template_ref.3) | copy-start | bytes 786436
  39.7 8.0 %collective-permute-start.7 = (f32[3,1,256,128]{3,2,1,0:T(8,128)S(1)}, f32[3,1,256,128]{3,2,1,0:T(8,128)S(1)}, u32[]{:S(2)}, u32[]{:S(2)}) collective-permute-start(f32[3,1,256,128]{3,2,1,0:T(8,128)S(1)} %get-tuple-element.36), channel_id=1, source_target_pairs={{0,1},{1,0},{2,3},{3,2},{4,5},{5,4},{6,7},{7,6},{8,9},{9,8},{10,11... | collective-permute-start | bytes 1179656 | tf_op jit(solution)/shard_map/ppermute | solution.py:339
  39.7 8.0 %collective-permute-start.8 = (f32[3,1,256,128]{3,2,1,0:T(8,128)S(1)}, f32[3,1,256,128]{3,2,1,0:T(8,128)S(1)}, u32[]{:S(2)}, u32[]{:S(2)}) collective-permute-start(f32[3,1,256,128]{3,2,1,0:T(8,128)S(1)} %get-tuple-element.37), channel_id=1, source_target_pairs={{1,2},{2,1},{3,4},{4,3},{5,6},{6,5},{9,10},{10,9},{11,12},{12,11},... | collective-permute-start | bytes 1179656 | tf_op jit(solution)/shard_map/ppermute | solution.py:344
  44.1 5.4 %collective-permute-start.11 = (f32[128,128]{1,0:T(8,128)S(1)}, f32[128,128]{1,0:T(8,128)S(1)}, u32[]{:S(2)}, u32[]{:S(2)}) collective-permute-start(f32[128,128]{1,0:T(8,128)S(1)} %shard_map.100.refs_0_), channel_id=1, source_target_pairs={{0,24},{8,16},{16,8},{24,0},{1,25},{9,17},{17,9},{25,1},{2,26},{10... | collective-permute-start | bytes 196616 | tf_op jit(solution)/shard_map/ppermute | solution.py:334
  44.9 5.9 %collective-permute-start.10 = (f32[128,128]{1,0:T(8,128)S(1)}, f32[128,128]{1,0:T(8,128)S(1)}, u32[]{:S(2)}, u32[]{:S(2)}) collective-permute-start(f32[128,128]{1,0:T(8,128)S(1)} %shard_map.100.refs_0_), channel_id=1, source_target_pairs={{0,16},{8,24},{16,0},{24,8},{1,17},{9,25},{17,1},{25,9},{2,18},{10... | collective-permute-start | bytes 196616 | tf_op jit(solution)/shard_map/ppermute | solution.py:334
  46.1 4.7 %collective-permute-start.9 = (f32[128,128]{1,0:T(8,128)S(1)}, f32[128,128]{1,0:T(8,128)S(1)}, u32[]{:S(2)}, u32[]{:S(2)}) collective-permute-start(f32[128,128]{1,0:T(8,128)S(1)} %shard_map.100.refs_0_), channel_id=1, source_target_pairs={{0,8},{8,0},{16,24},{24,16},{1,9},{9,1},{17,25},{25,17},{2,10},{10... | collective-permute-start | bytes 196616 | tf_op jit(solution)/shard_map/ppermute | solution.py:334

commit v9 on v8

--- a/solution.py
+++ b/solution.py
@@ -226,11 +226,9 @@
             [one_hot(wide == lane + t * LANES) for t in range(slots // LANES)], axis=1
         )
         picked[b] = joined(dot(pick, pair))
-    first.wait()
-    for i in list(range(loaded, chunks)) + list(range(loaded)):
-        if i == 0:
-            for copy in moves:
-                copy.wait()
+    for copy in [first] + moves:
+        copy.wait()
+    for i in range(chunks):
         here, h = (moved, i) if i < loaded else (kept_ref, i - loaded)
         at = slice(i * some, (i + 1) * some)
         sums = [jnp.zeros((some, width), jnp.float32) for _ in OFFSETS]

time: 52.2 us -> 52 us (level)
  transfers between devices with their start and end apart: 14 -> 14, of which waited for: 6 -> 6; matrix products, arithmetic and copies ran while one was open for 0% -> 0% of each run, Pallas kernels for 33% -> 32%
where the time goes in v9:
time: 52 us; the launch traced here: 51.6 us
  starting transfers between devices  22.9 us (44%)
  Pallas kernels  19.9 us (38%)
  waiting for transfers between devices  8.03 us (15%)
  between operations  0.75 us (1%)
    pallas_call x7, Pallas kernels, call(): pl.pallas_call(kernel, out_shape=tuple(shapes) if many else shapes[0], in...  19.9 us
    ppermute x6, starting transfers between devices, over_subjects(): lax.ppermute(values, 'subj', [(i, i ^ d) for i in range(count)])  7.13 us
    all_to_all x1, starting transfers between devices, per_device(): lax.all_to_all(sending, 'slab', split_axis=0, concat_axis=0, tiled=True)  6.34 us
    all_to_all x1, starting transfers between devices, per_device(): lax.all_to_all(sent, ('subj', 'slab'), split_axis=0, concat_axis=0, tiled...  4.39 us
    all_to_all x1, waiting for transfers between devices, per_device(): lax.all_to_all(sending, 'slab', split_axis=0, concat_axis=0, tiled=True)  3.33 us
    ppermute x3, starting transfers between devices, swap_far(): lax.ppermute(values, 'slab', [(i, i + 1 if i % 2 else i - 1) for i in ran...  2.86 us
    all_to_all x1, waiting for transfers between devices, per_device(): lax.all_to_all(sent, ('subj', 'slab'), split_axis=0, concat_axis=0, tiled...  2.75 us
    ppermute x3, starting transfers between devices, swap_near(): lax.ppermute(values, 'slab', [(i, i ^ 1) for i in range(lax.axis_size('sl...  2.15 us
  transfers between devices with their start and end apart: 14, of which 6 were waited for; matrix products, arithmetic and copies ran while one was open for 0% of the time, Pallas kernels for 32%

profile of v9, /device:TPU:0, one launch (start us, length us, event | category | flops | bytes accessed | tf_op | source)
XLA Modules:
  0.0 51.6 jit_solution(16876240642230722842)
XLA Ops:
  0.6 2.2 %shard_map.95 = f32[512,128]{1,0:T(8,128)} custom-call(s32[8,64]{1,0:T(8,128)} %bitcast.24, f32[512,128]{1,0:T(8,128)} %template_ref.3), custom_call_target="tpu_custom_call" | custom-call | tf_op jit(solution)/shard_map/pallas_call | solution.py:32
  2.8 6.3 %all-to-all-start = ((f32[8,64,128]{2,1,0:T(8,128)}), f32[8,64,128]{2,1,0:T(8,128)S(1)}, u32[]{:S(2)}, u32[]{:S(2)}) async-start(f32[8,64,128]{2,1,0:T(8,128)} %bitcast.8), calls=%async_computation | async-start | bytes 524288 | tf_op jit(solution)/shard_map/all_to_all | solution.py:592
  9.1 4.3 %shard_map.96 = (bf16[1,8,5,128,128]{4,3,2,1,0:T(8,128)(2,1)S(1)}, bf16[3,8,5,128,128]{4,3,2,1,0:T(8,128)(2,1)}, f32[5,1,256,128]{3,2,1,0:T(8,128)}, f32[5,1,256,128]{3,2,1,0:T(8,128)}) custom-call(s32[1]{0:T(128)} %bitcast.1.place_ref, s32[4096,128]{1,0:T(8,128)} %bitcast.34, bf16[4096,128]{1,0:T(8,128)(2,1)} %bitcast.35, f32[3,2,256,128]{3,2,1,0:T(8,128)} %bitcast.29, ...), custom_call_target="tpu_custom_call" | custom-call | tf_op jit(solution)/shard_map/pallas_call | solution.py:32
  13.5 0.6 %collective-permute-start = (f32[5,1,256,128]{3,2,1,0:T(8,128)}, f32[5,1,256,128]{3,2,1,0:T(8,128)}, u32[]{:S(2)}, u32[]{:S(2)}) collective-permute-start(f32[5,1,256,128]{3,2,1,0:T(8,128)} %get-tuple-element.29), channel_id=1, source_target_pairs={{0,1},{1,0},{2,3},{3,2},{4,5},{5,4},{6,7},{7,6},{8,9},{9,8},{10,11... | collective-permute-start | bytes 1966088 | tf_op jit(solution)/shard_map/ppermute | solution.py:337
  14.0 1.5 %collective-permute-start.1 = (f32[5,1,256,128]{3,2,1,0:T(8,128)}, f32[5,1,256,128]{3,2,1,0:T(8,128)}, u32[]{:S(2)}, u32[]{:S(2)}) collective-permute-start(f32[5,1,256,128]{3,2,1,0:T(8,128)} %get-tuple-element.30), channel_id=1, source_target_pairs={{1,2},{2,1},{3,4},{4,3},{5,6},{6,5},{9,10},{10,9},{11,12},{12,11},... | collective-permute-start | bytes 1966088 | tf_op jit(solution)/shard_map/ppermute | solution.py:342
  15.6 3.3 %all-to-all-done = f32[8,64,128]{2,1,0:T(8,128)S(1)} async-done(((f32[8,64,128]{2,1,0:T(8,128)}), f32[8,64,128]{2,1,0:T(8,128)S(1)}, u32[]{:S(2)}, u32[]{:S(2)}) %all-to-all-start) | async-done | bytes 262176 | tf_op jit(solution)/shard_map/all_to_all | solution.py:592
  18.9 6.9 %shard_map.97 = (f32[512,128]{1,0:T(8,128)S(1)}, f32[512,128]{1,0:T(8,128)}) custom-call(s32[8,512]{1,0:T(8,128)S(1)} %bitcast.23, f32[512,128]{1,0:T(8,128)S(1)} %bitcast.18, bf16[1,8,5,128,128]{4,3,2,1,0:T(8,128)(2,1)S(1)} %get-tuple-element.25.kept_ref, bf16[3,8,5,128,128]{4,3,2,1,0:T(8,128)(2,1)} %get-tuple-element.26.moved_ref, f32[512,128]{1,0:T(8,128)} %bitcast.32), custom_call_target="tpu_custom_call" | custom-call | tf_op jit(solution)/shard_map/pallas_call | solution.py:32
  25.8 0.7 %collective-permute-start.3 = (f32[2,256,128]{2,1,0:T(8,128)S(1)}, f32[2,256,128]{2,1,0:T(8,128)S(1)}, u32[]{:S(2)}, u32[]{:S(2)}) collective-permute-start(f32[2,256,128]{2,1,0:T(8,128)S(1)} %bitcast.20), channel_id=1, source_target_pairs={{1,2},{2,1},{3,4},{4,3},{5,6},{6,5},{9,10},{10,9},{11,12},{12,11},... | collective-permute-start | bytes 786440 | tf_op jit(solution)/shard_map/ppermute | solution.py:342
  26.5 1.6 %collective-permute-start.2 = (f32[2,256,128]{2,1,0:T(8,128)S(1)}, f32[2,256,128]{2,1,0:T(8,128)S(1)}, u32[]{:S(2)}, u32[]{:S(2)}) collective-permute-start(f32[2,256,128]{2,1,0:T(8,128)S(1)} %bitcast.21), channel_id=1, source_target_pairs={{0,1},{1,0},{2,3},{3,2},{4,5},{5,4},{6,7},{7,6},{8,9},{9,8},{10,11... | collective-permute-start | bytes 786440 | tf_op jit(solution)/shard_map/ppermute | solution.py:337
  28.1 4.4 %all-to-all-start.1 = ((f32[32,16,128]{2,1,0:T(8,128)}), f32[32,16,128]{2,1,0:T(8,128)S(1)}, u32[]{:S(2)}, u32[]{:S(2)}) async-start(f32[32,16,128]{2,1,0:T(8,128)} %bitcast.14), calls=%async_computation.1 | async-start | bytes 524288 | tf_op jit(solution)/shard_map/all_to_all | solution.py:647
  32.5 2.7 %collective-permute-start.6 = (s32[8,64]{1,0:T(8,128)S(1)}, s32[8,64]{1,0:T(8,128)S(1)}, u32[]{:S(2)}, u32[]{:S(2)}) collective-permute-start(s32[8,64]{1,0:T(8,128)S(1)} %bitcast.25), channel_id=1, source_target_pairs={{0,24},{8,16},{16,8},{24,0},{1,25},{9,17},{17,9},{25,1},{2,26},{10... | collective-permute-start | bytes 6152 | tf_op jit(solution)/shard_map/ppermute | solution.py:332
  35.2 0.6 %collective-permute-start.5 = (s32[8,64]{1,0:T(8,128)S(1)}, s32[8,64]{1,0:T(8,128)S(1)}, u32[]{:S(2)}, u32[]{:S(2)}) collective-permute-start(s32[8,64]{1,0:T(8,128)S(1)} %bitcast.26), channel_id=1, source_target_pairs={{0,16},{8,24},{16,0},{24,8},{1,17},{9,25},{17,1},{25,9},{2,18},{10... | collective-permute-start | bytes 6152 | tf_op jit(solution)/shard_map/ppermute | solution.py:332
  35.8 0.3 collective-permute-start.4
  36.0 2.9 %shard_map.98 = (f32[3,2,272,128]{3,2,1,0:T(8,128)S(1)}, f32[4,272,128]{2,1,0:T(8,128)S(1)}, f32[3,1,256,128]{3,2,1,0:T(8,128)S(1)}, f32[3,1,256,128]{3,2,1,0:T(8,128)S(1)}) custom-call(s32[1]{0:T(128)} %bitcast.1.place_ref, f32[3,2,256,128]{3,2,1,0:T(8,128)} %bitcast.30, f32[2,256,128]{2,1,0:T(8,128)} %bitcast.33, f32[2,256,128]{2,1,0:T(8,128)} %bitcast.37, ...), custom_call_target="tpu_custom_call" | custom-call | tf_op jit(solution)/shard_map/pallas_call | solution.py:32
  39.0 0.4 collective-permute-done.4.refs_1_
  39.4 0.7 %collective-permute-start.8 = (f32[3,1,256,128]{3,2,1,0:T(8,128)S(1)}, f32[3,1,256,128]{3,2,1,0:T(8,128)S(1)}, u32[]{:S(2)}, u32[]{:S(2)}) collective-permute-start(f32[3,1,256,128]{3,2,1,0:T(8,128)S(1)} %get-tuple-element.37), channel_id=1, source_target_pairs={{1,2},{2,1},{3,4},{4,3},{5,6},{6,5},{9,10},{10,9},{11,12},{12,11},... | collective-permute-start | bytes 1179656 | tf_op jit(solution)/shard_map/ppermute | solution.py:342
  40.1 2.7 %all-to-all-done.1 = f32[32,16,128]{2,1,0:T(8,128)S(1)} async-done(((f32[32,16,128]{2,1,0:T(8,128)}), f32[32,16,128]{2,1,0:T(8,128)S(1)}, u32[]{:S(2)}, u32[]{:S(2)}) %all-to-all-start.1) | async-done | bytes 262176 | tf_op jit(solution)/shard_map/all_to_all | solution.py:647
  42.8 0.9 %shard_map.100.refs_0_ = f32[128,128]{1,0:T(8,128)S(1)} custom-call(s32[1]{0:T(128)} %bitcast.me_ref, f32[512,128]{1,0:T(8,128)S(1)} %bitcast.19, s32[8,64]{1,0:T(8,128)S(1)} %bitcast.28, s32[8,64]{1,0:T(8,128)S(1)} %collective-permute-done.4.refs_1_, s32[8,64]{1,0:T(8,128)S(1)} %collective-permute-done.5.refs_2_, s32[8,64]{1,0:T(8,128)S(1)} %collective-permute-done.6.refs_3_), custom_call_target="tpu_custom_call" | custom-call | tf_op jit(solution)/shard_map/pallas_call | solution.py:32
  43.8 0.8 %collective-permute-start.11 = (f32[128,128]{1,0:T(8,128)S(1)}, f32[128,128]{1,0:T(8,128)S(1)}, u32[]{:S(2)}, u32[]{:S(2)}) collective-permute-start(f32[128,128]{1,0:T(8,128)S(1)} %shard_map.100.refs_0_), channel_id=1, source_target_pairs={{0,24},{8,16},{16,8},{24,0},{1,25},{9,17},{17,9},{25,1},{2,26},{10... | collective-permute-start | bytes 196616 | tf_op jit(solution)/shard_map/ppermute | solution.py:332
  44.6 1.2 %collective-permute-start.10 = (f32[128,128]{1,0:T(8,128)S(1)}, f32[128,128]{1,0:T(8,128)S(1)}, u32[]{:S(2)}, u32[]{:S(2)}) collective-permute-start(f32[128,128]{1,0:T(8,128)S(1)} %shard_map.100.refs_0_), channel_id=1, source_target_pairs={{0,16},{8,24},{16,0},{24,8},{1,17},{9,25},{17,1},{25,9},{2,18},{10... | collective-permute-start | bytes 196616 | tf_op jit(solution)/shard_map/ppermute | solution.py:332
  45.8 1.5 %collective-permute-start.9 = (f32[128,128]{1,0:T(8,128)S(1)}, f32[128,128]{1,0:T(8,128)S(1)}, u32[]{:S(2)}, u32[]{:S(2)}) collective-permute-start(f32[128,128]{1,0:T(8,128)S(1)} %shard_map.100.refs_0_), channel_id=1, source_target_pairs={{0,8},{8,0},{16,24},{24,16},{1,9},{9,1},{17,25},{25,17},{2,10},{10... | collective-permute-start | bytes 196616 | tf_op jit(solution)/shard_map/ppermute | solution.py:332
  47.4 1.6 %shard_map.99 = f32[3,2,256,128]{3,2,1,0:T(8,128)} custom-call(s32[1]{0:T(128)} %bitcast.1.place_ref, f32[3,2,272,128]{3,2,1,0:T(8,128)S(1)} %get-tuple-element.31.field_ref, f32[4,272,128]{2,1,0:T(8,128)S(1)} %get-tuple-element.32.coefs_ref, f32[3,1,256,128]{3,2,1,0:T(8,128)S(1)} %collective-permute-done.7.near_ref, ...), custom_call_target="tpu_custom_call" | custom-call | tf_op jit(solution)/shard_map/pallas_call | solution.py:32
  49.2 1.3 %collective-permute-done.10.refs_2_ = f32[128,128]{1,0:T(8,128)S(1)} collective-permute-done((f32[128,128]{1,0:T(8,128)S(1)}, f32[128,128]{1,0:T(8,128)S(1)}, u32[]{:S(2)}, u32[]{:S(2)}) %collective-permute-start.10) | collective-permute-done | bytes 65568 | tf_op jit(solution)/shard_map/ppermute | solution.py:332
  50.5 1.0 %shard_map.101 = f32[512,128]{1,0:T(8,128)} custom-call(s32[1]{0:T(128)} %bitcast.me_ref, f32[512,128]{1,0:T(8,128)S(1)} %copy-done, f32[128,128]{1,0:T(8,128)S(1)} %shard_map.100.refs_0_, f32[128,128]{1,0:T(8,128)S(1)} %collective-permute-done.9.refs_1_, f32[128,128]{1,0:T(8,128)S(1)} %collective-permute-done.10.refs_2_, ...), custom_call_target="tpu_custom_call" | custom-call | tf_op jit(solution)/shard_map/pallas_call | solution.py:32
  (17 shorter events, 0.3 us)
Async XLA Ops:
  2.8 16.1 %all-to-all-start = ((f32[8,64,128]{2,1,0:T(8,128)}), f32[8,64,128]{2,1,0:T(8,128)S(1)}, u32[]{:S(2)}, u32[]{:S(2)}) async-start(f32[8,64,128]{2,1,0:T(8,128)} %bitcast.8), calls=%async_computation | async-start | bytes 524288 | tf_op jit(solution)/shard_map/all_to_all | solution.py:592
  9.1 9.7 %copy-start.1 = (s32[1,512,8]{1,2,0:T(8,128)S(1)}, s32[1,512,8]{1,2,0:T(8,128)}, u32[]{:S(2)}) copy-start(s32[1,512,8]{1,2,0:T(8,128)} %param.13) | copy-start | bytes 49156
  13.5 21.7 %collective-permute-start = (f32[5,1,256,128]{3,2,1,0:T(8,128)}, f32[5,1,256,128]{3,2,1,0:T(8,128)}, u32[]{:S(2)}, u32[]{:S(2)}) collective-permute-start(f32[5,1,256,128]{3,2,1,0:T(8,128)} %get-tuple-element.29), channel_id=1, source_target_pairs={{0,1},{1,0},{2,3},{3,2},{4,5},{5,4},{6,7},{7,6},{8,9},{9,8},{10,11... | collective-permute-start | bytes 1966088 | tf_op jit(solution)/shard_map/ppermute | solution.py:337
  14.0 21.7 %collective-permute-start.1 = (f32[5,1,256,128]{3,2,1,0:T(8,128)}, f32[5,1,256,128]{3,2,1,0:T(8,128)}, u32[]{:S(2)}, u32[]{:S(2)}) collective-permute-start(f32[5,1,256,128]{3,2,1,0:T(8,128)} %get-tuple-element.30), channel_id=1, source_target_pairs={{1,2},{2,1},{3,4},{4,3},{5,6},{6,5},{9,10},{10,9},{11,12},{12,11},... | collective-permute-start | bytes 1966088 | tf_op jit(solution)/shard_map/ppermute | solution.py:342
  18.9 13.6 %copy-start.2 = (s32[1,1,8,64]{3,2,1,0:T(8,128)S(1)}, s32[1,1,8,64]{3,2,1,0:T(8,128)}, u32[]{:S(2)}) copy-start(s32[1,1,8,64]{3,2,1,0:T(8,128)} %param.12) | copy-start | bytes 6148
  25.8 10.2 %collective-permute-start.3 = (f32[2,256,128]{2,1,0:T(8,128)S(1)}, f32[2,256,128]{2,1,0:T(8,128)S(1)}, u32[]{:S(2)}, u32[]{:S(2)}) collective-permute-start(f32[2,256,128]{2,1,0:T(8,128)S(1)} %bitcast.20), channel_id=1, source_target_pairs={{1,2},{2,1},{3,4},{4,3},{5,6},{6,5},{9,10},{10,9},{11,12},{12,11},... | collective-permute-start | bytes 786440 | tf_op jit(solution)/shard_map/ppermute | solution.py:342
  26.5 9.5 %collective-permute-start.2 = (f32[2,256,128]{2,1,0:T(8,128)S(1)}, f32[2,256,128]{2,1,0:T(8,128)S(1)}, u32[]{:S(2)}, u32[]{:S(2)}) collective-permute-start(f32[2,256,128]{2,1,0:T(8,128)S(1)} %bitcast.21), channel_id=1, source_target_pairs={{0,1},{1,0},{2,3},{3,2},{4,5},{5,4},{6,7},{7,6},{8,9},{9,8},{10,11... | collective-permute-start | bytes 786440 | tf_op jit(solution)/shard_map/ppermute | solution.py:337
  28.1 14.8 %all-to-all-start.1 = ((f32[32,16,128]{2,1,0:T(8,128)}), f32[32,16,128]{2,1,0:T(8,128)S(1)}, u32[]{:S(2)}, u32[]{:S(2)}) async-start(f32[32,16,128]{2,1,0:T(8,128)} %bitcast.14), calls=%async_computation.1 | async-start | bytes 524288 | tf_op jit(solution)/shard_map/all_to_all | solution.py:647
  32.5 6.5 %collective-permute-start.6 = (s32[8,64]{1,0:T(8,128)S(1)}, s32[8,64]{1,0:T(8,128)S(1)}, u32[]{:S(2)}, u32[]{:S(2)}) collective-permute-start(s32[8,64]{1,0:T(8,128)S(1)} %bitcast.25), channel_id=1, source_target_pairs={{0,24},{8,16},{16,8},{24,0},{1,25},{9,17},{17,9},{25,1},{2,26},{10... | collective-permute-start | bytes 6152 | tf_op jit(solution)/shard_map/ppermute | solution.py:332
  35.2 3.8 %collective-permute-start.5 = (s32[8,64]{1,0:T(8,128)S(1)}, s32[8,64]{1,0:T(8,128)S(1)}, u32[]{:S(2)}, u32[]{:S(2)}) collective-permute-start(s32[8,64]{1,0:T(8,128)S(1)} %bitcast.26), channel_id=1, source_target_pairs={{0,16},{8,24},{16,0},{24,8},{1,17},{9,25},{17,1},{25,9},{2,18},{10... | collective-permute-start | bytes 6152 | tf_op jit(solution)/shard_map/ppermute | solution.py:332
  35.8 3.6 %collective-permute-start.4 = (s32[8,64]{1,0:T(8,128)S(1)}, s32[8,64]{1,0:T(8,128)S(1)}, u32[]{:S(2)}, u32[]{:S(2)}) collective-permute-start(s32[8,64]{1,0:T(8,128)S(1)} %bitcast.27), channel_id=1, source_target_pairs={{0,8},{8,0},{16,24},{24,16},{1,9},{9,1},{17,25},{25,17},{2,10},{10... | collective-permute-start | bytes 6152 | tf_op jit(solution)/shard_map/ppermute | solution.py:332
  38.9 11.6 %copy-start = (f32[512,128]{1,0:T(8,128)S(1)}, f32[512,128]{1,0:T(8,128)}, u32[]{:S(2)}) copy-start(f32[512,128]{1,0:T(8,128)} %template_ref.3) | copy-start | bytes 786436
  39.4 8.0 %collective-permute-start.7 = (f32[3,1,256,128]{3,2,1,0:T(8,128)S(1)}, f32[3,1,256,128]{3,2,1,0:T(8,128)S(1)}, u32[]{:S(2)}, u32[]{:S(2)}) collective-permute-start(f32[3,1,256,128]{3,2,1,0:T(8,128)S(1)} %get-tuple-element.36), channel_id=1, source_target_pairs={{0,1},{1,0},{2,3},{3,2},{4,5},{5,4},{6,7},{7,6},{8,9},{9,8},{10,11... | collective-permute-start | bytes 1179656 | tf_op jit(solution)/shard_map/ppermute | solution.py:337
  39.4 8.0 %collective-permute-start.8 = (f32[3,1,256,128]{3,2,1,0:T(8,128)S(1)}, f32[3,1,256,128]{3,2,1,0:T(8,128)S(1)}, u32[]{:S(2)}, u32[]{:S(2)}) collective-permute-start(f32[3,1,256,128]{3,2,1,0:T(8,128)S(1)} %get-tuple-element.37), channel_id=1, source_target_pairs={{1,2},{2,1},{3,4},{4,3},{5,6},{6,5},{9,10},{10,9},{11,12},{12,11},... | collective-permute-start | bytes 1179656 | tf_op jit(solution)/shard_map/ppermute | solution.py:342
  43.8 5.4 %collective-permute-start.11 = (f32[128,128]{1,0:T(8,128)S(1)}, f32[128,128]{1,0:T(8,128)S(1)}, u32[]{:S(2)}, u32[]{:S(2)}) collective-permute-start(f32[128,128]{1,0:T(8,128)S(1)} %shard_map.100.refs_0_), channel_id=1, source_target_pairs={{0,24},{8,16},{16,8},{24,0},{1,25},{9,17},{17,9},{25,1},{2,26},{10... | collective-permute-start | bytes 196616 | tf_op jit(solution)/shard_map/ppermute | solution.py:332
  44.6 5.9 %collective-permute-start.10 = (f32[128,128]{1,0:T(8,128)S(1)}, f32[128,128]{1,0:T(8,128)S(1)}, u32[]{:S(2)}, u32[]{:S(2)}) collective-permute-start(f32[128,128]{1,0:T(8,128)S(1)} %shard_map.100.refs_0_), channel_id=1, source_target_pairs={{0,16},{8,24},{16,0},{24,8},{1,17},{9,25},{17,1},{25,9},{2,18},{10... | collective-permute-start | bytes 196616 | tf_op jit(solution)/shard_map/ppermute | solution.py:332
  45.8 4.7 %collective-permute-start.9 = (f32[128,128]{1,0:T(8,128)S(1)}, f32[128,128]{1,0:T(8,128)S(1)}, u32[]{:S(2)}, u32[]{:S(2)}) collective-permute-start(f32[128,128]{1,0:T(8,128)S(1)} %shard_map.100.refs_0_), channel_id=1, source_target_pairs={{0,8},{8,0},{16,24},{24,16},{1,9},{9,1},{17,25},{25,17},{2,10},{10... | collective-permute-start | bytes 196616 | tf_op jit(solution)/shard_map/ppermute | solution.py:332

commit v10 on v9

--- a/solution.py
+++ b/solution.py
@@ -161,14 +161,14 @@
         at = i * step
         for copy in reads[i]:
             copy.wait()
-        plain[...] = weights[at : at + step, :].astype(jnp.float32)
+        plain[:step, :] = weights[at : at + step, :].astype(jnp.float32)
         for b in range(each):
             offset = columns[pl.ds(at + b, some, stride=each), :] - cell
             here = plain[pl.ds(b, some, stride=each), :]
             for j, o in enumerate(OFFSETS):
                 kept = jnp.where(offset == o, here, 0.0)
                 target, at_chunk = (moved, i) if i < chunks - held else (kept_ref, i - chunks + held)
-                target[at_chunk, b, j] = turned(kept, o).astype(jnp.bfloat16)
+                target[at_chunk, b, j] = turned(kept.astype(jnp.bfloat16), o)
         if i < chunks - held:
             writes[i].start()
         if i == 0:
@@ -614,9 +614,9 @@
         far=(1, 2, 3, 4, 5),
         out_far=(1, 2, 3),
         scratch=(
-            pltpu.VMEM((terms, width), jnp.int32),
+            pltpu.VMEM((terms + each, width), jnp.int32),
             pltpu.VMEM((terms, width), bf16),
-            pltpu.VMEM((terms // chunks, width), f32),
+            pltpu.VMEM((terms // chunks + each, width), f32),
             pltpu.VMEM(moved_shape, bf16),
             pltpu.VMEM((parts + 2,) + grid, f32),
             dma((2 * chunks,)),

time: 52 us -> 52 us (level)
  no operation moved by 1% of the time
where the time goes in v10:
time: 52 us; the launch traced here: 51.6 us
  starting transfers between devices  22.9 us (44%)
  Pallas kernels  19.9 us (38%)
  waiting for transfers between devices  8.02 us (15%)
  between operations  0.75 us (1%)
    pallas_call x7, Pallas kernels, call(): pl.pallas_call(kernel, out_shape=tuple(shapes) if many else shapes[0], in...  19.9 us
    ppermute x6, starting transfers between devices, over_subjects(): lax.ppermute(values, 'subj', [(i, i ^ d) for i in range(count)])  7.13 us
    all_to_all x1, starting transfers between devices, per_device(): lax.all_to_all(sending, 'slab', split_axis=0, concat_axis=0, tiled=True)  6.34 us
    all_to_all x1, starting transfers between devices, per_device(): lax.all_to_all(sent, ('subj', 'slab'), split_axis=0, concat_axis=0, tiled...  4.4 us
    all_to_all x1, waiting for transfers between devices, per_device(): lax.all_to_all(sending, 'slab', split_axis=0, concat_axis=0, tiled=True)  3.32 us
    ppermute x3, starting transfers between devices, swap_far(): lax.ppermute(values, 'slab', [(i, i + 1 if i % 2 else i - 1) for i in ran...  2.86 us
    all_to_all x1, waiting for transfers between devices, per_device(): lax.all_to_all(sent, ('subj', 'slab'), split_axis=0, concat_axis=0, tiled...  2.75 us
    ppermute x3, starting transfers between devices, swap_near(): lax.ppermute(values, 'slab', [(i, i ^ 1) for i in range(lax.axis_size('sl...  2.15 us
  transfers between devices with their start and end apart: 14, of which 6 were waited for; matrix products, arithmetic and copies ran while one was open for 0% of the time, Pallas kernels for 32%

profile of v10, /device:TPU:0, one launch (start us, length us, event | category | flops | bytes accessed | tf_op | source)
XLA Modules:
  0.0 51.6 jit_solution(5281160356186144587)
XLA Ops:
  0.6 2.2 %shard_map.95 = f32[512,128]{1,0:T(8,128)} custom-call(s32[8,64]{1,0:T(8,128)} %bitcast.24, f32[512,128]{1,0:T(8,128)} %template_ref.3), custom_call_target="tpu_custom_call" | custom-call | tf_op jit(solution)/shard_map/pallas_call | solution.py:32
  2.8 6.3 %all-to-all-start = ((f32[8,64,128]{2,1,0:T(8,128)}), f32[8,64,128]{2,1,0:T(8,128)S(1)}, u32[]{:S(2)}, u32[]{:S(2)}) async-start(f32[8,64,128]{2,1,0:T(8,128)} %bitcast.8), calls=%async_computation | async-start | bytes 524288 | tf_op jit(solution)/shard_map/all_to_all | solution.py:592
  9.1 4.3 %shard_map.96 = (bf16[1,8,5,128,128]{4,3,2,1,0:T(8,128)(2,1)S(1)}, bf16[3,8,5,128,128]{4,3,2,1,0:T(8,128)(2,1)}, f32[5,1,256,128]{3,2,1,0:T(8,128)}, f32[5,1,256,128]{3,2,1,0:T(8,128)}) custom-call(s32[1]{0:T(128)} %bitcast.1.place_ref, s32[4096,128]{1,0:T(8,128)} %bitcast.34, bf16[4096,128]{1,0:T(8,128)(2,1)} %bitcast.35, f32[3,2,256,128]{3,2,1,0:T(8,128)} %bitcast.29, ...), custom_call_target="tpu_custom_call" | custom-call | tf_op jit(solution)/shard_map/pallas_call | solution.py:32
  13.5 0.6 %collective-permute-start = (f32[5,1,256,128]{3,2,1,0:T(8,128)}, f32[5,1,256,128]{3,2,1,0:T(8,128)}, u32[]{:S(2)}, u32[]{:S(2)}) collective-permute-start(f32[5,1,256,128]{3,2,1,0:T(8,128)} %get-tuple-element.29), channel_id=1, source_target_pairs={{0,1},{1,0},{2,3},{3,2},{4,5},{5,4},{6,7},{7,6},{8,9},{9,8},{10,11... | collective-permute-start | bytes 1966088 | tf_op jit(solution)/shard_map/ppermute | solution.py:337
  14.1 1.5 %collective-permute-start.1 = (f32[5,1,256,128]{3,2,1,0:T(8,128)}, f32[5,1,256,128]{3,2,1,0:T(8,128)}, u32[]{:S(2)}, u32[]{:S(2)}) collective-permute-start(f32[5,1,256,128]{3,2,1,0:T(8,128)} %get-tuple-element.30), channel_id=1, source_target_pairs={{1,2},{2,1},{3,4},{4,3},{5,6},{6,5},{9,10},{10,9},{11,12},{12,11},... | collective-permute-start | bytes 1966088 | tf_op jit(solution)/shard_map/ppermute | solution.py:342
  15.6 3.3 %all-to-all-done = f32[8,64,128]{2,1,0:T(8,128)S(1)} async-done(((f32[8,64,128]{2,1,0:T(8,128)}), f32[8,64,128]{2,1,0:T(8,128)S(1)}, u32[]{:S(2)}, u32[]{:S(2)}) %all-to-all-start) | async-done | bytes 262176 | tf_op jit(solution)/shard_map/all_to_all | solution.py:592
  18.9 6.9 %shard_map.97 = (f32[512,128]{1,0:T(8,128)S(1)}, f32[512,128]{1,0:T(8,128)}) custom-call(s32[8,512]{1,0:T(8,128)S(1)} %bitcast.23, f32[512,128]{1,0:T(8,128)S(1)} %bitcast.18, bf16[1,8,5,128,128]{4,3,2,1,0:T(8,128)(2,1)S(1)} %get-tuple-element.25.kept_ref, bf16[3,8,5,128,128]{4,3,2,1,0:T(8,128)(2,1)} %get-tuple-element.26.moved_ref, f32[512,128]{1,0:T(8,128)} %bitcast.32), custom_call_target="tpu_custom_call" | custom-call | tf_op jit(solution)/shard_map/pallas_call | solution.py:32
  25.8 0.7 %collective-permute-start.3 = (f32[2,256,128]{2,1,0:T(8,128)S(1)}, f32[2,256,128]{2,1,0:T(8,128)S(1)}, u32[]{:S(2)}, u32[]{:S(2)}) collective-permute-start(f32[2,256,128]{2,1,0:T(8,128)S(1)} %bitcast.20), channel_id=1, source_target_pairs={{1,2},{2,1},{3,4},{4,3},{5,6},{6,5},{9,10},{10,9},{11,12},{12,11},... | collective-permute-start | bytes 786440 | tf_op jit(solution)/shard_map/ppermute | solution.py:342
  26.5 1.6 %collective-permute-start.2 = (f32[2,256,128]{2,1,0:T(8,128)S(1)}, f32[2,256,128]{2,1,0:T(8,128)S(1)}, u32[]{:S(2)}, u32[]{:S(2)}) collective-permute-start(f32[2,256,128]{2,1,0:T(8,128)S(1)} %bitcast.21), channel_id=1, source_target_pairs={{0,1},{1,0},{2,3},{3,2},{4,5},{5,4},{6,7},{7,6},{8,9},{9,8},{10,11... | collective-permute-start | bytes 786440 | tf_op jit(solution)/shard_map/ppermute | solution.py:337
  28.1 4.4 %all-to-all-start.1 = ((f32[32,16,128]{2,1,0:T(8,128)}), f32[32,16,128]{2,1,0:T(8,128)S(1)}, u32[]{:S(2)}, u32[]{:S(2)}) async-start(f32[32,16,128]{2,1,0:T(8,128)} %bitcast.14), calls=%async_computation.1 | async-start | bytes 524288 | tf_op jit(solution)/shard_map/all_to_all | solution.py:647
  32.5 2.7 %collective-permute-start.6 = (s32[8,64]{1,0:T(8,128)S(1)}, s32[8,64]{1,0:T(8,128)S(1)}, u32[]{:S(2)}, u32[]{:S(2)}) collective-permute-start(s32[8,64]{1,0:T(8,128)S(1)} %bitcast.25), channel_id=1, source_target_pairs={{0,24},{8,16},{16,8},{24,0},{1,25},{9,17},{17,9},{25,1},{2,26},{10... | collective-permute-start | bytes 6152 | tf_op jit(solution)/shard_map/ppermute | solution.py:332
  35.2 0.6 %collective-permute-start.5 = (s32[8,64]{1,0:T(8,128)S(1)}, s32[8,64]{1,0:T(8,128)S(1)}, u32[]{:S(2)}, u32[]{:S(2)}) collective-permute-start(s32[8,64]{1,0:T(8,128)S(1)} %bitcast.26), channel_id=1, source_target_pairs={{0,16},{8,24},{16,0},{24,8},{1,17},{9,25},{17,1},{25,9},{2,18},{10... | collective-permute-start | bytes 6152 | tf_op jit(solution)/shard_map/ppermute | solution.py:332
  35.8 0.3 collective-permute-start.4
  36.0 2.9 %shard_map.98 = (f32[3,2,272,128]{3,2,1,0:T(8,128)S(1)}, f32[4,272,128]{2,1,0:T(8,128)S(1)}, f32[3,1,256,128]{3,2,1,0:T(8,128)S(1)}, f32[3,1,256,128]{3,2,1,0:T(8,128)S(1)}) custom-call(s32[1]{0:T(128)} %bitcast.1.place_ref, f32[3,2,256,128]{3,2,1,0:T(8,128)} %bitcast.30, f32[2,256,128]{2,1,0:T(8,128)} %bitcast.33, f32[2,256,128]{2,1,0:T(8,128)} %bitcast.37, ...), custom_call_target="tpu_custom_call" | custom-call | tf_op jit(solution)/shard_map/pallas_call | solution.py:32
  39.0 0.4 collective-permute-done.4.refs_1_
  39.4 0.7 %collective-permute-start.8 = (f32[3,1,256,128]{3,2,1,0:T(8,128)S(1)}, f32[3,1,256,128]{3,2,1,0:T(8,128)S(1)}, u32[]{:S(2)}, u32[]{:S(2)}) collective-permute-start(f32[3,1,256,128]{3,2,1,0:T(8,128)S(1)} %get-tuple-element.37), channel_id=1, source_target_pairs={{1,2},{2,1},{3,4},{4,3},{5,6},{6,5},{9,10},{10,9},{11,12},{12,11},... | collective-permute-start | bytes 1179656 | tf_op jit(solution)/shard_map/ppermute | solution.py:342
  40.1 2.7 %all-to-all-done.1 = f32[32,16,128]{2,1,0:T(8,128)S(1)} async-done(((f32[32,16,128]{2,1,0:T(8,128)}), f32[32,16,128]{2,1,0:T(8,128)S(1)}, u32[]{:S(2)}, u32[]{:S(2)}) %all-to-all-start.1) | async-done | bytes 262176 | tf_op jit(solution)/shard_map/all_to_all | solution.py:647
  42.9 0.9 %shard_map.100.refs_0_ = f32[128,128]{1,0:T(8,128)S(1)} custom-call(s32[1]{0:T(128)} %bitcast.me_ref, f32[512,128]{1,0:T(8,128)S(1)} %bitcast.19, s32[8,64]{1,0:T(8,128)S(1)} %bitcast.28, s32[8,64]{1,0:T(8,128)S(1)} %collective-permute-done.4.refs_1_, s32[8,64]{1,0:T(8,128)S(1)} %collective-permute-done.5.refs_2_, s32[8,64]{1,0:T(8,128)S(1)} %collective-permute-done.6.refs_3_), custom_call_target="tpu_custom_call" | custom-call | tf_op jit(solution)/shard_map/pallas_call | solution.py:32
  43.8 0.8 %collective-permute-start.11 = (f32[128,128]{1,0:T(8,128)S(1)}, f32[128,128]{1,0:T(8,128)S(1)}, u32[]{:S(2)}, u32[]{:S(2)}) collective-permute-start(f32[128,128]{1,0:T(8,128)S(1)} %shard_map.100.refs_0_), channel_id=1, source_target_pairs={{0,24},{8,16},{16,8},{24,0},{1,25},{9,17},{17,9},{25,1},{2,26},{10... | collective-permute-start | bytes 196616 | tf_op jit(solution)/shard_map/ppermute | solution.py:332
  44.7 1.2 %collective-permute-start.10 = (f32[128,128]{1,0:T(8,128)S(1)}, f32[128,128]{1,0:T(8,128)S(1)}, u32[]{:S(2)}, u32[]{:S(2)}) collective-permute-start(f32[128,128]{1,0:T(8,128)S(1)} %shard_map.100.refs_0_), channel_id=1, source_target_pairs={{0,16},{8,24},{16,0},{24,8},{1,17},{9,25},{17,1},{25,9},{2,18},{10... | collective-permute-start | bytes 196616 | tf_op jit(solution)/shard_map/ppermute | solution.py:332
  45.8 1.5 %collective-permute-start.9 = (f32[128,128]{1,0:T(8,128)S(1)}, f32[128,128]{1,0:T(8,128)S(1)}, u32[]{:S(2)}, u32[]{:S(2)}) collective-permute-start(f32[128,128]{1,0:T(8,128)S(1)} %shard_map.100.refs_0_), channel_id=1, source_target_pairs={{0,8},{8,0},{16,24},{24,16},{1,9},{9,1},{17,25},{25,17},{2,10},{10... | collective-permute-start | bytes 196616 | tf_op jit(solution)/shard_map/ppermute | solution.py:332
  47.4 1.6 %shard_map.99 = f32[3,2,256,128]{3,2,1,0:T(8,128)} custom-call(s32[1]{0:T(128)} %bitcast.1.place_ref, f32[3,2,272,128]{3,2,1,0:T(8,128)S(1)} %get-tuple-element.31.field_ref, f32[4,272,128]{2,1,0:T(8,128)S(1)} %get-tuple-element.32.coefs_ref, f32[3,1,256,128]{3,2,1,0:T(8,128)S(1)} %collective-permute-done.7.near_ref, ...), custom_call_target="tpu_custom_call" | custom-call | tf_op jit(solution)/shard_map/pallas_call | solution.py:32
  49.2 1.3 %collective-permute-done.10.refs_2_ = f32[128,128]{1,0:T(8,128)S(1)} collective-permute-done((f32[128,128]{1,0:T(8,128)S(1)}, f32[128,128]{1,0:T(8,128)S(1)}, u32[]{:S(2)}, u32[]{:S(2)}) %collective-permute-start.10) | collective-permute-done | bytes 65568 | tf_op jit(solution)/shard_map/ppermute | solution.py:332
  50.5 1.0 %shard_map.101 = f32[512,128]{1,0:T(8,128)} custom-call(s32[1]{0:T(128)} %bitcast.me_ref, f32[512,128]{1,0:T(8,128)S(1)} %copy-done, f32[128,128]{1,0:T(8,128)S(1)} %shard_map.100.refs_0_, f32[128,128]{1,0:T(8,128)S(1)} %collective-permute-done.9.refs_1_, f32[128,128]{1,0:T(8,128)S(1)} %collective-permute-done.10.refs_2_, ...), custom_call_target="tpu_custom_call" | custom-call | tf_op jit(solution)/shard_map/pallas_call | solution.py:32
  (17 shorter events, 0.3 us)
Async XLA Ops:
  2.8 16.1 %all-to-all-start = ((f32[8,64,128]{2,1,0:T(8,128)}), f32[8,64,128]{2,1,0:T(8,128)S(1)}, u32[]{:S(2)}, u32[]{:S(2)}) async-start(f32[8,64,128]{2,1,0:T(8,128)} %bitcast.8), calls=%async_computation | async-start | bytes 524288 | tf_op jit(solution)/shard_map/all_to_all | solution.py:592
  9.1 9.7 %copy-start.1 = (s32[1,512,8]{1,2,0:T(8,128)S(1)}, s32[1,512,8]{1,2,0:T(8,128)}, u32[]{:S(2)}) copy-start(s32[1,512,8]{1,2,0:T(8,128)} %param.13) | copy-start | bytes 49156
  13.5 21.7 %collective-permute-start = (f32[5,1,256,128]{3,2,1,0:T(8,128)}, f32[5,1,256,128]{3,2,1,0:T(8,128)}, u32[]{:S(2)}, u32[]{:S(2)}) collective-permute-start(f32[5,1,256,128]{3,2,1,0:T(8,128)} %get-tuple-element.29), channel_id=1, source_target_pairs={{0,1},{1,0},{2,3},{3,2},{4,5},{5,4},{6,7},{7,6},{8,9},{9,8},{10,11... | collective-permute-start | bytes 1966088 | tf_op jit(solution)/shard_map/ppermute | solution.py:337
  14.1 21.7 %collective-permute-start.1 = (f32[5,1,256,128]{3,2,1,0:T(8,128)}, f32[5,1,256,128]{3,2,1,0:T(8,128)}, u32[]{:S(2)}, u32[]{:S(2)}) collective-permute-start(f32[5,1,256,128]{3,2,1,0:T(8,128)} %get-tuple-element.30), channel_id=1, source_target_pairs={{1,2},{2,1},{3,4},{4,3},{5,6},{6,5},{9,10},{10,9},{11,12},{12,11},... | collective-permute-start | bytes 1966088 | tf_op jit(solution)/shard_map/ppermute | solution.py:342
  18.9 13.6 %copy-start.2 = (s32[1,1,8,64]{3,2,1,0:T(8,128)S(1)}, s32[1,1,8,64]{3,2,1,0:T(8,128)}, u32[]{:S(2)}) copy-start(s32[1,1,8,64]{3,2,1,0:T(8,128)} %param.12) | copy-start | bytes 6148
  25.8 10.2 %collective-permute-start.3 = (f32[2,256,128]{2,1,0:T(8,128)S(1)}, f32[2,256,128]{2,1,0:T(8,128)S(1)}, u32[]{:S(2)}, u32[]{:S(2)}) collective-permute-start(f32[2,256,128]{2,1,0:T(8,128)S(1)} %bitcast.20), channel_id=1, source_target_pairs={{1,2},{2,1},{3,4},{4,3},{5,6},{6,5},{9,10},{10,9},{11,12},{12,11},... | collective-permute-start | bytes 786440 | tf_op jit(solution)/shard_map/ppermute | solution.py:342
  26.5 9.6 %collective-permute-start.2 = (f32[2,256,128]{2,1,0:T(8,128)S(1)}, f32[2,256,128]{2,1,0:T(8,128)S(1)}, u32[]{:S(2)}, u32[]{:S(2)}) collective-permute-start(f32[2,256,128]{2,1,0:T(8,128)S(1)} %bitcast.21), channel_id=1, source_target_pairs={{0,1},{1,0},{2,3},{3,2},{4,5},{5,4},{6,7},{7,6},{8,9},{9,8},{10,11... | collective-permute-start | bytes 786440 | tf_op jit(solution)/shard_map/ppermute | solution.py:337
  28.1 14.8 %all-to-all-start.1 = ((f32[32,16,128]{2,1,0:T(8,128)}), f32[32,16,128]{2,1,0:T(8,128)S(1)}, u32[]{:S(2)}, u32[]{:S(2)}) async-start(f32[32,16,128]{2,1,0:T(8,128)} %bitcast.14), calls=%async_computation.1 | async-start | bytes 524288 | tf_op jit(solution)/shard_map/all_to_all | solution.py:647
  32.5 6.5 %collective-permute-start.6 = (s32[8,64]{1,0:T(8,128)S(1)}, s32[8,64]{1,0:T(8,128)S(1)}, u32[]{:S(2)}, u32[]{:S(2)}) collective-permute-start(s32[8,64]{1,0:T(8,128)S(1)} %bitcast.25), channel_id=1, source_target_pairs={{0,24},{8,16},{16,8},{24,0},{1,25},{9,17},{17,9},{25,1},{2,26},{10... | collective-permute-start | bytes 6152 | tf_op jit(solution)/shard_map/ppermute | solution.py:332
  35.2 3.8 %collective-permute-start.5 = (s32[8,64]{1,0:T(8,128)S(1)}, s32[8,64]{1,0:T(8,128)S(1)}, u32[]{:S(2)}, u32[]{:S(2)}) collective-permute-start(s32[8,64]{1,0:T(8,128)S(1)} %bitcast.26), channel_id=1, source_target_pairs={{0,16},{8,24},{16,0},{24,8},{1,17},{9,25},{17,1},{25,9},{2,18},{10... | collective-permute-start | bytes 6152 | tf_op jit(solution)/shard_map/ppermute | solution.py:332
  35.8 3.6 %collective-permute-start.4 = (s32[8,64]{1,0:T(8,128)S(1)}, s32[8,64]{1,0:T(8,128)S(1)}, u32[]{:S(2)}, u32[]{:S(2)}) collective-permute-start(s32[8,64]{1,0:T(8,128)S(1)} %bitcast.27), channel_id=1, source_target_pairs={{0,8},{8,0},{16,24},{24,16},{1,9},{9,1},{17,25},{25,17},{2,10},{10... | collective-permute-start | bytes 6152 | tf_op jit(solution)/shard_map/ppermute | solution.py:332
  38.9 11.6 %copy-start = (f32[512,128]{1,0:T(8,128)S(1)}, f32[512,128]{1,0:T(8,128)}, u32[]{:S(2)}) copy-start(f32[512,128]{1,0:T(8,128)} %template_ref.3) | copy-start | bytes 786436
  39.4 8.0 %collective-permute-start.7 = (f32[3,1,256,128]{3,2,1,0:T(8,128)S(1)}, f32[3,1,256,128]{3,2,1,0:T(8,128)S(1)}, u32[]{:S(2)}, u32[]{:S(2)}) collective-permute-start(f32[3,1,256,128]{3,2,1,0:T(8,128)S(1)} %get-tuple-element.36), channel_id=1, source_target_pairs={{0,1},{1,0},{2,3},{3,2},{4,5},{5,4},{6,7},{7,6},{8,9},{9,8},{10,11... | collective-permute-start | bytes 1179656 | tf_op jit(solution)/shard_map/ppermute | solution.py:337
  39.4 8.0 %collective-permute-start.8 = (f32[3,1,256,128]{3,2,1,0:T(8,128)S(1)}, f32[3,1,256,128]{3,2,1,0:T(8,128)S(1)}, u32[]{:S(2)}, u32[]{:S(2)}) collective-permute-start(f32[3,1,256,128]{3,2,1,0:T(8,128)S(1)} %get-tuple-element.37), channel_id=1, source_target_pairs={{1,2},{2,1},{3,4},{4,3},{5,6},{6,5},{9,10},{10,9},{11,12},{12,11},... | collective-permute-start | bytes 1179656 | tf_op jit(solution)/shard_map/ppermute | solution.py:342
  43.8 5.4 %collective-permute-start.11 = (f32[128,128]{1,0:T(8,128)S(1)}, f32[128,128]{1,0:T(8,128)S(1)}, u32[]{:S(2)}, u32[]{:S(2)}) collective-permute-start(f32[128,128]{1,0:T(8,128)S(1)} %shard_map.100.refs_0_), channel_id=1, source_target_pairs={{0,24},{8,16},{16,8},{24,0},{1,25},{9,17},{17,9},{25,1},{2,26},{10... | collective-permute-start | bytes 196616 | tf_op jit(solution)/shard_map/ppermute | solution.py:332
  44.7 5.9 %collective-permute-start.10 = (f32[128,128]{1,0:T(8,128)S(1)}, f32[128,128]{1,0:T(8,128)S(1)}, u32[]{:S(2)}, u32[]{:S(2)}) collective-permute-start(f32[128,128]{1,0:T(8,128)S(1)} %shard_map.100.refs_0_), channel_id=1, source_target_pairs={{0,16},{8,24},{16,0},{24,8},{1,17},{9,25},{17,1},{25,9},{2,18},{10... | collective-permute-start | bytes 196616 | tf_op jit(solution)/shard_map/ppermute | solution.py:332
  45.8 4.7 %collective-permute-start.9 = (f32[128,128]{1,0:T(8,128)S(1)}, f32[128,128]{1,0:T(8,128)S(1)}, u32[]{:S(2)}, u32[]{:S(2)}) collective-permute-start(f32[128,128]{1,0:T(8,128)S(1)} %shard_map.100.refs_0_), channel_id=1, source_target_pairs={{0,8},{8,0},{16,24},{24,16},{1,9},{9,1},{17,25},{25,17},{2,10},{10... | collective-permute-start | bytes 196616 | tf_op jit(solution)/shard_map/ppermute | solution.py:332

commit v11 on v10

--- a/solution.py
+++ b/solution.py
@@ -194,8 +194,10 @@
     moved,
     picked,
     placed,
+    sent,
     first_sem,
     moved_sem,
+    sent_sem,
 ):
     slots, width = received_ref.shape
     each, count, some = moved.shape[1:4]
@@ -253,12 +255,18 @@
         total = total + dot(drop, placed[b])
     total = joined(total)
     place = lax.broadcasted_iota(jnp.int32, (group, width), 1) // block
+    writes = []
     groups = [total[q * group : (q + 1) * group, :] for q in range(subjects)]
     for p in range(subjects):
         out = jnp.zeros((group, width), jnp.float32)
         for q in range(subjects):
             out = jnp.where(place == q, turned(groups[q], (q - p) * block), out)
-        sent_ref[p * group : (p + 1) * group, :] = out
+        sent[p * group : (p + 1) * group, :] = out
+        rows_at = pl.ds(p * group, group)
+        writes.append(pltpu.make_async_copy(sent.at[rows_at], sent_ref.at[rows_at], sent_sem.at[p]))
+        writes[-1].start()
+    for copy in writes:
+        copy.wait()
 
 
 def collect_kernel(subjects, me_ref, returned_ref, *refs):
@@ -310,12 +318,13 @@
 
 
 def update_kernel(subjects, me_ref, template_ref, *refs):
-    parts, out_ref = refs[:-1], refs[-1]
+    parts, (out_ref, done, sem) = refs[:-3], refs[-3:]
     rows, width = template_ref.shape
     block = width // subjects
     part = rows // subjects
     me = me_ref[0]
     place = lax.broadcasted_iota(jnp.int32, (part, width), 1) // block
+    writes = []
     for p in range(subjects):
         total = jnp.zeros((part, width), jnp.float32)
         for d in range(subjects):
@@ -323,7 +332,12 @@
             turn = lax.rem((source - p) * block + width, width)
             total = jnp.where(place == source, pltpu.roll(parts[d][...], turn, axis=1), total)
         at = slice(p * part, (p + 1) * part)
-        out_ref[at, :] = template_ref[at, :] - template_rate * total / subjects
+        done[at, :] = template_ref[at, :] - template_rate * total / subjects
+        rows_at = pl.ds(p * part, part)
+        writes.append(pltpu.make_async_copy(done.at[rows_at], out_ref.at[rows_at], sem.at[p]))
+        writes[-1].start()
+    for copy in writes:
+        copy.wait()
 
 
 def over_subjects(values):
@@ -635,13 +649,16 @@
         moved,
         images[0],
         far=(3, 4),
+        out_far=(1,),
         scratch=(
             pltpu.VMEM((rows, width), f32),
             pltpu.VMEM(moved_shape, bf16),
             pltpu.VMEM((each, rows, width), f32),
             pltpu.VMEM((each, rows, 2 * width), bf16),
+            pltpu.VMEM((slots, width), f32),
             dma,
             dma((chunks - kept_chunks,)),
+            dma((subjects,)),
         ),
     )
     returned = lax.all_to_all(sent, ("subj", "slab"), split_axis=0, concat_axis=0, tiled=True)
@@ -712,6 +729,8 @@
         template,
         *pieces,
         smem=(0,),
+        out_far=(0,),
+        scratch=(pltpu.VMEM((rows, width), f32), dma((subjects,))),
     )
     velocity_out = field.reshape(parts, rows, width)[None]
     return (template_out, velocity_out)

time: 52 us -> 52 us (level)
  no operation moved by 1% of the time
where the time goes in v11:
time: 52 us; the launch traced here: 51.6 us
  starting transfers between devices  22.9 us (44%)
  Pallas kernels  19.9 us (38%)
  waiting for transfers between devices  8.02 us (15%)
  between operations  0.75 us (1%)
    pallas_call x7, Pallas kernels, call(): pl.pallas_call(kernel, out_shape=tuple(shapes) if many else shapes[0], in...  19.9 us
    ppermute x6, starting transfers between devices, over_subjects(): lax.ppermute(values, 'subj', [(i, i ^ d) for i in range(count)])  7.13 us
    all_to_all x1, starting transfers between devices, per_device(): lax.all_to_all(sending, 'slab', split_axis=0, concat_axis=0, tiled=True)  6.34 us
    all_to_all x1, starting transfers between devices, per_device(): lax.all_to_all(sent, ('subj', 'slab'), split_axis=0, concat_axis=0, tiled...  4.39 us
    all_to_all x1, waiting for transfers between devices, per_device(): lax.all_to_all(sending, 'slab', split_axis=0, concat_axis=0, tiled=True)  3.32 us
    ppermute x3, starting transfers between devices, swap_far(): lax.ppermute(values, 'slab', [(i, i + 1 if i % 2 else i - 1) for i in ran...  2.86 us
    all_to_all x1, waiting for transfers between devices, per_device(): lax.all_to_all(sent, ('subj', 'slab'), split_axis=0, concat_axis=0, tiled...  2.75 us
    ppermute x3, starting transfers between devices, swap_near(): lax.ppermute(values, 'slab', [(i, i ^ 1) for i in range(lax.axis_size('sl...  2.15 us
  transfers between devices with their start and end apart: 14, of which 6 were waited for; matrix products, arithmetic and copies ran while one was open for 0% of the time, Pallas kernels for 32%

profile of v11, /device:TPU:0, one launch (start us, length us, event | category | flops | bytes accessed | tf_op | source)
XLA Modules:
  0.0 51.6 jit_solution(15132751944788974886)
XLA Ops:
  0.6 2.2 %shard_map.95 = f32[512,128]{1,0:T(8,128)} custom-call(s32[8,64]{1,0:T(8,128)} %bitcast.24, f32[512,128]{1,0:T(8,128)} %template_ref.3), custom_call_target="tpu_custom_call" | custom-call | tf_op jit(solution)/shard_map/pallas_call | solution.py:32
  2.8 6.3 %all-to-all-start = ((f32[8,64,128]{2,1,0:T(8,128)}), f32[8,64,128]{2,1,0:T(8,128)S(1)}, u32[]{:S(2)}, u32[]{:S(2)}) async-start(f32[8,64,128]{2,1,0:T(8,128)} %bitcast.8), calls=%async_computation | async-start | bytes 524288 | tf_op jit(solution)/shard_map/all_to_all | solution.py:606
  9.1 4.3 %shard_map.96 = (bf16[1,8,5,128,128]{4,3,2,1,0:T(8,128)(2,1)S(1)}, bf16[3,8,5,128,128]{4,3,2,1,0:T(8,128)(2,1)}, f32[5,1,256,128]{3,2,1,0:T(8,128)}, f32[5,1,256,128]{3,2,1,0:T(8,128)}) custom-call(s32[1]{0:T(128)} %bitcast.1.place_ref, s32[4096,128]{1,0:T(8,128)} %bitcast.34, bf16[4096,128]{1,0:T(8,128)(2,1)} %bitcast.35, f32[3,2,256,128]{3,2,1,0:T(8,128)} %bitcast.29, ...), custom_call_target="tpu_custom_call" | custom-call | tf_op jit(solution)/shard_map/pallas_call | solution.py:32
  13.5 0.6 %collective-permute-start = (f32[5,1,256,128]{3,2,1,0:T(8,128)}, f32[5,1,256,128]{3,2,1,0:T(8,128)}, u32[]{:S(2)}, u32[]{:S(2)}) collective-permute-start(f32[5,1,256,128]{3,2,1,0:T(8,128)} %get-tuple-element.29), channel_id=1, source_target_pairs={{0,1},{1,0},{2,3},{3,2},{4,5},{5,4},{6,7},{7,6},{8,9},{9,8},{10,11... | collective-permute-start | bytes 1966088 | tf_op jit(solution)/shard_map/ppermute | solution.py:351
  14.1 1.5 %collective-permute-start.1 = (f32[5,1,256,128]{3,2,1,0:T(8,128)}, f32[5,1,256,128]{3,2,1,0:T(8,128)}, u32[]{:S(2)}, u32[]{:S(2)}) collective-permute-start(f32[5,1,256,128]{3,2,1,0:T(8,128)} %get-tuple-element.30), channel_id=1, source_target_pairs={{1,2},{2,1},{3,4},{4,3},{5,6},{6,5},{9,10},{10,9},{11,12},{12,11},... | collective-permute-start | bytes 1966088 | tf_op jit(solution)/shard_map/ppermute | solution.py:356
  15.6 3.3 %all-to-all-done = f32[8,64,128]{2,1,0:T(8,128)S(1)} async-done(((f32[8,64,128]{2,1,0:T(8,128)}), f32[8,64,128]{2,1,0:T(8,128)S(1)}, u32[]{:S(2)}, u32[]{:S(2)}) %all-to-all-start) | async-done | bytes 262176 | tf_op jit(solution)/shard_map/all_to_all | solution.py:606
  18.9 6.9 %shard_map.97 = (f32[512,128]{1,0:T(8,128)S(1)}, f32[512,128]{1,0:T(8,128)}) custom-call(s32[8,512]{1,0:T(8,128)S(1)} %bitcast.23, f32[512,128]{1,0:T(8,128)S(1)} %bitcast.18, bf16[1,8,5,128,128]{4,3,2,1,0:T(8,128)(2,1)S(1)} %get-tuple-element.25.kept_ref, bf16[3,8,5,128,128]{4,3,2,1,0:T(8,128)(2,1)} %get-tuple-element.26.moved_ref, f32[512,128]{1,0:T(8,128)} %bitcast.32), custom_call_target="tpu_custom_call" | custom-call | tf_op jit(solution)/shard_map/pallas_call | solution.py:32
  25.8 0.7 %collective-permute-start.3 = (f32[2,256,128]{2,1,0:T(8,128)S(1)}, f32[2,256,128]{2,1,0:T(8,128)S(1)}, u32[]{:S(2)}, u32[]{:S(2)}) collective-permute-start(f32[2,256,128]{2,1,0:T(8,128)S(1)} %bitcast.20), channel_id=1, source_target_pairs={{1,2},{2,1},{3,4},{4,3},{5,6},{6,5},{9,10},{10,9},{11,12},{12,11},... | collective-permute-start | bytes 786440 | tf_op jit(solution)/shard_map/ppermute | solution.py:356
  26.5 1.6 %collective-permute-start.2 = (f32[2,256,128]{2,1,0:T(8,128)S(1)}, f32[2,256,128]{2,1,0:T(8,128)S(1)}, u32[]{:S(2)}, u32[]{:S(2)}) collective-permute-start(f32[2,256,128]{2,1,0:T(8,128)S(1)} %bitcast.21), channel_id=1, source_target_pairs={{0,1},{1,0},{2,3},{3,2},{4,5},{5,4},{6,7},{7,6},{8,9},{9,8},{10,11... | collective-permute-start | bytes 786440 | tf_op jit(solution)/shard_map/ppermute | solution.py:351
  28.1 4.4 %all-to-all-start.1 = ((f32[32,16,128]{2,1,0:T(8,128)}), f32[32,16,128]{2,1,0:T(8,128)S(1)}, u32[]{:S(2)}, u32[]{:S(2)}) async-start(f32[32,16,128]{2,1,0:T(8,128)} %bitcast.39), calls=%async_computation.1 | async-start | bytes 524288 | tf_op jit(solution)/shard_map/all_to_all | solution.py:664
  32.5 2.7 %collective-permute-start.6 = (s32[8,64]{1,0:T(8,128)S(1)}, s32[8,64]{1,0:T(8,128)S(1)}, u32[]{:S(2)}, u32[]{:S(2)}) collective-permute-start(s32[8,64]{1,0:T(8,128)S(1)} %bitcast.25), channel_id=1, source_target_pairs={{0,24},{8,16},{16,8},{24,0},{1,25},{9,17},{17,9},{25,1},{2,26},{10... | collective-permute-start | bytes 6152 | tf_op jit(solution)/shard_map/ppermute | solution.py:346
  35.2 0.6 %collective-permute-start.5 = (s32[8,64]{1,0:T(8,128)S(1)}, s32[8,64]{1,0:T(8,128)S(1)}, u32[]{:S(2)}, u32[]{:S(2)}) collective-permute-start(s32[8,64]{1,0:T(8,128)S(1)} %bitcast.26), channel_id=1, source_target_pairs={{0,16},{8,24},{16,0},{24,8},{1,17},{9,25},{17,1},{25,9},{2,18},{10... | collective-permute-start | bytes 6152 | tf_op jit(solution)/shard_map/ppermute | solution.py:346
  35.8 0.3 collective-permute-start.4
  36.1 2.9 %shard_map.98 = (f32[3,2,272,128]{3,2,1,0:T(8,128)S(1)}, f32[4,272,128]{2,1,0:T(8,128)S(1)}, f32[3,1,256,128]{3,2,1,0:T(8,128)S(1)}, f32[3,1,256,128]{3,2,1,0:T(8,128)S(1)}) custom-call(s32[1]{0:T(128)} %bitcast.1.place_ref, f32[3,2,256,128]{3,2,1,0:T(8,128)} %bitcast.30, f32[2,256,128]{2,1,0:T(8,128)} %bitcast.33, f32[2,256,128]{2,1,0:T(8,128)} %bitcast.37, ...), custom_call_target="tpu_custom_call" | custom-call | tf_op jit(solution)/shard_map/pallas_call | solution.py:32
  39.1 0.4 collective-permute-done.4.refs_1_
  39.4 0.7 %collective-permute-start.8 = (f32[3,1,256,128]{3,2,1,0:T(8,128)S(1)}, f32[3,1,256,128]{3,2,1,0:T(8,128)S(1)}, u32[]{:S(2)}, u32[]{:S(2)}) collective-permute-start(f32[3,1,256,128]{3,2,1,0:T(8,128)S(1)} %get-tuple-element.37), channel_id=1, source_target_pairs={{1,2},{2,1},{3,4},{4,3},{5,6},{6,5},{9,10},{10,9},{11,12},{12,11},... | collective-permute-start | bytes 1179656 | tf_op jit(solution)/shard_map/ppermute | solution.py:356
  40.1 2.7 %all-to-all-done.1 = f32[32,16,128]{2,1,0:T(8,128)S(1)} async-done(((f32[32,16,128]{2,1,0:T(8,128)}), f32[32,16,128]{2,1,0:T(8,128)S(1)}, u32[]{:S(2)}, u32[]{:S(2)}) %all-to-all-start.1) | async-done | bytes 262176 | tf_op jit(solution)/shard_map/all_to_all | solution.py:664
  42.9 0.9 %shard_map.100.refs_0_ = f32[128,128]{1,0:T(8,128)S(1)} custom-call(s32[1]{0:T(128)} %bitcast.me_ref, f32[512,128]{1,0:T(8,128)S(1)} %bitcast.19, s32[8,64]{1,0:T(8,128)S(1)} %bitcast.28, s32[8,64]{1,0:T(8,128)S(1)} %collective-permute-done.4.refs_1_, s32[8,64]{1,0:T(8,128)S(1)} %collective-permute-done.5.refs_2_, s32[8,64]{1,0:T(8,128)S(1)} %collective-permute-done.6.refs_3_), custom_call_target="tpu_custom_call" | custom-call | tf_op jit(solution)/shard_map/pallas_call | solution.py:32
  43.8 0.8 %collective-permute-start.11 = (f32[128,128]{1,0:T(8,128)S(1)}, f32[128,128]{1,0:T(8,128)S(1)}, u32[]{:S(2)}, u32[]{:S(2)}) collective-permute-start(f32[128,128]{1,0:T(8,128)S(1)} %shard_map.100.refs_0_), channel_id=1, source_target_pairs={{0,24},{8,16},{16,8},{24,0},{1,25},{9,17},{17,9},{25,1},{2,26},{10... | collective-permute-start | bytes 196616 | tf_op jit(solution)/shard_map/ppermute | solution.py:346
  44.7 1.2 %collective-permute-start.10 = (f32[128,128]{1,0:T(8,128)S(1)}, f32[128,128]{1,0:T(8,128)S(1)}, u32[]{:S(2)}, u32[]{:S(2)}) collective-permute-start(f32[128,128]{1,0:T(8,128)S(1)} %shard_map.100.refs_0_), channel_id=1, source_target_pairs={{0,16},{8,24},{16,0},{24,8},{1,17},{9,25},{17,1},{25,9},{2,18},{10... | collective-permute-start | bytes 196616 | tf_op jit(solution)/shard_map/ppermute | solution.py:346
  45.9 1.5 %collective-permute-start.9 = (f32[128,128]{1,0:T(8,128)S(1)}, f32[128,128]{1,0:T(8,128)S(1)}, u32[]{:S(2)}, u32[]{:S(2)}) collective-permute-start(f32[128,128]{1,0:T(8,128)S(1)} %shard_map.100.refs_0_), channel_id=1, source_target_pairs={{0,8},{8,0},{16,24},{24,16},{1,9},{9,1},{17,25},{25,17},{2,10},{10... | collective-permute-start | bytes 196616 | tf_op jit(solution)/shard_map/ppermute | solution.py:346
  47.4 1.6 %shard_map.99 = f32[3,2,256,128]{3,2,1,0:T(8,128)} custom-call(s32[1]{0:T(128)} %bitcast.1.place_ref, f32[3,2,272,128]{3,2,1,0:T(8,128)S(1)} %get-tuple-element.31.field_ref, f32[4,272,128]{2,1,0:T(8,128)S(1)} %get-tuple-element.32.coefs_ref, f32[3,1,256,128]{3,2,1,0:T(8,128)S(1)} %collective-permute-done.7.near_ref, ...), custom_call_target="tpu_custom_call" | custom-call | tf_op jit(solution)/shard_map/pallas_call | solution.py:32
  49.3 1.3 %collective-permute-done.10.refs_2_ = f32[128,128]{1,0:T(8,128)S(1)} collective-permute-done((f32[128,128]{1,0:T(8,128)S(1)}, f32[128,128]{1,0:T(8,128)S(1)}, u32[]{:S(2)}, u32[]{:S(2)}) %collective-permute-start.10) | collective-permute-done | bytes 65568 | tf_op jit(solution)/shard_map/ppermute | solution.py:346
  50.5 1.0 %shard_map.101 = f32[512,128]{1,0:T(8,128)} custom-call(s32[1]{0:T(128)} %bitcast.me_ref, f32[512,128]{1,0:T(8,128)S(1)} %copy-done, f32[128,128]{1,0:T(8,128)S(1)} %shard_map.100.refs_0_, f32[128,128]{1,0:T(8,128)S(1)} %collective-permute-done.9.refs_1_, f32[128,128]{1,0:T(8,128)S(1)} %collective-permute-done.10.refs_2_, ...), custom_call_target="tpu_custom_call" | custom-call | tf_op jit(solution)/shard_map/pallas_call | solution.py:32
  (17 shorter events, 0.3 us)
Async XLA Ops:
  2.8 16.1 %all-to-all-start = ((f32[8,64,128]{2,1,0:T(8,128)}), f32[8,64,128]{2,1,0:T(8,128)S(1)}, u32[]{:S(2)}, u32[]{:S(2)}) async-start(f32[8,64,128]{2,1,0:T(8,128)} %bitcast.8), calls=%async_computation | async-start | bytes 524288 | tf_op jit(solution)/shard_map/all_to_all | solution.py:606
  9.1 9.7 %copy-start.1 = (s32[1,512,8]{1,2,0:T(8,128)S(1)}, s32[1,512,8]{1,2,0:T(8,128)}, u32[]{:S(2)}) copy-start(s32[1,512,8]{1,2,0:T(8,128)} %param.13) | copy-start | bytes 49156
  13.5 21.8 %collective-permute-start = (f32[5,1,256,128]{3,2,1,0:T(8,128)}, f32[5,1,256,128]{3,2,1,0:T(8,128)}, u32[]{:S(2)}, u32[]{:S(2)}) collective-permute-start(f32[5,1,256,128]{3,2,1,0:T(8,128)} %get-tuple-element.29), channel_id=1, source_target_pairs={{0,1},{1,0},{2,3},{3,2},{4,5},{5,4},{6,7},{7,6},{8,9},{9,8},{10,11... | collective-permute-start | bytes 1966088 | tf_op jit(solution)/shard_map/ppermute | solution.py:351
  14.1 21.7 %collective-permute-start.1 = (f32[5,1,256,128]{3,2,1,0:T(8,128)}, f32[5,1,256,128]{3,2,1,0:T(8,128)}, u32[]{:S(2)}, u32[]{:S(2)}) collective-permute-start(f32[5,1,256,128]{3,2,1,0:T(8,128)} %get-tuple-element.30), channel_id=1, source_target_pairs={{1,2},{2,1},{3,4},{4,3},{5,6},{6,5},{9,10},{10,9},{11,12},{12,11},... | collective-permute-start | bytes 1966088 | tf_op jit(solution)/shard_map/ppermute | solution.py:356
  18.9 13.6 %copy-start.2 = (s32[1,1,8,64]{3,2,1,0:T(8,128)S(1)}, s32[1,1,8,64]{3,2,1,0:T(8,128)}, u32[]{:S(2)}) copy-start(s32[1,1,8,64]{3,2,1,0:T(8,128)} %param.12) | copy-start | bytes 6148
  25.8 10.2 %collective-permute-start.3 = (f32[2,256,128]{2,1,0:T(8,128)S(1)}, f32[2,256,128]{2,1,0:T(8,128)S(1)}, u32[]{:S(2)}, u32[]{:S(2)}) collective-permute-start(f32[2,256,128]{2,1,0:T(8,128)S(1)} %bitcast.20), channel_id=1, source_target_pairs={{1,2},{2,1},{3,4},{4,3},{5,6},{6,5},{9,10},{10,9},{11,12},{12,11},... | collective-permute-start | bytes 786440 | tf_op jit(solution)/shard_map/ppermute | solution.py:356
  26.5 9.6 %collective-permute-start.2 = (f32[2,256,128]{2,1,0:T(8,128)S(1)}, f32[2,256,128]{2,1,0:T(8,128)S(1)}, u32[]{:S(2)}, u32[]{:S(2)}) collective-permute-start(f32[2,256,128]{2,1,0:T(8,128)S(1)} %bitcast.21), channel_id=1, source_target_pairs={{0,1},{1,0},{2,3},{3,2},{4,5},{5,4},{6,7},{7,6},{8,9},{9,8},{10,11... | collective-permute-start | bytes 786440 | tf_op jit(solution)/shard_map/ppermute | solution.py:351
  28.1 14.8 %all-to-all-start.1 = ((f32[32,16,128]{2,1,0:T(8,128)}), f32[32,16,128]{2,1,0:T(8,128)S(1)}, u32[]{:S(2)}, u32[]{:S(2)}) async-start(f32[32,16,128]{2,1,0:T(8,128)} %bitcast.39), calls=%async_computation.1 | async-start | bytes 524288 | tf_op jit(solution)/shard_map/all_to_all | solution.py:664
  32.5 6.5 %collective-permute-start.6 = (s32[8,64]{1,0:T(8,128)S(1)}, s32[8,64]{1,0:T(8,128)S(1)}, u32[]{:S(2)}, u32[]{:S(2)}) collective-permute-start(s32[8,64]{1,0:T(8,128)S(1)} %bitcast.25), channel_id=1, source_target_pairs={{0,24},{8,16},{16,8},{24,0},{1,25},{9,17},{17,9},{25,1},{2,26},{10... | collective-permute-start | bytes 6152 | tf_op jit(solution)/shard_map/ppermute | solution.py:346
  35.2 3.8 %collective-permute-start.5 = (s32[8,64]{1,0:T(8,128)S(1)}, s32[8,64]{1,0:T(8,128)S(1)}, u32[]{:S(2)}, u32[]{:S(2)}) collective-permute-start(s32[8,64]{1,0:T(8,128)S(1)} %bitcast.26), channel_id=1, source_target_pairs={{0,16},{8,24},{16,0},{24,8},{1,17},{9,25},{17,1},{25,9},{2,18},{10... | collective-permute-start | bytes 6152 | tf_op jit(solution)/shard_map/ppermute | solution.py:346
  35.8 3.6 %collective-permute-start.4 = (s32[8,64]{1,0:T(8,128)S(1)}, s32[8,64]{1,0:T(8,128)S(1)}, u32[]{:S(2)}, u32[]{:S(2)}) collective-permute-start(s32[8,64]{1,0:T(8,128)S(1)} %bitcast.27), channel_id=1, source_target_pairs={{0,8},{8,0},{16,24},{24,16},{1,9},{9,1},{17,25},{25,17},{2,10},{10... | collective-permute-start | bytes 6152 | tf_op jit(solution)/shard_map/ppermute | solution.py:346
  39.0 11.6 %copy-start = (f32[512,128]{1,0:T(8,128)S(1)}, f32[512,128]{1,0:T(8,128)}, u32[]{:S(2)}) copy-start(f32[512,128]{1,0:T(8,128)} %template_ref.3) | copy-start | bytes 786436
  39.4 8.0 %collective-permute-start.7 = (f32[3,1,256,128]{3,2,1,0:T(8,128)S(1)}, f32[3,1,256,128]{3,2,1,0:T(8,128)S(1)}, u32[]{:S(2)}, u32[]{:S(2)}) collective-permute-start(f32[3,1,256,128]{3,2,1,0:T(8,128)S(1)} %get-tuple-element.36), channel_id=1, source_target_pairs={{0,1},{1,0},{2,3},{3,2},{4,5},{5,4},{6,7},{7,6},{8,9},{9,8},{10,11... | collective-permute-start | bytes 1179656 | tf_op jit(solution)/shard_map/ppermute | solution.py:351
  39.4 8.0 %collective-permute-start.8 = (f32[3,1,256,128]{3,2,1,0:T(8,128)S(1)}, f32[3,1,256,128]{3,2,1,0:T(8,128)S(1)}, u32[]{:S(2)}, u32[]{:S(2)}) collective-permute-start(f32[3,1,256,128]{3,2,1,0:T(8,128)S(1)} %get-tuple-element.37), channel_id=1, source_target_pairs={{1,2},{2,1},{3,4},{4,3},{5,6},{6,5},{9,10},{10,9},{11,12},{12,11},... | collective-permute-start | bytes 1179656 | tf_op jit(solution)/shard_map/ppermute | solution.py:356
  43.8 5.4 %collective-permute-start.11 = (f32[128,128]{1,0:T(8,128)S(1)}, f32[128,128]{1,0:T(8,128)S(1)}, u32[]{:S(2)}, u32[]{:S(2)}) collective-permute-start(f32[128,128]{1,0:T(8,128)S(1)} %shard_map.100.refs_0_), channel_id=1, source_target_pairs={{0,24},{8,16},{16,8},{24,0},{1,25},{9,17},{17,9},{25,1},{2,26},{10... | collective-permute-start | bytes 196616 | tf_op jit(solution)/shard_map/ppermute | solution.py:346
  44.7 5.9 %collective-permute-start.10 = (f32[128,128]{1,0:T(8,128)S(1)}, f32[128,128]{1,0:T(8,128)S(1)}, u32[]{:S(2)}, u32[]{:S(2)}) collective-permute-start(f32[128,128]{1,0:T(8,128)S(1)} %shard_map.100.refs_0_), channel_id=1, source_target_pairs={{0,16},{8,24},{16,0},{24,8},{1,17},{9,25},{17,1},{25,9},{2,18},{10... | collective-permute-start | bytes 196616 | tf_op jit(solution)/shard_map/ppermute | solution.py:346
  45.9 4.7 %collective-permute-start.9 = (f32[128,128]{1,0:T(8,128)S(1)}, f32[128,128]{1,0:T(8,128)S(1)}, u32[]{:S(2)}, u32[]{:S(2)}) collective-permute-start(f32[128,128]{1,0:T(8,128)S(1)} %shard_map.100.refs_0_), channel_id=1, source_target_pairs={{0,8},{8,0},{16,24},{24,16},{1,9},{9,1},{17,25},{25,17},{2,10},{10... | collective-permute-start | bytes 196616 | tf_op jit(solution)/shard_map/ppermute | solution.py:346

commit v12 on v11

--- a/solution.py
+++ b/solution.py
@@ -532,10 +532,12 @@
     for copy in (copies[0], copies[3], copies[4]):
         copy.wait()
     weights = all_weights(coefs_ref)
-    for copy in copies[1:3] + copies[5:]:
+    for copy in (copies[1], copies[5], copies[6]):
         copy.wait()
-    for p in range(planes + 2):
-        force = forces(p, images[p])
+    every_force = [forces(p, images[p]) for p in range(planes + 2)]
+    for copy in (copies[2], copies[7], copies[8]):
+        copy.wait()
+    for p, force in enumerate(every_force):
         for a in range(parts):
             if p == 0:
                 outer[a, 0] = outer[a, 0] - force[a]

time: 52 us -> 52 us (level)
  transfers between devices with their start and end apart: 14 -> 14, of which waited for: 6 -> 5; matrix products, arithmetic and copies ran while one was open for 0% -> 0% of each run, Pallas kernels for 32% -> 33%
where the time goes in v12:
time: 52 us; the launch traced here: 51.6 us
  starting transfers between devices  22.9 us (44%)
  Pallas kernels  20 us (38%)
  waiting for transfers between devices  7.93 us (15%)
  between operations  0.75 us (1%)
    pallas_call x7, Pallas kernels, call(): pl.pallas_call(kernel, out_shape=tuple(shapes) if many else shapes[0], in...  20 us
    ppermute x6, starting transfers between devices, over_subjects(): lax.ppermute(values, 'subj', [(i, i ^ d) for i in range(count)])  7.13 us
    all_to_all x1, starting transfers between devices, per_device(): lax.all_to_all(sending, 'slab', split_axis=0, concat_axis=0, tiled=True)  6.34 us
    all_to_all x1, starting transfers between devices, per_device(): lax.all_to_all(sent, ('subj', 'slab'), split_axis=0, concat_axis=0, tiled...  4.39 us
    all_to_all x1, waiting for transfers between devices, per_device(): lax.all_to_all(sending, 'slab', split_axis=0, concat_axis=0, tiled=True)  3.32 us
    ppermute x3, starting transfers between devices, swap_far(): lax.ppermute(values, 'slab', [(i, i + 1 if i % 2 else i - 1) for i in ran...  2.86 us
    all_to_all x1, waiting for transfers between devices, per_device(): lax.all_to_all(sent, ('subj', 'slab'), split_axis=0, concat_axis=0, tiled...  2.75 us
    ppermute x3, starting transfers between devices, swap_near(): lax.ppermute(values, 'slab', [(i, i ^ 1) for i in range(lax.axis_size('sl...  2.15 us
  transfers between devices with their start and end apart: 14, of which 5 were waited for; matrix products, arithmetic and copies ran while one was open for 0% of the time, Pallas kernels for 33%

profile of v12, /device:TPU:0, one launch (start us, length us, event | category | flops | bytes accessed | tf_op | source)
XLA Modules:
  0.0 51.6 jit_solution(9914484818678515079)
XLA Ops:
  0.6 2.2 %shard_map.95 = f32[512,128]{1,0:T(8,128)} custom-call(s32[8,64]{1,0:T(8,128)} %bitcast.24, f32[512,128]{1,0:T(8,128)} %template_ref.3), custom_call_target="tpu_custom_call" | custom-call | tf_op jit(solution)/shard_map/pallas_call | solution.py:32
  2.8 6.3 %all-to-all-start = ((f32[8,64,128]{2,1,0:T(8,128)}), f32[8,64,128]{2,1,0:T(8,128)S(1)}, u32[]{:S(2)}, u32[]{:S(2)}) async-start(f32[8,64,128]{2,1,0:T(8,128)} %bitcast.8), calls=%async_computation | async-start | bytes 524288 | tf_op jit(solution)/shard_map/all_to_all | solution.py:608
  9.1 4.3 %shard_map.96 = (bf16[1,8,5,128,128]{4,3,2,1,0:T(8,128)(2,1)S(1)}, bf16[3,8,5,128,128]{4,3,2,1,0:T(8,128)(2,1)}, f32[5,1,256,128]{3,2,1,0:T(8,128)}, f32[5,1,256,128]{3,2,1,0:T(8,128)}) custom-call(s32[1]{0:T(128)} %bitcast.1.place_ref, s32[4096,128]{1,0:T(8,128)} %bitcast.34, bf16[4096,128]{1,0:T(8,128)(2,1)} %bitcast.35, f32[3,2,256,128]{3,2,1,0:T(8,128)} %bitcast.29, ...), custom_call_target="tpu_custom_call" | custom-call | tf_op jit(solution)/shard_map/pallas_call | solution.py:32
  13.5 0.6 %collective-permute-start = (f32[5,1,256,128]{3,2,1,0:T(8,128)}, f32[5,1,256,128]{3,2,1,0:T(8,128)}, u32[]{:S(2)}, u32[]{:S(2)}) collective-permute-start(f32[5,1,256,128]{3,2,1,0:T(8,128)} %get-tuple-element.29), channel_id=1, source_target_pairs={{0,1},{1,0},{2,3},{3,2},{4,5},{5,4},{6,7},{7,6},{8,9},{9,8},{10,11... | collective-permute-start | bytes 1966088 | tf_op jit(solution)/shard_map/ppermute | solution.py:351
  14.1 1.5 %collective-permute-start.1 = (f32[5,1,256,128]{3,2,1,0:T(8,128)}, f32[5,1,256,128]{3,2,1,0:T(8,128)}, u32[]{:S(2)}, u32[]{:S(2)}) collective-permute-start(f32[5,1,256,128]{3,2,1,0:T(8,128)} %get-tuple-element.30), channel_id=1, source_target_pairs={{1,2},{2,1},{3,4},{4,3},{5,6},{6,5},{9,10},{10,9},{11,12},{12,11},... | collective-permute-start | bytes 1966088 | tf_op jit(solution)/shard_map/ppermute | solution.py:356
  15.6 3.3 %all-to-all-done = f32[8,64,128]{2,1,0:T(8,128)S(1)} async-done(((f32[8,64,128]{2,1,0:T(8,128)}), f32[8,64,128]{2,1,0:T(8,128)S(1)}, u32[]{:S(2)}, u32[]{:S(2)}) %all-to-all-start) | async-done | bytes 262176 | tf_op jit(solution)/shard_map/all_to_all | solution.py:608
  18.9 6.9 %shard_map.97 = (f32[512,128]{1,0:T(8,128)S(1)}, f32[512,128]{1,0:T(8,128)}) custom-call(s32[8,512]{1,0:T(8,128)S(1)} %bitcast.23, f32[512,128]{1,0:T(8,128)S(1)} %bitcast.18, bf16[1,8,5,128,128]{4,3,2,1,0:T(8,128)(2,1)S(1)} %get-tuple-element.25.kept_ref, bf16[3,8,5,128,128]{4,3,2,1,0:T(8,128)(2,1)} %get-tuple-element.26.moved_ref, f32[512,128]{1,0:T(8,128)} %bitcast.32), custom_call_target="tpu_custom_call" | custom-call | tf_op jit(solution)/shard_map/pallas_call | solution.py:32
  25.8 0.7 %collective-permute-start.3 = (f32[2,256,128]{2,1,0:T(8,128)S(1)}, f32[2,256,128]{2,1,0:T(8,128)S(1)}, u32[]{:S(2)}, u32[]{:S(2)}) collective-permute-start(f32[2,256,128]{2,1,0:T(8,128)S(1)} %bitcast.20), channel_id=1, source_target_pairs={{1,2},{2,1},{3,4},{4,3},{5,6},{6,5},{9,10},{10,9},{11,12},{12,11},... | collective-permute-start | bytes 786440 | tf_op jit(solution)/shard_map/ppermute | solution.py:356
  26.5 1.6 %collective-permute-start.2 = (f32[2,256,128]{2,1,0:T(8,128)S(1)}, f32[2,256,128]{2,1,0:T(8,128)S(1)}, u32[]{:S(2)}, u32[]{:S(2)}) collective-permute-start(f32[2,256,128]{2,1,0:T(8,128)S(1)} %bitcast.21), channel_id=1, source_target_pairs={{0,1},{1,0},{2,3},{3,2},{4,5},{5,4},{6,7},{7,6},{8,9},{9,8},{10,11... | collective-permute-start | bytes 786440 | tf_op jit(solution)/shard_map/ppermute | solution.py:351
  28.1 4.4 %all-to-all-start.1 = ((f32[32,16,128]{2,1,0:T(8,128)}), f32[32,16,128]{2,1,0:T(8,128)S(1)}, u32[]{:S(2)}, u32[]{:S(2)}) async-start(f32[32,16,128]{2,1,0:T(8,128)} %bitcast.39), calls=%async_computation.1 | async-start | bytes 524288 | tf_op jit(solution)/shard_map/all_to_all | solution.py:666
  32.5 2.7 %collective-permute-start.6 = (s32[8,64]{1,0:T(8,128)S(1)}, s32[8,64]{1,0:T(8,128)S(1)}, u32[]{:S(2)}, u32[]{:S(2)}) collective-permute-start(s32[8,64]{1,0:T(8,128)S(1)} %bitcast.25), channel_id=1, source_target_pairs={{0,24},{8,16},{16,8},{24,0},{1,25},{9,17},{17,9},{25,1},{2,26},{10... | collective-permute-start | bytes 6152 | tf_op jit(solution)/shard_map/ppermute | solution.py:346
  35.2 0.6 %collective-permute-start.5 = (s32[8,64]{1,0:T(8,128)S(1)}, s32[8,64]{1,0:T(8,128)S(1)}, u32[]{:S(2)}, u32[]{:S(2)}) collective-permute-start(s32[8,64]{1,0:T(8,128)S(1)} %bitcast.26), channel_id=1, source_target_pairs={{0,16},{8,24},{16,0},{24,8},{1,17},{9,25},{17,1},{25,9},{2,18},{10... | collective-permute-start | bytes 6152 | tf_op jit(solution)/shard_map/ppermute | solution.py:346
  35.8 0.3 collective-permute-start.4
  36.1 3.0 %shard_map.98 = (f32[3,2,272,128]{3,2,1,0:T(8,128)S(1)}, f32[4,272,128]{2,1,0:T(8,128)S(1)}, f32[3,1,256,128]{3,2,1,0:T(8,128)S(1)}, f32[3,1,256,128]{3,2,1,0:T(8,128)S(1)}) custom-call(s32[1]{0:T(128)} %bitcast.1.place_ref, f32[3,2,256,128]{3,2,1,0:T(8,128)} %bitcast.30, f32[2,256,128]{2,1,0:T(8,128)} %bitcast.33, f32[2,256,128]{2,1,0:T(8,128)} %bitcast.37, ...), custom_call_target="tpu_custom_call" | custom-call | tf_op jit(solution)/shard_map/pallas_call | solution.py:32
  39.1 0.4 collective-permute-done.4.refs_1_
  39.4 0.7 %collective-permute-start.8 = (f32[3,1,256,128]{3,2,1,0:T(8,128)S(1)}, f32[3,1,256,128]{3,2,1,0:T(8,128)S(1)}, u32[]{:S(2)}, u32[]{:S(2)}) collective-permute-start(f32[3,1,256,128]{3,2,1,0:T(8,128)S(1)} %get-tuple-element.37), channel_id=1, source_target_pairs={{1,2},{2,1},{3,4},{4,3},{5,6},{6,5},{9,10},{10,9},{11,12},{12,11},... | collective-permute-start | bytes 1179656 | tf_op jit(solution)/shard_map/ppermute | solution.py:356
  40.1 2.7 %all-to-all-done.1 = f32[32,16,128]{2,1,0:T(8,128)S(1)} async-done(((f32[32,16,128]{2,1,0:T(8,128)}), f32[32,16,128]{2,1,0:T(8,128)S(1)}, u32[]{:S(2)}, u32[]{:S(2)}) %all-to-all-start.1) | async-done | bytes 262176 | tf_op jit(solution)/shard_map/all_to_all | solution.py:666
  42.9 0.9 %shard_map.100.refs_0_ = f32[128,128]{1,0:T(8,128)S(1)} custom-call(s32[1]{0:T(128)} %bitcast.me_ref, f32[512,128]{1,0:T(8,128)S(1)} %bitcast.19, s32[8,64]{1,0:T(8,128)S(1)} %bitcast.28, s32[8,64]{1,0:T(8,128)S(1)} %collective-permute-done.4.refs_1_, s32[8,64]{1,0:T(8,128)S(1)} %collective-permute-done.5.refs_2_, s32[8,64]{1,0:T(8,128)S(1)} %collective-permute-done.6.refs_3_), custom_call_target="tpu_custom_call" | custom-call | tf_op jit(solution)/shard_map/pallas_call | solution.py:32
  43.8 0.8 %collective-permute-start.11 = (f32[128,128]{1,0:T(8,128)S(1)}, f32[128,128]{1,0:T(8,128)S(1)}, u32[]{:S(2)}, u32[]{:S(2)}) collective-permute-start(f32[128,128]{1,0:T(8,128)S(1)} %shard_map.100.refs_0_), channel_id=1, source_target_pairs={{0,24},{8,16},{16,8},{24,0},{1,25},{9,17},{17,9},{25,1},{2,26},{10... | collective-permute-start | bytes 196616 | tf_op jit(solution)/shard_map/ppermute | solution.py:346
  44.7 1.2 %collective-permute-start.10 = (f32[128,128]{1,0:T(8,128)S(1)}, f32[128,128]{1,0:T(8,128)S(1)}, u32[]{:S(2)}, u32[]{:S(2)}) collective-permute-start(f32[128,128]{1,0:T(8,128)S(1)} %shard_map.100.refs_0_), channel_id=1, source_target_pairs={{0,16},{8,24},{16,0},{24,8},{1,17},{9,25},{17,1},{25,9},{2,18},{10... | collective-permute-start | bytes 196616 | tf_op jit(solution)/shard_map/ppermute | solution.py:346
  45.9 1.5 %collective-permute-start.9 = (f32[128,128]{1,0:T(8,128)S(1)}, f32[128,128]{1,0:T(8,128)S(1)}, u32[]{:S(2)}, u32[]{:S(2)}) collective-permute-start(f32[128,128]{1,0:T(8,128)S(1)} %shard_map.100.refs_0_), channel_id=1, source_target_pairs={{0,8},{8,0},{16,24},{24,16},{1,9},{9,1},{17,25},{25,17},{2,10},{10... | collective-permute-start | bytes 196616 | tf_op jit(solution)/shard_map/ppermute | solution.py:346
  47.4 1.6 %shard_map.99 = f32[3,2,256,128]{3,2,1,0:T(8,128)} custom-call(s32[1]{0:T(128)} %bitcast.1.place_ref, f32[3,2,272,128]{3,2,1,0:T(8,128)S(1)} %get-tuple-element.31.field_ref, f32[4,272,128]{2,1,0:T(8,128)S(1)} %get-tuple-element.32.coefs_ref, f32[3,1,256,128]{3,2,1,0:T(8,128)S(1)} %collective-permute-done.7.near_ref, ...), custom_call_target="tpu_custom_call" | custom-call | tf_op jit(solution)/shard_map/pallas_call | solution.py:32
  49.3 1.3 %collective-permute-done.10.refs_2_ = f32[128,128]{1,0:T(8,128)S(1)} collective-permute-done((f32[128,128]{1,0:T(8,128)S(1)}, f32[128,128]{1,0:T(8,128)S(1)}, u32[]{:S(2)}, u32[]{:S(2)}) %collective-permute-start.10) | collective-permute-done | bytes 65568 | tf_op jit(solution)/shard_map/ppermute | solution.py:346
  50.5 1.0 %shard_map.101 = f32[512,128]{1,0:T(8,128)} custom-call(s32[1]{0:T(128)} %bitcast.me_ref, f32[512,128]{1,0:T(8,128)S(1)} %copy-done, f32[128,128]{1,0:T(8,128)S(1)} %shard_map.100.refs_0_, f32[128,128]{1,0:T(8,128)S(1)} %collective-permute-done.9.refs_1_, f32[128,128]{1,0:T(8,128)S(1)} %collective-permute-done.10.refs_2_, ...), custom_call_target="tpu_custom_call" | custom-call | tf_op jit(solution)/shard_map/pallas_call | solution.py:32
  (17 shorter events, 0.2 us)
Async XLA Ops:
  2.8 16.1 %all-to-all-start = ((f32[8,64,128]{2,1,0:T(8,128)}), f32[8,64,128]{2,1,0:T(8,128)S(1)}, u32[]{:S(2)}, u32[]{:S(2)}) async-start(f32[8,64,128]{2,1,0:T(8,128)} %bitcast.8), calls=%async_computation | async-start | bytes 524288 | tf_op jit(solution)/shard_map/all_to_all | solution.py:608
  9.1 9.7 %copy-start.1 = (s32[1,512,8]{1,2,0:T(8,128)S(1)}, s32[1,512,8]{1,2,0:T(8,128)}, u32[]{:S(2)}) copy-start(s32[1,512,8]{1,2,0:T(8,128)} %param.13) | copy-start | bytes 49156
  13.5 21.8 %collective-permute-start = (f32[5,1,256,128]{3,2,1,0:T(8,128)}, f32[5,1,256,128]{3,2,1,0:T(8,128)}, u32[]{:S(2)}, u32[]{:S(2)}) collective-permute-start(f32[5,1,256,128]{3,2,1,0:T(8,128)} %get-tuple-element.29), channel_id=1, source_target_pairs={{0,1},{1,0},{2,3},{3,2},{4,5},{5,4},{6,7},{7,6},{8,9},{9,8},{10,11... | collective-permute-start | bytes 1966088 | tf_op jit(solution)/shard_map/ppermute | solution.py:351
  14.1 21.7 %collective-permute-start.1 = (f32[5,1,256,128]{3,2,1,0:T(8,128)}, f32[5,1,256,128]{3,2,1,0:T(8,128)}, u32[]{:S(2)}, u32[]{:S(2)}) collective-permute-start(f32[5,1,256,128]{3,2,1,0:T(8,128)} %get-tuple-element.30), channel_id=1, source_target_pairs={{1,2},{2,1},{3,4},{4,3},{5,6},{6,5},{9,10},{10,9},{11,12},{12,11},... | collective-permute-start | bytes 1966088 | tf_op jit(solution)/shard_map/ppermute | solution.py:356
  18.9 13.6 %copy-start.2 = (s32[1,1,8,64]{3,2,1,0:T(8,128)S(1)}, s32[1,1,8,64]{3,2,1,0:T(8,128)}, u32[]{:S(2)}) copy-start(s32[1,1,8,64]{3,2,1,0:T(8,128)} %param.12) | copy-start | bytes 6148
  25.8 10.2 %collective-permute-start.3 = (f32[2,256,128]{2,1,0:T(8,128)S(1)}, f32[2,256,128]{2,1,0:T(8,128)S(1)}, u32[]{:S(2)}, u32[]{:S(2)}) collective-permute-start(f32[2,256,128]{2,1,0:T(8,128)S(1)} %bitcast.20), channel_id=1, source_target_pairs={{1,2},{2,1},{3,4},{4,3},{5,6},{6,5},{9,10},{10,9},{11,12},{12,11},... | collective-permute-start | bytes 786440 | tf_op jit(solution)/shard_map/ppermute | solution.py:356
  26.5 9.6 %collective-permute-start.2 = (f32[2,256,128]{2,1,0:T(8,128)S(1)}, f32[2,256,128]{2,1,0:T(8,128)S(1)}, u32[]{:S(2)}, u32[]{:S(2)}) collective-permute-start(f32[2,256,128]{2,1,0:T(8,128)S(1)} %bitcast.21), channel_id=1, source_target_pairs={{0,1},{1,0},{2,3},{3,2},{4,5},{5,4},{6,7},{7,6},{8,9},{9,8},{10,11... | collective-permute-start | bytes 786440 | tf_op jit(solution)/shard_map/ppermute | solution.py:351
  28.1 14.8 %all-to-all-start.1 = ((f32[32,16,128]{2,1,0:T(8,128)}), f32[32,16,128]{2,1,0:T(8,128)S(1)}, u32[]{:S(2)}, u32[]{:S(2)}) async-start(f32[32,16,128]{2,1,0:T(8,128)} %bitcast.39), calls=%async_computation.1 | async-start | bytes 524288 | tf_op jit(solution)/shard_map/all_to_all | solution.py:666
  32.5 6.5 %collective-permute-start.6 = (s32[8,64]{1,0:T(8,128)S(1)}, s32[8,64]{1,0:T(8,128)S(1)}, u32[]{:S(2)}, u32[]{:S(2)}) collective-permute-start(s32[8,64]{1,0:T(8,128)S(1)} %bitcast.25), channel_id=1, source_target_pairs={{0,24},{8,16},{16,8},{24,0},{1,25},{9,17},{17,9},{25,1},{2,26},{10... | collective-permute-start | bytes 6152 | tf_op jit(solution)/shard_map/ppermute | solution.py:346
  35.2 3.8 %collective-permute-start.5 = (s32[8,64]{1,0:T(8,128)S(1)}, s32[8,64]{1,0:T(8,128)S(1)}, u32[]{:S(2)}, u32[]{:S(2)}) collective-permute-start(s32[8,64]{1,0:T(8,128)S(1)} %bitcast.26), channel_id=1, source_target_pairs={{0,16},{8,24},{16,0},{24,8},{1,17},{9,25},{17,1},{25,9},{2,18},{10... | collective-permute-start | bytes 6152 | tf_op jit(solution)/shard_map/ppermute | solution.py:346
  35.8 3.6 %collective-permute-start.4 = (s32[8,64]{1,0:T(8,128)S(1)}, s32[8,64]{1,0:T(8,128)S(1)}, u32[]{:S(2)}, u32[]{:S(2)}) collective-permute-start(s32[8,64]{1,0:T(8,128)S(1)} %bitcast.27), channel_id=1, source_target_pairs={{0,8},{8,0},{16,24},{24,16},{1,9},{9,1},{17,25},{25,17},{2,10},{10... | collective-permute-start | bytes 6152 | tf_op jit(solution)/shard_map/ppermute | solution.py:346
  39.0 11.5 %copy-start = (f32[512,128]{1,0:T(8,128)S(1)}, f32[512,128]{1,0:T(8,128)}, u32[]{:S(2)}) copy-start(f32[512,128]{1,0:T(8,128)} %template_ref.3) | copy-start | bytes 786436
  39.4 8.0 %collective-permute-start.7 = (f32[3,1,256,128]{3,2,1,0:T(8,128)S(1)}, f32[3,1,256,128]{3,2,1,0:T(8,128)S(1)}, u32[]{:S(2)}, u32[]{:S(2)}) collective-permute-start(f32[3,1,256,128]{3,2,1,0:T(8,128)S(1)} %get-tuple-element.36), channel_id=1, source_target_pairs={{0,1},{1,0},{2,3},{3,2},{4,5},{5,4},{6,7},{7,6},{8,9},{9,8},{10,11... | collective-permute-start | bytes 1179656 | tf_op jit(solution)/shard_map/ppermute | solution.py:351
  39.4 8.0 %collective-permute-start.8 = (f32[3,1,256,128]{3,2,1,0:T(8,128)S(1)}, f32[3,1,256,128]{3,2,1,0:T(8,128)S(1)}, u32[]{:S(2)}, u32[]{:S(2)}) collective-permute-start(f32[3,1,256,128]{3,2,1,0:T(8,128)S(1)} %get-tuple-element.37), channel_id=1, source_target_pairs={{1,2},{2,1},{3,4},{4,3},{5,6},{6,5},{9,10},{10,9},{11,12},{12,11},... | collective-permute-start | bytes 1179656 | tf_op jit(solution)/shard_map/ppermute | solution.py:356
  43.8 5.4 %collective-permute-start.11 = (f32[128,128]{1,0:T(8,128)S(1)}, f32[128,128]{1,0:T(8,128)S(1)}, u32[]{:S(2)}, u32[]{:S(2)}) collective-permute-start(f32[128,128]{1,0:T(8,128)S(1)} %shard_map.100.refs_0_), channel_id=1, source_target_pairs={{0,24},{8,16},{16,8},{24,0},{1,25},{9,17},{17,9},{25,1},{2,26},{10... | collective-permute-start | bytes 196616 | tf_op jit(solution)/shard_map/ppermute | solution.py:346
  44.7 5.9 %collective-permute-start.10 = (f32[128,128]{1,0:T(8,128)S(1)}, f32[128,128]{1,0:T(8,128)S(1)}, u32[]{:S(2)}, u32[]{:S(2)}) collective-permute-start(f32[128,128]{1,0:T(8,128)S(1)} %shard_map.100.refs_0_), channel_id=1, source_target_pairs={{0,16},{8,24},{16,0},{24,8},{1,17},{9,25},{17,1},{25,9},{2,18},{10... | collective-permute-start | bytes 196616 | tf_op jit(solution)/shard_map/ppermute | solution.py:346
  45.9 4.7 %collective-permute-start.9 = (f32[128,128]{1,0:T(8,128)S(1)}, f32[128,128]{1,0:T(8,128)S(1)}, u32[]{:S(2)}, u32[]{:S(2)}) collective-permute-start(f32[128,128]{1,0:T(8,128)S(1)} %shard_map.100.refs_0_), channel_id=1, source_target_pairs={{0,8},{8,0},{16,24},{24,16},{1,9},{9,1},{17,25},{25,17},{2,10},{10... | collective-permute-start | bytes 196616 | tf_op jit(solution)/shard_map/ppermute | solution.py:346
